TPU v7x, 128 devices: a whole 4x4x4 slice. The times are simulated.
128 devices in a mesh: role: 2 (over y_lo), grp: 16 (over x, z), tp: 4 (over y_hi, core).
Axes of the slice: x: 4, y: 4 (y_hi: 2, y_lo: 2; y = y_hi * 2 + y_lo), z: 4, core: 2. Of those that a mesh axis runs over, the one named last changes fastest.
Arguments:
- q_latent: bfloat16 [1024, 64, 576], P(('role', 'grp', 'tp')), may hold values from -60 to 60
- kv_new: bfloat16 [1024, 576], P(('role', 'grp', 'tp')), may hold values from -6 to 6
- kv_cache: bfloat16 [1024, 1024, 576], P(('role', 'grp', 'tp')), may hold values from -6 to 6
- lengths: int32 [1024], P(('role', 'grp', 'tp')), may hold values from 2 to 1024, as said below
- members: int32 [1024], P(('role', 'grp', 'tp')), may hold values from 0 to 7, as said below
- hidden_in: bfloat16 [1024, 7168], P('role', 'grp'), may hold values from -40 to 40
- w_uv: bfloat16 [64, 512, 128], P('tp'), may hold values from -1.5 to 1.5
- w_o: bfloat16 [8192, 7168], P('tp', 'grp'), may hold values from -0.0625 to 0.0625
- norm_gain: bfloat16 [7168], P('grp'), may hold values from 0.5 to 1.5
- w_gate: bfloat16 [7168, 18432], P('grp', ('role', 'tp')), may hold values from -0.09375 to 0.09375
- w_up: bfloat16 [7168, 18432], P('grp', ('role', 'tp')), may hold values from -0.0625 to 0.0625
- w_down: bfloat16 [18432, 7168], P(('role', 'tp'), 'grp'), may hold values from -0.046875 to 0.046875
Outputs:
- layer_out: bfloat16 [1024, 7168], P(('role', 'grp'))
Inputs may be any that keep to these rules, and one draw needn't show every extreme that they name: `lengths`: each request's cache is valid at positions 0 to its length - 1. Within each aligned block of 8 tokens, members is a permutation of 0 to 7.
All inputs are finite; a program needn't handle non-finite values.
Results may differ from a plain program's by a relative error of at most 0.017.
Values may be sent and summed in bfloat16 or wider, within the bound.
No kernel may reach another device: no remote copies, remote signals or barrier semaphores. Data moves between devices by JAX's collectives and lax.ppermute only.
A program may use at most 128 MiB of HBM per device.

v0:
```python
import functools

import jax
import jax.numpy as jnp
from jax import lax
from jax.experimental import pallas as pl
from jax.experimental.pallas import tpu as pltpu
from jax.sharding import PartitionSpec as P

epsilon = 1e-06
VMEM_LIMIT = 48 * 1024 * 1024


SHIFTS = (0, 1, -1, 2)
FACING = (0, 2, 1, 3)


def attend_kernel(scale, latent, members_ref, lengths_ref, q_ref, new_ref, kv_ref, out_ref):
    token = pl.program_id(0)
    length = lengths_ref[members_ref[token]]
    queries = q_ref[0]
    cache = kv_ref[0]
    newest = new_ref[0]
    scores = scale * jnp.dot(queries, cache, preferred_element_type=jnp.float32)
    own = scale * jnp.sum(queries.astype(jnp.float32) * newest, axis=1, keepdims=True)
    usable = lax.broadcasted_iota(jnp.int32, scores.shape, 1) < length
    scores = jnp.where(usable, scores, -1e30)
    peak = jnp.maximum(jnp.max(scores, axis=1, keepdims=True), own)
    probs = jnp.exp(scores - peak).astype(jnp.bfloat16)
    self_weight = jnp.exp(own - peak)
    denom = jnp.sum(probs.astype(jnp.float32), axis=1, keepdims=True) + self_weight
    accum = lax.dot_general(
        probs, cache[:latent], (((1,), (1,)), ((), ())), preferred_element_type=jnp.float32
    )
    accum = accum + self_weight * newest[:, :latent]
    out_ref[...] = (accum / denom).astype(out_ref.dtype).reshape(out_ref.shape)


def attend(q_latent, kv_new, kv_cache, lengths, members, scale, latent, splits):
    tokens, heads, kv = q_latent.shape
    ctx = kv_cache.shape[1]
    grid_spec = pltpu.PrefetchScalarGridSpec(
        num_scalar_prefetch=2,
        grid=(tokens,),
        in_specs=[
            pl.BlockSpec((1, heads, kv), lambda t, m, n: (t, 0, 0)),
            pl.BlockSpec((1, 1, kv), lambda t, m, n: (t, 0, 0)),
            pl.BlockSpec((1, kv, ctx), lambda t, m, n: (m[t], 0, 0)),
        ],
        out_specs=pl.BlockSpec((splits, 1, heads // splits, latent), lambda t, m, n: (0, t, 0, 0)),
    )
    return pl.pallas_call(
        functools.partial(attend_kernel, scale, latent),
        grid_spec=grid_spec,
        out_shape=jax.ShapeDtypeStruct((splits, tokens, heads // splits, latent), jnp.bfloat16),
        compiler_params=pltpu.CompilerParams(vmem_limit_bytes=VMEM_LIMIT),
        name="attend",
    )(
        members,
        lengths,
        q_latent,
        kv_new.astype(jnp.float32)[:, None, :],
        jnp.swapaxes(kv_cache, 1, 2),
    )


def partial_kernel(jobs, squares, half, *refs):
    count = 1 + max(rows for pieces in jobs for rows, _ in pieces)
    row_refs, gain_ref, weight_ref, outs = (
        refs[:count],
        refs[count],
        refs[count + 1],
        refs[count + 2 :],
    )
    gain = gain_ref[...]
    ready = []
    for ref in row_refs:
        x = ref[...].reshape(-1, ref.shape[-1]).astype(jnp.float32)
        ready.append(((x * gain).astype(jnp.bfloat16), jnp.sum(x * x, axis=1, keepdims=True)))
    for pieces, out in zip(jobs, outs):
        start = 0
        for rows, side in pieces:
            scaled, square = ready[rows]
            out[:, start : start + half] = jnp.dot(
                scaled,
                weight_ref[:, side * half : (side + 1) * half],
                preferred_element_type=jnp.float32,
            ).astype(jnp.bfloat16)
            start += half
            if squares and side == 0:
                high = square.astype(jnp.bfloat16).astype(jnp.float32)
                lane = lax.broadcasted_iota(jnp.int32, (scaled.shape[0], 128), 1)
                out[:, start : start + 128] = jnp.where(lane < 64, high, square - high).astype(
                    jnp.bfloat16
                )
                start += 128


def partial_sums(rows, axis, places, gain, weight, jobs, squares):
    _, _, per_group, width = rows.shape
    hidden = weight.shape[1]
    half = hidden // 2
    count = 4 * per_group
    whole = lambda i: (0, 0)
    block = (4, 1, per_group, width) if axis == 1 else (1, 4, per_group, width)

    def at(place):
        return lambda i: (0, place, 0, 0) if axis == 1 else (place, 0, 0, 0)

    widths = [
        sum(half + (128 if squares and side == 0 else 0) for _, side in pieces) for pieces in jobs
    ]
    return pl.pallas_call(
        functools.partial(partial_kernel, jobs, squares, half),
        grid=(1,),
        in_specs=[pl.BlockSpec(block, at(p)) for p in places]
        + [pl.BlockSpec((1, width), whole), pl.BlockSpec((width, hidden), whole)],
        out_specs=[pl.BlockSpec((count, w), whole) for w in widths],
        out_shape=[jax.ShapeDtypeStruct((count, w), jnp.bfloat16) for w in widths],
        compiler_params=pltpu.CompilerParams(vmem_limit_bytes=VMEM_LIMIT),
        cost_estimate=pl.CostEstimate(
            flops=2 * count * width * sum(widths),
            bytes_accessed=2 * (width * hidden + count * sum(widths)),
            transcendentals=0,
        ),
        name="partial_sums",
    )(*([rows] * len(places)), gain, weight)


def scatter_step(plus, minus, ahead_a, behind_c, shift):
    wide_a, wide_c = ahead_a.shape[1], behind_c.shape[1]
    plus, minus = shift(plus, 1), shift(minus, -1)
    relay_a = shift(add(ahead_a, plus[:, :wide_a]).astype(jnp.bfloat16), 1)
    relay_c = shift(add(behind_c, minus[:, :wide_c]).astype(jnp.bfloat16), -1)
    return plus, minus, relay_a, relay_c


def merge_kernel(
    own_a, own_c, plus, minus, relay_a, relay_c, plus2, minus2, ahead_a2, behind_c2, own_a2, own_c2
):
    wide_a, wide_c = own_a.shape[1], own_c.shape[1]
    rows = plus2.shape[0]
    for place, outs_a, outs_c in (
        (3, (plus2, 0), (minus2, 0)),
        (FACING[1], (ahead_a2, 0), (plus2, wide_a)),
        (FACING[2], (minus2, wide_c), (behind_c2, 0)),
        (0, (own_a2, 0), (own_c2, 0)),
    ):
        part = pl.ds(place * rows, rows)
        total = wide(own_a[part, :]) + wide(relay_a[part, :]) + wide(minus[part, wide_c:])
        outs_a[0][:, outs_a[1] : outs_a[1] + wide_a] = total.astype(jnp.bfloat16)
        total = wide(own_c[part, :]) + wide(relay_c[part, :]) + wide(plus[part, wide_a:])
        outs_c[0][:, outs_c[1] : outs_c[1] + wide_c] = total.astype(jnp.bfloat16)


def merge(own_a, own_c, plus, minus, relay_a, relay_c):
    rows = own_a.shape[0] // 4
    a, c = own_a.shape[1], own_c.shape[1]
    operands = (own_a, own_c, plus, minus, relay_a, relay_c)
    widths = (a + c, a + c, a, c, a, c)
    return pl.pallas_call(
        merge_kernel,
        out_shape=[jax.ShapeDtypeStruct((rows, w), jnp.bfloat16) for w in widths],
        in_specs=[pl.BlockSpec(memory_space=pltpu.VMEM)] * 6,
        out_specs=[pl.BlockSpec(memory_space=pltpu.VMEM)] * 6,
        compiler_params=pltpu.CompilerParams(vmem_limit_bytes=VMEM_LIMIT),
        cost_estimate=pl.CostEstimate(
            flops=12 * rows * (a + c), bytes_accessed=32 * rows * (a + c), transcendentals=0
        ),
        name="merge",
    )(*operands)


def shift_x(value, shift):
    return lax.ppermute(value, "grp", [(g, (g // 4 + shift) % 4 * 4 + g % 4) for g in range(16)])


def shift_z(value, shift):
    return lax.ppermute(value, "grp", [(g, g // 4 * 4 + (g + shift) % 4) for g in range(16)])


def shift_y(value, shift):
    def moved(place):
        role, tp = place // 4, place % 4
        y = (tp // 2 * 2 + role + shift) % 4
        return y % 2 * 4 + y // 2 * 2 + tp % 2

    return lax.ppermute(value, ("role", "tp"), [(p, moved(p)) for p in range(8)])


def swap_core(value):
    return lax.ppermute(value, "tp", [(t, t ^ 1) for t in range(4)])


def gather(block, shift):
    return jnp.stack([block] + [shift(block, s) for s in SHIFTS[1:]])


def gather_ring(block, shift):
    behind, ahead = shift(block, 1), shift(block, -1)
    middle = block.shape[0] // 2
    far = [shift(behind[:middle], 1), shift(ahead[middle:], -1)]
    return jnp.stack([block, behind, ahead, jnp.concatenate(far)])


def wide(value):
    return value.astype(jnp.float32)


def add(*values):
    return sum(wide(v) for v in values)


def absolute(blocks, place, axis):
    take = lambda i: lax.slice_in_dim(blocks, i, i + 1, axis=axis)
    doubled = jnp.concatenate([take(i) for i in (2, 3, 1, 0, 2, 3, 1)], axis=axis)
    return lax.dynamic_slice_in_dim(doubled, (3 - place) % 4, 4, axis=axis)


def relative(blocks, place, axis):
    doubled = jnp.concatenate([blocks, lax.slice_in_dim(blocks, 0, 3, axis=axis)], axis=axis)
    turned = lax.dynamic_slice_in_dim(doubled, place, 4, axis=axis)
    return jnp.concatenate(
        [lax.slice_in_dim(turned, i, i + 1, axis=axis) for i in (0, 3, 1, 2)], axis=axis
    )


def body(
    q_latent,
    kv_new,
    kv_cache,
    lengths,
    members,
    hidden_in,
    w_uv,
    w_o,
    norm_gain,
    w_gate,
    w_up,
    w_down,
):
    groups = lax.axis_size("grp")
    splits = lax.axis_size("tp")
    place_x, place_z = lax.axis_index("grp") // 4, lax.axis_index("grp") % 4
    tokens, heads, kv = q_latent.shape
    latent = w_uv.shape[1]
    value_width = w_uv.shape[2]
    width = w_o.shape[1]
    model_width = width * groups
    hidden = w_gate.shape[1]
    half = hidden // 2
    score_scale = (value_width + kv - latent) ** (-0.5)

    core = lax.axis_index("tp") % 2
    residual = lax.dynamic_index_in_dim(
        hidden_in.reshape(4, 4, 2, 2, tokens, width), core, 3, keepdims=False
    )
    residual = wide(relative(relative(residual, place_x, 0), place_z, 1))
    residual = jnp.swapaxes(residual, 0, 1)

    context = attend(q_latent, kv_new, kv_cache, lengths, members, score_scale, latent, splits)
    spread = lax.all_to_all(context, "tp", split_axis=0, concat_axis=0)
    spread = spread.reshape(splits * tokens, heads // splits, latent)
    values = jnp.einsum("thl,hlv->thv", spread, w_uv, preferred_element_type=jnp.float32)
    values = values.astype(jnp.bfloat16).reshape(2, splits * tokens // 2, -1)
    first = gather(gather(values[0], shift_x), shift_z)
    second = gather(gather(values[1], shift_z), shift_x)
    second = jnp.swapaxes(second, 0, 1)
    first, second = (
        jnp.dot(v.reshape(-1, v.shape[-1]), w_o, preferred_element_type=jnp.float32).reshape(
            4, 4, 2, tokens, width
        )
        for v in (first, second)
    )
    attn_part = jnp.stack([first, second], axis=2)
    mine = jnp.where(core == 0, attn_part[:, :, :, 0], attn_part[:, :, :, 1])
    theirs = jnp.where(core == 0, attn_part[:, :, :, 1], attn_part[:, :, :, 0])
    shared = 0.5 * residual + mine + wide(swap_core(theirs.astype(jnp.bfloat16)))
    sent = shared.astype(jnp.bfloat16)
    behind, ahead, far = (shift_y(sent, s) for s in SHIFTS[1:])
    stream = shared + wide(far)
    rows = jnp.stack([stream, add(behind, ahead)]).astype(jnp.bfloat16)
    rows = jnp.stack([rows, swap_core(rows)])
    rows = jnp.transpose(rows, (2, 3, 0, 1, 4, 5, 6)).reshape(4, 4, 8 * tokens, width)

    gain = wide(norm_gain)[None]
    places = (3, FACING[1], FACING[2])
    sends = (((0, 0), (1, 1)), ((0, 1), (2, 0)))
    gate_sends = partial_sums(rows, 1, places, gain, w_gate, sends, True)
    up_sends = partial_sums(rows, 0, places, gain, w_up, sends, False)
    places = (FACING[1], FACING[2], 0)
    rest = (((0, 0),), ((1, 1),), ((2, 0),), ((2, 1),))
    gate_rest = partial_sums(rows, 1, places, gain, w_gate, rest, True)
    up_rest = partial_sums(rows, 0, places, gain, w_up, rest, False)
    gate = scatter_step(*gate_sends, *gate_rest[:2], shift_x)
    up = scatter_step(*up_sends, *up_rest[:2], shift_z)
    gate = merge(*gate_rest[2:], *gate)
    up = merge(*up_rest[2:], *up)
    sums = []
    for whole, shift in ((gate, shift_z), (up, shift_x)):
        plus, minus, relay_a, relay_c = scatter_step(*whole[:4], shift)
        own_a, own_c = whole[4:]
        sums.append(add(own_a, relay_a, minus[:, own_c.shape[1] :]))
        sums.append(add(own_c, relay_c, plus[:, own_a.shape[1] :]))
    gate_a, gate_c, up_a, up_c = sums
    square = gate_a[:, half : half + 1] + gate_a[:, half + 64 : half + 65]
    scale = lax.rsqrt(square / model_width + epsilon)
    activated = jnp.concatenate(
        [
            (jax.nn.silu(g * scale) * (u * scale)).astype(jnp.bfloat16)
            for g, u in ((gate_a[:, :half], up_a), (gate_c, up_c))
        ],
        axis=1,
    )

    own_core, other_core = activated[: 4 * tokens], activated[4 * tokens :]
    own_core = gather_ring(gather_ring(own_core, shift_x).reshape(-1, hidden), shift_z)
    other_core = gather_ring(gather_ring(other_core, shift_z).reshape(-1, hidden), shift_x)
    own_core, other_core = (
        jnp.dot(a.reshape(-1, hidden), w_down, preferred_element_type=jnp.float32)
        .astype(jnp.bfloat16)
        .reshape(4, 4, 4, tokens, width)
        for a in (own_core, other_core)
    )
    down = add(own_core, swap_core(jnp.swapaxes(other_core, 0, 1)))
    down = down.reshape(4, 4, 2, 2, tokens, width)
    near = down[:, :, 1].astype(jnp.bfloat16)
    total = add(
        stream,
        down[:, :, 0],
        shift_y(near, 1),
        shift_y(near, -1),
        shift_y(down[:, :, 0].astype(jnp.bfloat16), 2),
    )
    result = jnp.swapaxes(total.astype(jnp.bfloat16), 0, 1)
    result = absolute(absolute(result, place_x, 0), place_z, 1)
    result = result.reshape(groups, 2 * tokens, width)
    whole = lax.all_to_all(result, "grp", split_axis=0, concat_axis=2, tiled=True)
    whole = whole.reshape(2, tokens, model_width)
    other = swap_core(whole)
    whole = jnp.stack(
        [jnp.where(core == 0, whole, other), jnp.where(core == 0, other, whole)], axis=1
    )
    return whole.reshape(splits * tokens, model_width)


def solution(mesh):
    in_specs = (
        P(("role", "grp", "tp"), None, None),
        P(("role", "grp", "tp"), None),
        P(("role", "grp", "tp"), None, None),
        P(("role", "grp", "tp")),
        P(("role", "grp", "tp")),
        P("role", "grp"),
        P("tp", None, None),
        P("tp", "grp"),
        P("grp"),
        P("grp", ("role", "tp")),
        P("grp", ("role", "tp")),
        P(("role", "tp"), "grp"),
    )
    out_specs = P(("role", "grp"), None)
    return jax.shard_map(body, mesh=mesh, in_specs=in_specs, out_specs=out_specs, check_vma=False)
```

profile of v0, /device:TPU:1, one launch (start us, length us, event | category | flops | bytes accessed | tf_op | source)
XLA Modules:
  0.0 254.5 jit_solution(16834556156931188329)
XLA Ops:
  3.3 10.7 %attend.1 = bf16[4,8,16,512]{3,2,1,0:T(8,128)(2,1)} custom-call(s32[8]{0:T(128)S(1)} %copy-done.5, s32[8]{0:T(128)S(1)} %copy-done.6, bf16[8,64,576]{2,1,0:T(8,128)(2,1)S(1)} %copy-done.4, f32[8,1,576]{2,1,0:T(1,128)S(1)} %reshape.128.new_ref, bf16[8,576,1024]{2,1,0:T(8,128)(2,1)} %bitcast.175), custom_call_target="tpu_custom_call" | custom-call | tf_op jit(solution)/shard_map/attend/pallas_call | solution.py:52
  14.0 6.0 %all-to-all-start = ((bf16[4,8,16,512]{3,2,1,0:T(8,128)(2,1)}), bf16[4,8,16,512]{3,2,1,0:T(8,128)(2,1)S(1)}, u32[]{:S(2)}, u32[]{:S(2)}) async-start(bf16[4,8,16,512]{3,2,1,0:T(8,128)(2,1)} %attend.1), calls=%async_computation | async-start | bytes 1048576 | tf_op jit(solution)/shard_map/all_to_all | solution.py:262
  19.9 1.2 copy.65
  21.2 8.2 %all-to-all-done = bf16[4,8,16,512]{3,2,1,0:T(8,128)(2,1)S(1)} async-done(((bf16[4,8,16,512]{3,2,1,0:T(8,128)(2,1)}), bf16[4,8,16,512]{3,2,1,0:T(8,128)(2,1)S(1)}, u32[]{:S(2)}, u32[]{:S(2)}) %all-to-all-start) | async-done | bytes 524320 | tf_op jit(solution)/shard_map/all_to_all | solution.py:262
  30.1 1.7 collective-permute-start.6
  31.8 2.2 collective-permute-start.7
  34.0 1.2 collective-permute-start.8
  35.3 1.3 collective-permute-start
  36.6 1.5 collective-permute-start.1
  38.2 1.6 collective-permute-start.2
  40.2 2.4 collective-permute-start.10
  44.4 1.9 collective-permute-start.4
  46.3 1.5 collective-permute-done.9
  47.8 2.2 collective-permute-start.5
  49.9 3.8 %collective-permute-done.11 = bf16[4,16,2048]{2,1,0:T(8,128)(2,1)S(1)} collective-permute-done((bf16[4,16,2048]{2,1,0:T(8,128)(2,1)S(1)}, bf16[4,16,2048]{2,1,0:T(8,128)(2,1)S(1)}, u32[]{:S(2)}, u32[]{:S(2)}) %collective-permute-start.11) | collective-permute-done | bytes 262176 | tf_op jit(solution)/shard_map/ppermute | solution.py:175
  53.7 2.4 fusion.8
  57.2 6.3 %collective-permute-start.12 = (bf16[4,4,2,8,448]{4,3,1,0,2:T(8,128)(2,1)S(1)}, bf16[4,4,2,8,448]{4,3,1,0,2:T(8,128)(2,1)S(1)}, u32[]{:S(2)}, u32[]{:S(2)}) collective-permute-start(bf16[4,4,2,8,448]{4,3,1,0,2:T(8,128)(2,1)S(1)} %fusion.40), channel_id=1, source_target_pairs={{0,1},{1,0},{2,3},{3,2},{4,5},{5,4},{6,7},{7,6},{8,9},{9,8},{10,11... | collective-permute-start | bytes 688136 | tf_op jit(solution)/shard_map/ppermute | solution.py:192
  64.8 2.0 collective-permute-start.13
  67.2 2.3 collective-permute-start.15
  69.5 4.5 %collective-permute-done.13 = bf16[4,4,2,8,448]{4,3,1,0,2:T(8,128)(2,1)S(1)} collective-permute-done((bf16[4,4,2,8,448]{4,3,1,0,2:T(8,128)(2,1)S(1)}, bf16[4,4,2,8,448]{4,3,1,0,2:T(8,128)(2,1)S(1)}, u32[]{:S(2)}, u32[]{:S(2)}) %collective-permute-start.13) | collective-permute-done | bytes 229408 | tf_op jit(solution)/shard_map/ppermute | solution.py:188
  74.1 6.2 %collective-permute-done.14 = bf16[4,4,2,8,448]{4,3,1,0,2:T(8,128)(2,1)S(1)} collective-permute-done((bf16[4,4,2,8,448]{4,3,1,0,2:T(8,128)(2,1)S(1)}, bf16[4,4,2,8,448]{4,3,1,0,2:T(8,128)(2,1)S(1)}, u32[]{:S(2)}, u32[]{:S(2)}) %collective-permute-start.14) | collective-permute-done | bytes 229408 | tf_op jit(solution)/shard_map/ppermute | solution.py:188
  81.0 1.5 collective-permute-done.16
  82.9 1.3 copy-done.2
  84.1 2.7 %partial_sums.7 = (bf16[256,2304]{1,0:T(8,128)(2,1)}, bf16[256,2304]{1,0:T(8,128)(2,1)}) custom-call(bf16[4,4,64,448]{3,2,1,0:T(8,128)(2,1)S(1)} %bitcast.159, bf16[4,4,64,448]{3,2,1,0:T(8,128)(2,1)S(1)} %bitcast.160, bf16[4,4,64,448]{3,2,1,0:T(8,128)(2,1)S(1)} %bitcast.161, f32[1,448]{1,0:T(1,128)S(1)} %bitcast.171, bf16[448,2304]{1,0:T(8,128)(2,1)S(1)} %copy-done.2), custom_call_target="tpu_custom_call" | custom-call | flops 1056964608 | bytes 4423680 | tf_op jit(solution)/shard_map/partial_sums/pallas_call | solution.py:113
  86.9 10.0 %collective-permute-start.24 = (bf16[256,2304]{1,0:T(8,128)(2,1)}, bf16[256,2304]{1,0:T(8,128)(2,1)S(1)}, u32[]{:S(2)}, u32[]{:S(2)}) collective-permute-start(bf16[256,2304]{1,0:T(8,128)(2,1)} %get-tuple-element.41), channel_id=1, source_target_pairs={{0,4},{4,8},{8,12},{12,0},{16,20},{20,24},{24,28},{28,16},{32,36},... | collective-permute-start | bytes 3538952 | tf_op jit(solution)/shard_map/ppermute | solution.py:179
  96.8 2.9 %partial_sums.5 = (bf16[256,2432]{1,0:T(8,128)(2,1)}, bf16[256,2432]{1,0:T(8,128)(2,1)}) custom-call(bf16[4,4,64,448]{3,2,1,0:T(8,128)(2,1)S(1)} %bitcast.162, bf16[4,4,64,448]{3,2,1,0:T(8,128)(2,1)S(1)} %bitcast.163, bf16[4,4,64,448]{3,2,1,0:T(8,128)(2,1)S(1)} %bitcast.164, f32[1,448]{1,0:T(1,128)S(1)} %bitcast.172, bf16[448,2304]{1,0:T(8,128)(2,1)S(1)} %copy-done.3), custom_call_target="tpu_custom_call" | custom-call | flops 1115684864 | bytes 4554752 | tf_op jit(solution)/shard_map/partial_sums/pallas_call | solution.py:113
  99.7 1.5 collective-permute-start.17
  101.2 1.5 partial_sums.6
  102.8 1.5 partial_sums.4
  104.3 9.9 %collective-permute-done.25.minus = bf16[256,2304]{1,0:T(8,128)(2,1)S(1)} collective-permute-done((bf16[256,2304]{1,0:T(8,128)(2,1)}, bf16[256,2304]{1,0:T(8,128)(2,1)S(1)}, u32[]{:S(2)}, u32[]{:S(2)}) %collective-permute-start.25) | collective-permute-done | bytes 1179680 | tf_op jit(solution)/shard_map/ppermute | solution.py:179
  114.4 1.6 collective-permute-start.27
  116.0 8.9 %collective-permute-done.24.plus = bf16[256,2304]{1,0:T(8,128)(2,1)S(1)} collective-permute-done((bf16[256,2304]{1,0:T(8,128)(2,1)}, bf16[256,2304]{1,0:T(8,128)(2,1)S(1)}, u32[]{:S(2)}, u32[]{:S(2)}) %collective-permute-start.24) | collective-permute-done | bytes 1179680 | tf_op jit(solution)/shard_map/ppermute | solution.py:179
  125.2 3.9 %collective-permute-done.17.plus = bf16[256,2432]{1,0:T(8,128)(2,1)S(1)} collective-permute-done((bf16[256,2432]{1,0:T(8,128)(2,1)}, bf16[256,2432]{1,0:T(8,128)(2,1)S(1)}, u32[]{:S(2)}, u32[]{:S(2)}) %collective-permute-start.17) | collective-permute-done | bytes 1245216 | tf_op jit(solution)/shard_map/ppermute | solution.py:175
  129.5 2.7 %collective-permute-start.20 = (bf16[256,1152]{1,0:T(8,128)(2,1)S(1)}, bf16[256,1152]{1,0:T(8,128)(2,1)S(1)}, u32[]{:S(2)}, u32[]{:S(2)}) collective-permute-start(bf16[256,1152]{1,0:T(8,128)(2,1)S(1)} %add_convert_fusion.3), channel_id=1, source_target_pairs={{0,48},{4,52},{8,56},{12,60},{16,0},{20,4},{24,8},{28,12},{32,16},... | collective-permute-start | bytes 1769480 | tf_op jit(solution)/shard_map/ppermute | solution.py:175
  132.2 7.7 %collective-permute-done.26.relay_a = bf16[256,1152]{1,0:T(8,128)(2,1)S(1)} collective-permute-done((bf16[256,1152]{1,0:T(8,128)(2,1)S(1)}, bf16[256,1152]{1,0:T(8,128)(2,1)S(1)}, u32[]{:S(2)}, u32[]{:S(2)}) %collective-permute-start.26) | collective-permute-done | bytes 589856 | tf_op jit(solution)/shard_map/ppermute | solution.py:179
  140.5 1.5 collective-permute-start.28
  142.7 2.2 collective-permute-done.19.relay_a
  145.4 2.3 collective-permute-start.21
  148.4 1.2 collective-permute-done.30
  149.6 2.9 %collective-permute-start.32 = (bf16[64,1152]{1,0:T(8,128)(2,1)S(1)}, bf16[64,1152]{1,0:T(8,128)(2,1)S(1)}, u32[]{:S(2)}, u32[]{:S(2)}) collective-permute-start(bf16[64,1152]{1,0:T(8,128)(2,1)S(1)} %add_convert_fusion.7), channel_id=1, source_target_pairs={{0,48},{4,52},{8,56},{12,60},{16,0},{20,4},{24,8},{28,12},{32,16},... | collective-permute-start | bytes 442376 | tf_op jit(solution)/shard_map/ppermute | solution.py:175
  152.9 2.0 collective-permute-start.22
  155.8 4.0 %collective-permute-done.22 = bf16[64,1280]{1,0:T(8,128)(2,1)S(1)} collective-permute-done((bf16[64,1280]{1,0:T(8,128)(2,1)S(1)}, bf16[64,1280]{1,0:T(8,128)(2,1)S(1)}, u32[]{:S(2)}, u32[]{:S(2)}) %collective-permute-start.22) | collective-permute-done | bytes 163872 | tf_op jit(solution)/shard_map/ppermute | solution.py:179
  160.5 5.5 %collective-permute-done.29 = bf16[64,1152]{1,0:T(8,128)(2,1)S(1)} collective-permute-done((bf16[64,1152]{1,0:T(8,128)(2,1)S(1)}, bf16[64,1152]{1,0:T(8,128)(2,1)S(1)}, u32[]{:S(2)}, u32[]{:S(2)}) %collective-permute-start.29) | collective-permute-done | bytes 147488 | tf_op jit(solution)/shard_map/ppermute | solution.py:175
  166.2 1.5 collective-permute-start.41
  167.7 1.4 collective-permute-start.42
  169.1 2.7 %collective-permute-start.34 = (bf16[32,2304]{1,0:T(8,128)(2,1)S(1)}, bf16[32,2304]{1,0:T(8,128)(2,1)S(1)}, u32[]{:S(2)}, u32[]{:S(2)}) collective-permute-start(bf16[32,2304]{1,0:T(8,128)(2,1)S(1)} %get-tuple-element.64), channel_id=1, source_target_pairs={{0,48},{4,52},{8,56},{12,60},{16,0},{20,4},{24,8},{28,12},{32,16},... | collective-permute-start | bytes 442376 | tf_op jit(solution)/shard_map/ppermute | solution.py:175
  172.0 2.7 %collective-permute-start.44 = (bf16[16,2304]{1,0:T(8,128)(2,1)S(1)}, bf16[16,2304]{1,0:T(8,128)(2,1)S(1)}, u32[]{:S(2)}, u32[]{:S(2)}) collective-permute-start(bf16[16,2304]{1,0:T(8,128)(2,1)S(1)} %slice.245), channel_id=1, source_target_pairs={{0,12},{4,0},{8,4},{12,8},{16,28},{20,16},{24,20},{28,24},{32,44},... | collective-permute-start | bytes 221192 | tf_op jit(solution)/shard_map/ppermute | solution.py:179
  174.8 2.7 %collective-permute-start.36 = (bf16[16,2304]{1,0:T(8,128)(2,1)S(1)}, bf16[16,2304]{1,0:T(8,128)(2,1)S(1)}, u32[]{:S(2)}, u32[]{:S(2)}) collective-permute-start(bf16[16,2304]{1,0:T(8,128)(2,1)S(1)} %slice.241), channel_id=1, source_target_pairs={{0,48},{4,52},{8,56},{12,60},{16,0},{20,4},{24,8},{28,12},{32,16},... | collective-permute-start | bytes 221192 | tf_op jit(solution)/shard_map/ppermute | solution.py:175
  177.8 2.7 %collective-permute-start.46 = (bf16[128,2304]{1,0:T(8,128)(2,1)S(1)}, bf16[128,2304]{1,0:T(8,128)(2,1)S(1)}, u32[]{:S(2)}, u32[]{:S(2)}) collective-permute-start(bf16[128,2304]{1,0:T(8,128)(2,1)S(1)} %bitcast.183), channel_id=1, source_target_pairs={{0,48},{4,52},{8,56},{12,60},{16,0},{20,4},{24,8},{28,12},{32,16},... | collective-permute-start | bytes 1769480 | tf_op jit(solution)/shard_map/ppermute | solution.py:175
  181.1 2.2 collective-permute-start.38
  183.3 6.0 %collective-permute-done.45 = bf16[128,2304]{1,0:T(8,128)(2,1)S(1)} collective-permute-done((bf16[128,2304]{1,0:T(8,128)(2,1)S(1)}, bf16[128,2304]{1,0:T(8,128)(2,1)S(1)}, u32[]{:S(2)}, u32[]{:S(2)}) %collective-permute-start.45) | collective-permute-done | bytes 589856 | tf_op jit(solution)/shard_map/ppermute | solution.py:175
  189.4 2.7 %collective-permute-start.48 = (bf16[64,2304]{1,0:T(8,128)(2,1)S(1)}, bf16[64,2304]{1,0:T(8,128)(2,1)S(1)}, u32[]{:S(2)}, u32[]{:S(2)}) collective-permute-start(bf16[64,2304]{1,0:T(8,128)(2,1)S(1)} %slice.247), channel_id=1, source_target_pairs={{0,48},{4,52},{8,56},{12,60},{16,0},{20,4},{24,8},{28,12},{32,16},... | collective-permute-start | bytes 884744 | tf_op jit(solution)/shard_map/ppermute | solution.py:175
  194.1 2.2 collective-permute-start.40
  196.3 2.1 collective-permute-done.47
  198.7 1.3 copy-done.11
  200.0 1.3 convolution_convert_fusion
  202.3 13.2 %collective-permute-start.49 = (bf16[4,4,4,8,448]{4,3,2,1,0:T(8,128)(2,1)}, bf16[4,4,4,8,448]{4,3,2,1,0:T(8,128)(2,1)S(1)}, u32[]{:S(2)}, u32[]{:S(2)}) collective-permute-start(bf16[4,4,4,8,448]{4,3,2,1,0:T(8,128)(2,1)} %bitcast.156), channel_id=1, source_target_pairs={{0,1},{1,0},{2,3},{3,2},{4,5},{5,4},{6,7},{7,6},{8,9},{9,8},{10,11... | collective-permute-start | bytes 1376264 | tf_op jit(solution)/shard_map/ppermute | solution.py:192
  216.9 1.3 copy-done.12
  218.2 1.3 fusion.4
  220.7 2.3 collective-permute-start.51
  223.2 5.5 %collective-permute-done.50 = bf16[4,4,2,8,448]{4,3,1,0,2:T(8,128)(2,1)S(1)} collective-permute-done((bf16[4,4,2,8,448]{4,3,1,0,2:T(8,128)(2,1)S(1)}, bf16[4,4,2,8,448]{4,3,1,0,2:T(8,128)(2,1)S(1)}, u32[]{:S(2)}, u32[]{:S(2)}) %collective-permute-start.50) | collective-permute-done | bytes 229408 | tf_op jit(solution)/shard_map/ppermute | solution.py:188
  228.7 5.9 %collective-permute-done.52 = bf16[4,4,2,8,448]{4,3,1,0,2:T(8,128)(2,1)S(1)} collective-permute-done((bf16[4,4,2,8,448]{4,3,1,0,2:T(8,128)(2,1)S(1)}, bf16[4,4,2,8,448]{4,3,1,0,2:T(8,128)(2,1)S(1)}, u32[]{:S(2)}, u32[]{:S(2)}) %collective-permute-start.52) | collective-permute-done | bytes 229408 | tf_op jit(solution)/shard_map/ppermute | solution.py:188
  235.1 14.3 %all_to_all.20 = bf16[16,16,448]{2,1,0:T(8,128)(2,1)S(1)} all-to-all(bf16[16,16,448]{2,1,0:T(8,128)(2,1)S(1)} %bitcast.194), channel_id=1, replica_groups=mesh['role'=2,'grp'=16,'tp'=4] {'grp'}, dimensions={0} | all-to-all | bytes 458752 | tf_op jit(solution)/shard_map/all_to_all | solution.py:338
  249.8 2.3 collective-permute-start.53
  (168 shorter events, 26.0 us)
Async XLA Ops:
  0.0 29.4 %copy-start = (bf16[16,512,128]{2,1,0:T(8,128)(2,1)S(1)}, bf16[16,512,128]{2,1,0:T(8,128)(2,1)}, u32[]{:S(2)}) copy-start(bf16[16,512,128]{2,1,0:T(8,128)(2,1)} %param.18) | copy-start | bytes 6291460
  14.0 15.4 %all-to-all-start = ((bf16[4,8,16,512]{3,2,1,0:T(8,128)(2,1)}), bf16[4,8,16,512]{3,2,1,0:T(8,128)(2,1)S(1)}, u32[]{:S(2)}, u32[]{:S(2)}) async-start(bf16[4,8,16,512]{3,2,1,0:T(8,128)(2,1)} %attend.1), calls=%async_computation | async-start | bytes 1048576 | tf_op jit(solution)/shard_map/all_to_all | solution.py:262
  30.1 8.1 %collective-permute-start.6 = (bf16[16,2048]{1,0:T(8,128)(2,1)S(1)}, bf16[16,2048]{1,0:T(8,128)(2,1)S(1)}, u32[]{:S(2)}, u32[]{:S(2)}) collective-permute-start(bf16[16,2048]{1,0:T(8,128)(2,1)S(1)} %bitcast.209), channel_id=1, source_target_pairs={{0,4},{4,8},{8,12},{12,0},{16,20},{20,24},{24,28},{28,16},{32,36},... | collective-permute-start | bytes 196616 | tf_op jit(solution)/shard_map/ppermute | solution.py:179
  31.8 8.0 %collective-permute-start.7 = (bf16[16,2048]{1,0:T(8,128)(2,1)S(1)}, bf16[16,2048]{1,0:T(8,128)(2,1)S(1)}, u32[]{:S(2)}, u32[]{:S(2)}) collective-permute-start(bf16[16,2048]{1,0:T(8,128)(2,1)S(1)} %bitcast.210), channel_id=1, source_target_pairs={{0,12},{4,0},{8,4},{12,8},{16,28},{20,16},{24,20},{28,24},{32,44},... | collective-permute-start | bytes 196616 | tf_op jit(solution)/shard_map/ppermute | solution.py:179
  34.0 5.8 %collective-permute-start.8 = (bf16[16,2048]{1,0:T(8,128)(2,1)S(1)}, bf16[16,2048]{1,0:T(8,128)(2,1)S(1)}, u32[]{:S(2)}, u32[]{:S(2)}) collective-permute-start(bf16[16,2048]{1,0:T(8,128)(2,1)S(1)} %bitcast.211), channel_id=1, source_target_pairs={{0,8},{4,12},{8,0},{12,4},{16,24},{20,28},{24,16},{28,20},{32,40},... | collective-permute-start | bytes 196616 | tf_op jit(solution)/shard_map/ppermute | solution.py:179
  35.3 20.7 %copy-start.9 = (bf16[4,4,2,8,448]{4,3,0,1,2:T(8,128)(2,1)}, bf16[4,4,2,8,448]{4,3,0,1,2:T(8,128)(2,1)S(1)}, u32[]{:S(2)}) copy-start(bf16[4,4,2,8,448]{4,3,0,1,2:T(8,128)(2,1)S(1)} %fusion.37) | copy-start | bytes 688132
  35.3 7.2 %collective-permute-start = (bf16[16,2048]{1,0:T(8,128)(2,1)S(1)}, bf16[16,2048]{1,0:T(8,128)(2,1)S(1)}, u32[]{:S(2)}, u32[]{:S(2)}) collective-permute-start(bf16[16,2048]{1,0:T(8,128)(2,1)S(1)} %bitcast.206), channel_id=1, source_target_pairs={{0,16},{4,20},{8,24},{12,28},{16,32},{20,36},{24,40},{28,44},{32,4... | collective-permute-start | bytes 196616 | tf_op jit(solution)/shard_map/ppermute | solution.py:175
  36.6 6.6 %collective-permute-start.1 = (bf16[16,2048]{1,0:T(8,128)(2,1)S(1)}, bf16[16,2048]{1,0:T(8,128)(2,1)S(1)}, u32[]{:S(2)}, u32[]{:S(2)}) collective-permute-start(bf16[16,2048]{1,0:T(8,128)(2,1)S(1)} %bitcast.207), channel_id=1, source_target_pairs={{0,48},{4,52},{8,56},{12,60},{16,0},{20,4},{24,8},{28,12},{32,16},... | collective-permute-start | bytes 196616 | tf_op jit(solution)/shard_map/ppermute | solution.py:175
  38.2 5.4 %collective-permute-start.2 = (bf16[16,2048]{1,0:T(8,128)(2,1)S(1)}, bf16[16,2048]{1,0:T(8,128)(2,1)S(1)}, u32[]{:S(2)}, u32[]{:S(2)}) collective-permute-start(bf16[16,2048]{1,0:T(8,128)(2,1)S(1)} %bitcast.208), channel_id=1, source_target_pairs={{0,32},{4,36},{8,40},{12,44},{16,48},{20,52},{24,56},{28,60},{32,0... | collective-permute-start | bytes 196616 | tf_op jit(solution)/shard_map/ppermute | solution.py:175
  39.8 7.9 %collective-permute-start.9 = (bf16[4,16,2048]{2,1,0:T(8,128)(2,1)S(1)}, bf16[4,16,2048]{2,1,0:T(8,128)(2,1)S(1)}, u32[]{:S(2)}, u32[]{:S(2)}) collective-permute-start(bf16[4,16,2048]{2,1,0:T(8,128)(2,1)S(1)} %get-tuple-element.74), channel_id=1, source_target_pairs={{0,16},{4,20},{8,24},{12,28},{16,32},{20,36},{24,40},{28,44},{32,4... | collective-permute-start | bytes 786440 | tf_op jit(solution)/shard_map/ppermute | solution.py:175
  40.2 9.7 %collective-permute-start.10 = (bf16[4,16,2048]{2,1,0:T(8,128)(2,1)S(1)}, bf16[4,16,2048]{2,1,0:T(8,128)(2,1)S(1)}, u32[]{:S(2)}, u32[]{:S(2)}) collective-permute-start(bf16[4,16,2048]{2,1,0:T(8,128)(2,1)S(1)} %get-tuple-element.74), channel_id=1, source_target_pairs={{0,48},{4,52},{8,56},{12,60},{16,0},{20,4},{24,8},{28,12},{32,16},... | collective-permute-start | bytes 786440 | tf_op jit(solution)/shard_map/ppermute | solution.py:175
  42.6 11.1 %collective-permute-start.11 = (bf16[4,16,2048]{2,1,0:T(8,128)(2,1)S(1)}, bf16[4,16,2048]{2,1,0:T(8,128)(2,1)S(1)}, u32[]{:S(2)}, u32[]{:S(2)}) collective-permute-start(bf16[4,16,2048]{2,1,0:T(8,128)(2,1)S(1)} %get-tuple-element.74), channel_id=1, source_target_pairs={{0,32},{4,36},{8,40},{12,44},{16,48},{20,52},{24,56},{28,60},{32,0... | collective-permute-start | bytes 786440 | tf_op jit(solution)/shard_map/ppermute | solution.py:175
  43.6 12.5 %collective-permute-start.3 = (bf16[4,16,2048]{2,1,0:T(8,128)(2,1)S(1)}, bf16[4,16,2048]{2,1,0:T(8,128)(2,1)S(1)}, u32[]{:S(2)}, u32[]{:S(2)}) collective-permute-start(bf16[4,16,2048]{2,1,0:T(8,128)(2,1)S(1)} %pad_maximum_fusion.7), channel_id=1, source_target_pairs={{0,4},{4,8},{8,12},{12,0},{16,20},{20,24},{24,28},{28,16},{32,36},... | collective-permute-start | bytes 786440 | tf_op jit(solution)/shard_map/ppermute | solution.py:179
  44.4 11.7 %collective-permute-start.4 = (bf16[4,16,2048]{2,1,0:T(8,128)(2,1)S(1)}, bf16[4,16,2048]{2,1,0:T(8,128)(2,1)S(1)}, u32[]{:S(2)}, u32[]{:S(2)}) collective-permute-start(bf16[4,16,2048]{2,1,0:T(8,128)(2,1)S(1)} %pad_maximum_fusion.7), channel_id=1, source_target_pairs={{0,12},{4,0},{8,4},{12,8},{16,28},{20,16},{24,20},{28,24},{32,44},... | collective-permute-start | bytes 786440 | tf_op jit(solution)/shard_map/ppermute | solution.py:179
  47.8 8.6 %collective-permute-start.5 = (bf16[4,16,2048]{2,1,0:T(8,128)(2,1)S(1)}, bf16[4,16,2048]{2,1,0:T(8,128)(2,1)S(1)}, u32[]{:S(2)}, u32[]{:S(2)}) collective-permute-start(bf16[4,16,2048]{2,1,0:T(8,128)(2,1)S(1)} %pad_maximum_fusion.7), channel_id=1, source_target_pairs={{0,8},{4,12},{8,0},{12,4},{16,24},{20,28},{24,16},{28,20},{32,40},... | collective-permute-start | bytes 786440 | tf_op jit(solution)/shard_map/ppermute | solution.py:179
  53.7 2.6 %copy-start.13 = (bf16[2048,448]{0,1:T(8,128)(2,1)S(1)}, bf16[2048,448]{0,1:T(8,128)(2,1)}, u32[]{:S(2)}) copy-start(bf16[2048,448]{0,1:T(8,128)(2,1)} %param.19) | copy-start | bytes 5505028
  56.3 7.1 %slice-start = ((bf16[4,4,2,8,448]{4,3,0,1,2:T(8,128)(2,1)}), bf16[2,4,2,8,448]{4,3,0,1,2:T(8,128)(2,1)S(1)}, s32[]{:S(2)}) async-start(bf16[4,4,2,8,448]{4,3,0,1,2:T(8,128)(2,1)} %copy-done.9), calls=%async_computation.2 | async-start | bytes 262144 | tf_op jit(solution)/shard_map/slice | solution.py:224
  57.2 7.4 %collective-permute-start.12 = (bf16[4,4,2,8,448]{4,3,1,0,2:T(8,128)(2,1)S(1)}, bf16[4,4,2,8,448]{4,3,1,0,2:T(8,128)(2,1)S(1)}, u32[]{:S(2)}, u32[]{:S(2)}) collective-permute-start(bf16[4,4,2,8,448]{4,3,1,0,2:T(8,128)(2,1)S(1)} %fusion.40), channel_id=1, source_target_pairs={{0,1},{1,0},{2,3},{3,2},{4,5},{5,4},{6,7},{7,6},{8,9},{9,8},{10,11... | collective-permute-start | bytes 688136 | tf_op jit(solution)/shard_map/ppermute | solution.py:192
  64.8 17.9 %copy-start.7 = (f32[4,4,2,8,448]{4,3,1,0,2:T(8,128)}, f32[4,4,2,8,448]{4,3,1,0,2:T(8,128)S(1)}, u32[]{:S(2)}) copy-start(f32[4,4,2,8,448]{4,3,1,0,2:T(8,128)S(1)} %get-tuple-element.54) | copy-start | bytes 1376260
  64.8 16.2 %copy-start.10 = (bf16[448]{0:T(512)(128)(2,1)S(1)}, bf16[448]{0:T(512)(128)(2,1)}, u32[]{:S(2)}) copy-start(bf16[448]{0:T(512)(128)(2,1)} %param.20) | copy-start | bytes 2692
  64.8 9.1 %collective-permute-start.13 = (bf16[4,4,2,8,448]{4,3,1,0,2:T(8,128)(2,1)S(1)}, bf16[4,4,2,8,448]{4,3,1,0,2:T(8,128)(2,1)S(1)}, u32[]{:S(2)}, u32[]{:S(2)}) collective-permute-start(bf16[4,4,2,8,448]{4,3,1,0,2:T(8,128)(2,1)S(1)} %get-tuple-element.53), channel_id=1, source_target_pairs={{0,2},{1,3},{2,0},{3,1},{64,66},{65,67},{66,64},{67,65},{4,6},{5,7... | collective-permute-start | bytes 688136 | tf_op jit(solution)/shard_map/ppermute | solution.py:188
  66.8 13.5 %collective-permute-start.14 = (bf16[4,4,2,8,448]{4,3,1,0,2:T(8,128)(2,1)S(1)}, bf16[4,4,2,8,448]{4,3,1,0,2:T(8,128)(2,1)S(1)}, u32[]{:S(2)}, u32[]{:S(2)}) collective-permute-start(bf16[4,4,2,8,448]{4,3,1,0,2:T(8,128)(2,1)S(1)} %get-tuple-element.53), channel_id=1, source_target_pairs={{0,64},{1,65},{2,66},{3,67},{64,2},{65,3},{66,0},{67,1},{4,68},{5,... | collective-permute-start | bytes 688136 | tf_op jit(solution)/shard_map/ppermute | solution.py:188
  67.2 13.1 %collective-permute-start.15 = (bf16[4,4,2,8,448]{4,3,1,0,2:T(8,128)(2,1)S(1)}, bf16[4,4,2,8,448]{4,3,1,0,2:T(8,128)(2,1)S(1)}, u32[]{:S(2)}, u32[]{:S(2)}) collective-permute-start(bf16[4,4,2,8,448]{4,3,1,0,2:T(8,128)(2,1)S(1)} %get-tuple-element.53), channel_id=1, source_target_pairs={{0,66},{1,67},{2,64},{3,65},{64,0},{65,1},{66,2},{67,3},{4,70},{5,... | collective-permute-start | bytes 688136 | tf_op jit(solution)/shard_map/ppermute | solution.py:188
  80.4 2.1 collective-permute-start.16
  84.1 12.7 %copy-start.3 = (bf16[448,2304]{1,0:T(8,128)(2,1)S(1)}, bf16[448,2304]{1,0:T(8,128)(2,1)}, u32[]{:S(2)}) copy-start(bf16[448,2304]{1,0:T(8,128)(2,1)} %refs_4_.5) | copy-start | bytes 6193156
  86.9 27.4 %collective-permute-start.25 = (bf16[256,2304]{1,0:T(8,128)(2,1)}, bf16[256,2304]{1,0:T(8,128)(2,1)S(1)}, u32[]{:S(2)}, u32[]{:S(2)}) collective-permute-start(bf16[256,2304]{1,0:T(8,128)(2,1)} %get-tuple-element.42), channel_id=1, source_target_pairs={{0,12},{4,0},{8,4},{12,8},{16,28},{20,16},{24,20},{28,24},{32,44},... | collective-permute-start | bytes 3538952 | tf_op jit(solution)/shard_map/ppermute | solution.py:179
  86.9 38.0 %collective-permute-start.24 = (bf16[256,2304]{1,0:T(8,128)(2,1)}, bf16[256,2304]{1,0:T(8,128)(2,1)S(1)}, u32[]{:S(2)}, u32[]{:S(2)}) collective-permute-start(bf16[256,2304]{1,0:T(8,128)(2,1)} %get-tuple-element.41), channel_id=1, source_target_pairs={{0,4},{4,8},{8,12},{12,0},{16,20},{20,24},{24,28},{28,16},{32,36},... | collective-permute-start | bytes 3538952 | tf_op jit(solution)/shard_map/ppermute | solution.py:179
  99.7 29.6 %collective-permute-start.18 = (bf16[256,2432]{1,0:T(8,128)(2,1)}, bf16[256,2432]{1,0:T(8,128)(2,1)S(1)}, u32[]{:S(2)}, u32[]{:S(2)}) collective-permute-start(bf16[256,2432]{1,0:T(8,128)(2,1)} %get-tuple-element.32), channel_id=1, source_target_pairs={{0,48},{4,52},{8,56},{12,60},{16,0},{20,4},{24,8},{28,12},{32,16},... | collective-permute-start | bytes 3735560 | tf_op jit(solution)/shard_map/ppermute | solution.py:175
  99.7 29.4 %collective-permute-start.17 = (bf16[256,2432]{1,0:T(8,128)(2,1)}, bf16[256,2432]{1,0:T(8,128)(2,1)S(1)}, u32[]{:S(2)}, u32[]{:S(2)}) collective-permute-start(bf16[256,2432]{1,0:T(8,128)(2,1)} %get-tuple-element.31), channel_id=1, source_target_pairs={{0,16},{4,20},{8,24},{12,28},{16,32},{20,36},{24,40},{28,44},{32,4... | collective-permute-start | bytes 3735560 | tf_op jit(solution)/shard_map/ppermute | solution.py:175
  114.4 17.8 %collective-permute-start.27 = (bf16[256,1152]{1,0:T(8,128)(2,1)S(1)}, bf16[256,1152]{1,0:T(8,128)(2,1)S(1)}, u32[]{:S(2)}, u32[]{:S(2)}) collective-permute-start(bf16[256,1152]{1,0:T(8,128)(2,1)S(1)} %add_convert_fusion.1), channel_id=1, source_target_pairs={{0,12},{4,0},{8,4},{12,8},{16,28},{20,16},{24,20},{28,24},{32,44},... | collective-permute-start | bytes 1769480 | tf_op jit(solution)/shard_map/ppermute | solution.py:179
  125.1 14.9 %collective-permute-start.26 = (bf16[256,1152]{1,0:T(8,128)(2,1)S(1)}, bf16[256,1152]{1,0:T(8,128)(2,1)S(1)}, u32[]{:S(2)}, u32[]{:S(2)}) collective-permute-start(bf16[256,1152]{1,0:T(8,128)(2,1)S(1)} %add_convert_fusion.2), channel_id=1, source_target_pairs={{0,4},{4,8},{8,12},{12,0},{16,20},{20,24},{24,28},{28,16},{32,36},... | collective-permute-start | bytes 1769480 | tf_op jit(solution)/shard_map/ppermute | solution.py:179
  129.3 15.7 %collective-permute-start.19 = (bf16[256,1280]{1,0:T(8,128)(2,1)S(1)}, bf16[256,1280]{1,0:T(8,128)(2,1)S(1)}, u32[]{:S(2)}, u32[]{:S(2)}) collective-permute-start(bf16[256,1280]{1,0:T(8,128)(2,1)S(1)} %add_convert_fusion), channel_id=1, source_target_pairs={{0,16},{4,20},{8,24},{12,28},{16,32},{20,36},{24,40},{28,44},{32,4... | collective-permute-start | bytes 1966088 | tf_op jit(solution)/shard_map/ppermute | solution.py:175
  129.5 13.2 %collective-permute-start.20 = (bf16[256,1152]{1,0:T(8,128)(2,1)S(1)}, bf16[256,1152]{1,0:T(8,128)(2,1)S(1)}, u32[]{:S(2)}, u32[]{:S(2)}) collective-permute-start(bf16[256,1152]{1,0:T(8,128)(2,1)S(1)} %add_convert_fusion.3), channel_id=1, source_target_pairs={{0,48},{4,52},{8,56},{12,60},{16,0},{20,4},{24,8},{28,12},{32,16},... | collective-permute-start | bytes 1769480 | tf_op jit(solution)/shard_map/ppermute | solution.py:175
  140.4 9.2 %collective-permute-start.30 = (bf16[64,2304]{1,0:T(8,128)(2,1)S(1)}, bf16[64,2304]{1,0:T(8,128)(2,1)S(1)}, u32[]{:S(2)}, u32[]{:S(2)}) collective-permute-start(bf16[64,2304]{1,0:T(8,128)(2,1)S(1)} %get-tuple-element.48), channel_id=1, source_target_pairs={{0,48},{4,52},{8,56},{12,60},{16,0},{20,4},{24,8},{28,12},{32,16},... | collective-permute-start | bytes 884744 | tf_op jit(solution)/shard_map/ppermute | solution.py:175
  140.5 19.5 %collective-permute-start.28 = (bf16[64,2304]{1,0:T(8,128)(2,1)S(1)}, bf16[64,2304]{1,0:T(8,128)(2,1)S(1)}, u32[]{:S(2)}, u32[]{:S(2)}) collective-permute-start(bf16[64,2304]{1,0:T(8,128)(2,1)S(1)} %get-tuple-element.47), channel_id=1, source_target_pairs={{0,16},{4,20},{8,24},{12,28},{16,32},{20,36},{24,40},{28,44},{32,4... | collective-permute-start | bytes 884744 | tf_op jit(solution)/shard_map/ppermute | solution.py:175
  145.4 7.5 %collective-permute-start.21 = (bf16[64,2432]{1,0:T(8,128)(2,1)S(1)}, bf16[64,2432]{1,0:T(8,128)(2,1)S(1)}, u32[]{:S(2)}, u32[]{:S(2)}) collective-permute-start(bf16[64,2432]{1,0:T(8,128)(2,1)S(1)} %get-tuple-element.37), channel_id=1, source_target_pairs={{0,4},{4,8},{8,12},{12,0},{16,20},{20,24},{24,28},{28,16},{32,36},... | collective-permute-start | bytes 933896 | tf_op jit(solution)/shard_map/ppermute | solution.py:179
  147.7 7.2 %collective-permute-start.23 = (bf16[64,2432]{1,0:T(8,128)(2,1)S(1)}, bf16[64,2432]{1,0:T(8,128)(2,1)S(1)}, u32[]{:S(2)}, u32[]{:S(2)}) collective-permute-start(bf16[64,2432]{1,0:T(8,128)(2,1)S(1)} %get-tuple-element.38), channel_id=1, source_target_pairs={{0,12},{4,0},{8,4},{12,8},{16,28},{20,16},{24,20},{28,24},{32,44},... | collective-permute-start | bytes 933896 | tf_op jit(solution)/shard_map/ppermute | solution.py:179
  149.6 10.4 %collective-permute-start.32 = (bf16[64,1152]{1,0:T(8,128)(2,1)S(1)}, bf16[64,1152]{1,0:T(8,128)(2,1)S(1)}, u32[]{:S(2)}, u32[]{:S(2)}) collective-permute-start(bf16[64,1152]{1,0:T(8,128)(2,1)S(1)} %add_convert_fusion.7), channel_id=1, source_target_pairs={{0,48},{4,52},{8,56},{12,60},{16,0},{20,4},{24,8},{28,12},{32,16},... | collective-permute-start | bytes 442376 | tf_op jit(solution)/shard_map/ppermute | solution.py:175
  152.9 6.9 %collective-permute-start.22 = (bf16[64,1280]{1,0:T(8,128)(2,1)S(1)}, bf16[64,1280]{1,0:T(8,128)(2,1)S(1)}, u32[]{:S(2)}, u32[]{:S(2)}) collective-permute-start(bf16[64,1280]{1,0:T(8,128)(2,1)S(1)} %add_convert_fusion.6), channel_id=1, source_target_pairs={{0,4},{4,8},{8,12},{12,0},{16,20},{20,24},{24,28},{28,16},{32,36},... | collective-permute-start | bytes 491528 | tf_op jit(solution)/shard_map/ppermute | solution.py:179
  154.9 5.3 %collective-permute-start.31 = (bf16[64,1152]{1,0:T(8,128)(2,1)S(1)}, bf16[64,1152]{1,0:T(8,128)(2,1)S(1)}, u32[]{:S(2)}, u32[]{:S(2)}) collective-permute-start(bf16[64,1152]{1,0:T(8,128)(2,1)S(1)} %add_convert_fusion.8), channel_id=1, source_target_pairs={{0,12},{4,0},{8,4},{12,8},{16,28},{20,16},{24,20},{28,24},{32,44},... | collective-permute-start | bytes 442376 | tf_op jit(solution)/shard_map/ppermute | solution.py:179
  160.4 5.6 %collective-permute-start.29 = (bf16[64,1152]{1,0:T(8,128)(2,1)S(1)}, bf16[64,1152]{1,0:T(8,128)(2,1)S(1)}, u32[]{:S(2)}, u32[]{:S(2)}) collective-permute-start(bf16[64,1152]{1,0:T(8,128)(2,1)S(1)} %get-tuple-element.66), channel_id=1, source_target_pairs={{0,16},{4,20},{8,24},{12,28},{16,32},{20,36},{24,40},{28,44},{32,4... | collective-permute-start | bytes 442376 | tf_op jit(solution)/shard_map/ppermute | solution.py:175
  166.2 5.7 %collective-permute-start.41 = (bf16[32,2304]{1,0:T(8,128)(2,1)S(1)}, bf16[32,2304]{1,0:T(8,128)(2,1)S(1)}, u32[]{:S(2)}, u32[]{:S(2)}) collective-permute-start(bf16[32,2304]{1,0:T(8,128)(2,1)S(1)} %get-tuple-element.63), channel_id=1, source_target_pairs={{0,4},{4,8},{8,12},{12,0},{16,20},{20,24},{24,28},{28,16},{32,36},... | collective-permute-start | bytes 442376 | tf_op jit(solution)/shard_map/ppermute | solution.py:179
  167.7 4.3 %collective-permute-start.42 = (bf16[32,2304]{1,0:T(8,128)(2,1)S(1)}, bf16[32,2304]{1,0:T(8,128)(2,1)S(1)}, u32[]{:S(2)}, u32[]{:S(2)}) collective-permute-start(bf16[32,2304]{1,0:T(8,128)(2,1)S(1)} %get-tuple-element.63), channel_id=1, source_target_pairs={{0,12},{4,0},{8,4},{12,8},{16,28},{20,16},{24,20},{28,24},{32,44},... | collective-permute-start | bytes 442376 | tf_op jit(solution)/shard_map/ppermute | solution.py:179
  169.1 5.6 %collective-permute-start.33 = (bf16[32,2304]{1,0:T(8,128)(2,1)S(1)}, bf16[32,2304]{1,0:T(8,128)(2,1)S(1)}, u32[]{:S(2)}, u32[]{:S(2)}) collective-permute-start(bf16[32,2304]{1,0:T(8,128)(2,1)S(1)} %get-tuple-element.64), channel_id=1, source_target_pairs={{0,16},{4,20},{8,24},{12,28},{16,32},{20,36},{24,40},{28,44},{32,4... | collective-permute-start | bytes 442376 | tf_op jit(solution)/shard_map/ppermute | solution.py:175
  169.1 5.7 %collective-permute-start.34 = (bf16[32,2304]{1,0:T(8,128)(2,1)S(1)}, bf16[32,2304]{1,0:T(8,128)(2,1)S(1)}, u32[]{:S(2)}, u32[]{:S(2)}) collective-permute-start(bf16[32,2304]{1,0:T(8,128)(2,1)S(1)} %get-tuple-element.64), channel_id=1, source_target_pairs={{0,48},{4,52},{8,56},{12,60},{16,0},{20,4},{24,8},{28,12},{32,16},... | collective-permute-start | bytes 442376 | tf_op jit(solution)/shard_map/ppermute | solution.py:175
  172.0 5.6 %collective-permute-start.43 = (bf16[16,2304]{1,0:T(8,128)(2,1)S(1)}, bf16[16,2304]{1,0:T(8,128)(2,1)S(1)}, u32[]{:S(2)}, u32[]{:S(2)}) collective-permute-start(bf16[16,2304]{1,0:T(8,128)(2,1)S(1)} %slice.244), channel_id=1, source_target_pairs={{0,4},{4,8},{8,12},{12,0},{16,20},{20,24},{24,28},{28,16},{32,36},... | collective-permute-start | bytes 221192 | tf_op jit(solution)/shard_map/ppermute | solution.py:179
  172.0 5.6 %collective-permute-start.44 = (bf16[16,2304]{1,0:T(8,128)(2,1)S(1)}, bf16[16,2304]{1,0:T(8,128)(2,1)S(1)}, u32[]{:S(2)}, u32[]{:S(2)}) collective-permute-start(bf16[16,2304]{1,0:T(8,128)(2,1)S(1)} %slice.245), channel_id=1, source_target_pairs={{0,12},{4,0},{8,4},{12,8},{16,28},{20,16},{24,20},{28,24},{32,44},... | collective-permute-start | bytes 221192 | tf_op jit(solution)/shard_map/ppermute | solution.py:179
  174.7 5.7 %collective-permute-start.35 = (bf16[16,2304]{1,0:T(8,128)(2,1)S(1)}, bf16[16,2304]{1,0:T(8,128)(2,1)S(1)}, u32[]{:S(2)}, u32[]{:S(2)}) collective-permute-start(bf16[16,2304]{1,0:T(8,128)(2,1)S(1)} %slice.240), channel_id=1, source_target_pairs={{0,16},{4,20},{8,24},{12,28},{16,32},{20,36},{24,40},{28,44},{32,4... | collective-permute-start | bytes 221192 | tf_op jit(solution)/shard_map/ppermute | solution.py:175
  174.8 5.6 %collective-permute-start.36 = (bf16[16,2304]{1,0:T(8,128)(2,1)S(1)}, bf16[16,2304]{1,0:T(8,128)(2,1)S(1)}, u32[]{:S(2)}, u32[]{:S(2)}) collective-permute-start(bf16[16,2304]{1,0:T(8,128)(2,1)S(1)} %slice.241), channel_id=1, source_target_pairs={{0,48},{4,52},{8,56},{12,60},{16,0},{20,4},{24,8},{28,12},{32,16},... | collective-permute-start | bytes 221192 | tf_op jit(solution)/shard_map/ppermute | solution.py:175
  177.7 11.6 %collective-permute-start.45 = (bf16[128,2304]{1,0:T(8,128)(2,1)S(1)}, bf16[128,2304]{1,0:T(8,128)(2,1)S(1)}, u32[]{:S(2)}, u32[]{:S(2)}) collective-permute-start(bf16[128,2304]{1,0:T(8,128)(2,1)S(1)} %bitcast.182), channel_id=1, source_target_pairs={{0,16},{4,20},{8,24},{12,28},{16,32},{20,36},{24,40},{28,44},{32,4... | collective-permute-start | bytes 1769480 | tf_op jit(solution)/shard_map/ppermute | solution.py:175
  177.8 11.6 %collective-permute-start.46 = (bf16[128,2304]{1,0:T(8,128)(2,1)S(1)}, bf16[128,2304]{1,0:T(8,128)(2,1)S(1)}, u32[]{:S(2)}, u32[]{:S(2)}) collective-permute-start(bf16[128,2304]{1,0:T(8,128)(2,1)S(1)} %bitcast.183), channel_id=1, source_target_pairs={{0,48},{4,52},{8,56},{12,60},{16,0},{20,4},{24,8},{28,12},{32,16},... | collective-permute-start | bytes 1769480 | tf_op jit(solution)/shard_map/ppermute | solution.py:175
  180.5 11.6 %collective-permute-start.37 = (bf16[128,2304]{1,0:T(8,128)(2,1)S(1)}, bf16[128,2304]{1,0:T(8,128)(2,1)S(1)}, u32[]{:S(2)}, u32[]{:S(2)}) collective-permute-start(bf16[128,2304]{1,0:T(8,128)(2,1)S(1)} %bitcast.179), channel_id=1, source_target_pairs={{0,4},{4,8},{8,12},{12,0},{16,20},{20,24},{24,28},{28,16},{32,36},... | collective-permute-start | bytes 1769480 | tf_op jit(solution)/shard_map/ppermute | solution.py:179
  181.1 12.3 %collective-permute-start.38 = (bf16[128,2304]{1,0:T(8,128)(2,1)S(1)}, bf16[128,2304]{1,0:T(8,128)(2,1)S(1)}, u32[]{:S(2)}, u32[]{:S(2)}) collective-permute-start(bf16[128,2304]{1,0:T(8,128)(2,1)S(1)} %bitcast.180), channel_id=1, source_target_pairs={{0,12},{4,0},{8,4},{12,8},{16,28},{20,16},{24,20},{28,24},{32,44},... | collective-permute-start | bytes 1769480 | tf_op jit(solution)/shard_map/ppermute | solution.py:179
  189.3 9.1 %collective-permute-start.47 = (bf16[64,2304]{1,0:T(8,128)(2,1)S(1)}, bf16[64,2304]{1,0:T(8,128)(2,1)S(1)}, u32[]{:S(2)}, u32[]{:S(2)}) collective-permute-start(bf16[64,2304]{1,0:T(8,128)(2,1)S(1)} %slice.246), channel_id=1, source_target_pairs={{0,16},{4,20},{8,24},{12,28},{16,32},{20,36},{24,40},{28,44},{32,4... | collective-permute-start | bytes 884744 | tf_op jit(solution)/shard_map/ppermute | solution.py:175
  189.4 9.0 %collective-permute-start.48 = (bf16[64,2304]{1,0:T(8,128)(2,1)S(1)}, bf16[64,2304]{1,0:T(8,128)(2,1)S(1)}, u32[]{:S(2)}, u32[]{:S(2)}) collective-permute-start(bf16[64,2304]{1,0:T(8,128)(2,1)S(1)} %slice.247), channel_id=1, source_target_pairs={{0,48},{4,52},{8,56},{12,60},{16,0},{20,4},{24,8},{28,12},{32,16},... | collective-permute-start | bytes 884744 | tf_op jit(solution)/shard_map/ppermute | solution.py:175
  192.9 22.7 %collective-permute-start.39 = (bf16[64,2304]{1,0:T(8,128)(2,1)}, bf16[64,2304]{1,0:T(8,128)(2,1)}, u32[]{:S(2)}, u32[]{:S(2)}) collective-permute-start(bf16[64,2304]{1,0:T(8,128)(2,1)} %slice.242), channel_id=1, source_target_pairs={{0,4},{4,8},{8,12},{12,0},{16,20},{20,24},{24,28},{28,16},{32,36},... | collective-permute-start | bytes 884744 | tf_op jit(solution)/shard_map/ppermute | solution.py:179
  194.1 21.4 %collective-permute-start.40 = (bf16[64,2304]{1,0:T(8,128)(2,1)}, bf16[64,2304]{1,0:T(8,128)(2,1)}, u32[]{:S(2)}, u32[]{:S(2)}) collective-permute-start(bf16[64,2304]{1,0:T(8,128)(2,1)} %slice.243), channel_id=1, source_target_pairs={{0,12},{4,0},{8,4},{12,8},{16,28},{20,16},{24,20},{28,24},{32,44},... | collective-permute-start | bytes 884744 | tf_op jit(solution)/shard_map/ppermute | solution.py:179
  202.3 17.5 %collective-permute-start.49 = (bf16[4,4,4,8,448]{4,3,2,1,0:T(8,128)(2,1)}, bf16[4,4,4,8,448]{4,3,2,1,0:T(8,128)(2,1)S(1)}, u32[]{:S(2)}, u32[]{:S(2)}) collective-permute-start(bf16[4,4,4,8,448]{4,3,2,1,0:T(8,128)(2,1)} %bitcast.156), channel_id=1, source_target_pairs={{0,1},{1,0},{2,3},{3,2},{4,5},{5,4},{6,7},{7,6},{8,9},{9,8},{10,11... | collective-permute-start | bytes 1376264 | tf_op jit(solution)/shard_map/ppermute | solution.py:192
  220.0 14.6 %copy-start.8 = (f32[4,4,2,8,448]{4,3,1,0,2:T(8,128)S(1)}, f32[4,4,2,8,448]{4,3,1,0,2:T(8,128)}, u32[]{:S(2)}) copy-start(f32[4,4,2,8,448]{4,3,1,0,2:T(8,128)} %copy-done.7) | copy-start | bytes 1376260
  220.2 8.5 %collective-permute-start.50 = (bf16[4,4,2,8,448]{4,3,1,0,2:T(8,128)(2,1)S(1)}, bf16[4,4,2,8,448]{4,3,1,0,2:T(8,128)(2,1)S(1)}, u32[]{:S(2)}, u32[]{:S(2)}) collective-permute-start(bf16[4,4,2,8,448]{4,3,1,0,2:T(8,128)(2,1)S(1)} %get-tuple-element.55), channel_id=1, source_target_pairs={{0,64},{1,65},{2,66},{3,67},{64,2},{65,3},{66,0},{67,1},{4,68},{5,... | collective-permute-start | bytes 688136 | tf_op jit(solution)/shard_map/ppermute | solution.py:188
  220.7 8.1 %collective-permute-start.51 = (bf16[4,4,2,8,448]{4,3,1,0,2:T(8,128)(2,1)S(1)}, bf16[4,4,2,8,448]{4,3,1,0,2:T(8,128)(2,1)S(1)}, u32[]{:S(2)}, u32[]{:S(2)}) collective-permute-start(bf16[4,4,2,8,448]{4,3,1,0,2:T(8,128)(2,1)S(1)} %get-tuple-element.55), channel_id=1, source_target_pairs={{0,66},{1,67},{2,64},{3,65},{64,0},{65,1},{66,2},{67,3},{4,70},{5,... | collective-permute-start | bytes 688136 | tf_op jit(solution)/shard_map/ppermute | solution.py:188
  222.9 11.7 %collective-permute-start.52 = (bf16[4,4,2,8,448]{4,3,1,0,2:T(8,128)(2,1)S(1)}, bf16[4,4,2,8,448]{4,3,1,0,2:T(8,128)(2,1)S(1)}, u32[]{:S(2)}, u32[]{:S(2)}) collective-permute-start(bf16[4,4,2,8,448]{4,3,1,0,2:T(8,128)(2,1)S(1)} %get-tuple-element.56), channel_id=1, source_target_pairs={{0,2},{1,3},{2,0},{3,1},{64,66},{65,67},{66,64},{67,65},{4,6},{5,7... | collective-permute-start | bytes 688136 | tf_op jit(solution)/shard_map/ppermute | solution.py:188
  249.4 4.7 %copy-start.1 = (bf16[16,512,128]{2,1,0:T(8,128)(2,1)S(1)}, bf16[16,512,128]{2,1,0:T(8,128)(2,1)}, u32[]{:S(2)}) copy-start(bf16[16,512,128]{2,1,0:T(8,128)(2,1)} %param.18) | copy-start | bytes 6291460
  249.8 3.4 %collective-permute-start.53 = (bf16[2,8,7168]{2,1,0:T(8,128)(2,1)S(1)}, bf16[2,8,7168]{2,1,0:T(8,128)(2,1)S(1)}, u32[]{:S(2)}, u32[]{:S(2)}) collective-permute-start(bf16[2,8,7168]{2,1,0:T(8,128)(2,1)S(1)} %reshape.126), channel_id=1, source_target_pairs={{0,1},{1,0},{2,3},{3,2},{4,5},{5,4},{6,7},{7,6},{8,9},{9,8},{10,11... | collective-permute-start | bytes 688136 | tf_op jit(solution)/shard_map/ppermute | solution.py:192
  (6 other events, 7.1 us)
where the time goes:
time: 259 us; the launch traced here: 255 us
  starting transfers between devices  102 us (39%)
  waiting for transfers between devices  92.6 us (36%)
  Pallas kernels  20.3 us (8%)
  blocking collectives  14.3 us (6%)
  local copies, waits for them, and re-layouts  13.2 us (5%)
  matrix products  6.24 us (2%)
  other arithmetic  4.79 us (2%)
    ppermute x22, starting transfers between devices, shift_z(): lax.ppermute(value, 'grp', [(g, g // 4 * 4 + (g + shift) % 4) for g in ra...  38.6 us
    ppermute x22, waiting for transfers between devices, shift_z(): lax.ppermute(value, 'grp', [(g, g // 4 * 4 + (g + shift) % 4) for g in ra...  31.5 us
    ppermute x22, starting transfers between devices, shift_x(): lax.ppermute(value, 'grp', [(g, (g // 4 + shift) % 4 * 4 + g % 4) for g i...  27.4 us
    ppermute x22, waiting for transfers between devices, shift_x(): lax.ppermute(value, 'grp', [(g, (g // 4 + shift) % 4 * 4 + g % 4) for g i...  27.2 us
    ppermute x4, starting transfers between devices, swap_core(): return lax.ppermute(value, 'tp', [(t, t ^ 1) for t in range(4)])  22.3 us
    ppermute x6, waiting for transfers between devices, shift_y(): lax.ppermute(value, ('role', 'tp'), [(p, moved(p)) for p in range(8)])  22.1 us
    all_to_all x1, blocking collectives, body(): lax.all_to_all(result, 'grp', split_axis=0, concat_axis=2, tiled=True)  14.3 us
    pallas_call x1, Pallas kernels, attend(): pl.pallas_call(functools.partial(attend_kernel, scale, latent), grid_spec...  10.7 us
  transfers between devices with their start and end apart: 55, of which 26 were waited for; matrix products, arithmetic and copies ran while one was open for 5% of the time, Pallas kernels for 3%

commit v1 on v0

v1 whole, which is shorter than its diff:
```python
import functools

import jax
import jax.numpy as jnp
from jax import lax
from jax.experimental import pallas as pl
from jax.experimental.pallas import tpu as pltpu
from jax.sharding import Mesh
from jax.sharding import PartitionSpec as P

epsilon = 1e-06
VMEM_LIMIT = 48 * 1024 * 1024


SHIFTS = (0, 1, -1, 2)
FACING = (0, 2, 1, 3)


def attend_kernel(
    scale, latent, members_ref, lengths_ref, place_ref, q_ref, new_ref, kv_ref, near_ref, far_ref
):
    token = pl.program_id(0)
    length = lengths_ref[members_ref[token]]
    place = place_ref[0]
    queries = jnp.concatenate([q_ref[0, place ^ i] for i in range(4)], axis=0)
    cache = kv_ref[0]
    newest = new_ref[0]
    scores = scale * jnp.dot(queries, cache, preferred_element_type=jnp.float32)
    own = scale * jnp.sum(queries.astype(jnp.float32) * newest, axis=1, keepdims=True)
    usable = lax.broadcasted_iota(jnp.int32, scores.shape, 1) < length
    scores = jnp.where(usable, scores, -1e30)
    peak = jnp.maximum(jnp.max(scores, axis=1, keepdims=True), own)
    probs = jnp.exp(scores - peak).astype(jnp.bfloat16)
    self_weight = jnp.exp(own - peak)
    denom = jnp.sum(probs.astype(jnp.float32), axis=1, keepdims=True) + self_weight
    accum = lax.dot_general(
        probs, cache[:latent], (((1,), (1,)), ((), ())), preferred_element_type=jnp.float32
    )
    accum = accum + self_weight * newest[:, :latent]
    context = (accum / denom).astype(near_ref.dtype)
    half = context.shape[0] // 2
    near_ref[...] = context[:half].reshape(near_ref.shape)
    far_ref[...] = context[half:].reshape(far_ref.shape)


def attend(q_latent, kv_new, kv_cache, lengths, members, place, scale, latent):
    tokens, heads, kv = q_latent.shape
    ctx = kv_cache.shape[1]
    block = heads // 4
    grid_spec = pltpu.PrefetchScalarGridSpec(
        num_scalar_prefetch=3,
        grid=(tokens,),
        in_specs=[
            pl.BlockSpec((1, 4, block, kv), lambda t, m, n, p: (t, 0, 0, 0)),
            pl.BlockSpec((1, 1, kv), lambda t, m, n, p: (t, 0, 0)),
            pl.BlockSpec((1, kv, ctx), lambda t, m, n, p: (m[t], 0, 0)),
        ],
        out_specs=[pl.BlockSpec((2, 1, block, latent), lambda t, m, n, p: (0, t, 0, 0))] * 2,
    )
    return pl.pallas_call(
        functools.partial(attend_kernel, scale, latent),
        grid_spec=grid_spec,
        out_shape=[jax.ShapeDtypeStruct((2, tokens, block, latent), jnp.bfloat16)] * 2,
        compiler_params=pltpu.CompilerParams(vmem_limit_bytes=VMEM_LIMIT),
        cost_estimate=pl.CostEstimate(
            flops=2 * tokens * heads * ctx * (kv + latent),
            bytes_accessed=2 * tokens * ctx * kv,
            transcendentals=tokens * heads * ctx,
        ),
        name="attend",
    )(
        members,
        lengths,
        place,
        q_latent.reshape(tokens, 4, block, kv),
        kv_new.astype(jnp.float32)[:, None, :],
        jnp.swapaxes(kv_cache, 1, 2),
    )


def partial_kernel(jobs, *refs):
    count = 1 + max(rows for pieces in jobs for rows, _ in pieces)
    row_refs, gain_ref, weight_refs, outs = (
        refs[:count],
        refs[count],
        refs[count + 1 : count + 3],
        refs[count + 3 :],
    )
    half = weight_refs[0].shape[1]
    gain = gain_ref[...]
    ready = []
    for ref in row_refs:
        x = ref[...].reshape(-1, ref.shape[-1]).astype(jnp.float32)
        ready.append(((x * gain).astype(jnp.bfloat16), jnp.sum(x * x, axis=1, keepdims=True)))
    for pieces, out in zip(jobs, outs):
        start = 0
        for rows, side in pieces:
            scaled, square = ready[rows]
            out[:, start : start + half] = jnp.dot(
                scaled, weight_refs[side][...], preferred_element_type=jnp.float32
            ).astype(jnp.bfloat16)
            start += half
            if side == 0:
                high = square.astype(jnp.bfloat16).astype(jnp.float32)
                lane = lax.broadcasted_iota(jnp.int32, (scaled.shape[0], 128), 1)
                out[:, start : start + 128] = jnp.where(lane < 64, high, square - high).astype(
                    jnp.bfloat16
                )
                start += 128


def partial_sums(rows, places, gain, weights, jobs):
    _, _, per_group, width = rows.shape
    half = weights[0].shape[1]
    count = 4 * per_group
    whole = lambda i: (0, 0)

    def at(place):
        return lambda i: (0, place, 0, 0)

    widths = [sum(half + (128 if side == 0 else 0) for _, side in pieces) for pieces in jobs]
    return pl.pallas_call(
        functools.partial(partial_kernel, jobs),
        grid=(1,),
        in_specs=[pl.BlockSpec((4, 1, per_group, width), at(p)) for p in places]
        + [pl.BlockSpec((1, width), whole)]
        + [pl.BlockSpec((width, half), whole)] * 2,
        out_specs=[pl.BlockSpec((count, w), whole) for w in widths],
        out_shape=[jax.ShapeDtypeStruct((count, w), jnp.bfloat16) for w in widths],
        compiler_params=pltpu.CompilerParams(vmem_limit_bytes=VMEM_LIMIT),
        cost_estimate=pl.CostEstimate(
            flops=2 * count * width * sum(widths),
            bytes_accessed=2 * (2 * width * half + count * sum(widths)),
            transcendentals=0,
        ),
        name="partial_sums",
    )(*([rows] * len(places)), gain, *weights)


def merge_kernel(own_a, own_c, plus, minus, relay_a, relay_c, *outs):
    wide_a, wide_c = own_a.shape[1], own_c.shape[1]
    rows = outs[0].shape[0]
    for out, place in zip(outs, FACING):
        part = pl.ds(place * rows, rows)
        total = wide(own_a[part, :]) + wide(relay_a[part, :]) + wide(minus[part, wide_c:])
        out[:, :wide_a] = total.astype(jnp.bfloat16)
        total = wide(own_c[part, :]) + wide(relay_c[part, :]) + wide(plus[part, wide_a:])
        out[:, wide_a:] = total.astype(jnp.bfloat16)


def merge(*operands):
    own_a, own_c = operands[:2]
    rows = own_a.shape[0] // 4
    cols = own_a.shape[1] + own_c.shape[1]
    return pl.pallas_call(
        merge_kernel,
        out_shape=[jax.ShapeDtypeStruct((rows, cols), jnp.bfloat16)] * 4,
        in_specs=[pl.BlockSpec(memory_space=pltpu.VMEM)] * 6,
        out_specs=[pl.BlockSpec(memory_space=pltpu.VMEM)] * 4,
        compiler_params=pltpu.CompilerParams(vmem_limit_bytes=VMEM_LIMIT),
        cost_estimate=pl.CostEstimate(
            flops=12 * rows * cols, bytes_accessed=32 * rows * cols, transcendentals=0
        ),
        name="merge",
    )(*operands)


def ring(first):
    def shift(value, by):
        pairs = []
        for g in range(16):
            for tp in range(4):
                x, z = g // 4, g % 4
                if (tp % 2 == 0) == first:
                    x = (x + by) % 4
                else:
                    z = (z + by) % 4
                pairs.append((g * 4 + tp, (x * 4 + z) * 4 + tp))
        return lax.ppermute(value, ("grp", "yh", "core"), pairs)

    return shift


shift_1, shift_2 = ring(True), ring(False)


def shift_y(value, by):
    def moved(place):
        role, yh, core = place // 4, place // 2 % 2, place % 2
        y = (yh * 2 + role + by) % 4
        return y % 2 * 4 + y // 2 * 2 + core

    return lax.ppermute(value, ("role", "yh", "core"), [(p, moved(p)) for p in range(8)])


def swap(value, axis):
    return lax.ppermute(value, axis, [(0, 1), (1, 0)])


def gather(block, shift):
    return jnp.stack([block] + [shift(block, s) for s in SHIFTS[1:]])


def gather_ring(block, shift):
    behind, ahead = shift(block, 1), shift(block, -1)
    middle = block.shape[0] // 2
    far = [shift(behind[:middle], 1), shift(ahead[middle:], -1)]
    return jnp.stack([block, behind, ahead, jnp.concatenate(far)])


def wide(value):
    return value.astype(jnp.float32)


def add(*values):
    return sum(wide(v) for v in values)


def scatter_step(plus, minus, ahead_a, behind_c, shift):
    wide_a, wide_c = ahead_a.shape[1], behind_c.shape[1]
    plus, minus = shift(plus, 1), shift(minus, -1)
    relay_a = shift(add(ahead_a, plus[:, :wide_a]).astype(jnp.bfloat16), 1)
    relay_c = shift(add(behind_c, minus[:, :wide_c]).astype(jnp.bfloat16), -1)
    return plus, minus, relay_a, relay_c


def absolute(blocks, place, axis):
    take = lambda i: lax.slice_in_dim(blocks, i, i + 1, axis=axis)
    doubled = jnp.concatenate([take(i) for i in (2, 3, 1, 0, 2, 3, 1)], axis=axis)
    return lax.dynamic_slice_in_dim(doubled, (3 - place) % 4, 4, axis=axis)


def relative(blocks, place, axis):
    doubled = jnp.concatenate([blocks, lax.slice_in_dim(blocks, 0, 3, axis=axis)], axis=axis)
    turned = lax.dynamic_slice_in_dim(doubled, place, 4, axis=axis)
    return jnp.concatenate(
        [lax.slice_in_dim(turned, i, i + 1, axis=axis) for i in (0, 3, 1, 2)], axis=axis
    )


def body(
    q_latent,
    kv_new,
    kv_cache,
    lengths,
    members,
    hidden_in,
    w_uv,
    w_o,
    norm_gain,
    w_gate,
    w_up,
    w_down,
):
    groups = lax.axis_size("grp")
    place_x, place_z = lax.axis_index("grp") // 4, lax.axis_index("grp") % 4
    core, yh = lax.axis_index("core"), lax.axis_index("yh")
    place_1 = jnp.where(core == 0, place_x, place_z)
    place_2 = jnp.where(core == 0, place_z, place_x)
    tokens, heads, kv = q_latent.shape
    latent = w_uv.shape[1]
    value_width = w_uv.shape[2]
    width = w_o.shape[1]
    model_width = width * groups
    hidden = w_gate.shape[1]
    score_scale = (value_width + kv - latent) ** (-0.5)

    uv_pair = (w_uv, swap(w_uv, "core"))
    o_pair = (w_o, swap(w_o, "core"))
    down_pair = (w_down, swap(w_down, "core"))
    in_pair = (
        jnp.where(core == 0, w_gate, w_up),
        swap(jnp.where(core == 0, w_up, w_gate), "core"),
    )

    residual = lax.dynamic_index_in_dim(
        hidden_in.reshape(4, 4, 2, 2, tokens, width), core, 3, keepdims=False
    )
    residual = jnp.where(core == 0, jnp.swapaxes(residual, 0, 1), residual)
    residual = wide(relative(relative(residual, place_2, 0), place_1, 1))

    near, far = attend(
        q_latent,
        kv_new,
        kv_cache,
        lengths,
        members,
        (2 * yh + core).astype(jnp.int32)[None],
        score_scale,
        latent,
    )
    far = swap(far, "yh")
    context = jnp.stack([jnp.where(yh == 0, near, far), jnp.where(yh == 0, far, near)], axis=1)
    context = context.reshape(2, 2 * tokens, heads // 4, latent)
    values = jnp.concatenate(
        [
            jnp.einsum("thl,hlv->thv", c, w, preferred_element_type=jnp.float32)
            .astype(jnp.bfloat16)
            .reshape(2 * tokens, -1)
            for c, w in zip(context, uv_pair)
        ],
        axis=1,
    )
    values = gather(gather(values, shift_1), shift_2)
    values = values.reshape(groups * 2 * tokens, 2, -1)
    attn_part = sum(
        jnp.dot(values[:, i], o_pair[i], preferred_element_type=jnp.float32) for i in range(2)
    ).reshape(4, 4, 2, tokens, width)
    shared = 0.5 * residual + attn_part
    sent = shared.astype(jnp.bfloat16)
    behind, ahead, across = (shift_y(sent, s) for s in SHIFTS[1:])
    stream = shared + wide(across)
    rows = jnp.stack([stream, add(behind, ahead)]).astype(jnp.bfloat16)
    rows = jnp.stack([rows, jnp.swapaxes(swap(rows, "core"), 1, 2)])
    rows = jnp.transpose(rows, (2, 3, 0, 1, 4, 5, 6)).reshape(4, 4, 8 * tokens, width)

    gain = wide(norm_gain)[None]
    places = (3, FACING[1], FACING[2])
    (plus,) = partial_sums(rows, places[:2], gain, in_pair, (((0, 0), (1, 1)),))
    (minus,) = partial_sums(rows, places[::2], gain, in_pair, (((0, 1), (1, 0)),))
    places = (FACING[1], FACING[2], 0)
    rest = (((0, 0),), ((1, 1),), ((2, 0),), ((2, 1),))
    ahead_a, behind_c, own_a, own_c = partial_sums(rows, places, gain, in_pair, rest)
    arrived = scatter_step(plus, minus, ahead_a, behind_c, shift_1)
    blocks = merge(own_a, own_c, *arrived)
    sums = add(blocks[0], *(shift_2(blocks[i], SHIFTS[i]) for i in range(1, 4)))
    square = sums[:, hidden : hidden + 1] + sums[:, hidden + 64 : hidden + 65]
    scale = lax.rsqrt(square / model_width + epsilon)
    sums = [sums[:, :hidden] * scale, sums[:, hidden + 128 :] * scale]
    own = [s[: 4 * tokens] for s in sums]
    other = swap(
        jnp.concatenate([s[4 * tokens :].astype(jnp.bfloat16) for s in sums], axis=1), "core"
    )
    other = [wide(other[:, hidden:]), wide(other[:, :hidden])]
    activated = jnp.concatenate(
        [
            (jax.nn.silu(jnp.where(core == 0, a, b)) * jnp.where(core == 0, b, a)).astype(
                jnp.bfloat16
            )
            for a, b in zip(own, other)
        ],
        axis=1,
    )

    activated = gather(activated, shift_1).reshape(-1, 2 * hidden)
    activated = gather_ring(activated, shift_2).reshape(-1, 2, hidden)
    down = sum(
        jnp.dot(activated[:, i], down_pair[i], preferred_element_type=jnp.float32)
        for i in range(2)
    ).reshape(4, 4, 2, 2, tokens, width)
    at_home = jnp.arange(2)[None, None, :, None, None] == yh
    down = jnp.stack([down[:, :, 0] + jnp.where(at_home, stream, 0.0), down[:, :, 1]])
    down = down.astype(jnp.bfloat16)
    down = absolute(absolute(down, place_2, 1), place_1, 2)
    down = jnp.where(core == 0, jnp.swapaxes(down, 1, 2), down)
    role = lax.axis_index("role")
    down = jnp.where(role == 0, down, down[::-1])
    down = down.reshape(2 * groups * 2, tokens, width)
    landed = lax.all_to_all(down, ("role", "grp", "yh"), split_axis=0, concat_axis=0)
    landed = landed.reshape(2, groups, 2, tokens, width)
    result = jnp.sum(wide(landed), axis=(0, 2)).astype(jnp.bfloat16)
    result = jnp.swapaxes(result, 0, 1).reshape(tokens, model_width)
    return lax.all_gather(result, ("yh", "core"), axis=0, tiled=True)


def solution(mesh):
    tp = ("yh", "core")
    in_specs = (
        P(("role", "grp") + tp, None, None),
        P(("role", "grp") + tp, None),
        P(("role", "grp") + tp, None, None),
        P(("role", "grp") + tp),
        P(("role", "grp") + tp),
        P("role", "grp"),
        P(tp, None, None),
        P(tp, "grp"),
        P("grp"),
        P("grp", ("role",) + tp),
        P("grp", ("role",) + tp),
        P(("role",) + tp, "grp"),
    )
    out_specs = P(("role", "grp"), None)
    sizes = dict(mesh.shape)
    split_mesh = Mesh(
        mesh.devices.reshape(sizes["role"], sizes["grp"], 2, 2), ("role", "grp", "yh", "core")
    )
    return jax.shard_map(
        body, mesh=split_mesh, in_specs=in_specs, out_specs=out_specs, check_vma=False
    )
```

time: 259 us -> 276 us (1.066); the launches traced: 255 us -> 275 us
  starting transfers between devices: 102 us -> 47.9 us
  local copies, waits for them, and re-layouts: 13.2 us -> 38.4 us
  blocking collectives: 14.3 us -> 32.1 us
  other arithmetic: 4.79 us -> 13.4 us
  waiting for transfers between devices: 92.6 us -> 101 us
  Pallas kernels: 20.3 us -> 27.5 us
  matrix products: 6.24 us -> 13.4 us
    ppermute x54 -> x30, starting transfers between devices: 96 us -> 47.9 us  [the longest x20 28.9 us: shift(): return lax.ppermute(value, ('grp', 'yh', 'core'), pairs)]
    ppermute x54 -> x30, waiting for transfers between devices: 84.4 us -> 101 us  [the longest x20 90.5 us: shift(): return lax.ppermute(value, ('grp', 'yh', 'core'), pairs)]
    slice x5 -> x4, local copies, waits for them, and re-layouts: 0.14 us -> 15.4 us  [the longest x1 9.8 us: body(): activated[:, i]]
    all_gather x0 -> x1, blocking collectives: none -> 12.1 us  [body(): return lax.all_gather(result, ('yh', 'core'), axis=0, tiled=True)]
    reshape x2 -> x3, local copies, waits for them, and re-layouts: 1.11 us -> 11.9 us  [the longest x1 7.26 us: body(): activated = gather_ring(activated, shift_2).reshape(-1, 2, hidden)]
    all_to_all x1 -> x0, waiting for transfers between devices: 8.17 us -> none  [body(): spread = lax.all_to_all(context, 'tp', split_axis=0, concat_axis=0)]
    pallas_call x6 -> x4, Pallas kernels: 9.63 us -> 17.5 us  [the longest x3 13.9 us: partial_sums(): pl.pallas_call(functools.partial(partial_kernel, jobs), grid=(1,), in_spe...]
    dot_general x5 -> x6, matrix products: 6.24 us -> 13.4 us  [the longest x2 5.7 us: body(): jnp.dot(activated[:, i], down_pair[i], preferred_element_type=jnp.float32)]
  transfers between devices with their start and end apart: 55 -> 30, of which waited for: 26 -> 23; matrix products, arithmetic and copies ran while one was open for 5% -> 19% of each run, Pallas kernels for 3% -> 7%
where the time goes in v1:
time: 276 us; the launch traced here: 275 us
  waiting for transfers between devices  101 us (37%)
  starting transfers between devices  47.9 us (17%)
  local copies, waits for them, and re-layouts  38.4 us (14%)
  blocking collectives  32.1 us (12%)
  Pallas kernels  27.5 us (10%)
  other arithmetic  13.4 us (5%)
  matrix products  13.4 us (5%)
    ppermute x20, waiting for transfers between devices, shift(): return lax.ppermute(value, ('grp', 'yh', 'core'), pairs)  90.5 us
    ppermute x20, starting transfers between devices, shift(): return lax.ppermute(value, ('grp', 'yh', 'core'), pairs)  28.9 us
    all_to_all x1, blocking collectives, body(): lax.all_to_all(down, ('role', 'grp', 'yh'), split_axis=0, concat_axis=0)  20 us
    ppermute x7, starting transfers between devices, swap(): return lax.ppermute(value, axis, [(0, 1), (1, 0)])  15.4 us
    pallas_call x3, Pallas kernels, partial_sums(): pl.pallas_call(functools.partial(partial_kernel, jobs), grid=(1,), in_spe...  13.9 us
    all_gather x1, blocking collectives, body(): return lax.all_gather(result, ('yh', 'core'), axis=0, tiled=True)  12.1 us
    pallas_call x1, Pallas kernels, attend(): pl.pallas_call(functools.partial(attend_kernel, scale, latent), grid_spec...  10 us
    slice x1, local copies, waits for them, and re-layouts, body(): activated[:, i]  9.8 us
  transfers between devices with their start and end apart: 30, of which 23 were waited for; matrix products, arithmetic and copies ran while one was open for 19% of the time, Pallas kernels for 7%

profile of v1, /device:TPU:1, one launch (start us, length us, event | category | flops | bytes accessed | tf_op | source)
XLA Modules:
  0.0 274.7 jit_solution(18417577167958544522)
XLA Ops:
  0.0 1.4 collective-permute-start.1
  2.2 1.1 copy-done.1
  4.5 10.0 %attend.1 = (bf16[2,8,16,512]{3,2,1,0:T(8,128)(2,1)S(1)}, bf16[2,8,16,512]{3,2,1,0:T(8,128)(2,1)S(1)}) custom-call(s32[8]{0:T(128)S(1)} %copy-done.2, s32[8]{0:T(128)S(1)} %copy-done.3, s32[1]{0:T(128)} %bitcast.3.place_ref, bf16[8,4,16,576]{3,2,1,0:T(8,128)(2,1)S(1)} %bitcast.109, f32[8,1,576]{2,1,0:T(1,128)S(1)} %reshape.95.new_ref, ...), custom_call_target="tpu_custom_call" | custom-call | flops 1140850688 | bytes 9437184 | tf_op jit(solution)/shard_map/attend/pallas_call | solution.py:60
  14.6 3.1 %collective-permute-start = (bf16[2,8,16,512]{3,2,1,0:T(8,128)(2,1)S(1)}, bf16[2,8,16,512]{3,2,1,0:T(8,128)(2,1)S(1)}, u32[]{:S(2)}, u32[]{:S(2)}) collective-permute-start(bf16[2,8,16,512]{3,2,1,0:T(8,128)(2,1)S(1)} %get-tuple-element.16), channel_id=1, source_target_pairs={{0,2},{2,0},{1,3},{3,1},{4,6},{6,4},{5,7},{7,5},{8,10},{10,8},{9,1... | collective-permute-start | bytes 786440 | tf_op jit(solution)/shard_map/ppermute | solution.py:197
  17.9 3.8 %broadcast_select_fusion = (bf16[448,2304]{1,0:T(8,128)(2,1)}, bf16[448,2304]{1,0:T(8,128)(2,1)S(1)}) fusion(bf16[448,2304]{1,0:T(8,128)(2,1)} %param.22, bf16[448,2304]{1,0:T(8,128)(2,1)} %param.21, pred[]{:T(512)S(6)} %eq.35), kind=kLoop, calls=%fused_computation.10 | loop fusion | flops 2064384 | bytes 8257537 | tf_op jit(solution)/shard_map/jit(_where)/select_n | solution.py:273
  22.0 1.6 copy.76
  25.7 2.1 fusion.10
  27.8 1.7 collective-permute-start.2
  29.5 2.2 collective-permute-start.3
  31.7 1.2 collective-permute-start.4
  34.0 3.4 %collective-permute-done.4 = bf16[16,4096]{1,0:T(8,128)(2,1)} collective-permute-done((bf16[16,4096]{1,0:T(8,128)(2,1)S(1)}, bf16[16,4096]{1,0:T(8,128)(2,1)}, u32[]{:S(2)}, u32[]{:S(2)}) %collective-permute-start.4) | collective-permute-done | bytes 131104 | tf_op jit(solution)/shard_map/ppermute | solution.py:179
  39.4 1.8 collective-permute-start.6
  41.1 1.2 collective-permute-start.7
  42.6 5.4 %collective-permute-done.5 = bf16[4,16,4096]{2,1,0:T(8,128)(2,1)S(1)} collective-permute-done((bf16[4,16,4096]{2,1,0:T(8,128)(2,1)S(1)}, bf16[4,16,4096]{2,1,0:T(8,128)(2,1)S(1)}, u32[]{:S(2)}, u32[]{:S(2)}) %collective-permute-start.5) | collective-permute-done | bytes 524320 | tf_op jit(solution)/shard_map/ppermute | solution.py:179
  48.0 4.9 %collective-permute-done.6 = bf16[4,16,4096]{2,1,0:T(8,128)(2,1)S(1)} collective-permute-done((bf16[4,16,4096]{2,1,0:T(8,128)(2,1)S(1)}, bf16[4,16,4096]{2,1,0:T(8,128)(2,1)S(1)}, u32[]{:S(2)}, u32[]{:S(2)}) %collective-permute-start.6) | collective-permute-done | bytes 524320 | tf_op jit(solution)/shard_map/ppermute | solution.py:179
  52.9 1.4 collective-permute-done.7
  54.3 1.6 pad_maximum_fusion.1
  56.0 4.5 %reshape.86 = bf16[256,2,2048]{2,1,0:T(2,128)(2,1)} reshape(bf16[4,4,16,4096]{3,2,1,0:T(8,128)(2,1)} %pad_maximum_fusion.1) | data formatting | bytes 4194304 | tf_op jit(solution)/shard_map/reshape | solution.py:305
  60.5 5.5 %fusion.42 = (bf16[256,1,2048]{2,1,0:T(2,128)(2,1)S(1)}, bf16[256,1,2048]{2,1,0:T(2,128)(2,1)S(1)}) fusion(bf16[256,2,2048]{2,1,0:T(2,128)(2,1)} %reshape.86), kind=kLoop, calls=%fused_computation.109 | loop fusion | bytes 4194304 | tf_op jit(solution)/shard_map/slice | solution.py:307
  66.0 2.6 fusion.11
  68.6 2.6 convolution_add_fusion
  72.1 2.2 collective-permute-start.11
  75.2 2.9 %collective-permute-done.10 = bf16[4,4,2,8,448]{4,3,2,0,1:T(8,128)(2,1)S(1)} collective-permute-done((bf16[4,4,2,8,448]{4,3,2,0,1:T(8,128)(2,1)S(1)}, bf16[4,4,2,8,448]{4,3,2,0,1:T(8,128)(2,1)S(1)}, u32[]{:S(2)}, u32[]{:S(2)}) %collective-permute-start.10) | collective-permute-done | bytes 229408 | tf_op jit(solution)/shard_map/ppermute | solution.py:193
  78.1 2.9 %collective-permute-done.11 = bf16[4,4,2,8,448]{4,3,2,0,1:T(8,128)(2,1)S(1)} collective-permute-done((bf16[4,4,2,8,448]{4,3,2,0,1:T(8,128)(2,1)S(1)}, bf16[4,4,2,8,448]{4,3,2,0,1:T(8,128)(2,1)S(1)}, u32[]{:S(2)}, u32[]{:S(2)}) %collective-permute-start.11) | collective-permute-done | bytes 229408 | tf_op jit(solution)/shard_map/ppermute | solution.py:193
  81.1 1.8 collective-permute-done.9
  83.1 4.9 %collective-permute-start.12 = (bf16[2,4,4,2,8,448]{5,4,3,2,1,0:T(8,128)(2,1)S(1)}, bf16[2,4,4,2,8,448]{5,4,3,2,1,0:T(8,128)(2,1)S(1)}, u32[]{:S(2)}, u32[]{:S(2)}) collective-permute-start(bf16[2,4,4,2,8,448]{5,4,3,2,1,0:T(8,128)(2,1)S(1)} %pad_maximum_fusion.4), channel_id=1, source_target_pairs={{0,1},{1,0},{2,3},{3,2},{4,5},{5,4},{6,7},{7,6},{8,9},{9,8},{10,11... | collective-permute-start | bytes 1376264 | tf_op jit(solution)/shard_map/ppermute | solution.py:197
  88.1 1.5 collective-permute-done.12
  89.8 4.5 %partial_sums.4 = bf16[256,4736]{1,0:T(8,128)(2,1)} custom-call(bf16[4,4,64,448]{3,2,1,0:T(8,128)(2,1)S(1)} %bitcast.102, bf16[4,4,64,448]{3,2,1,0:T(8,128)(2,1)S(1)} %bitcast.103, f32[1,448]{1,0:T(1,128)S(1)} %bitcast.110, bf16[448,2304]{1,0:T(8,128)(2,1)S(1)} %get-tuple-element.28.refs_4_.refs_3_, bf16[448,2304]{1,0:T(8,128)(2,1)} %collective-permute-done.13.refs_5_.refs_4_), custom_call_target="tpu_custom_call" | custom-call | flops 1086324736 | bytes 6553600 | tf_op jit(solution)/shard_map/partial_sums/pallas_call | solution.py:122
  94.8 4.5 %partial_sums.5 = bf16[256,4736]{1,0:T(8,128)(2,1)} custom-call(bf16[4,4,64,448]{3,2,1,0:T(8,128)(2,1)S(1)} %bitcast.104, bf16[4,4,64,448]{3,2,1,0:T(8,128)(2,1)S(1)} %bitcast.105, f32[1,448]{1,0:T(1,128)S(1)} %bitcast.111, bf16[448,2304]{1,0:T(8,128)(2,1)S(1)} %get-tuple-element.28.refs_4_.refs_3_, bf16[448,2304]{1,0:T(8,128)(2,1)} %collective-permute-done.13.refs_5_.refs_4_), custom_call_target="tpu_custom_call" | custom-call | flops 1086324736 | bytes 6553600 | tf_op jit(solution)/shard_map/partial_sums/pallas_call | solution.py:122
  99.2 2.3 collective-permute-start.15
  101.5 4.9 %partial_sums.3 = (bf16[256,2432]{1,0:T(8,128)(2,1)S(1)}, bf16[256,2304]{1,0:T(8,128)(2,1)S(1)}, bf16[256,2432]{1,0:T(8,128)(2,1)S(1)}, bf16[256,2304]{1,0:T(8,128)(2,1)S(1)}) custom-call(bf16[4,4,64,448]{3,2,1,0:T(8,128)(2,1)S(1)} %bitcast.106, bf16[4,4,64,448]{3,2,1,0:T(8,128)(2,1)S(1)} %bitcast.107, bf16[4,4,64,448]{3,2,1,0:T(8,128)(2,1)S(1)} %bitcast.108, ...), custom_call_target="tpu_custom_call" | custom-call | flops 2172649472 | bytes 8978432 | tf_op jit(solution)/shard_map/partial_sums/pallas_call | solution.py:122
  106.4 18.1 %collective-permute-done.14.plus = bf16[256,4736]{1,0:T(8,128)(2,1)S(1)} collective-permute-done((bf16[256,4736]{1,0:T(8,128)(2,1)}, bf16[256,4736]{1,0:T(8,128)(2,1)S(1)}, u32[]{:S(2)}, u32[]{:S(2)}) %collective-permute-start.14) | collective-permute-done | bytes 2424864 | tf_op jit(solution)/shard_map/ppermute | solution.py:179
  124.9 3.5 %collective-permute-done.15.minus = bf16[256,4736]{1,0:T(8,128)(2,1)S(1)} collective-permute-done((bf16[256,4736]{1,0:T(8,128)(2,1)}, bf16[256,4736]{1,0:T(8,128)(2,1)S(1)}, u32[]{:S(2)}, u32[]{:S(2)}) %collective-permute-start.15) | collective-permute-done | bytes 2424864 | tf_op jit(solution)/shard_map/ppermute | solution.py:179
  128.6 3.1 %collective-permute-start.17 = (bf16[256,2304]{1,0:T(8,128)(2,1)S(1)}, bf16[256,2304]{1,0:T(8,128)(2,1)S(1)}, u32[]{:S(2)}, u32[]{:S(2)}) collective-permute-start(bf16[256,2304]{1,0:T(8,128)(2,1)S(1)} %add_convert_fusion.1), channel_id=1, source_target_pairs={{0,48},{1,13},{2,50},{3,15},{4,52},{5,1},{6,54},{7,3},{8,56},{9,5}... | collective-permute-start | bytes 3538952 | tf_op jit(solution)/shard_map/ppermute | solution.py:179
  131.7 13.1 %collective-permute-done.17.relay_c = bf16[256,2304]{1,0:T(8,128)(2,1)S(1)} collective-permute-done((bf16[256,2304]{1,0:T(8,128)(2,1)S(1)}, bf16[256,2304]{1,0:T(8,128)(2,1)S(1)}, u32[]{:S(2)}, u32[]{:S(2)}) %collective-permute-start.17) | collective-permute-done | bytes 1179680 | tf_op jit(solution)/shard_map/ppermute | solution.py:179
  144.9 1.1 copy-done.9
  145.9 3.6 %merge.1 = (bf16[64,4736]{1,0:T(8,128)(2,1)S(1)}, bf16[64,4736]{1,0:T(8,128)(2,1)S(1)}, bf16[64,4736]{1,0:T(8,128)(2,1)S(1)}, bf16[64,4736]{1,0:T(8,128)(2,1)S(1)}) custom-call(bf16[256,2432]{1,0:T(8,128)(2,1)S(1)} %get-tuple-element.17.own_a, bf16[256,2304]{1,0:T(8,128)(2,1)S(1)} %get-tuple-element.18.own_c, bf16[256,4736]{1,0:T(8,128)(2,1)} %copy-done.4, ...), custom_call_target="tpu_custom_call" | custom-call | flops 3637248 | bytes 9699328 | tf_op jit(solution)/shard_map/merge/pallas_call | solution.py:155
  150.5 1.8 collective-permute-start.19
  153.1 7.0 %collective-permute-done.18 = bf16[64,4736]{1,0:T(8,128)(2,1)S(1)} collective-permute-done((bf16[64,4736]{1,0:T(8,128)(2,1)S(1)}, bf16[64,4736]{1,0:T(8,128)(2,1)S(1)}, u32[]{:S(2)}, u32[]{:S(2)}) %collective-permute-start.18) | collective-permute-done | bytes 606240 | tf_op jit(solution)/shard_map/ppermute | solution.py:179
  160.0 5.8 %collective-permute-done.19 = bf16[64,4736]{1,0:T(8,128)(2,1)S(1)} collective-permute-done((bf16[64,4736]{1,0:T(8,128)(2,1)S(1)}, bf16[64,4736]{1,0:T(8,128)(2,1)S(1)}, u32[]{:S(2)}, u32[]{:S(2)}) %collective-permute-start.19) | collective-permute-done | bytes 606240 | tf_op jit(solution)/shard_map/ppermute | solution.py:179
  165.8 1.5 collective-permute-done.20
  168.1 2.8 %collective-permute-start.21 = (bf16[32,4608]{1,0:T(8,128)(2,1)S(1)}, bf16[32,4608]{1,0:T(8,128)(2,1)S(1)}, u32[]{:S(2)}, u32[]{:S(2)}) collective-permute-start(bf16[32,4608]{1,0:T(8,128)(2,1)S(1)} %pad_maximum_fusion.5), channel_id=1, source_target_pairs={{0,1},{1,0},{2,3},{3,2},{4,5},{5,4},{6,7},{7,6},{8,9},{9,8},{10,11... | collective-permute-start | bytes 884744 | tf_op jit(solution)/shard_map/ppermute | solution.py:197
  170.9 1.2 collective-permute-done.21
  172.3 1.2 collective-permute-start.22
  173.5 1.9 collective-permute-start.23
  175.4 1.1 collective-permute-start.24
  176.5 3.2 %collective-permute-done.22 = bf16[32,4608]{1,0:T(8,128)(2,1)S(1)} collective-permute-done((bf16[32,4608]{1,0:T(8,128)(2,1)S(1)}, bf16[32,4608]{1,0:T(8,128)(2,1)S(1)}, u32[]{:S(2)}, u32[]{:S(2)}) %collective-permute-start.22) | collective-permute-done | bytes 294944 | tf_op jit(solution)/shard_map/ppermute | solution.py:179
  179.8 2.5 collective-permute-done.23
  182.3 1.8 collective-permute-done.24
  184.3 3.4 %collective-permute-start.26 = (bf16[128,4608]{1,0:T(8,128)(2,1)S(1)}, bf16[128,4608]{1,0:T(8,128)(2,1)S(1)}, u32[]{:S(2)}, u32[]{:S(2)}) collective-permute-start(bf16[128,4608]{1,0:T(8,128)(2,1)S(1)} %bitcast.115), channel_id=1, source_target_pairs={{0,12},{1,49},{2,14},{3,51},{4,0},{5,53},{6,2},{7,55},{8,4},{9,57}... | collective-permute-start | bytes 3538952 | tf_op jit(solution)/shard_map/ppermute | solution.py:179
  187.7 13.6 %collective-permute-done.25 = bf16[128,4608]{1,0:T(8,128)(2,1)S(1)} collective-permute-done((bf16[128,4608]{1,0:T(8,128)(2,1)S(1)}, bf16[128,4608]{1,0:T(8,128)(2,1)S(1)}, u32[]{:S(2)}, u32[]{:S(2)}) %collective-permute-start.25) | collective-permute-done | bytes 1179680 | tf_op jit(solution)/shard_map/ppermute | solution.py:179
  202.2 1.0 copy-done.6
  204.1 2.7 collective-permute-start.28
  206.7 2.7 collective-permute-start.29
  209.4 3.3 %collective-permute-done.27 = bf16[64,4608]{1,0:T(8,128)(2,1)} collective-permute-done((bf16[64,4608]{1,0:T(8,128)(2,1)}, bf16[64,4608]{1,0:T(8,128)(2,1)}, u32[]{:S(2)}, u32[]{:S(2)}) %collective-permute-start.27) | collective-permute-done | bytes 589856 | tf_op jit(solution)/shard_map/ppermute | solution.py:179
  212.8 1.1 collective-permute-done.28
  213.9 1.3 maximum_bitcast_fusion
  215.2 2.5 pad_maximum_fusion
  217.7 7.3 %reshape.90 = bf16[512,2,2304]{2,1,0:T(2,128)(2,1)} reshape(bf16[4,128,4608]{2,1,0:T(8,128)(2,1)} %pad_maximum_fusion) | data formatting | bytes 9437184 | tf_op jit(solution)/shard_map/reshape | solution.py:346
  225.0 9.8 %fusion.41 = (bf16[512,1,2304]{2,1,0:T(2,128)(2,1)S(1)}, bf16[512,1,2304]{2,1,0:T(2,128)(2,1)S(1)}) fusion(bf16[512,2,2304]{2,1,0:T(2,128)(2,1)} %reshape.90), kind=kLoop, calls=%fused_computation.108 | loop fusion | bytes 9437184 | tf_op jit(solution)/shard_map/slice | solution.py:348
  234.8 2.8 %fusion = f32[512,448]{0,1:T(8,128)S(1)} fusion(bf16[2304,448]{0,1:T(8,128)(2,1)} %collective-permute-done.29, bf16[512,1,2304]{2,1,0:T(2,128)(2,1)S(1)} %get-tuple-element.26), kind=kOutput, calls=%fused_computation.2 | convolution fusion | flops 1056964608 | bytes 5341184 | tf_op jit(solution)/shard_map/dot_general | solution.py:348
  237.6 2.9 %fusion.6 = f32[512,448]{0,1:T(8,128)S(1)} fusion(f32[512,448]{0,1:T(8,128)S(1)} %fusion, bf16[2304,448]{0,1:T(8,128)(2,1)} %param.23, bf16[512,1,2304]{2,1,0:T(2,128)(2,1)S(1)} %get-tuple-element.25), kind=kOutput, calls=%fused_computation.12 | convolution fusion | flops 1057193984 | bytes 6258688 | tf_op jit(solution)/shard_map/dot_general | solution.py:348
  241.6 20.0 %all_to_all.5 = bf16[64,8,448]{2,1,0:T(8,128)(2,1)S(1)} all-to-all(bf16[64,8,448]{2,1,0:T(8,128)(2,1)S(1)} %bitcast.123), channel_id=1, replica_groups=mesh['role'=2,'grp'=16,'yh'=2,'core'=2] {'role','grp','yh'}, dimensions={0} | all-to-all | bytes 917504 | tf_op jit(solution)/shard_map/all_to_all | solution.py:359
  261.9 12.1 %all_gather.3 = bf16[32,7168]{1,0:T(8,128)(2,1)S(1)} all-gather(bf16[8,7168]{1,0:T(8,128)(2,1)S(1)} %reshape.94), channel_id=1, replica_groups=mesh['role'=2,'grp'=16,'yh'=2,'core'=2] {'yh','core'}, dimensions={0}, use_global_device_ids=true | all-gather | bytes 573440 | tf_op jit(solution)/shard_map/all_gather | solution.py:363
  (101 shorter events, 17.7 us)
Async XLA Ops:
  0.0 25.7 %collective-permute-start.1 = (bf16[16,512,128]{2,1,0:T(8,128)(2,1)}, bf16[16,512,128]{2,1,0:T(8,128)(2,1)}, u32[]{:S(2)}, u32[]{:S(2)}) collective-permute-start(bf16[16,512,128]{2,1,0:T(8,128)(2,1)} %param.18), channel_id=1, source_target_pairs={{0,1},{1,0},{2,3},{3,2},{4,5},{5,4},{6,7},{7,6},{8,9},{9,8},{10,11... | collective-permute-start | bytes 6291464 | tf_op jit(solution)/shard_map/ppermute | solution.py:197
  2.1 1.1 copy-start.1
  3.2 0.7 copy-start.2
  3.9 0.7 copy-start.3
  14.6 9.6 %collective-permute-start = (bf16[2,8,16,512]{3,2,1,0:T(8,128)(2,1)S(1)}, bf16[2,8,16,512]{3,2,1,0:T(8,128)(2,1)S(1)}, u32[]{:S(2)}, u32[]{:S(2)}) collective-permute-start(bf16[2,8,16,512]{3,2,1,0:T(8,128)(2,1)S(1)} %get-tuple-element.16), channel_id=1, source_target_pairs={{0,2},{2,0},{1,3},{3,1},{4,6},{6,4},{5,7},{7,5},{8,10},{10,8},{9,1... | collective-permute-start | bytes 786440 | tf_op jit(solution)/shard_map/ppermute | solution.py:197
  17.7 51.0 %collective-permute-start.8 = (bf16[2048,448]{0,1:T(8,128)(2,1)}, bf16[2048,448]{0,1:T(8,128)(2,1)}, u32[]{:S(2)}, u32[]{:S(2)}) collective-permute-start(bf16[2048,448]{0,1:T(8,128)(2,1)} %param.19), channel_id=1, source_target_pairs={{0,1},{1,0},{2,3},{3,2},{4,5},{5,4},{6,7},{7,6},{8,9},{9,8},{10,11... | collective-permute-start | bytes 5505032 | tf_op jit(solution)/shard_map/ppermute | solution.py:197
  21.8 73.0 %copy-start = (bf16[448,2304]{1,0:T(8,128)(2,1)}, bf16[448,2304]{1,0:T(8,128)(2,1)S(1)}, u32[]{:S(2)}) copy-start(bf16[448,2304]{1,0:T(8,128)(2,1)S(1)} %get-tuple-element.28.refs_4_.refs_3_) | copy-start | bytes 6193156
  21.8 68.1 %collective-permute-start.13 = (bf16[448,2304]{1,0:T(8,128)(2,1)}, bf16[448,2304]{1,0:T(8,128)(2,1)}, u32[]{:S(2)}, u32[]{:S(2)}) collective-permute-start(bf16[448,2304]{1,0:T(8,128)(2,1)} %get-tuple-element.27), channel_id=1, source_target_pairs={{0,1},{1,0},{2,3},{3,2},{4,5},{5,4},{6,7},{7,6},{8,9},{9,8},{10,11... | collective-permute-start | bytes 6193160 | tf_op jit(solution)/shard_map/ppermute | solution.py:197
  23.6 1.6 copy-start.8
  27.8 6.2 %collective-permute-start.2 = (bf16[16,4096]{1,0:T(8,128)(2,1)S(1)}, bf16[16,4096]{1,0:T(8,128)(2,1)S(1)}, u32[]{:S(2)}, u32[]{:S(2)}) collective-permute-start(bf16[16,4096]{1,0:T(8,128)(2,1)S(1)} %bitcast_dynamic-update-slice_fusion), channel_id=1, source_target_pairs={{0,16},{1,5},{2,18},{3,7},{4,20},{5,9},{6,22},{7,11},{8,24},{9,13}... | collective-permute-start | bytes 393224 | tf_op jit(solution)/shard_map/ppermute | solution.py:179
  29.5 4.5 %collective-permute-start.3 = (bf16[16,4096]{1,0:T(8,128)(2,1)S(1)}, bf16[16,4096]{1,0:T(8,128)(2,1)S(1)}, u32[]{:S(2)}, u32[]{:S(2)}) collective-permute-start(bf16[16,4096]{1,0:T(8,128)(2,1)S(1)} %bitcast_dynamic-update-slice_fusion), channel_id=1, source_target_pairs={{0,48},{1,13},{2,50},{3,15},{4,52},{5,1},{6,54},{7,3},{8,56},{9,5}... | collective-permute-start | bytes 393224 | tf_op jit(solution)/shard_map/ppermute | solution.py:179
  31.7 5.7 %collective-permute-start.4 = (bf16[16,4096]{1,0:T(8,128)(2,1)S(1)}, bf16[16,4096]{1,0:T(8,128)(2,1)}, u32[]{:S(2)}, u32[]{:S(2)}) collective-permute-start(bf16[16,4096]{1,0:T(8,128)(2,1)S(1)} %bitcast_dynamic-update-slice_fusion), channel_id=1, source_target_pairs={{0,32},{1,9},{2,34},{3,11},{4,36},{5,13},{6,38},{7,15},{8,40},{9,1... | collective-permute-start | bytes 393224 | tf_op jit(solution)/shard_map/ppermute | solution.py:179
  38.4 9.6 %collective-permute-start.5 = (bf16[4,16,4096]{2,1,0:T(8,128)(2,1)S(1)}, bf16[4,16,4096]{2,1,0:T(8,128)(2,1)S(1)}, u32[]{:S(2)}, u32[]{:S(2)}) collective-permute-start(bf16[4,16,4096]{2,1,0:T(8,128)(2,1)S(1)} %get-tuple-element.36), channel_id=1, source_target_pairs={{0,4},{1,17},{2,6},{3,19},{4,8},{5,21},{6,10},{7,23},{8,12},{9,25}... | collective-permute-start | bytes 1572872 | tf_op jit(solution)/shard_map/ppermute | solution.py:179
  39.4 13.5 %collective-permute-start.6 = (bf16[4,16,4096]{2,1,0:T(8,128)(2,1)S(1)}, bf16[4,16,4096]{2,1,0:T(8,128)(2,1)S(1)}, u32[]{:S(2)}, u32[]{:S(2)}) collective-permute-start(bf16[4,16,4096]{2,1,0:T(8,128)(2,1)S(1)} %get-tuple-element.36), channel_id=1, source_target_pairs={{0,12},{1,49},{2,14},{3,51},{4,0},{5,53},{6,2},{7,55},{8,4},{9,57}... | collective-permute-start | bytes 1572872 | tf_op jit(solution)/shard_map/ppermute | solution.py:179
  41.1 13.2 %collective-permute-start.7 = (bf16[4,16,4096]{2,1,0:T(8,128)(2,1)S(1)}, bf16[4,16,4096]{2,1,0:T(8,128)(2,1)S(1)}, u32[]{:S(2)}, u32[]{:S(2)}) collective-permute-start(bf16[4,16,4096]{2,1,0:T(8,128)(2,1)S(1)} %get-tuple-element.36), channel_id=1, source_target_pairs={{0,8},{1,33},{2,10},{3,35},{4,12},{5,37},{6,14},{7,39},{8,0},{9,41... | collective-permute-start | bytes 1572872 | tf_op jit(solution)/shard_map/ppermute | solution.py:179
  42.6 13.4 %copy-start.10 = (bf16[4,4,2,8,448]{4,3,2,1,0:T(8,128)(2,1)}, bf16[4,4,2,8,448]{4,3,2,1,0:T(8,128)(2,1)S(1)}, u32[]{:S(2)}) copy-start(bf16[4,4,2,8,448]{4,3,2,1,0:T(8,128)(2,1)S(1)} %fusion.20) | copy-start | bytes 688132
  68.6 2.8 %slice-start = ((bf16[4,4,2,8,448]{4,3,2,1,0:T(8,128)(2,1)}), bf16[4,2,2,8,448]{4,3,2,1,0:T(8,128)(2,1)S(1)}, s32[]{:S(2)}) async-start(bf16[4,4,2,8,448]{4,3,2,1,0:T(8,128)(2,1)} %copy-done.10), calls=%async_computation.1 | async-start | bytes 262144 | tf_op jit(solution)/shard_map/slice | solution.py:237
  71.6 16.5 %copy-start.11 = (bf16[448]{0:T(512)(128)(2,1)S(1)}, bf16[448]{0:T(512)(128)(2,1)}, u32[]{:S(2)}) copy-start(bf16[448]{0:T(512)(128)(2,1)} %param.20) | copy-start | bytes 2692
  71.6 6.5 %collective-permute-start.10 = (bf16[4,4,2,8,448]{4,3,2,0,1:T(8,128)(2,1)S(1)}, bf16[4,4,2,8,448]{4,3,2,0,1:T(8,128)(2,1)S(1)}, u32[]{:S(2)}, u32[]{:S(2)}) collective-permute-start(bf16[4,4,2,8,448]{4,3,2,0,1:T(8,128)(2,1)S(1)} %copy.141), channel_id=1, source_target_pairs={{0,64},{1,65},{2,66},{3,67},{64,2},{65,3},{66,0},{67,1},{4,68},{5,... | collective-permute-start | bytes 688136 | tf_op jit(solution)/shard_map/ppermute | solution.py:193
  72.1 8.9 %collective-permute-start.11 = (bf16[4,4,2,8,448]{4,3,2,0,1:T(8,128)(2,1)S(1)}, bf16[4,4,2,8,448]{4,3,2,0,1:T(8,128)(2,1)S(1)}, u32[]{:S(2)}, u32[]{:S(2)}) collective-permute-start(bf16[4,4,2,8,448]{4,3,2,0,1:T(8,128)(2,1)S(1)} %copy.141), channel_id=1, source_target_pairs={{0,66},{1,67},{2,64},{3,65},{64,0},{65,1},{66,2},{67,3},{4,70},{5,... | collective-permute-start | bytes 688136 | tf_op jit(solution)/shard_map/ppermute | solution.py:193
  74.4 8.6 %collective-permute-start.9 = (bf16[4,4,2,8,448]{4,3,2,0,1:T(8,128)(2,1)S(1)}, bf16[4,4,2,8,448]{4,3,2,0,1:T(8,128)(2,1)S(1)}, u32[]{:S(2)}, u32[]{:S(2)}) collective-permute-start(bf16[4,4,2,8,448]{4,3,2,0,1:T(8,128)(2,1)S(1)} %copy.141), channel_id=1, source_target_pairs={{0,2},{1,3},{2,0},{3,1},{64,66},{65,67},{66,64},{67,65},{4,6},{5,7... | collective-permute-start | bytes 688136 | tf_op jit(solution)/shard_map/ppermute | solution.py:193
  83.1 6.5 %collective-permute-start.12 = (bf16[2,4,4,2,8,448]{5,4,3,2,1,0:T(8,128)(2,1)S(1)}, bf16[2,4,4,2,8,448]{5,4,3,2,1,0:T(8,128)(2,1)S(1)}, u32[]{:S(2)}, u32[]{:S(2)}) collective-permute-start(bf16[2,4,4,2,8,448]{5,4,3,2,1,0:T(8,128)(2,1)S(1)} %pad_maximum_fusion.4), channel_id=1, source_target_pairs={{0,1},{1,0},{2,3},{3,2},{4,5},{5,4},{6,7},{7,6},{8,9},{9,8},{10,11... | collective-permute-start | bytes 1376264 | tf_op jit(solution)/shard_map/ppermute | solution.py:197
  94.4 30.1 %collective-permute-start.14 = (bf16[256,4736]{1,0:T(8,128)(2,1)}, bf16[256,4736]{1,0:T(8,128)(2,1)S(1)}, u32[]{:S(2)}, u32[]{:S(2)}) collective-permute-start(bf16[256,4736]{1,0:T(8,128)(2,1)} %partial_sums.4), channel_id=1, source_target_pairs={{0,16},{1,5},{2,18},{3,7},{4,20},{5,9},{6,22},{7,11},{8,24},{9,13}... | collective-permute-start | bytes 7274504 | tf_op jit(solution)/shard_map/ppermute | solution.py:179
  99.2 29.1 %collective-permute-start.15 = (bf16[256,4736]{1,0:T(8,128)(2,1)}, bf16[256,4736]{1,0:T(8,128)(2,1)S(1)}, u32[]{:S(2)}, u32[]{:S(2)}) collective-permute-start(bf16[256,4736]{1,0:T(8,128)(2,1)} %partial_sums.5), channel_id=1, source_target_pairs={{0,48},{1,13},{2,50},{3,15},{4,52},{5,1},{6,54},{7,3},{8,56},{9,5}... | collective-permute-start | bytes 7274504 | tf_op jit(solution)/shard_map/ppermute | solution.py:179
  124.5 4.1 %copy-start.4 = (bf16[256,4736]{1,0:T(8,128)(2,1)}, bf16[256,4736]{1,0:T(8,128)(2,1)S(1)}, u32[]{:S(2)}) copy-start(bf16[256,4736]{1,0:T(8,128)(2,1)S(1)} %collective-permute-done.14.plus) | copy-start | bytes 7274500
  124.8 20.1 %collective-permute-start.16 = (bf16[256,2432]{1,0:T(8,128)(2,1)S(1)}, bf16[256,2432]{1,0:T(8,128)(2,1)S(1)}, u32[]{:S(2)}, u32[]{:S(2)}) collective-permute-start(bf16[256,2432]{1,0:T(8,128)(2,1)S(1)} %add_convert_fusion), channel_id=1, source_target_pairs={{0,16},{1,5},{2,18},{3,7},{4,20},{5,9},{6,22},{7,11},{8,24},{9,13}... | collective-permute-start | bytes 3735560 | tf_op jit(solution)/shard_map/ppermute | solution.py:179
  128.3 16.5 %copy-start.5 = (bf16[256,4736]{1,0:T(8,128)(2,1)}, bf16[256,4736]{1,0:T(8,128)(2,1)S(1)}, u32[]{:S(2)}) copy-start(bf16[256,4736]{1,0:T(8,128)(2,1)S(1)} %collective-permute-done.15.minus) | copy-start | bytes 7274500
  128.6 16.2 %collective-permute-start.17 = (bf16[256,2304]{1,0:T(8,128)(2,1)S(1)}, bf16[256,2304]{1,0:T(8,128)(2,1)S(1)}, u32[]{:S(2)}, u32[]{:S(2)}) collective-permute-start(bf16[256,2304]{1,0:T(8,128)(2,1)S(1)} %add_convert_fusion.1), channel_id=1, source_target_pairs={{0,48},{1,13},{2,50},{3,15},{4,52},{5,1},{6,54},{7,3},{8,56},{9,5}... | collective-permute-start | bytes 3538952 | tf_op jit(solution)/shard_map/ppermute | solution.py:179
  144.8 1.1 copy-start.9
  149.6 10.5 %collective-permute-start.18 = (bf16[64,4736]{1,0:T(8,128)(2,1)S(1)}, bf16[64,4736]{1,0:T(8,128)(2,1)S(1)}, u32[]{:S(2)}, u32[]{:S(2)}) collective-permute-start(bf16[64,4736]{1,0:T(8,128)(2,1)S(1)} %get-tuple-element.22), channel_id=1, source_target_pairs={{0,4},{1,17},{2,6},{3,19},{4,8},{5,21},{6,10},{7,23},{8,12},{9,25}... | collective-permute-start | bytes 1818632 | tf_op jit(solution)/shard_map/ppermute | solution.py:179
  150.5 15.3 %collective-permute-start.19 = (bf16[64,4736]{1,0:T(8,128)(2,1)S(1)}, bf16[64,4736]{1,0:T(8,128)(2,1)S(1)}, u32[]{:S(2)}, u32[]{:S(2)}) collective-permute-start(bf16[64,4736]{1,0:T(8,128)(2,1)S(1)} %get-tuple-element.23), channel_id=1, source_target_pairs={{0,12},{1,49},{2,14},{3,51},{4,0},{5,53},{6,2},{7,55},{8,4},{9,57}... | collective-permute-start | bytes 1818632 | tf_op jit(solution)/shard_map/ppermute | solution.py:179
  152.3 15.0 %collective-permute-start.20 = (bf16[64,4736]{1,0:T(8,128)(2,1)S(1)}, bf16[64,4736]{1,0:T(8,128)(2,1)S(1)}, u32[]{:S(2)}, u32[]{:S(2)}) collective-permute-start(bf16[64,4736]{1,0:T(8,128)(2,1)S(1)} %get-tuple-element.24), channel_id=1, source_target_pairs={{0,8},{1,33},{2,10},{3,35},{4,12},{5,37},{6,14},{7,39},{8,0},{9,41... | collective-permute-start | bytes 1818632 | tf_op jit(solution)/shard_map/ppermute | solution.py:179
  168.1 4.0 %collective-permute-start.21 = (bf16[32,4608]{1,0:T(8,128)(2,1)S(1)}, bf16[32,4608]{1,0:T(8,128)(2,1)S(1)}, u32[]{:S(2)}, u32[]{:S(2)}) collective-permute-start(bf16[32,4608]{1,0:T(8,128)(2,1)S(1)} %pad_maximum_fusion.5), channel_id=1, source_target_pairs={{0,1},{1,0},{2,3},{3,2},{4,5},{5,4},{6,7},{7,6},{8,9},{9,8},{10,11... | collective-permute-start | bytes 884744 | tf_op jit(solution)/shard_map/ppermute | solution.py:197
  172.3 7.4 %collective-permute-start.22 = (bf16[32,4608]{1,0:T(8,128)(2,1)S(1)}, bf16[32,4608]{1,0:T(8,128)(2,1)S(1)}, u32[]{:S(2)}, u32[]{:S(2)}) collective-permute-start(bf16[32,4608]{1,0:T(8,128)(2,1)S(1)} %get-tuple-element.42), channel_id=1, source_target_pairs={{0,16},{1,5},{2,18},{3,7},{4,20},{5,9},{6,22},{7,11},{8,24},{9,13}... | collective-permute-start | bytes 884744 | tf_op jit(solution)/shard_map/ppermute | solution.py:179
  173.5 8.8 %collective-permute-start.23 = (bf16[32,4608]{1,0:T(8,128)(2,1)S(1)}, bf16[32,4608]{1,0:T(8,128)(2,1)S(1)}, u32[]{:S(2)}, u32[]{:S(2)}) collective-permute-start(bf16[32,4608]{1,0:T(8,128)(2,1)S(1)} %get-tuple-element.42), channel_id=1, source_target_pairs={{0,48},{1,13},{2,50},{3,15},{4,52},{5,1},{6,54},{7,3},{8,56},{9,5}... | collective-permute-start | bytes 884744 | tf_op jit(solution)/shard_map/ppermute | solution.py:179
  175.4 8.7 %collective-permute-start.24 = (bf16[32,4608]{1,0:T(8,128)(2,1)S(1)}, bf16[32,4608]{1,0:T(8,128)(2,1)S(1)}, u32[]{:S(2)}, u32[]{:S(2)}) collective-permute-start(bf16[32,4608]{1,0:T(8,128)(2,1)S(1)} %get-tuple-element.42), channel_id=1, source_target_pairs={{0,32},{1,9},{2,34},{3,11},{4,36},{5,13},{6,38},{7,15},{8,40},{9,1... | collective-permute-start | bytes 884744 | tf_op jit(solution)/shard_map/ppermute | solution.py:179
  184.3 17.1 %collective-permute-start.25 = (bf16[128,4608]{1,0:T(8,128)(2,1)S(1)}, bf16[128,4608]{1,0:T(8,128)(2,1)S(1)}, u32[]{:S(2)}, u32[]{:S(2)}) collective-permute-start(bf16[128,4608]{1,0:T(8,128)(2,1)S(1)} %bitcast.114), channel_id=1, source_target_pairs={{0,4},{1,17},{2,6},{3,19},{4,8},{5,21},{6,10},{7,23},{8,12},{9,25}... | collective-permute-start | bytes 3538952 | tf_op jit(solution)/shard_map/ppermute | solution.py:179
  184.3 17.9 %collective-permute-start.26 = (bf16[128,4608]{1,0:T(8,128)(2,1)S(1)}, bf16[128,4608]{1,0:T(8,128)(2,1)S(1)}, u32[]{:S(2)}, u32[]{:S(2)}) collective-permute-start(bf16[128,4608]{1,0:T(8,128)(2,1)S(1)} %bitcast.115), channel_id=1, source_target_pairs={{0,12},{1,49},{2,14},{3,51},{4,0},{5,53},{6,2},{7,55},{8,4},{9,57}... | collective-permute-start | bytes 3538952 | tf_op jit(solution)/shard_map/ppermute | solution.py:179
  202.2 10.6 %collective-permute-start.27 = (bf16[64,4608]{1,0:T(8,128)(2,1)}, bf16[64,4608]{1,0:T(8,128)(2,1)}, u32[]{:S(2)}, u32[]{:S(2)}) collective-permute-start(bf16[64,4608]{1,0:T(8,128)(2,1)} %slice.178), channel_id=1, source_target_pairs={{0,4},{1,17},{2,6},{3,19},{4,8},{5,21},{6,10},{7,23},{8,12},{9,25}... | collective-permute-start | bytes 1769480 | tf_op jit(solution)/shard_map/ppermute | solution.py:179
  202.2 1.0 copy-start.6
  204.1 9.8 %collective-permute-start.28 = (bf16[64,4608]{1,0:T(8,128)(2,1)}, bf16[64,4608]{1,0:T(8,128)(2,1)}, u32[]{:S(2)}, u32[]{:S(2)}) collective-permute-start(bf16[64,4608]{1,0:T(8,128)(2,1)} %slice.179), channel_id=1, source_target_pairs={{0,12},{1,49},{2,14},{3,51},{4,0},{5,53},{6,2},{7,55},{8,4},{9,57}... | collective-permute-start | bytes 1769480 | tf_op jit(solution)/shard_map/ppermute | solution.py:179
  206.7 28.0 %collective-permute-start.29 = (bf16[2304,448]{0,1:T(8,128)(2,1)}, bf16[2304,448]{0,1:T(8,128)(2,1)}, u32[]{:S(2)}, u32[]{:S(2)}) collective-permute-start(bf16[2304,448]{0,1:T(8,128)(2,1)} %param.23), channel_id=1, source_target_pairs={{0,1},{1,0},{2,3},{3,2},{4,5},{5,4},{6,7},{7,6},{8,9},{9,8},{10,11... | collective-permute-start | bytes 6193160 | tf_op jit(solution)/shard_map/ppermute | solution.py:197
  209.4 5.8 %copy-start.7 = (bf16[128,4608]{1,0:T(8,128)(2,1)S(1)}, bf16[128,4608]{1,0:T(8,128)(2,1)}, u32[]{:S(2)}) copy-start(bf16[128,4608]{1,0:T(8,128)(2,1)} %copy-done.6) | copy-start | bytes 3538948

commit v2 on v1

--- a/solution.py
+++ b/solution.py
@@ -9,7 +9,7 @@
 from jax.sharding import PartitionSpec as P
 
 epsilon = 1e-06
-VMEM_LIMIT = 48 * 1024 * 1024
+VMEM_LIMIT = 20 * 1024 * 1024
 
 
 SHIFTS = (0, 1, -1, 2)
@@ -137,14 +137,14 @@
     )(*([rows] * len(places)), gain, *weights)
 
 
-def merge_kernel(own_a, own_c, plus, minus, relay_a, relay_c, *outs):
-    wide_a, wide_c = own_a.shape[1], own_c.shape[1]
+def merge_kernel(own_a, own_c, direct_a, direct_c, relay_a, relay_c, *outs):
+    wide_a = own_a.shape[1]
     rows = outs[0].shape[0]
     for out, place in zip(outs, FACING):
         part = pl.ds(place * rows, rows)
-        total = wide(own_a[part, :]) + wide(relay_a[part, :]) + wide(minus[part, wide_c:])
+        total = wide(own_a[part, :]) + wide(relay_a[part, :]) + wide(direct_a[part, :])
         out[:, :wide_a] = total.astype(jnp.bfloat16)
-        total = wide(own_c[part, :]) + wide(relay_c[part, :]) + wide(plus[part, wide_a:])
+        total = wide(own_c[part, :]) + wide(relay_c[part, :]) + wide(direct_c[part, :])
         out[:, wide_a:] = total.astype(jnp.bfloat16)
 
 
@@ -198,14 +198,7 @@
 
 
 def gather(block, shift):
-    return jnp.stack([block] + [shift(block, s) for s in SHIFTS[1:]])
-
-
-def gather_ring(block, shift):
-    behind, ahead = shift(block, 1), shift(block, -1)
-    middle = block.shape[0] // 2
-    far = [shift(behind[:middle], 1), shift(ahead[middle:], -1)]
-    return jnp.stack([block, behind, ahead, jnp.concatenate(far)])
+    return [block] + [shift(block, s) for s in SHIFTS[1:]]
 
 
 def wide(value):
@@ -214,14 +207,6 @@
 
 def add(*values):
     return sum(wide(v) for v in values)
-
-
-def scatter_step(plus, minus, ahead_a, behind_c, shift):
-    wide_a, wide_c = ahead_a.shape[1], behind_c.shape[1]
-    plus, minus = shift(plus, 1), shift(minus, -1)
-    relay_a = shift(add(ahead_a, plus[:, :wide_a]).astype(jnp.bfloat16), 1)
-    relay_c = shift(add(behind_c, minus[:, :wide_c]).astype(jnp.bfloat16), -1)
-    return plus, minus, relay_a, relay_c
 
 
 def absolute(blocks, place, axis):
@@ -266,8 +251,8 @@
     score_scale = (value_width + kv - latent) ** (-0.5)
 
     uv_pair = (w_uv, swap(w_uv, "core"))
-    o_pair = (w_o, swap(w_o, "core"))
-    down_pair = (w_down, swap(w_down, "core"))
+    o_chip = jnp.concatenate([w_o, swap(w_o, "core")], axis=0)
+    down_chip = jnp.concatenate([w_down, swap(w_down, "core")], axis=0)
     in_pair = (
         jnp.where(core == 0, w_gate, w_up),
         swap(jnp.where(core == 0, w_up, w_gate), "core"),
@@ -301,10 +286,12 @@
         ],
         axis=1,
     )
-    values = gather(gather(values, shift_1), shift_2)
-    values = values.reshape(groups * 2 * tokens, 2, -1)
-    attn_part = sum(
-        jnp.dot(values[:, i], o_pair[i], preferred_element_type=jnp.float32) for i in range(2)
+    values = jnp.concatenate(gather(values, shift_1))
+    attn_part = jnp.stack(
+        [
+            jnp.dot(v, o_chip, preferred_element_type=jnp.float32)
+            for v in gather(values, shift_2)
+        ]
     ).reshape(4, 4, 2, tokens, width)
     shared = 0.5 * residual + attn_part
     sent = shared.astype(jnp.bfloat16)
@@ -315,14 +302,17 @@
     rows = jnp.transpose(rows, (2, 3, 0, 1, 4, 5, 6)).reshape(4, 4, 8 * tokens, width)
 
     gain = wide(norm_gain)[None]
-    places = (3, FACING[1], FACING[2])
-    (plus,) = partial_sums(rows, places[:2], gain, in_pair, (((0, 0), (1, 1)),))
-    (minus,) = partial_sums(rows, places[::2], gain, in_pair, (((0, 1), (1, 0)),))
-    places = (FACING[1], FACING[2], 0)
-    rest = (((0, 0),), ((1, 1),), ((2, 0),), ((2, 1),))
-    ahead_a, behind_c, own_a, own_c = partial_sums(rows, places, gain, in_pair, rest)
-    arrived = scatter_step(plus, minus, ahead_a, behind_c, shift_1)
-    blocks = merge(own_a, own_c, *arrived)
+    behind, ahead, far = FACING[2], FACING[1], FACING[3]
+    far_a, far_c = partial_sums(rows, (far,), gain, in_pair, (((0, 0),), ((0, 1),)))
+    ahead_c, behind_a = partial_sums(rows, (ahead, behind), gain, in_pair, (((0, 1),), ((1, 0),)))
+    ahead_a, behind_c, own_a, own_c = partial_sums(
+        rows, (ahead, behind, 0), gain, in_pair, (((0, 0),), ((1, 1),), ((2, 0),), ((2, 1),))
+    )
+    far_a, far_c = shift_1(far_a, 1), shift_1(far_c, -1)
+    direct_c, direct_a = shift_1(ahead_c, 1), shift_1(behind_a, -1)
+    relay_a = shift_1(add(ahead_a, far_a).astype(jnp.bfloat16), 1)
+    relay_c = shift_1(add(behind_c, far_c).astype(jnp.bfloat16), -1)
+    blocks = merge(own_a, own_c, direct_a, direct_c, relay_a, relay_c)
     sums = add(blocks[0], *(shift_2(blocks[i], SHIFTS[i]) for i in range(1, 4)))
     square = sums[:, hidden : hidden + 1] + sums[:, hidden + 64 : hidden + 65]
     scale = lax.rsqrt(square / model_width + epsilon)
@@ -342,11 +332,14 @@
         axis=1,
     )
 
-    activated = gather(activated, shift_1).reshape(-1, 2 * hidden)
-    activated = gather_ring(activated, shift_2).reshape(-1, 2, hidden)
-    down = sum(
-        jnp.dot(activated[:, i], down_pair[i], preferred_element_type=jnp.float32)
-        for i in range(2)
+    own, behind, ahead, far = gather(activated, shift_1)
+    low, high = jnp.concatenate([own, behind]), jnp.concatenate([ahead, far])
+    behind_low, ahead_high = shift_2(low, 1), shift_2(high, -1)
+    behind_high, ahead_low = shift_2(high, 1), shift_2(low, -1)
+    far_low, far_high = shift_2(behind_low, 1), shift_2(ahead_high, -1)
+    pieces = (low, high, behind_low, behind_high, ahead_low, ahead_high, far_low, far_high)
+    down = jnp.stack(
+        [jnp.dot(p, down_chip, preferred_element_type=jnp.float32) for p in pieces]
     ).reshape(4, 4, 2, 2, tokens, width)
     at_home = jnp.arange(2)[None, None, :, None, None] == yh
     down = jnp.stack([down[:, :, 0] + jnp.where(at_home, stream, 0.0), down[:, :, 1]])

time: 276 us -> 219 us (0.79)
  waiting for transfers between devices: 101 us -> 78.1 us
  local copies, waits for them, and re-layouts: 38.4 us -> 16.1 us
  Pallas kernels: 27.5 us -> 18.3 us
  matrix products: 13.4 us -> 19.2 us
  other arithmetic: 13.4 us -> 9.3 us
    ppermute x20 -> x24, waiting for transfers between devices: 90.5 us -> 65.4 us  [shift(): return lax.ppermute(value, ('grp', 'yh', 'core'), pairs)]
    slice x4 -> x0, local copies, waits for them, and re-layouts: 17.1 us -> none  [the longest x1 9.8 us: body(): activated[:, i]]
    reshape x2 -> x0, local copies, waits for them, and re-layouts: 11.8 us -> none  [the longest x1 7.26 us: body(): activated = gather_ring(activated, shift_2).reshape(-1, 2, hidden)]
    ppermute x7, starting transfers between devices: 15.4 us -> 8.02 us  [swap(): return lax.ppermute(value, axis, [(0, 1), (1, 0)])]
    another operation x6 -> x0, other arithmetic: 6.61 us -> none  [the longest x2 3.79 us: gather_ring(): return jnp.stack([block, behind, ahead, jnp.concatenate(far)])]
    ppermute x20 -> x24, starting transfers between devices: 28.9 us -> 34.5 us  [shift(): return lax.ppermute(value, ('grp', 'yh', 'core'), pairs)]
    dot_general x4 -> x12, matrix products: 10.9 us -> 15.1 us  [the longest x8 10.4 us: body(): jnp.dot(p, down_chip, preferred_element_type=jnp.float32)]
    unnamed x31 -> x20, local copies, waits for them, and re-layouts: 7.8 us -> 11.5 us
  transfers between devices with their start and end apart: 30 -> 34, of which waited for: 23 -> 20; matrix products, arithmetic and copies ran while one was open for 19% -> 16% of each run, Pallas kernels for 7% -> 3%
where the time goes in v2:
time: 219 us; the launch traced here: 218 us
  waiting for transfers between devices  78.1 us (36%)
  starting transfers between devices  45.6 us (21%)
  blocking collectives  30.8 us (14%)
  matrix products  19.2 us (9%)
  Pallas kernels  18.3 us (8%)
  local copies, waits for them, and re-layouts  16.1 us (7%)
  other arithmetic  9.3 us (4%)
    ppermute x24, waiting for transfers between devices, shift(): return lax.ppermute(value, ('grp', 'yh', 'core'), pairs)  65.4 us
    ppermute x24, starting transfers between devices, shift(): return lax.ppermute(value, ('grp', 'yh', 'core'), pairs)  34.5 us
    all_to_all x1, blocking collectives, body(): lax.all_to_all(down, ('role', 'grp', 'yh'), split_axis=0, concat_axis=0)  19.7 us
    unnamed x20, local copies, waits for them, and re-layouts  11.5 us
    ppermute x3, waiting for transfers between devices, shift_y(): lax.ppermute(value, ('role', 'yh', 'core'), [(p, moved(p)) for p in range...  11.3 us
    all_gather x1, blocking collectives, body(): return lax.all_gather(result, ('yh', 'core'), axis=0, tiled=True)  11 us
    dot_general x8, matrix products, body(): jnp.dot(p, down_chip, preferred_element_type=jnp.float32)  10.4 us
    pallas_call x3, Pallas kernels, partial_sums(): pl.pallas_call(functools.partial(partial_kernel, jobs), grid=(1,), in_spe...  10.2 us
  transfers between devices with their start and end apart: 34, of which 20 were waited for; matrix products, arithmetic and copies ran while one was open for 16% of the time, Pallas kernels for 3%

profile of v2, /device:TPU:1, one launch (start us, length us, event | category | flops | bytes accessed | tf_op | source)
XLA Modules:
  0.0 218.1 jit_solution(542414541291097273)
XLA Ops:
  0.7 3.7 %copy-done = bf16[8,1024,576]{1,2,0:T(8,128)(2,1)S(1)} copy-done((bf16[8,1024,576]{1,2,0:T(8,128)(2,1)S(1)}, bf16[8,1024,576]{1,2,0:T(8,128)(2,1)}, u32[]{:S(2)}) %copy-start) | copy-done | bytes 9437208
  6.8 7.2 %attend.1 = (bf16[2,8,16,512]{3,2,1,0:T(8,128)(2,1)S(1)}, bf16[2,8,16,512]{3,2,1,0:T(8,128)(2,1)S(1)}) custom-call(s32[8]{0:T(128)S(1)} %copy-done.2, s32[8]{0:T(128)S(1)} %copy-done.3, s32[1]{0:T(128)} %bitcast.3.place_ref, bf16[8,4,16,576]{3,2,1,0:T(8,128)(2,1)S(1)} %bitcast.124, f32[8,1,576]{2,1,0:T(1,128)S(1)} %reshape.88.new_ref, ...), custom_call_target="tpu_custom_call" | custom-call | flops 1140850688 | bytes 9437184 | tf_op jit(solution)/shard_map/attend/pallas_call | solution.py:60
  14.0 3.8 %collective-permute-start = (bf16[2,8,16,512]{3,2,1,0:T(8,128)(2,1)S(1)}, bf16[2,8,16,512]{3,2,1,0:T(8,128)(2,1)}, u32[]{:S(2)}, u32[]{:S(2)}) collective-permute-start(bf16[2,8,16,512]{3,2,1,0:T(8,128)(2,1)S(1)} %get-tuple-element.20), channel_id=1, source_target_pairs={{0,2},{2,0},{1,3},{3,1},{4,6},{6,4},{5,7},{7,5},{8,10},{10,8},{9,1... | collective-permute-start | bytes 786440 | tf_op jit(solution)/shard_map/ppermute | solution.py:197
  18.8 3.8 %broadcast_select_fusion = (bf16[448,2304]{1,0:T(8,128)(2,1)}, bf16[448,2304]{1,0:T(8,128)(2,1)S(1)}) fusion(bf16[448,2304]{1,0:T(8,128)(2,1)} %param.22, bf16[448,2304]{1,0:T(8,128)(2,1)} %param.21, pred[]{:T(512)S(6)} %eq.35), kind=kLoop, calls=%fused_computation.2 | loop fusion | flops 2064384 | bytes 8257537 | tf_op jit(solution)/shard_map/jit(_where)/select_n | solution.py:258
  23.1 1.2 copy.71
  24.8 1.6 constant_dynamic-update-slice_fusion.1
  27.4 2.1 fusion.8
  29.5 2.1 fusion.9
  31.6 1.7 collective-permute-start.2
  33.3 2.2 %collective-permute-start.3 = (bf16[16,4096]{1,0:T(8,128)(2,1)S(1)}, bf16[16,4096]{1,0:T(8,128)(2,1)S(1)}, u32[]{:S(2)}, u32[]{:S(2)}) collective-permute-start(bf16[16,4096]{1,0:T(8,128)(2,1)S(1)} %bitcast_dynamic-update-slice_fusion), channel_id=1, source_target_pairs={{0,48},{1,13},{2,50},{3,15},{4,52},{5,1},{6,54},{7,3},{8,56},{9,5}... | collective-permute-start | bytes 393224 | tf_op jit(solution)/shard_map/ppermute | solution.py:179
  35.5 1.2 collective-permute-start.4
  37.8 3.2 %collective-permute-done.4 = bf16[16,4096]{1,0:T(8,128)(2,1)S(1)} collective-permute-done((bf16[16,4096]{1,0:T(8,128)(2,1)S(1)}, bf16[16,4096]{1,0:T(8,128)(2,1)S(1)}, u32[]{:S(2)}, u32[]{:S(2)}) %collective-permute-start.4) | collective-permute-done | bytes 131104 | tf_op jit(solution)/shard_map/ppermute | solution.py:179
  41.1 1.1 collective-permute-start.6
  42.2 1.6 constant_dynamic-update-slice_fusion
  43.8 1.7 collective-permute-start.7
  45.5 1.4 collective-permute-start.8
  46.9 1.2 fusion.37
  48.0 2.6 %collective-permute-done.6 = bf16[64,4096]{1,0:T(8,128)(2,1)S(1)} collective-permute-done((bf16[64,4096]{1,0:T(8,128)(2,1)S(1)}, bf16[64,4096]{1,0:T(8,128)(2,1)S(1)}, u32[]{:S(2)}, u32[]{:S(2)}) %collective-permute-start.6) | collective-permute-done | bytes 524320 | tf_op jit(solution)/shard_map/ppermute | solution.py:179
  50.7 1.2 fusion.40
  51.8 5.4 %collective-permute-done.7 = bf16[64,4096]{1,0:T(8,128)(2,1)S(1)} collective-permute-done((bf16[64,4096]{1,0:T(8,128)(2,1)S(1)}, bf16[64,4096]{1,0:T(8,128)(2,1)S(1)}, u32[]{:S(2)}, u32[]{:S(2)}) %collective-permute-start.7) | collective-permute-done | bytes 524320 | tf_op jit(solution)/shard_map/ppermute | solution.py:179
  57.2 1.2 fusion.41
  58.4 1.2 fusion.42
  60.2 1.1 collective-permute-start.10
  61.3 1.5 collective-permute-start.11
  62.9 3.8 %collective-permute-done.9 = bf16[4,4,2,8,448]{4,3,2,0,1:T(8,128)(2,1)S(1)} collective-permute-done((bf16[4,4,2,8,448]{4,3,2,0,1:T(8,128)(2,1)S(1)}, bf16[4,4,2,8,448]{4,3,2,0,1:T(8,128)(2,1)S(1)}, u32[]{:S(2)}, u32[]{:S(2)}) %collective-permute-start.9) | collective-permute-done | bytes 229408 | tf_op jit(solution)/shard_map/ppermute | solution.py:193
  66.8 7.5 %collective-permute-done.10 = bf16[4,4,2,8,448]{4,3,2,0,1:T(8,128)(2,1)S(1)} collective-permute-done((bf16[4,4,2,8,448]{4,3,2,0,1:T(8,128)(2,1)S(1)}, bf16[4,4,2,8,448]{4,3,2,0,1:T(8,128)(2,1)S(1)}, u32[]{:S(2)}, u32[]{:S(2)}) %collective-permute-start.10) | collective-permute-done | bytes 229408 | tf_op jit(solution)/shard_map/ppermute | solution.py:193
  74.4 1.7 collective-permute-start.12
  76.2 1.4 collective-permute-done.12
  77.9 3.0 %partial_sums.5 = (bf16[256,2432]{1,0:T(8,128)(2,1)S(1)}, bf16[256,2304]{1,0:T(8,128)(2,1)S(1)}) custom-call(bf16[4,4,64,448]{3,2,1,0:T(8,128)(2,1)S(1)} %bitcast.117, f32[1,448]{1,0:T(1,128)S(1)} %bitcast.125, bf16[448,2304]{1,0:T(8,128)(2,1)S(1)} %get-tuple-element.34.refs_4_.refs_3_.refs_2_, bf16[448,2304]{1,0:T(8,128)(2,1)} %collective-permute-done.13.refs_5_.refs_4_.refs_3_), custom_call_target="tpu_custom_call" | custom-call | flops 1086324736 | bytes 6553600 | tf_op jit(solution)/shard_map/partial_sums/pallas_call | solution.py:122
  81.3 2.3 %collective-permute-start.18 = (bf16[256,2304]{1,0:T(8,128)(2,1)S(1)}, bf16[256,2304]{1,0:T(8,128)(2,1)S(1)}, u32[]{:S(2)}, u32[]{:S(2)}) collective-permute-start(bf16[256,2304]{1,0:T(8,128)(2,1)S(1)} %get-tuple-element.28), channel_id=1, source_target_pairs={{0,48},{1,13},{2,50},{3,15},{4,52},{5,1},{6,54},{7,3},{8,56},{9,5}... | collective-permute-start | bytes 3538952 | tf_op jit(solution)/shard_map/ppermute | solution.py:179
  83.6 3.0 %partial_sums.4 = (bf16[256,2304]{1,0:T(8,128)(2,1)S(1)}, bf16[256,2432]{1,0:T(8,128)(2,1)S(1)}) custom-call(bf16[4,4,64,448]{3,2,1,0:T(8,128)(2,1)S(1)} %bitcast.118, bf16[4,4,64,448]{3,2,1,0:T(8,128)(2,1)S(1)} %bitcast.119, f32[1,448]{1,0:T(1,128)S(1)} %bitcast.126, bf16[448,2304]{1,0:T(8,128)(2,1)S(1)} %get-tuple-element.34.refs_4_.refs_3_.refs_2_, ...), custom_call_target="tpu_custom_call" | custom-call | flops 1086324736 | bytes 6553600 | tf_op jit(solution)/shard_map/partial_sums/pallas_call | solution.py:122
  86.9 1.3 collective-permute-start.15
  88.2 4.2 %partial_sums.3 = (bf16[256,2432]{1,0:T(8,128)(2,1)S(1)}, bf16[256,2304]{1,0:T(8,128)(2,1)S(1)}, bf16[256,2432]{1,0:T(8,128)(2,1)S(1)}, bf16[256,2304]{1,0:T(8,128)(2,1)S(1)}) custom-call(bf16[4,4,64,448]{3,2,1,0:T(8,128)(2,1)S(1)} %bitcast.120, bf16[4,4,64,448]{3,2,1,0:T(8,128)(2,1)S(1)} %bitcast.121, bf16[4,4,64,448]{3,2,1,0:T(8,128)(2,1)S(1)} %bitcast.122, ...), custom_call_target="tpu_custom_call" | custom-call | flops 2172649472 | bytes 8978432 | tf_op jit(solution)/shard_map/partial_sums/pallas_call | solution.py:122
  92.4 5.8 %collective-permute-done.16 = bf16[256,2432]{1,0:T(8,128)(2,1)S(1)} collective-permute-done((bf16[256,2432]{1,0:T(8,128)(2,1)S(1)}, bf16[256,2432]{1,0:T(8,128)(2,1)S(1)}, u32[]{:S(2)}, u32[]{:S(2)}) %collective-permute-start.16) | collective-permute-done | bytes 1245216 | tf_op jit(solution)/shard_map/ppermute | solution.py:179
  98.9 2.7 %collective-permute-start.19 = (bf16[256,2304]{1,0:T(8,128)(2,1)S(1)}, bf16[256,2304]{1,0:T(8,128)(2,1)S(1)}, u32[]{:S(2)}, u32[]{:S(2)}) collective-permute-start(bf16[256,2304]{1,0:T(8,128)(2,1)S(1)} %add_convert_fusion.1), channel_id=1, source_target_pairs={{0,48},{1,13},{2,50},{3,15},{4,52},{5,1},{6,54},{7,3},{8,56},{9,5}... | collective-permute-start | bytes 3538952 | tf_op jit(solution)/shard_map/ppermute | solution.py:179
  101.6 9.2 %collective-permute-done.15.direct_c = bf16[256,2304]{1,0:T(8,128)(2,1)S(1)} collective-permute-done((bf16[256,2304]{1,0:T(8,128)(2,1)S(1)}, bf16[256,2304]{1,0:T(8,128)(2,1)S(1)}, u32[]{:S(2)}, u32[]{:S(2)}) %collective-permute-start.15) | collective-permute-done | bytes 1179680 | tf_op jit(solution)/shard_map/ppermute | solution.py:179
  110.9 11.9 %collective-permute-done.19.relay_c = bf16[256,2304]{1,0:T(8,128)(2,1)S(1)} collective-permute-done((bf16[256,2304]{1,0:T(8,128)(2,1)S(1)}, bf16[256,2304]{1,0:T(8,128)(2,1)S(1)}, u32[]{:S(2)}, u32[]{:S(2)}) %collective-permute-start.19) | collective-permute-done | bytes 1179680 | tf_op jit(solution)/shard_map/ppermute | solution.py:179
  122.8 1.4 collective-permute-done.17.relay_a
  125.8 2.8 %collective-permute-start.21 = (bf16[64,4736]{1,0:T(8,128)(2,1)S(1)}, bf16[64,4736]{1,0:T(8,128)(2,1)}, u32[]{:S(2)}, u32[]{:S(2)}) collective-permute-start(bf16[64,4736]{1,0:T(8,128)(2,1)S(1)} %get-tuple-element.31), channel_id=1, source_target_pairs={{0,12},{1,49},{2,14},{3,51},{4,0},{5,53},{6,2},{7,55},{8,4},{9,57}... | collective-permute-start | bytes 1818632 | tf_op jit(solution)/shard_map/ppermute | solution.py:179
  130.1 6.3 %collective-permute-done.20 = bf16[64,4736]{1,0:T(8,128)(2,1)} collective-permute-done((bf16[64,4736]{1,0:T(8,128)(2,1)S(1)}, bf16[64,4736]{1,0:T(8,128)(2,1)}, u32[]{:S(2)}, u32[]{:S(2)}) %collective-permute-start.20) | collective-permute-done | bytes 606240 | tf_op jit(solution)/shard_map/ppermute | solution.py:179
  136.4 5.7 %collective-permute-done.21 = bf16[64,4736]{1,0:T(8,128)(2,1)} collective-permute-done((bf16[64,4736]{1,0:T(8,128)(2,1)S(1)}, bf16[64,4736]{1,0:T(8,128)(2,1)}, u32[]{:S(2)}, u32[]{:S(2)}) %collective-permute-start.21) | collective-permute-done | bytes 606240 | tf_op jit(solution)/shard_map/ppermute | solution.py:179
  142.1 1.9 collective-permute-done.22
  144.0 1.7 convert_add_fusion
  146.9 1.7 constant_dynamic-update-slice_fusion.3
  149.8 1.7 constant_dynamic-update-slice_fusion.2
  151.5 2.5 %collective-permute-start.26 = (bf16[32,4608]{1,0:T(8,128)(2,1)S(1)}, bf16[32,4608]{1,0:T(8,128)(2,1)S(1)}, u32[]{:S(2)}, u32[]{:S(2)}) collective-permute-start(bf16[32,4608]{1,0:T(8,128)(2,1)S(1)} %pad_maximum_fusion.4), channel_id=1, source_target_pairs={{0,48},{1,13},{2,50},{3,15},{4,52},{5,1},{6,54},{7,3},{8,56},{9,5}... | collective-permute-start | bytes 884744 | tf_op jit(solution)/shard_map/ppermute | solution.py:179
  154.0 1.3 collective-permute-start.27
  155.2 1.1 collective-permute-done.24
  156.6 2.5 %collective-permute-start.30 = (bf16[64,4608]{1,0:T(8,128)(2,1)S(1)}, bf16[64,4608]{1,0:T(8,128)(2,1)S(1)}, u32[]{:S(2)}, u32[]{:S(2)}) collective-permute-start(bf16[64,4608]{1,0:T(8,128)(2,1)S(1)} %pad_maximum_fusion), channel_id=1, source_target_pairs={{0,12},{1,49},{2,14},{3,51},{4,0},{5,53},{6,2},{7,55},{8,4},{9,57}... | collective-permute-start | bytes 1769480 | tf_op jit(solution)/shard_map/ppermute | solution.py:179
  159.1 1.7 collective-permute-done.26
  161.7 2.4 %collective-permute-start.31 = (bf16[64,4608]{1,0:T(8,128)(2,1)S(1)}, bf16[64,4608]{1,0:T(8,128)(2,1)S(1)}, u32[]{:S(2)}, u32[]{:S(2)}) collective-permute-start(bf16[64,4608]{1,0:T(8,128)(2,1)S(1)} %constant_dynamic-update-slice_fusion.4), channel_id=1, source_target_pairs={{0,12},{1,49},{2,14},{3,51},{4,0},{5,53},{6,2},{7,55},{8,4},{9,57}... | collective-permute-start | bytes 1769480 | tf_op jit(solution)/shard_map/ppermute | solution.py:179
  164.1 1.3 fusion.7
  165.4 1.3 fusion.6
  166.7 1.4 collective-permute-done.28
  168.1 5.9 %collective-permute-done.31 = bf16[64,4608]{1,0:T(8,128)(2,1)S(1)} collective-permute-done((bf16[64,4608]{1,0:T(8,128)(2,1)S(1)}, bf16[64,4608]{1,0:T(8,128)(2,1)S(1)}, u32[]{:S(2)}, u32[]{:S(2)}) %collective-permute-start.31) | collective-permute-done | bytes 589856 | tf_op jit(solution)/shard_map/ppermute | solution.py:179
  174.0 3.3 %collective-permute-start.33 = (bf16[64,4608]{1,0:T(8,128)(2,1)S(1)}, bf16[64,4608]{1,0:T(8,128)(2,1)S(1)}, u32[]{:S(2)}, u32[]{:S(2)}) collective-permute-start(bf16[64,4608]{1,0:T(8,128)(2,1)S(1)} %collective-permute-done.31), channel_id=1, source_target_pairs={{0,12},{1,49},{2,14},{3,51},{4,0},{5,53},{6,2},{7,55},{8,4},{9,57}... | collective-permute-start | bytes 1769480 | tf_op jit(solution)/shard_map/ppermute | solution.py:179
  177.3 1.3 fusion.5
  178.6 1.3 fusion.4
  179.9 1.3 fusion.3
  181.2 1.3 fusion.2
  182.5 1.3 fusion.1
  184.1 1.3 fusion
  186.2 19.7 %all_to_all.5 = bf16[64,8,448]{2,1,0:T(8,128)(2,1)S(1)} all-to-all(bf16[64,8,448]{2,1,0:T(8,128)(2,1)S(1)} %bitcast.140), channel_id=1, replica_groups=mesh['role'=2,'grp'=16,'yh'=2,'core'=2] {'role','grp','yh'}, dimensions={0} | all-to-all | bytes 917504 | tf_op jit(solution)/shard_map/all_to_all | solution.py:352
  206.2 11.0 %all_gather.3 = bf16[32,7168]{1,0:T(8,128)(2,1)S(1)} all-gather(bf16[8,7168]{1,0:T(8,128)(2,1)S(1)} %reshape.87), channel_id=1, replica_groups=mesh['role'=2,'grp'=16,'yh'=2,'core'=2] {'yh','core'}, dimensions={0}, use_global_device_ids=true | all-gather | bytes 573440 | tf_op jit(solution)/shard_map/all_gather | solution.py:356
  (98 shorter events, 18.2 us)
Async XLA Ops:
  0.7 3.7 %copy-start = (bf16[8,1024,576]{1,2,0:T(8,128)(2,1)S(1)}, bf16[8,1024,576]{1,2,0:T(8,128)(2,1)}, u32[]{:S(2)}) copy-start(bf16[8,1024,576]{1,2,0:T(8,128)(2,1)} %param.14) | copy-start | bytes 28311556
  4.4 1.1 copy-start.1
  5.5 0.7 copy-start.2
  6.2 0.7 copy-start.3
  14.0 12.4 %collective-permute-start = (bf16[2,8,16,512]{3,2,1,0:T(8,128)(2,1)S(1)}, bf16[2,8,16,512]{3,2,1,0:T(8,128)(2,1)}, u32[]{:S(2)}, u32[]{:S(2)}) collective-permute-start(bf16[2,8,16,512]{3,2,1,0:T(8,128)(2,1)S(1)} %get-tuple-element.20), channel_id=1, source_target_pairs={{0,2},{2,0},{1,3},{3,1},{4,6},{6,4},{5,7},{7,5},{8,10},{10,8},{9,1... | collective-permute-start | bytes 786440 | tf_op jit(solution)/shard_map/ppermute | solution.py:197
  17.8 11.7 %collective-permute-start.1 = (bf16[16,512,128]{2,1,0:T(8,128)(2,1)}, bf16[16,512,128]{2,1,0:T(8,128)(2,1)}, u32[]{:S(2)}, u32[]{:S(2)}) collective-permute-start(bf16[16,512,128]{2,1,0:T(8,128)(2,1)} %param.18), channel_id=1, source_target_pairs={{0,1},{1,0},{2,3},{3,2},{4,5},{5,4},{6,7},{7,6},{8,9},{9,8},{10,11... | collective-permute-start | bytes 6291464 | tf_op jit(solution)/shard_map/ppermute | solution.py:197
  18.8 23.4 %collective-permute-start.5 = (bf16[2048,448]{0,1:T(8,128)(2,1)}, bf16[2048,448]{0,1:T(8,128)(2,1)}, u32[]{:S(2)}, u32[]{:S(2)}) collective-permute-start(bf16[2048,448]{0,1:T(8,128)(2,1)} %param.19), channel_id=1, source_target_pairs={{0,1},{1,0},{2,3},{3,2},{4,5},{5,4},{6,7},{7,6},{8,9},{9,8},{10,11... | collective-permute-start | bytes 5505032 | tf_op jit(solution)/shard_map/ppermute | solution.py:197
  22.5 55.3 %collective-permute-start.13 = (bf16[448,2304]{1,0:T(8,128)(2,1)}, bf16[448,2304]{1,0:T(8,128)(2,1)}, u32[]{:S(2)}, u32[]{:S(2)}) collective-permute-start(bf16[448,2304]{1,0:T(8,128)(2,1)} %get-tuple-element.33), channel_id=1, source_target_pairs={{0,1},{1,0},{2,3},{3,2},{4,5},{5,4},{6,7},{7,6},{8,9},{9,8},{10,11... | collective-permute-start | bytes 6193160 | tf_op jit(solution)/shard_map/ppermute | solution.py:197
  31.6 6.2 %collective-permute-start.2 = (bf16[16,4096]{1,0:T(8,128)(2,1)S(1)}, bf16[16,4096]{1,0:T(8,128)(2,1)S(1)}, u32[]{:S(2)}, u32[]{:S(2)}) collective-permute-start(bf16[16,4096]{1,0:T(8,128)(2,1)S(1)} %bitcast_dynamic-update-slice_fusion), channel_id=1, source_target_pairs={{0,16},{1,5},{2,18},{3,7},{4,20},{5,9},{6,22},{7,11},{8,24},{9,13}... | collective-permute-start | bytes 393224 | tf_op jit(solution)/shard_map/ppermute | solution.py:179
  33.3 4.5 %collective-permute-start.3 = (bf16[16,4096]{1,0:T(8,128)(2,1)S(1)}, bf16[16,4096]{1,0:T(8,128)(2,1)S(1)}, u32[]{:S(2)}, u32[]{:S(2)}) collective-permute-start(bf16[16,4096]{1,0:T(8,128)(2,1)S(1)} %bitcast_dynamic-update-slice_fusion), channel_id=1, source_target_pairs={{0,48},{1,13},{2,50},{3,15},{4,52},{5,1},{6,54},{7,3},{8,56},{9,5}... | collective-permute-start | bytes 393224 | tf_op jit(solution)/shard_map/ppermute | solution.py:179
  35.5 5.5 %collective-permute-start.4 = (bf16[16,4096]{1,0:T(8,128)(2,1)S(1)}, bf16[16,4096]{1,0:T(8,128)(2,1)S(1)}, u32[]{:S(2)}, u32[]{:S(2)}) collective-permute-start(bf16[16,4096]{1,0:T(8,128)(2,1)S(1)} %bitcast_dynamic-update-slice_fusion), channel_id=1, source_target_pairs={{0,32},{1,9},{2,34},{3,11},{4,36},{5,13},{6,38},{7,15},{8,40},{9,1... | collective-permute-start | bytes 393224 | tf_op jit(solution)/shard_map/ppermute | solution.py:179
  41.1 9.6 %collective-permute-start.6 = (bf16[64,4096]{1,0:T(8,128)(2,1)S(1)}, bf16[64,4096]{1,0:T(8,128)(2,1)S(1)}, u32[]{:S(2)}, u32[]{:S(2)}) collective-permute-start(bf16[64,4096]{1,0:T(8,128)(2,1)S(1)} %pad_maximum_fusion.1), channel_id=1, source_target_pairs={{0,4},{1,17},{2,6},{3,19},{4,8},{5,21},{6,10},{7,23},{8,12},{9,25}... | collective-permute-start | bytes 1572872 | tf_op jit(solution)/shard_map/ppermute | solution.py:179
  43.8 13.4 %collective-permute-start.7 = (bf16[64,4096]{1,0:T(8,128)(2,1)S(1)}, bf16[64,4096]{1,0:T(8,128)(2,1)S(1)}, u32[]{:S(2)}, u32[]{:S(2)}) collective-permute-start(bf16[64,4096]{1,0:T(8,128)(2,1)S(1)} %pad_maximum_fusion.1), channel_id=1, source_target_pairs={{0,12},{1,49},{2,14},{3,51},{4,0},{5,53},{6,2},{7,55},{8,4},{9,57}... | collective-permute-start | bytes 1572872 | tf_op jit(solution)/shard_map/ppermute | solution.py:179
  45.5 12.9 %collective-permute-start.8 = (bf16[64,4096]{1,0:T(8,128)(2,1)S(1)}, bf16[64,4096]{1,0:T(8,128)(2,1)S(1)}, u32[]{:S(2)}, u32[]{:S(2)}) collective-permute-start(bf16[64,4096]{1,0:T(8,128)(2,1)S(1)} %pad_maximum_fusion.1), channel_id=1, source_target_pairs={{0,8},{1,33},{2,10},{3,35},{4,12},{5,37},{6,14},{7,39},{8,0},{9,41... | collective-permute-start | bytes 1572872 | tf_op jit(solution)/shard_map/ppermute | solution.py:179
  59.7 16.4 %copy-start.4 = (bf16[448]{0:T(512)(128)(2,1)S(1)}, bf16[448]{0:T(512)(128)(2,1)}, u32[]{:S(2)}) copy-start(bf16[448]{0:T(512)(128)(2,1)} %param.20) | copy-start | bytes 2692
  59.7 6.9 %collective-permute-start.9 = (bf16[4,4,2,8,448]{4,3,2,0,1:T(8,128)(2,1)S(1)}, bf16[4,4,2,8,448]{4,3,2,0,1:T(8,128)(2,1)S(1)}, u32[]{:S(2)}, u32[]{:S(2)}) collective-permute-start(bf16[4,4,2,8,448]{4,3,2,0,1:T(8,128)(2,1)S(1)} %copy.114), channel_id=1, source_target_pairs={{0,2},{1,3},{2,0},{3,1},{64,66},{65,67},{66,64},{67,65},{4,6},{5,7... | collective-permute-start | bytes 688136 | tf_op jit(solution)/shard_map/ppermute | solution.py:193
  60.2 14.1 %collective-permute-start.10 = (bf16[4,4,2,8,448]{4,3,2,0,1:T(8,128)(2,1)S(1)}, bf16[4,4,2,8,448]{4,3,2,0,1:T(8,128)(2,1)S(1)}, u32[]{:S(2)}, u32[]{:S(2)}) collective-permute-start(bf16[4,4,2,8,448]{4,3,2,0,1:T(8,128)(2,1)S(1)} %copy.114), channel_id=1, source_target_pairs={{0,64},{1,65},{2,66},{3,67},{64,2},{65,3},{66,0},{67,1},{4,68},{5,... | collective-permute-start | bytes 688136 | tf_op jit(solution)/shard_map/ppermute | solution.py:193
  61.3 12.9 %collective-permute-start.11 = (bf16[4,4,2,8,448]{4,3,2,0,1:T(8,128)(2,1)S(1)}, bf16[4,4,2,8,448]{4,3,2,0,1:T(8,128)(2,1)S(1)}, u32[]{:S(2)}, u32[]{:S(2)}) collective-permute-start(bf16[4,4,2,8,448]{4,3,2,0,1:T(8,128)(2,1)S(1)} %copy.114), channel_id=1, source_target_pairs={{0,66},{1,67},{2,64},{3,65},{64,0},{65,1},{66,2},{67,3},{4,70},{5,... | collective-permute-start | bytes 688136 | tf_op jit(solution)/shard_map/ppermute | solution.py:193
  74.4 3.2 %collective-permute-start.12 = (bf16[2,4,4,2,8,448]{5,4,3,2,1,0:T(8,128)(2,1)S(1)}, bf16[2,4,4,2,8,448]{5,4,3,2,1,0:T(8,128)(2,1)S(1)}, u32[]{:S(2)}, u32[]{:S(2)}) collective-permute-start(bf16[2,4,4,2,8,448]{5,4,3,2,1,0:T(8,128)(2,1)S(1)} %pad_maximum_fusion.2), channel_id=1, source_target_pairs={{0,1},{1,0},{2,3},{3,2},{4,5},{5,4},{6,7},{7,6},{8,9},{9,8},{10,11... | collective-permute-start | bytes 1376264 | tf_op jit(solution)/shard_map/ppermute | solution.py:197
  80.9 17.3 %collective-permute-start.16 = (bf16[256,2432]{1,0:T(8,128)(2,1)S(1)}, bf16[256,2432]{1,0:T(8,128)(2,1)S(1)}, u32[]{:S(2)}, u32[]{:S(2)}) collective-permute-start(bf16[256,2432]{1,0:T(8,128)(2,1)S(1)} %get-tuple-element.26), channel_id=1, source_target_pairs={{0,16},{1,5},{2,18},{3,7},{4,20},{5,9},{6,22},{7,11},{8,24},{9,13}... | collective-permute-start | bytes 3735560 | tf_op jit(solution)/shard_map/ppermute | solution.py:179
  81.3 17.3 %collective-permute-start.18 = (bf16[256,2304]{1,0:T(8,128)(2,1)S(1)}, bf16[256,2304]{1,0:T(8,128)(2,1)S(1)}, u32[]{:S(2)}, u32[]{:S(2)}) collective-permute-start(bf16[256,2304]{1,0:T(8,128)(2,1)S(1)} %get-tuple-element.28), channel_id=1, source_target_pairs={{0,48},{1,13},{2,50},{3,15},{4,52},{5,1},{6,54},{7,3},{8,56},{9,5}... | collective-permute-start | bytes 3538952 | tf_op jit(solution)/shard_map/ppermute | solution.py:179
  86.6 24.2 %collective-permute-start.14 = (bf16[256,2432]{1,0:T(8,128)(2,1)S(1)}, bf16[256,2432]{1,0:T(8,128)(2,1)S(1)}, u32[]{:S(2)}, u32[]{:S(2)}) collective-permute-start(bf16[256,2432]{1,0:T(8,128)(2,1)S(1)} %get-tuple-element.23), channel_id=1, source_target_pairs={{0,48},{1,13},{2,50},{3,15},{4,52},{5,1},{6,54},{7,3},{8,56},{9,5}... | collective-permute-start | bytes 3735560 | tf_op jit(solution)/shard_map/ppermute | solution.py:179
  86.9 24.0 %collective-permute-start.15 = (bf16[256,2304]{1,0:T(8,128)(2,1)S(1)}, bf16[256,2304]{1,0:T(8,128)(2,1)S(1)}, u32[]{:S(2)}, u32[]{:S(2)}) collective-permute-start(bf16[256,2304]{1,0:T(8,128)(2,1)S(1)} %get-tuple-element.24), channel_id=1, source_target_pairs={{0,16},{1,5},{2,18},{3,7},{4,20},{5,9},{6,22},{7,11},{8,24},{9,13}... | collective-permute-start | bytes 3538952 | tf_op jit(solution)/shard_map/ppermute | solution.py:179
  98.5 25.7 %collective-permute-start.17 = (bf16[256,2432]{1,0:T(8,128)(2,1)S(1)}, bf16[256,2432]{1,0:T(8,128)(2,1)S(1)}, u32[]{:S(2)}, u32[]{:S(2)}) collective-permute-start(bf16[256,2432]{1,0:T(8,128)(2,1)S(1)} %add_convert_fusion), channel_id=1, source_target_pairs={{0,16},{1,5},{2,18},{3,7},{4,20},{5,9},{6,22},{7,11},{8,24},{9,13}... | collective-permute-start | bytes 3735560 | tf_op jit(solution)/shard_map/ppermute | solution.py:179
  98.9 23.9 %collective-permute-start.19 = (bf16[256,2304]{1,0:T(8,128)(2,1)S(1)}, bf16[256,2304]{1,0:T(8,128)(2,1)S(1)}, u32[]{:S(2)}, u32[]{:S(2)}) collective-permute-start(bf16[256,2304]{1,0:T(8,128)(2,1)S(1)} %add_convert_fusion.1), channel_id=1, source_target_pairs={{0,48},{1,13},{2,50},{3,15},{4,52},{5,1},{6,54},{7,3},{8,56},{9,5}... | collective-permute-start | bytes 3538952 | tf_op jit(solution)/shard_map/ppermute | solution.py:179
  125.1 11.3 %collective-permute-start.20 = (bf16[64,4736]{1,0:T(8,128)(2,1)S(1)}, bf16[64,4736]{1,0:T(8,128)(2,1)}, u32[]{:S(2)}, u32[]{:S(2)}) collective-permute-start(bf16[64,4736]{1,0:T(8,128)(2,1)S(1)} %get-tuple-element.30), channel_id=1, source_target_pairs={{0,4},{1,17},{2,6},{3,19},{4,8},{5,21},{6,10},{7,23},{8,12},{9,25}... | collective-permute-start | bytes 1818632 | tf_op jit(solution)/shard_map/ppermute | solution.py:179
  125.8 16.3 %collective-permute-start.21 = (bf16[64,4736]{1,0:T(8,128)(2,1)S(1)}, bf16[64,4736]{1,0:T(8,128)(2,1)}, u32[]{:S(2)}, u32[]{:S(2)}) collective-permute-start(bf16[64,4736]{1,0:T(8,128)(2,1)S(1)} %get-tuple-element.31), channel_id=1, source_target_pairs={{0,12},{1,49},{2,14},{3,51},{4,0},{5,53},{6,2},{7,55},{8,4},{9,57}... | collective-permute-start | bytes 1818632 | tf_op jit(solution)/shard_map/ppermute | solution.py:179
  128.6 15.4 %collective-permute-start.22 = (bf16[64,4736]{1,0:T(8,128)(2,1)S(1)}, bf16[64,4736]{1,0:T(8,128)(2,1)}, u32[]{:S(2)}, u32[]{:S(2)}) collective-permute-start(bf16[64,4736]{1,0:T(8,128)(2,1)S(1)} %get-tuple-element.32), channel_id=1, source_target_pairs={{0,8},{1,33},{2,10},{3,35},{4,12},{5,37},{6,14},{7,39},{8,0},{9,41... | collective-permute-start | bytes 1818632 | tf_op jit(solution)/shard_map/ppermute | solution.py:179
  129.7 20.0 %collective-permute-start.25 = (bf16[2304,448]{0,1:T(8,128)(2,1)}, bf16[2304,448]{0,1:T(8,128)(2,1)}, u32[]{:S(2)}, u32[]{:S(2)}) collective-permute-start(bf16[2304,448]{0,1:T(8,128)(2,1)} %param.23), channel_id=1, source_target_pairs={{0,1},{1,0},{2,3},{3,2},{4,5},{5,4},{6,7},{7,6},{8,9},{9,8},{10,11... | collective-permute-start | bytes 6193160 | tf_op jit(solution)/shard_map/ppermute | solution.py:197
  146.2 2.5 %collective-permute-start.23 = (bf16[32,4608]{1,0:T(8,128)(2,1)S(1)}, bf16[32,4608]{1,0:T(8,128)(2,1)S(1)}, u32[]{:S(2)}, u32[]{:S(2)}) collective-permute-start(bf16[32,4608]{1,0:T(8,128)(2,1)S(1)} %pad_maximum_fusion.3), channel_id=1, source_target_pairs={{0,1},{1,0},{2,3},{3,2},{4,5},{5,4},{6,7},{7,6},{8,9},{9,8},{10,11... | collective-permute-start | bytes 884744 | tf_op jit(solution)/shard_map/ppermute | solution.py:197
  148.9 7.4 %collective-permute-start.24 = (bf16[32,4608]{1,0:T(8,128)(2,1)S(1)}, bf16[32,4608]{1,0:T(8,128)(2,1)S(1)}, u32[]{:S(2)}, u32[]{:S(2)}) collective-permute-start(bf16[32,4608]{1,0:T(8,128)(2,1)S(1)} %pad_maximum_fusion.4), channel_id=1, source_target_pairs={{0,16},{1,5},{2,18},{3,7},{4,20},{5,9},{6,22},{7,11},{8,24},{9,13}... | collective-permute-start | bytes 884744 | tf_op jit(solution)/shard_map/ppermute | solution.py:179
  151.5 9.3 %collective-permute-start.26 = (bf16[32,4608]{1,0:T(8,128)(2,1)S(1)}, bf16[32,4608]{1,0:T(8,128)(2,1)S(1)}, u32[]{:S(2)}, u32[]{:S(2)}) collective-permute-start(bf16[32,4608]{1,0:T(8,128)(2,1)S(1)} %pad_maximum_fusion.4), channel_id=1, source_target_pairs={{0,48},{1,13},{2,50},{3,15},{4,52},{5,1},{6,54},{7,3},{8,56},{9,5}... | collective-permute-start | bytes 884744 | tf_op jit(solution)/shard_map/ppermute | solution.py:179
  154.0 7.4 %collective-permute-start.27 = (bf16[32,4608]{1,0:T(8,128)(2,1)S(1)}, bf16[32,4608]{1,0:T(8,128)(2,1)S(1)}, u32[]{:S(2)}, u32[]{:S(2)}) collective-permute-start(bf16[32,4608]{1,0:T(8,128)(2,1)S(1)} %pad_maximum_fusion.4), channel_id=1, source_target_pairs={{0,32},{1,9},{2,34},{3,11},{4,36},{5,13},{6,38},{7,15},{8,40},{9,1... | collective-permute-start | bytes 884744 | tf_op jit(solution)/shard_map/ppermute | solution.py:179
  156.4 11.7 %collective-permute-start.28 = (bf16[64,4608]{1,0:T(8,128)(2,1)S(1)}, bf16[64,4608]{1,0:T(8,128)(2,1)S(1)}, u32[]{:S(2)}, u32[]{:S(2)}) collective-permute-start(bf16[64,4608]{1,0:T(8,128)(2,1)S(1)} %pad_maximum_fusion), channel_id=1, source_target_pairs={{0,4},{1,17},{2,6},{3,19},{4,8},{5,21},{6,10},{7,23},{8,12},{9,25}... | collective-permute-start | bytes 1769480 | tf_op jit(solution)/shard_map/ppermute | solution.py:179
  156.6 23.3 %collective-permute-start.30 = (bf16[64,4608]{1,0:T(8,128)(2,1)S(1)}, bf16[64,4608]{1,0:T(8,128)(2,1)S(1)}, u32[]{:S(2)}, u32[]{:S(2)}) collective-permute-start(bf16[64,4608]{1,0:T(8,128)(2,1)S(1)} %pad_maximum_fusion), channel_id=1, source_target_pairs={{0,12},{1,49},{2,14},{3,51},{4,0},{5,53},{6,2},{7,55},{8,4},{9,57}... | collective-permute-start | bytes 1769480 | tf_op jit(solution)/shard_map/ppermute | solution.py:179
  161.4 17.3 %collective-permute-start.29 = (bf16[64,4608]{1,0:T(8,128)(2,1)S(1)}, bf16[64,4608]{1,0:T(8,128)(2,1)S(1)}, u32[]{:S(2)}, u32[]{:S(2)}) collective-permute-start(bf16[64,4608]{1,0:T(8,128)(2,1)S(1)} %constant_dynamic-update-slice_fusion.4), channel_id=1, source_target_pairs={{0,4},{1,17},{2,6},{3,19},{4,8},{5,21},{6,10},{7,23},{8,12},{9,25}... | collective-permute-start | bytes 1769480 | tf_op jit(solution)/shard_map/ppermute | solution.py:179
  161.7 12.2 %collective-permute-start.31 = (bf16[64,4608]{1,0:T(8,128)(2,1)S(1)}, bf16[64,4608]{1,0:T(8,128)(2,1)S(1)}, u32[]{:S(2)}, u32[]{:S(2)}) collective-permute-start(bf16[64,4608]{1,0:T(8,128)(2,1)S(1)} %constant_dynamic-update-slice_fusion.4), channel_id=1, source_target_pairs={{0,12},{1,49},{2,14},{3,51},{4,0},{5,53},{6,2},{7,55},{8,4},{9,57}... | collective-permute-start | bytes 1769480 | tf_op jit(solution)/shard_map/ppermute | solution.py:179
  168.1 14.4 %collective-permute-start.32 = (bf16[64,4608]{1,0:T(8,128)(2,1)S(1)}, bf16[64,4608]{1,0:T(8,128)(2,1)S(1)}, u32[]{:S(2)}, u32[]{:S(2)}) collective-permute-start(bf16[64,4608]{1,0:T(8,128)(2,1)S(1)} %collective-permute-done.28), channel_id=1, source_target_pairs={{0,4},{1,17},{2,6},{3,19},{4,8},{5,21},{6,10},{7,23},{8,12},{9,25}... | collective-permute-start | bytes 1769480 | tf_op jit(solution)/shard_map/ppermute | solution.py:179
  174.0 10.1 %collective-permute-start.33 = (bf16[64,4608]{1,0:T(8,128)(2,1)S(1)}, bf16[64,4608]{1,0:T(8,128)(2,1)S(1)}, u32[]{:S(2)}, u32[]{:S(2)}) collective-permute-start(bf16[64,4608]{1,0:T(8,128)(2,1)S(1)} %collective-permute-done.31), channel_id=1, source_target_pairs={{0,12},{1,49},{2,14},{3,51},{4,0},{5,53},{6,2},{7,55},{8,4},{9,57}... | collective-permute-start | bytes 1769480 | tf_op jit(solution)/shard_map/ppermute | solution.py:179

commit v3 on v2

--- a/solution.py
+++ b/solution.py
@@ -78,91 +78,181 @@
     )
 
 
-def partial_kernel(jobs, *refs):
-    count = 1 + max(rows for pieces in jobs for rows, _ in pieces)
-    row_refs, gain_ref, weight_refs, outs = (
-        refs[:count],
-        refs[count],
-        refs[count + 1 : count + 3],
-        refs[count + 3 :],
-    )
-    half = weight_refs[0].shape[1]
+def whole_call(kernel, name, out_shapes, operands, cost, limit=VMEM_LIMIT):
+    return pl.pallas_call(
+        kernel,
+        out_shape=out_shapes,
+        in_specs=[pl.BlockSpec(memory_space=pltpu.VMEM)] * len(operands),
+        out_specs=[pl.BlockSpec(memory_space=pltpu.VMEM)] * len(out_shapes),
+        compiler_params=pltpu.CompilerParams(vmem_limit_bytes=limit),
+        cost_estimate=pl.CostEstimate(flops=cost[0], bytes_accessed=cost[1], transcendentals=0),
+        name=name,
+    )(*operands)
+
+
+BODY, TAIL = 512, 64
+
+
+def tail_at(block, odd, upper):
+    block = block.astype(jnp.float32)
+    turned = pltpu.roll(block, TAIL, 1)
+    return jnp.where((odd == 1) != upper, turned, block)
+
+
+def cut_in_kernel(chunk_ref, gate, gate_tail, up, up_tail, gain_ref, out_ref):
+    odd = chunk_ref[0] % 2
     gain = gain_ref[...]
-    ready = []
-    for ref in row_refs:
-        x = ref[...].reshape(-1, ref.shape[-1]).astype(jnp.float32)
-        ready.append(((x * gain).astype(jnp.bfloat16), jnp.sum(x * x, axis=1, keepdims=True)))
-    for pieces, out in zip(jobs, outs):
-        start = 0
-        for rows, side in pieces:
-            scaled, square = ready[rows]
-            out[:, start : start + half] = jnp.dot(
-                scaled, weight_refs[side][...], preferred_element_type=jnp.float32
-            ).astype(jnp.bfloat16)
-            start += half
-            if side == 0:
-                high = square.astype(jnp.bfloat16).astype(jnp.float32)
-                lane = lax.broadcasted_iota(jnp.int32, (scaled.shape[0], 128), 1)
-                out[:, start : start + 128] = jnp.where(lane < 64, high, square - high).astype(
-                    jnp.bfloat16
-                )
-                start += 128
-
-
-def partial_sums(rows, places, gain, weights, jobs):
-    _, _, per_group, width = rows.shape
-    half = weights[0].shape[1]
-    count = 4 * per_group
-    whole = lambda i: (0, 0)
-
-    def at(place):
-        return lambda i: (0, place, 0, 0)
-
-    widths = [sum(half + (128 if side == 0 else 0) for _, side in pieces) for pieces in jobs]
+    out_ref[:, :BODY] = (wide(gate[...]) * gain).astype(jnp.bfloat16)
+    out_ref[:, BODY : 2 * BODY] = (wide(up[...]) * gain).astype(jnp.bfloat16)
+    lane = lax.broadcasted_iota(jnp.int32, gate_tail.shape, 1)
+    tails = jnp.where(
+        lane < TAIL, tail_at(gate_tail[...], odd, False), tail_at(up_tail[...], odd, True)
+    )
+    out_ref[:, 2 * BODY :] = (tails * gain).astype(jnp.bfloat16)
+
+
+def chunk_specs(width):
+    tails = 4 * BODY // 128
+    return [
+        pl.BlockSpec((width, BODY), lambda i, c: (0, c[i])),
+        pl.BlockSpec((width, 2 * TAIL), lambda i, c: (0, tails + c[i] // 2)),
+    ]
+
+
+def cut_in(chunk, w_gate, w_up, gain):
+    width = w_gate.shape[0]
+    cols = 2 * (BODY + TAIL)
     return pl.pallas_call(
-        functools.partial(partial_kernel, jobs),
-        grid=(1,),
-        in_specs=[pl.BlockSpec((4, 1, per_group, width), at(p)) for p in places]
-        + [pl.BlockSpec((1, width), whole)]
-        + [pl.BlockSpec((width, half), whole)] * 2,
-        out_specs=[pl.BlockSpec((count, w), whole) for w in widths],
-        out_shape=[jax.ShapeDtypeStruct((count, w), jnp.bfloat16) for w in widths],
+        cut_in_kernel,
+        grid_spec=pltpu.PrefetchScalarGridSpec(
+            num_scalar_prefetch=1,
+            grid=(1,),
+            in_specs=chunk_specs(width) * 2 + [pl.BlockSpec((width, 1), lambda i, c: (0, 0))],
+            out_specs=pl.BlockSpec((width, cols), lambda i, c: (0, 0)),
+        ),
+        out_shape=jax.ShapeDtypeStruct((width, cols), jnp.bfloat16),
         compiler_params=pltpu.CompilerParams(vmem_limit_bytes=VMEM_LIMIT),
         cost_estimate=pl.CostEstimate(
-            flops=2 * count * width * sum(widths),
-            bytes_accessed=2 * (2 * width * half + count * sum(widths)),
-            transcendentals=0,
+            flops=width * cols, bytes_accessed=4 * width * cols, transcendentals=0
         ),
-        name="partial_sums",
-    )(*([rows] * len(places)), gain, *weights)
-
-
-def merge_kernel(own_a, own_c, direct_a, direct_c, relay_a, relay_c, *outs):
-    wide_a = own_a.shape[1]
-    rows = outs[0].shape[0]
-    for out, place in zip(outs, FACING):
-        part = pl.ds(place * rows, rows)
-        total = wide(own_a[part, :]) + wide(relay_a[part, :]) + wide(direct_a[part, :])
-        out[:, :wide_a] = total.astype(jnp.bfloat16)
-        total = wide(own_c[part, :]) + wide(relay_c[part, :]) + wide(direct_c[part, :])
-        out[:, wide_a:] = total.astype(jnp.bfloat16)
-
-
-def merge(*operands):
-    own_a, own_c = operands[:2]
-    rows = own_a.shape[0] // 4
-    cols = own_a.shape[1] + own_c.shape[1]
+        name="cut_in",
+    )(chunk.astype(jnp.int32)[None], w_gate, w_gate, w_up, w_up, gain)
+
+
+def cut_down_kernel(chunk_ref, down, down_tail, out_ref):
+    out_ref[0, :, :BODY] = down[...]
+    lane = lax.broadcasted_iota(jnp.int32, down_tail.shape, 1)
+    tail = tail_at(down_tail[...], chunk_ref[pl.program_id(0)] % 2, False)
+    out_ref[0, :, BODY:] = jnp.where(lane < TAIL, tail, 0.0).astype(jnp.bfloat16)
+
+
+def cut_down(chunks, w_down):
+    width = w_down.shape[1]
+    cols = BODY + 2 * TAIL
+    turned = jnp.swapaxes(w_down, 0, 1)
     return pl.pallas_call(
-        merge_kernel,
-        out_shape=[jax.ShapeDtypeStruct((rows, cols), jnp.bfloat16)] * 4,
-        in_specs=[pl.BlockSpec(memory_space=pltpu.VMEM)] * 6,
-        out_specs=[pl.BlockSpec(memory_space=pltpu.VMEM)] * 4,
+        cut_down_kernel,
+        grid_spec=pltpu.PrefetchScalarGridSpec(
+            num_scalar_prefetch=1,
+            grid=(4,),
+            in_specs=chunk_specs(width),
+            out_specs=pl.BlockSpec((1, width, cols), lambda i, c: (i, 0, 0)),
+        ),
+        out_shape=jax.ShapeDtypeStruct((4, width, cols), jnp.bfloat16),
         compiler_params=pltpu.CompilerParams(vmem_limit_bytes=VMEM_LIMIT),
         cost_estimate=pl.CostEstimate(
-            flops=12 * rows * cols, bytes_accessed=32 * rows * cols, transcendentals=0
+            flops=4 * width * cols, bytes_accessed=16 * width * cols, transcendentals=0
         ),
-        name="merge",
-    )(*operands)
+        name="cut_down",
+    )(chunks.astype(jnp.int32), turned, turned)
+
+
+def source_place(place, source):
+    return SHIFTS.index((SHIFTS[place] - SHIFTS[source] + 1) % 4 - 1)
+
+
+def partial_kernel(part, *refs):
+    rows, weights, out = refs[:4], refs[4:8], refs[8]
+    cols = weights[0].shape[1]
+    total, square = 0.0, 0.0
+    for source in range(4):
+        x = jnp.concatenate([rows[source][part, source_place(p, source)] for p in range(4)])
+        total += jnp.dot(x, weights[source][...], preferred_element_type=jnp.float32)
+        square += jnp.sum(wide(x) * wide(x), axis=1, keepdims=True)
+    out[:, :cols] = total.astype(jnp.bfloat16)
+    high = wide(square.astype(jnp.bfloat16))
+    lane = lax.broadcasted_iota(jnp.int32, (total.shape[0], 128), 1)
+    out[:, cols:] = jnp.where(lane < 64, high, square - high).astype(jnp.bfloat16)
+
+
+def partial_sums(rows, part, weights):
+    _, _, per_group, width = rows[0].shape
+    count, cols = 4 * per_group, weights[0].shape[1]
+    return whole_call(
+        functools.partial(partial_kernel, part),
+        "partial_sums",
+        [jax.ShapeDtypeStruct((count, cols + 128), jnp.bfloat16)],
+        (*rows, *weights),
+        (8 * count * width * cols, 8 * width * cols + 2 * count * cols),
+    )[0]
+
+
+def activate_kernel(model_width, *refs):
+    out = refs[4]
+    total = sum(wide(r[...]) for r in refs[:4])
+    cols = 2 * (BODY + TAIL)
+    square = total[:, cols : cols + 1] + total[:, cols + 64 : cols + 65]
+    scale = lax.rsqrt(square / model_width + epsilon)
+    gated = lambda g, u: jax.nn.silu(g * scale) * (u * scale)
+    out[:, :BODY] = gated(total[:, :BODY], total[:, BODY : 2 * BODY]).astype(jnp.bfloat16)
+    tails = total[:, 2 * BODY : cols]
+    lane = lax.broadcasted_iota(jnp.int32, tails.shape, 1)
+    tails = jnp.where(lane < TAIL, gated(tails, pltpu.roll(tails, TAIL, 1)), 0.0)
+    out[:, BODY:] = tails.astype(jnp.bfloat16)
+
+
+def activate(sums, model_width):
+    count = sums[0].shape[0]
+    cols = BODY + 2 * TAIL
+    return whole_call(
+        functools.partial(activate_kernel, model_width),
+        "activate",
+        [jax.ShapeDtypeStruct((count, cols), jnp.bfloat16)],
+        sums,
+        (20 * count * cols, 20 * count * cols),
+    )[0]
+
+
+def down_kernel(low, high, weights, mine, theirs):
+    count = low.shape[1] // 4
+    total = 0.0
+    for source in range(4):
+        ref = (low, high)[source // 2]
+        x = jnp.concatenate(
+            [
+                ref[source % 2, pl.ds(source_place(p, source) * count, count), :]
+                for p in range(4)
+            ]
+        )
+        total += lax.dot_general(
+            x, weights[source], (((1,), (1,)), ((), ())), preferred_element_type=jnp.float32
+        )
+    for p in range(4):
+        mine[p] = total[p * count : p * count + count // 2]
+        theirs[p] = total[p * count + count // 2 : (p + 1) * count].astype(jnp.bfloat16)
+
+
+def down_block(low, high, weights):
+    count = low.shape[1] // 4
+    width = weights.shape[1]
+    shape = (4, count // 2, width)
+    return whole_call(
+        down_kernel,
+        "down_block",
+        [jax.ShapeDtypeStruct(shape, jnp.float32), jax.ShapeDtypeStruct(shape, jnp.bfloat16)],
+        (low, high, weights),
+        (32 * count * width * low.shape[2], 8 * width * low.shape[2]),
+    )
 
 
 def ring(first):
@@ -252,11 +342,13 @@
 
     uv_pair = (w_uv, swap(w_uv, "core"))
     o_chip = jnp.concatenate([w_o, swap(w_o, "core")], axis=0)
-    down_chip = jnp.concatenate([w_down, swap(w_down, "core")], axis=0)
-    in_pair = (
-        jnp.where(core == 0, w_gate, w_up),
-        swap(jnp.where(core == 0, w_up, w_gate), "core"),
-    )
+    gain = wide(norm_gain)[:, None]
+    steps = jnp.array(SHIFTS)
+    in_weights = [
+        shift_1(cut_in((place_1 + s) % 4, w_gate, w_up, gain), s) for s in SHIFTS[1:]
+    ]
+    in_weights = [cut_in(place_1, w_gate, w_up, gain)] + in_weights
+    down_weights = cut_down((place_1 - steps) % 4, w_down)
 
     residual = lax.dynamic_index_in_dim(
         hidden_in.reshape(4, 4, 2, 2, tokens, width), core, 3, keepdims=False
@@ -301,46 +393,30 @@
     rows = jnp.stack([rows, jnp.swapaxes(swap(rows, "core"), 1, 2)])
     rows = jnp.transpose(rows, (2, 3, 0, 1, 4, 5, 6)).reshape(4, 4, 8 * tokens, width)
 
-    gain = wide(norm_gain)[None]
-    behind, ahead, far = FACING[2], FACING[1], FACING[3]
-    far_a, far_c = partial_sums(rows, (far,), gain, in_pair, (((0, 0),), ((0, 1),)))
-    ahead_c, behind_a = partial_sums(rows, (ahead, behind), gain, in_pair, (((0, 1),), ((1, 0),)))
-    ahead_a, behind_c, own_a, own_c = partial_sums(
-        rows, (ahead, behind, 0), gain, in_pair, (((0, 0),), ((1, 1),), ((2, 0),), ((2, 1),))
-    )
-    far_a, far_c = shift_1(far_a, 1), shift_1(far_c, -1)
-    direct_c, direct_a = shift_1(ahead_c, 1), shift_1(behind_a, -1)
-    relay_a = shift_1(add(ahead_a, far_a).astype(jnp.bfloat16), 1)
-    relay_c = shift_1(add(behind_c, far_c).astype(jnp.bfloat16), -1)
-    blocks = merge(own_a, own_c, direct_a, direct_c, relay_a, relay_c)
-    sums = add(blocks[0], *(shift_2(blocks[i], SHIFTS[i]) for i in range(1, 4)))
-    square = sums[:, hidden : hidden + 1] + sums[:, hidden + 64 : hidden + 65]
-    scale = lax.rsqrt(square / model_width + epsilon)
-    sums = [sums[:, :hidden] * scale, sums[:, hidden + 128 :] * scale]
-    own = [s[: 4 * tokens] for s in sums]
-    other = swap(
-        jnp.concatenate([s[4 * tokens :].astype(jnp.bfloat16) for s in sums], axis=1), "core"
-    )
-    other = [wide(other[:, hidden:]), wide(other[:, :hidden])]
-    activated = jnp.concatenate(
-        [
-            (jax.nn.silu(jnp.where(core == 0, a, b)) * jnp.where(core == 0, b, a)).astype(
-                jnp.bfloat16
-            )
-            for a, b in zip(own, other)
-        ],
-        axis=1,
-    )
+    rows_low, rows_high = rows[:2], rows[2:]
+    rows_high = gather(rows_high, shift_1)
+    rows_low = gather(rows_low, shift_1)
+    far = shift_2(partial_sums(rows_high, FACING[3] - 2, in_weights), SHIFTS[3])
+    behind = shift_2(partial_sums(rows_high, FACING[1] - 2, in_weights), SHIFTS[1])
+    ahead = shift_2(partial_sums(rows_low, FACING[2], in_weights), SHIFTS[2])
+    own = partial_sums(rows_low, FACING[0], in_weights)
+    activated = activate((own, behind, ahead, far), model_width)
 
     own, behind, ahead, far = gather(activated, shift_1)
-    low, high = jnp.concatenate([own, behind]), jnp.concatenate([ahead, far])
+    low, high = jnp.stack([own, behind]), jnp.stack([ahead, far])
     behind_low, ahead_high = shift_2(low, 1), shift_2(high, -1)
     behind_high, ahead_low = shift_2(high, 1), shift_2(low, -1)
     far_low, far_high = shift_2(behind_low, 1), shift_2(ahead_high, -1)
-    pieces = (low, high, behind_low, behind_high, ahead_low, ahead_high, far_low, far_high)
-    down = jnp.stack(
-        [jnp.dot(p, down_chip, preferred_element_type=jnp.float32) for p in pieces]
-    ).reshape(4, 4, 2, 2, tokens, width)
+    pairs = (
+        (low, high),
+        (behind_low, behind_high),
+        (ahead_low, ahead_high),
+        (far_low, far_high),
+    )
+    mine, theirs = zip(*(down_block(a, b, down_weights) for a, b in pairs))
+    theirs = swap(jnp.stack(theirs), "core")
+    down = jnp.stack(mine) + wide(jnp.swapaxes(theirs, 0, 1))
+    down = down.reshape(4, 4, 2, 2, tokens, width)
     at_home = jnp.arange(2)[None, None, :, None, None] == yh
     down = jnp.stack([down[:, :, 0] + jnp.where(at_home, stream, 0.0), down[:, :, 1]])
     down = down.astype(jnp.bfloat16)

time: 219 us -> 231 us (1.055)
  waiting for transfers between devices: 78.1 us -> 91.7 us
  matrix products: 19.2 us -> 7.25 us
  Pallas kernels: 18.3 us -> 27.7 us
  starting transfers between devices: 45.6 us -> 51.8 us
  other arithmetic: 9.3 us -> 5.59 us
  blocking collectives: 30.8 us -> 27.8 us
    ppermute x24 -> x27, waiting for transfers between devices: 65.4 us -> 82.8 us  [shift(): return lax.ppermute(value, ('grp', 'yh', 'core'), pairs)]
    dot_general x8 -> x0, matrix products: 10.4 us -> none  [body(): jnp.dot(p, down_chip, preferred_element_type=jnp.float32)]
    pallas_call x4 -> x14, Pallas kernels: 11.1 us -> 20.5 us  [the longest x9 15.4 us: whole_call(): pl.pallas_call(kernel, out_shape=out_shapes, in_specs=[pl.BlockSpec(memor...]
    ppermute x3, waiting for transfers between devices: 11.3 us -> 5.73 us  [shift_y(): lax.ppermute(value, ('role', 'yh', 'core'), [(p, moved(p)) for p in range...]
    ppermute x7 -> x5, starting transfers between devices: 8.02 us -> 13 us  [swap(): return lax.ppermute(value, axis, [(0, 1), (1, 0)])]
    select_n x1, other arithmetic: 3.78 us -> 0.01 us  [body(): down_weights = cut_down((place_1 - steps) % 4, w_down)]
    unnamed x20 -> x72, local copies, waits for them, and re-layouts: 11.5 us -> 14.7 us
    ppermute x3, starting transfers between devices: 3.12 us -> 5.63 us  [shift_y(): lax.ppermute(value, ('role', 'yh', 'core'), [(p, moved(p)) for p in range...]
  transfers between devices with their start and end apart: 34 -> 35, of which waited for: 20 -> 25; matrix products, arithmetic and copies ran while one was open for 16% -> 6% of each run, Pallas kernels for 3% -> 8%
where the time goes in v3:
time: 231 us; the launch traced here: 230 us
  waiting for transfers between devices  91.7 us (40%)
  starting transfers between devices  51.8 us (22%)
  blocking collectives  27.8 us (12%)
  Pallas kernels  27.7 us (12%)
  local copies, waits for them, and re-layouts  17.8 us (8%)
  matrix products  7.25 us (3%)
  other arithmetic  5.59 us (2%)
    ppermute x27, waiting for transfers between devices, shift(): return lax.ppermute(value, ('grp', 'yh', 'core'), pairs)  82.8 us
    ppermute x27, starting transfers between devices, shift(): return lax.ppermute(value, ('grp', 'yh', 'core'), pairs)  33.2 us
    all_to_all x1, blocking collectives, body(): lax.all_to_all(down, ('role', 'grp', 'yh'), split_axis=0, concat_axis=0)  18.1 us
    pallas_call x9, Pallas kernels, whole_call(): pl.pallas_call(kernel, out_shape=out_shapes, in_specs=[pl.BlockSpec(memor...  15.4 us
    unnamed x72, local copies, waits for them, and re-layouts  14.7 us
    ppermute x5, starting transfers between devices, swap(): return lax.ppermute(value, axis, [(0, 1), (1, 0)])  13 us
    all_gather x1, blocking collectives, body(): return lax.all_gather(result, ('yh', 'core'), axis=0, tiled=True)  9.69 us
    pallas_call x1, Pallas kernels, attend(): pl.pallas_call(functools.partial(attend_kernel, scale, latent), grid_spec...  7.19 us
  transfers between devices with their start and end apart: 35, of which 25 were waited for; matrix products, arithmetic and copies ran while one was open for 6% of the time, Pallas kernels for 8%

profile of v3, /device:TPU:1, one launch (start us, length us, event | category | flops | bytes accessed | tf_op | source)
XLA Modules:
  0.0 230.5 jit_solution(1412555845332557051)
XLA Ops:
  0.7 3.7 %copy-done.5 = bf16[8,1024,576]{1,2,0:T(8,128)(2,1)S(1)} copy-done((bf16[8,1024,576]{1,2,0:T(8,128)(2,1)S(1)}, bf16[8,1024,576]{1,2,0:T(8,128)(2,1)}, u32[]{:S(2)}) %copy-start.5) | copy-done | bytes 9437208
  4.4 1.1 copy-done.7
  6.8 7.2 %attend.1 = (bf16[2,8,16,512]{3,2,1,0:T(8,128)(2,1)S(1)}, bf16[2,8,16,512]{3,2,1,0:T(8,128)(2,1)S(1)}) custom-call(s32[8]{0:T(128)S(1)} %copy-done.8, s32[8]{0:T(128)S(1)} %copy-done.9, s32[1]{0:T(128)} %bitcast.3.place_ref, bf16[8,4,16,576]{3,2,1,0:T(8,128)(2,1)S(1)} %bitcast.104, f32[8,1,576]{2,1,0:T(1,128)S(1)} %reshape.87.new_ref, ...), custom_call_target="tpu_custom_call" | custom-call | flops 1140850688 | bytes 9437184 | tf_op jit(solution)/shard_map/attend/pallas_call | solution.py:60
  14.0 3.8 %collective-permute-start = (bf16[2,8,16,512]{3,2,1,0:T(8,128)(2,1)S(1)}, bf16[2,8,16,512]{3,2,1,0:T(8,128)(2,1)}, u32[]{:S(2)}, u32[]{:S(2)}) collective-permute-start(bf16[2,8,16,512]{3,2,1,0:T(8,128)(2,1)S(1)} %get-tuple-element.16), channel_id=1, source_target_pairs={{0,2},{2,0},{1,3},{3,1},{4,6},{6,4},{5,7},{7,5},{8,10},{10,8},{9,1... | collective-permute-start | bytes 786440 | tf_op jit(solution)/shard_map/ppermute | solution.py:287
  18.8 1.2 copy.85
  20.5 1.6 constant_dynamic-update-slice_fusion.1
  22.1 1.6 collective-permute-done
  25.3 2.1 fusion.1
  27.4 1.7 collective-permute-start.2
  29.1 2.2 collective-permute-start.3
  31.3 1.2 collective-permute-start.4
  32.6 1.3 collective-permute-done.2
  33.9 3.0 %collective-permute-done.4 = bf16[16,4096]{1,0:T(8,128)(2,1)S(1)} collective-permute-done((bf16[16,4096]{1,0:T(8,128)(2,1)S(1)}, bf16[16,4096]{1,0:T(8,128)(2,1)S(1)}, u32[]{:S(2)}, u32[]{:S(2)}) %collective-permute-start.4) | collective-permute-done | bytes 131104 | tf_op jit(solution)/shard_map/ppermute | solution.py:269
  38.0 1.6 constant_dynamic-update-slice_fusion
  39.6 1.8 collective-permute-start.7
  41.4 1.2 collective-permute-start.8
  42.7 1.2 fusion.22
  43.8 2.8 %collective-permute-done.6 = bf16[64,4096]{1,0:T(8,128)(2,1)S(1)} collective-permute-done((bf16[64,4096]{1,0:T(8,128)(2,1)S(1)}, bf16[64,4096]{1,0:T(8,128)(2,1)S(1)}, u32[]{:S(2)}, u32[]{:S(2)}) %collective-permute-start.6) | collective-permute-done | bytes 524320 | tf_op jit(solution)/shard_map/ppermute | solution.py:269
  46.6 1.2 fusion.26
  47.8 5.4 %collective-permute-done.7 = bf16[64,4096]{1,0:T(8,128)(2,1)S(1)} collective-permute-done((bf16[64,4096]{1,0:T(8,128)(2,1)S(1)}, bf16[64,4096]{1,0:T(8,128)(2,1)S(1)}, u32[]{:S(2)}, u32[]{:S(2)}) %collective-permute-start.7) | collective-permute-done | bytes 524320 | tf_op jit(solution)/shard_map/ppermute | solution.py:269
  53.2 1.2 fusion.27
  54.4 1.2 fusion.28
  55.7 3.0 %collective-permute-start.9 = (bf16[4,4,2,8,448]{4,3,2,0,1:T(8,128)(2,1)S(1)}, bf16[4,4,2,8,448]{4,3,2,0,1:T(8,128)(2,1)S(1)}, u32[]{:S(2)}, u32[]{:S(2)}) collective-permute-start(bf16[4,4,2,8,448]{4,3,2,0,1:T(8,128)(2,1)S(1)} %copy.133), channel_id=1, source_target_pairs={{0,2},{1,3},{2,0},{3,1},{64,66},{65,67},{66,64},{67,65},{4,6},{5,7... | collective-permute-start | bytes 688136 | tf_op jit(solution)/shard_map/ppermute | solution.py:283
  59.1 2.3 collective-permute-start.11
  61.3 1.2 collective-permute-done.9
  62.7 4.3 %collective-permute-done.10 = bf16[4,4,2,8,448]{4,3,2,0,1:T(8,128)(2,1)S(1)} collective-permute-done((bf16[4,4,2,8,448]{4,3,2,0,1:T(8,128)(2,1)S(1)}, bf16[4,4,2,8,448]{4,3,2,0,1:T(8,128)(2,1)S(1)}, u32[]{:S(2)}, u32[]{:S(2)}) %collective-permute-start.10) | collective-permute-done | bytes 229408 | tf_op jit(solution)/shard_map/ppermute | solution.py:283
  68.9 4.7 %collective-permute-start.12 = (bf16[2,4,4,2,8,448]{5,4,3,2,1,0:T(8,128)(2,1)}, bf16[2,4,4,2,8,448]{5,4,3,2,1,0:T(8,128)(2,1)}, u32[]{:S(2)}, u32[]{:S(2)}) collective-permute-start(bf16[2,4,4,2,8,448]{5,4,3,2,1,0:T(8,128)(2,1)} %pad_maximum_fusion.3), channel_id=1, source_target_pairs={{0,1},{1,0},{2,3},{3,2},{4,5},{5,4},{6,7},{7,6},{8,9},{9,8},{10,11... | collective-permute-start | bytes 1376264 | tf_op jit(solution)/shard_map/ppermute | solution.py:287
  73.8 1.6 copy-done.1
  75.4 1.4 cut_in.5
  77.2 1.6 copy-done.2
  78.8 1.4 cut_in.6
  80.2 2.2 collective-permute-start.17
  82.4 1.6 copy-done.3
  85.3 1.2 maximum_bitcast_fusion
  87.6 1.9 collective-permute-start.20
  89.5 2.5 %collective-permute-done.16.refs_5_ = bf16[448,1152]{1,0:T(8,128)(2,1)S(1)} collective-permute-done((bf16[448,1152]{1,0:T(8,128)(2,1)}, bf16[448,1152]{1,0:T(8,128)(2,1)S(1)}, u32[]{:S(2)}, u32[]{:S(2)}) %collective-permute-start.16) | collective-permute-done | bytes 1032224 | tf_op jit(solution)/shard_map/ppermute | solution.py:269
  92.1 13.3 %collective-permute-done.17.refs_6_ = bf16[448,1152]{1,0:T(8,128)(2,1)} collective-permute-done((bf16[448,1152]{1,0:T(8,128)(2,1)}, bf16[448,1152]{1,0:T(8,128)(2,1)}, u32[]{:S(2)}, u32[]{:S(2)}) %collective-permute-start.17) | collective-permute-done | bytes 1032224 | tf_op jit(solution)/shard_map/ppermute | solution.py:269
  105.4 3.3 %collective-permute-start.14 = (bf16[2,4,64,448]{3,2,1,0:T(8,128)(2,1)S(1)}, bf16[2,4,64,448]{3,2,1,0:T(8,128)(2,1)S(1)}, u32[]{:S(2)}, u32[]{:S(2)}) collective-permute-start(bf16[2,4,64,448]{3,2,1,0:T(8,128)(2,1)S(1)} %bitcast.99), channel_id=1, source_target_pairs={{0,48},{1,13},{2,50},{3,15},{4,52},{5,1},{6,54},{7,3},{8,56},{9,5}... | collective-permute-start | bytes 1376264 | tf_op jit(solution)/shard_map/ppermute | solution.py:269
  108.7 1.3 collective-permute-start.15
  110.4 6.1 %collective-permute-done.20.refs_2_ = bf16[2,4,64,448]{3,2,1,0:T(8,128)(2,1)S(1)} collective-permute-done((bf16[2,4,64,448]{3,2,1,0:T(8,128)(2,1)S(1)}, bf16[2,4,64,448]{3,2,1,0:T(8,128)(2,1)S(1)}, u32[]{:S(2)}, u32[]{:S(2)}) %collective-permute-start.20) | collective-permute-done | bytes 458784 | tf_op jit(solution)/shard_map/ppermute | solution.py:269
  116.5 2.7 %partial_sums.7 = bf16[256,1280]{1,0:T(8,128)(2,1)S(1)} custom-call(bf16[2,4,64,448]{3,2,1,0:T(8,128)(2,1)S(1)} %bitcast.96, bf16[2,4,64,448]{3,2,1,0:T(8,128)(2,1)S(1)} %collective-permute-done.19.refs_1_, bf16[2,4,64,448]{3,2,1,0:T(8,128)(2,1)S(1)} %collective-permute-done.20.refs_2_, bf16[2,4,64,448]{3,2,1,0:T(8,128)(2,1)S(1)} %collective-permute-done.21.refs_3_, ...), custom_call_target="tpu_custom_call" | custom-call | flops 1056964608 | bytes 4718592 | tf_op jit(solution)/shard_map/partial_sums/pallas_call | solution.py:82
  120.4 14.3 %collective-permute-done.14.refs_2_ = bf16[2,4,64,448]{3,2,1,0:T(8,128)(2,1)S(1)} collective-permute-done((bf16[2,4,64,448]{3,2,1,0:T(8,128)(2,1)S(1)}, bf16[2,4,64,448]{3,2,1,0:T(8,128)(2,1)S(1)}, u32[]{:S(2)}, u32[]{:S(2)}) %collective-permute-start.14) | collective-permute-done | bytes 458784 | tf_op jit(solution)/shard_map/ppermute | solution.py:269
  134.8 2.7 %partial_sums.6 = bf16[256,1280]{1,0:T(8,128)(2,1)S(1)} custom-call(bf16[2,4,64,448]{3,2,1,0:T(8,128)(2,1)S(1)} %bitcast.101, bf16[2,4,64,448]{3,2,1,0:T(8,128)(2,1)S(1)} %collective-permute-done.13.refs_1_, bf16[2,4,64,448]{3,2,1,0:T(8,128)(2,1)S(1)} %collective-permute-done.14.refs_2_, bf16[2,4,64,448]{3,2,1,0:T(8,128)(2,1)S(1)} %collective-permute-done.15.refs_3_, ...), custom_call_target="tpu_custom_call" | custom-call | flops 1056964608 | bytes 4718592 | tf_op jit(solution)/shard_map/partial_sums/pallas_call | solution.py:82
  137.5 3.5 %collective-permute-start.23 = (bf16[256,1280]{1,0:T(8,128)(2,1)S(1)}, bf16[256,1280]{1,0:T(8,128)(2,1)S(1)}, u32[]{:S(2)}, u32[]{:S(2)}) collective-permute-start(bf16[256,1280]{1,0:T(8,128)(2,1)S(1)} %partial_sums.6), channel_id=1, source_target_pairs={{0,12},{1,49},{2,14},{3,51},{4,0},{5,53},{6,2},{7,55},{8,4},{9,57}... | collective-permute-start | bytes 1966088 | tf_op jit(solution)/shard_map/ppermute | solution.py:269
  141.0 2.7 %partial_sums.5 = bf16[256,1280]{1,0:T(8,128)(2,1)S(1)} custom-call(bf16[2,4,64,448]{3,2,1,0:T(8,128)(2,1)S(1)} %bitcast.97, bf16[2,4,64,448]{3,2,1,0:T(8,128)(2,1)S(1)} %collective-permute-done.19.refs_1_, bf16[2,4,64,448]{3,2,1,0:T(8,128)(2,1)S(1)} %collective-permute-done.20.refs_2_, bf16[2,4,64,448]{3,2,1,0:T(8,128)(2,1)S(1)} %collective-permute-done.21.refs_3_, ...), custom_call_target="tpu_custom_call" | custom-call | flops 1056964608 | bytes 4718592 | tf_op jit(solution)/shard_map/partial_sums/pallas_call | solution.py:82
  143.8 2.7 %partial_sums.4.refs_0_ = bf16[256,1280]{1,0:T(8,128)(2,1)S(1)} custom-call(bf16[2,4,64,448]{3,2,1,0:T(8,128)(2,1)S(1)} %bitcast.102, bf16[2,4,64,448]{3,2,1,0:T(8,128)(2,1)S(1)} %collective-permute-done.13.refs_1_, bf16[2,4,64,448]{3,2,1,0:T(8,128)(2,1)S(1)} %collective-permute-done.14.refs_2_, bf16[2,4,64,448]{3,2,1,0:T(8,128)(2,1)S(1)} %collective-permute-done.15.refs_3_, ...), custom_call_target="tpu_custom_call" | custom-call | flops 1056964608 | bytes 4718592 | tf_op jit(solution)/shard_map/partial_sums/pallas_call | solution.py:82
  146.6 1.9 collective-permute-done.23.refs_2_
  148.5 6.2 %collective-permute-done.22.refs_1_ = bf16[256,1280]{1,0:T(8,128)(2,1)S(1)} collective-permute-done((bf16[256,1280]{1,0:T(8,128)(2,1)S(1)}, bf16[256,1280]{1,0:T(8,128)(2,1)S(1)}, u32[]{:S(2)}, u32[]{:S(2)}) %collective-permute-start.22) | collective-permute-done | bytes 655392 | tf_op jit(solution)/shard_map/ppermute | solution.py:269
  155.2 2.9 %collective-permute-start.26 = (bf16[256,640]{1,0:T(8,128)(2,1)S(1)}, bf16[256,640]{1,0:T(8,128)(2,1)S(1)}, u32[]{:S(2)}, u32[]{:S(2)}) collective-permute-start(bf16[256,640]{1,0:T(8,128)(2,1)S(1)} %activate.1), channel_id=1, source_target_pairs={{0,48},{1,13},{2,50},{3,15},{4,52},{5,1},{6,54},{7,3},{8,56},{9,5}... | collective-permute-start | bytes 983048 | tf_op jit(solution)/shard_map/ppermute | solution.py:269
  158.8 6.9 %collective-permute-done.26 = bf16[256,640]{1,0:T(8,128)(2,1)S(1)} collective-permute-done((bf16[256,640]{1,0:T(8,128)(2,1)S(1)}, bf16[256,640]{1,0:T(8,128)(2,1)S(1)}, u32[]{:S(2)}, u32[]{:S(2)}) %collective-permute-start.26) | collective-permute-done | bytes 327712 | tf_op jit(solution)/shard_map/ppermute | solution.py:269
  166.0 3.0 %collective-permute-done.25 = bf16[256,640]{1,0:T(8,128)(2,1)S(1)} collective-permute-done((bf16[256,640]{1,0:T(8,128)(2,1)S(1)}, bf16[256,640]{1,0:T(8,128)(2,1)S(1)}, u32[]{:S(2)}, u32[]{:S(2)}) %collective-permute-start.25) | collective-permute-done | bytes 327712 | tf_op jit(solution)/shard_map/ppermute | solution.py:269
  169.5 2.7 %collective-permute-start.30 = (bf16[2,256,640]{2,1,0:T(8,128)(2,1)S(1)}, bf16[2,256,640]{2,1,0:T(8,128)(2,1)S(1)}, u32[]{:S(2)}, u32[]{:S(2)}) collective-permute-start(bf16[2,256,640]{2,1,0:T(8,128)(2,1)S(1)} %pad_maximum_fusion.low), channel_id=1, source_target_pairs={{0,12},{1,49},{2,14},{3,51},{4,0},{5,53},{6,2},{7,55},{8,4},{9,57}... | collective-permute-start | bytes 1966088 | tf_op jit(solution)/shard_map/ppermute | solution.py:269
  172.2 3.6 %collective-permute-done.31.high = bf16[2,256,640]{2,1,0:T(8,128)(2,1)S(1)} collective-permute-done((bf16[2,256,640]{2,1,0:T(8,128)(2,1)S(1)}, bf16[2,256,640]{2,1,0:T(8,128)(2,1)S(1)}, u32[]{:S(2)}, u32[]{:S(2)}) %collective-permute-start.31) | collective-permute-done | bytes 655392 | tf_op jit(solution)/shard_map/ppermute | solution.py:269
  175.7 2.2 collective-permute-start.33
  178.0 2.4 %collective-permute-done.28.low = bf16[2,256,640]{2,1,0:T(8,128)(2,1)S(1)} collective-permute-done((bf16[2,256,640]{2,1,0:T(8,128)(2,1)S(1)}, bf16[2,256,640]{2,1,0:T(8,128)(2,1)S(1)}, u32[]{:S(2)}, u32[]{:S(2)}) %collective-permute-start.28) | collective-permute-done | bytes 655392 | tf_op jit(solution)/shard_map/ppermute | solution.py:269
  180.4 1.5 cut_down.1.weights
  181.9 1.0 down_block.4
  182.9 4.5 %collective-permute-done.29.high = bf16[2,256,640]{2,1,0:T(8,128)(2,1)S(1)} collective-permute-done((bf16[2,256,640]{2,1,0:T(8,128)(2,1)S(1)}, bf16[2,256,640]{2,1,0:T(8,128)(2,1)S(1)}, u32[]{:S(2)}, u32[]{:S(2)}) %collective-permute-start.29) | collective-permute-done | bytes 655392 | tf_op jit(solution)/shard_map/ppermute | solution.py:269
  188.4 1.0 down_block.6
  189.8 4.6 %collective-permute-done.32.low = bf16[2,256,640]{2,1,0:T(8,128)(2,1)S(1)} collective-permute-done((bf16[2,256,640]{2,1,0:T(8,128)(2,1)S(1)}, bf16[2,256,640]{2,1,0:T(8,128)(2,1)S(1)}, u32[]{:S(2)}, u32[]{:S(2)}) %collective-permute-start.32) | collective-permute-done | bytes 655392 | tf_op jit(solution)/shard_map/ppermute | solution.py:269
  195.5 3.5 %collective-permute-start.34 = (bf16[4,4,32,448]{3,2,1,0:T(8,128)(2,1)S(1)}, bf16[4,4,32,448]{3,2,1,0:T(8,128)(2,1)S(1)}, u32[]{:S(2)}, u32[]{:S(2)}) collective-permute-start(bf16[4,4,32,448]{3,2,1,0:T(8,128)(2,1)S(1)} %pad_maximum_fusion.4), channel_id=1, source_target_pairs={{0,1},{1,0},{2,3},{3,2},{4,5},{5,4},{6,7},{7,6},{8,9},{9,8},{10,11... | collective-permute-start | bytes 1376264 | tf_op jit(solution)/shard_map/ppermute | solution.py:287
  199.1 1.5 collective-permute-done.34
  201.6 18.1 %all_to_all.5 = bf16[64,8,448]{2,1,0:T(8,128)(2,1)S(1)} all-to-all(bf16[64,8,448]{2,1,0:T(8,128)(2,1)S(1)} %bitcast.127), channel_id=1, replica_groups=mesh['role'=2,'grp'=16,'yh'=2,'core'=2] {'role','grp','yh'}, dimensions={0} | all-to-all | bytes 917504 | tf_op jit(solution)/shard_map/all_to_all | solution.py:428
  220.0 9.7 %all_gather.3 = bf16[32,7168]{1,0:T(8,128)(2,1)S(1)} all-gather(bf16[8,7168]{1,0:T(8,128)(2,1)S(1)} %reshape.86), channel_id=1, replica_groups=mesh['role'=2,'grp'=16,'yh'=2,'core'=2] {'yh','core'}, dimensions={0}, use_global_device_ids=true | all-gather | bytes 573440 | tf_op jit(solution)/shard_map/all_gather | solution.py:432
  (148 shorter events, 19.8 us)
Async XLA Ops:
  0.7 3.7 %copy-start.5 = (bf16[8,1024,576]{1,2,0:T(8,128)(2,1)S(1)}, bf16[8,1024,576]{1,2,0:T(8,128)(2,1)}, u32[]{:S(2)}) copy-start(bf16[8,1024,576]{1,2,0:T(8,128)(2,1)} %param.15) | copy-start | bytes 28311556
  4.4 1.1 copy-start.7
  6.8 11.0 %copy-start.22 = (bf16[16,512,128]{2,1,0:T(8,128)(2,1)S(1)}, bf16[16,512,128]{2,1,0:T(8,128)(2,1)}, u32[]{:S(2)}) copy-start(bf16[16,512,128]{2,1,0:T(8,128)(2,1)} %param.19) | copy-start | bytes 6291460
  14.0 9.7 %collective-permute-start = (bf16[2,8,16,512]{3,2,1,0:T(8,128)(2,1)S(1)}, bf16[2,8,16,512]{3,2,1,0:T(8,128)(2,1)}, u32[]{:S(2)}, u32[]{:S(2)}) collective-permute-start(bf16[2,8,16,512]{3,2,1,0:T(8,128)(2,1)S(1)} %get-tuple-element.16), channel_id=1, source_target_pairs={{0,2},{2,0},{1,3},{3,1},{4,6},{6,4},{5,7},{7,5},{8,10},{10,8},{9,1... | collective-permute-start | bytes 786440 | tf_op jit(solution)/shard_map/ppermute | solution.py:287
  17.8 7.5 %collective-permute-start.1 = (bf16[16,512,128]{2,1,0:T(8,128)(2,1)S(1)}, bf16[16,512,128]{2,1,0:T(8,128)(2,1)}, u32[]{:S(2)}, u32[]{:S(2)}) collective-permute-start(bf16[16,512,128]{2,1,0:T(8,128)(2,1)S(1)} %copy-done.22), channel_id=1, source_target_pairs={{0,1},{1,0},{2,3},{3,2},{4,5},{5,4},{6,7},{7,6},{8,9},{9,8},{10,11... | collective-permute-start | bytes 6291464 | tf_op jit(solution)/shard_map/ppermute | solution.py:287
  18.8 19.2 %collective-permute-start.5 = (bf16[2048,448]{0,1:T(8,128)(2,1)}, bf16[2048,448]{0,1:T(8,128)(2,1)}, u32[]{:S(2)}, u32[]{:S(2)}) collective-permute-start(bf16[2048,448]{0,1:T(8,128)(2,1)} %param.20), channel_id=1, source_target_pairs={{0,1},{1,0},{2,3},{3,2},{4,5},{5,4},{6,7},{7,6},{8,9},{9,8},{10,11... | collective-permute-start | bytes 5505032 | tf_op jit(solution)/shard_map/ppermute | solution.py:287
  27.4 6.5 %collective-permute-start.2 = (bf16[16,4096]{1,0:T(8,128)(2,1)S(1)}, bf16[16,4096]{1,0:T(8,128)(2,1)S(1)}, u32[]{:S(2)}, u32[]{:S(2)}) collective-permute-start(bf16[16,4096]{1,0:T(8,128)(2,1)S(1)} %bitcast_dynamic-update-slice_fusion), channel_id=1, source_target_pairs={{0,16},{1,5},{2,18},{3,7},{4,20},{5,9},{6,22},{7,11},{8,24},{9,13}... | collective-permute-start | bytes 393224 | tf_op jit(solution)/shard_map/ppermute | solution.py:269
  29.1 4.8 %collective-permute-start.3 = (bf16[16,4096]{1,0:T(8,128)(2,1)S(1)}, bf16[16,4096]{1,0:T(8,128)(2,1)S(1)}, u32[]{:S(2)}, u32[]{:S(2)}) collective-permute-start(bf16[16,4096]{1,0:T(8,128)(2,1)S(1)} %bitcast_dynamic-update-slice_fusion), channel_id=1, source_target_pairs={{0,48},{1,13},{2,50},{3,15},{4,52},{5,1},{6,54},{7,3},{8,56},{9,5}... | collective-permute-start | bytes 393224 | tf_op jit(solution)/shard_map/ppermute | solution.py:269
  31.3 5.6 %collective-permute-start.4 = (bf16[16,4096]{1,0:T(8,128)(2,1)S(1)}, bf16[16,4096]{1,0:T(8,128)(2,1)S(1)}, u32[]{:S(2)}, u32[]{:S(2)}) collective-permute-start(bf16[16,4096]{1,0:T(8,128)(2,1)S(1)} %bitcast_dynamic-update-slice_fusion), channel_id=1, source_target_pairs={{0,32},{1,9},{2,34},{3,11},{4,36},{5,13},{6,38},{7,15},{8,40},{9,1... | collective-permute-start | bytes 393224 | tf_op jit(solution)/shard_map/ppermute | solution.py:269
  32.6 30.0 %copy-start.26 = (bf16[4,1,2,8,448]{4,3,2,1,0:T(8,128)(2,1)}, bf16[4,1,2,8,448]{4,3,2,1,0:T(8,128)(2,1)S(1)}, u32[]{:S(2)}) copy-start(bf16[4,1,2,8,448]{4,3,2,1,0:T(8,128)(2,1)S(1)} %get-tuple-element.34) | copy-start | bytes 172036
  37.0 9.6 %collective-permute-start.6 = (bf16[64,4096]{1,0:T(8,128)(2,1)S(1)}, bf16[64,4096]{1,0:T(8,128)(2,1)S(1)}, u32[]{:S(2)}, u32[]{:S(2)}) collective-permute-start(bf16[64,4096]{1,0:T(8,128)(2,1)S(1)} %pad_maximum_fusion.2), channel_id=1, source_target_pairs={{0,4},{1,17},{2,6},{3,19},{4,8},{5,21},{6,10},{7,23},{8,12},{9,25}... | collective-permute-start | bytes 1572872 | tf_op jit(solution)/shard_map/ppermute | solution.py:269
  39.6 13.6 %collective-permute-start.7 = (bf16[64,4096]{1,0:T(8,128)(2,1)S(1)}, bf16[64,4096]{1,0:T(8,128)(2,1)S(1)}, u32[]{:S(2)}, u32[]{:S(2)}) collective-permute-start(bf16[64,4096]{1,0:T(8,128)(2,1)S(1)} %pad_maximum_fusion.2), channel_id=1, source_target_pairs={{0,12},{1,49},{2,14},{3,51},{4,0},{5,53},{6,2},{7,55},{8,4},{9,57}... | collective-permute-start | bytes 1572872 | tf_op jit(solution)/shard_map/ppermute | solution.py:269
  41.4 12.9 %collective-permute-start.8 = (bf16[64,4096]{1,0:T(8,128)(2,1)S(1)}, bf16[64,4096]{1,0:T(8,128)(2,1)S(1)}, u32[]{:S(2)}, u32[]{:S(2)}) collective-permute-start(bf16[64,4096]{1,0:T(8,128)(2,1)S(1)} %pad_maximum_fusion.2), channel_id=1, source_target_pairs={{0,8},{1,33},{2,10},{3,35},{4,12},{5,37},{6,14},{7,39},{8,0},{9,41... | collective-permute-start | bytes 1572872 | tf_op jit(solution)/shard_map/ppermute | solution.py:269
  43.8 18.7 %copy-start.23 = (f32[64,448]{1,0:T(8,128)}, f32[64,448]{1,0:T(8,128)S(1)}, u32[]{:S(2)}) copy-start(f32[64,448]{1,0:T(8,128)S(1)} %fusion.22) | copy-start | bytes 344068
  47.8 14.8 %copy-start.10 = (f32[64,448]{1,0:T(8,128)}, f32[64,448]{1,0:T(8,128)S(1)}, u32[]{:S(2)}) copy-start(f32[64,448]{1,0:T(8,128)S(1)} %fusion.26) | copy-start | bytes 344068
  54.3 8.2 %copy-start.13 = (f32[64,448]{1,0:T(8,128)}, f32[64,448]{1,0:T(8,128)S(1)}, u32[]{:S(2)}) copy-start(f32[64,448]{1,0:T(8,128)S(1)} %fusion.27) | copy-start | bytes 344068
  55.5 13.4 %copy-start.16 = (f32[64,448]{1,0:T(8,128)}, f32[64,448]{1,0:T(8,128)S(1)}, u32[]{:S(2)}) copy-start(f32[64,448]{1,0:T(8,128)S(1)} %fusion.28) | copy-start | bytes 344068
  55.6 18.0 %copy-start.30 = (bf16[448]{0:T(512)(128)(2,1)S(1)}, bf16[448]{0:T(512)(128)(2,1)}, u32[]{:S(2)}) copy-start(bf16[448]{0:T(512)(128)(2,1)} %param.21) | copy-start | bytes 2692
  55.6 18.1 %copy-start = (bf16[448,2304]{1,0:T(8,128)(2,1)S(1)}, bf16[448,2304]{1,0:T(8,128)(2,1)}, u32[]{:S(2)}) copy-start(bf16[448,2304]{1,0:T(8,128)(2,1)} %gate_tail.7) | copy-start | bytes 6193156
  55.7 6.8 %collective-permute-start.9 = (bf16[4,4,2,8,448]{4,3,2,0,1:T(8,128)(2,1)S(1)}, bf16[4,4,2,8,448]{4,3,2,0,1:T(8,128)(2,1)S(1)}, u32[]{:S(2)}, u32[]{:S(2)}) collective-permute-start(bf16[4,4,2,8,448]{4,3,2,0,1:T(8,128)(2,1)S(1)} %copy.133), channel_id=1, source_target_pairs={{0,2},{1,3},{2,0},{3,1},{64,66},{65,67},{66,64},{67,65},{4,6},{5,7... | collective-permute-start | bytes 688136 | tf_op jit(solution)/shard_map/ppermute | solution.py:283
  58.7 8.3 %collective-permute-start.10 = (bf16[4,4,2,8,448]{4,3,2,0,1:T(8,128)(2,1)S(1)}, bf16[4,4,2,8,448]{4,3,2,0,1:T(8,128)(2,1)S(1)}, u32[]{:S(2)}, u32[]{:S(2)}) collective-permute-start(bf16[4,4,2,8,448]{4,3,2,0,1:T(8,128)(2,1)S(1)} %copy.133), channel_id=1, source_target_pairs={{0,64},{1,65},{2,66},{3,67},{64,2},{65,3},{66,0},{67,1},{4,68},{5,... | collective-permute-start | bytes 688136 | tf_op jit(solution)/shard_map/ppermute | solution.py:283
  59.1 8.2 %collective-permute-start.11 = (bf16[4,4,2,8,448]{4,3,2,0,1:T(8,128)(2,1)S(1)}, bf16[4,4,2,8,448]{4,3,2,0,1:T(8,128)(2,1)S(1)}, u32[]{:S(2)}, u32[]{:S(2)}) collective-permute-start(bf16[4,4,2,8,448]{4,3,2,0,1:T(8,128)(2,1)S(1)} %copy.133), channel_id=1, source_target_pairs={{0,66},{1,67},{2,64},{3,65},{64,0},{65,1},{66,2},{67,3},{4,70},{5,... | collective-permute-start | bytes 688136 | tf_op jit(solution)/shard_map/ppermute | solution.py:283
  62.5 11.2 %copy-start.19 = (bf16[4,4,2,8,448]{4,3,2,0,1:T(8,128)(2,1)}, bf16[4,4,2,8,448]{4,3,2,0,1:T(8,128)(2,1)S(1)}, u32[]{:S(2)}) copy-start(bf16[4,4,2,8,448]{4,3,2,0,1:T(8,128)(2,1)S(1)} %collective-permute-done.9) | copy-start | bytes 688132
  68.9 16.4 %collective-permute-start.12 = (bf16[2,4,4,2,8,448]{5,4,3,2,1,0:T(8,128)(2,1)}, bf16[2,4,4,2,8,448]{5,4,3,2,1,0:T(8,128)(2,1)}, u32[]{:S(2)}, u32[]{:S(2)}) collective-permute-start(bf16[2,4,4,2,8,448]{5,4,3,2,1,0:T(8,128)(2,1)} %pad_maximum_fusion.3), channel_id=1, source_target_pairs={{0,1},{1,0},{2,3},{3,2},{4,5},{5,4},{6,7},{7,6},{8,9},{9,8},{10,11... | collective-permute-start | bytes 1376264 | tf_op jit(solution)/shard_map/ppermute | solution.py:287
  73.8 1.6 copy-start.1
  76.8 15.2 %collective-permute-start.16 = (bf16[448,1152]{1,0:T(8,128)(2,1)}, bf16[448,1152]{1,0:T(8,128)(2,1)S(1)}, u32[]{:S(2)}, u32[]{:S(2)}) collective-permute-start(bf16[448,1152]{1,0:T(8,128)(2,1)} %cut_in.5), channel_id=1, source_target_pairs={{0,16},{1,5},{2,18},{3,7},{4,20},{5,9},{6,22},{7,11},{8,24},{9,13}... | collective-permute-start | bytes 3096584 | tf_op jit(solution)/shard_map/ppermute | solution.py:269
  77.2 1.6 copy-start.2
  80.2 25.2 %collective-permute-start.17 = (bf16[448,1152]{1,0:T(8,128)(2,1)}, bf16[448,1152]{1,0:T(8,128)(2,1)}, u32[]{:S(2)}, u32[]{:S(2)}) collective-permute-start(bf16[448,1152]{1,0:T(8,128)(2,1)} %cut_in.6), channel_id=1, source_target_pairs={{0,48},{1,13},{2,50},{3,15},{4,52},{5,1},{6,54},{7,3},{8,56},{9,5}... | collective-permute-start | bytes 3096584 | tf_op jit(solution)/shard_map/ppermute | solution.py:269
  82.4 1.6 copy-start.3
  84.0 1.1 copy-start.14
  84.0 1.1 copy-start.17
  84.0 1.1 copy-start.20
  84.0 1.2 copy-start.24
  84.0 1.2 copy-start.27
  84.0 1.3 copy-start.29
  84.5 20.9 %collective-permute-start.18 = (bf16[448,1152]{1,0:T(8,128)(2,1)S(1)}, bf16[448,1152]{1,0:T(8,128)(2,1)S(1)}, u32[]{:S(2)}, u32[]{:S(2)}) collective-permute-start(bf16[448,1152]{1,0:T(8,128)(2,1)S(1)} %cut_in.7), channel_id=1, source_target_pairs={{0,32},{1,9},{2,34},{3,11},{4,36},{5,13},{6,38},{7,15},{8,40},{9,1... | collective-permute-start | bytes 3096584 | tf_op jit(solution)/shard_map/ppermute | solution.py:269
  86.6 23.4 %copy-start.4 = (bf16[448,2304]{1,0:T(8,128)(2,1)S(1)}, bf16[448,2304]{1,0:T(8,128)(2,1)}, u32[]{:S(2)}) copy-start(bf16[448,2304]{1,0:T(8,128)(2,1)} %up_tail.7) | copy-start | bytes 6193156
  86.7 22.0 %collective-permute-start.19 = (bf16[2,4,64,448]{3,2,1,0:T(8,128)(2,1)S(1)}, bf16[2,4,64,448]{3,2,1,0:T(8,128)(2,1)S(1)}, u32[]{:S(2)}, u32[]{:S(2)}) collective-permute-start(bf16[2,4,64,448]{3,2,1,0:T(8,128)(2,1)S(1)} %bitcast.93), channel_id=1, source_target_pairs={{0,16},{1,5},{2,18},{3,7},{4,20},{5,9},{6,22},{7,11},{8,24},{9,13}... | collective-permute-start | bytes 1376264 | tf_op jit(solution)/shard_map/ppermute | solution.py:269
  87.6 28.9 %collective-permute-start.20 = (bf16[2,4,64,448]{3,2,1,0:T(8,128)(2,1)S(1)}, bf16[2,4,64,448]{3,2,1,0:T(8,128)(2,1)S(1)}, u32[]{:S(2)}, u32[]{:S(2)}) collective-permute-start(bf16[2,4,64,448]{3,2,1,0:T(8,128)(2,1)S(1)} %bitcast.94), channel_id=1, source_target_pairs={{0,48},{1,13},{2,50},{3,15},{4,52},{5,1},{6,54},{7,3},{8,56},{9,5}... | collective-permute-start | bytes 1376264 | tf_op jit(solution)/shard_map/ppermute | solution.py:269
  92.0 24.5 %collective-permute-start.21 = (bf16[2,4,64,448]{3,2,1,0:T(8,128)(2,1)S(1)}, bf16[2,4,64,448]{3,2,1,0:T(8,128)(2,1)S(1)}, u32[]{:S(2)}, u32[]{:S(2)}) collective-permute-start(bf16[2,4,64,448]{3,2,1,0:T(8,128)(2,1)S(1)} %bitcast.95), channel_id=1, source_target_pairs={{0,32},{1,9},{2,34},{3,11},{4,36},{5,13},{6,38},{7,15},{8,40},{9,1... | collective-permute-start | bytes 1376264 | tf_op jit(solution)/shard_map/ppermute | solution.py:269
  105.4 15.0 %collective-permute-start.13 = (bf16[2,4,64,448]{3,2,1,0:T(8,128)(2,1)S(1)}, bf16[2,4,64,448]{3,2,1,0:T(8,128)(2,1)S(1)}, u32[]{:S(2)}, u32[]{:S(2)}) collective-permute-start(bf16[2,4,64,448]{3,2,1,0:T(8,128)(2,1)S(1)} %bitcast.98), channel_id=1, source_target_pairs={{0,16},{1,5},{2,18},{3,7},{4,20},{5,9},{6,22},{7,11},{8,24},{9,13}... | collective-permute-start | bytes 1376264 | tf_op jit(solution)/shard_map/ppermute | solution.py:269
  105.4 29.3 %collective-permute-start.14 = (bf16[2,4,64,448]{3,2,1,0:T(8,128)(2,1)S(1)}, bf16[2,4,64,448]{3,2,1,0:T(8,128)(2,1)S(1)}, u32[]{:S(2)}, u32[]{:S(2)}) collective-permute-start(bf16[2,4,64,448]{3,2,1,0:T(8,128)(2,1)S(1)} %bitcast.99), channel_id=1, source_target_pairs={{0,48},{1,13},{2,50},{3,15},{4,52},{5,1},{6,54},{7,3},{8,56},{9,5}... | collective-permute-start | bytes 1376264 | tf_op jit(solution)/shard_map/ppermute | solution.py:269
  108.7 26.1 %collective-permute-start.15 = (bf16[2,4,64,448]{3,2,1,0:T(8,128)(2,1)S(1)}, bf16[2,4,64,448]{3,2,1,0:T(8,128)(2,1)S(1)}, u32[]{:S(2)}, u32[]{:S(2)}) collective-permute-start(bf16[2,4,64,448]{3,2,1,0:T(8,128)(2,1)S(1)} %bitcast.100), channel_id=1, source_target_pairs={{0,32},{1,9},{2,34},{3,11},{4,36},{5,13},{6,38},{7,15},{8,40},{9,1... | collective-permute-start | bytes 1376264 | tf_op jit(solution)/shard_map/ppermute | solution.py:269
  119.2 27.3 %collective-permute-start.24 = (bf16[256,1280]{1,0:T(8,128)(2,1)S(1)}, bf16[256,1280]{1,0:T(8,128)(2,1)S(1)}, u32[]{:S(2)}, u32[]{:S(2)}) collective-permute-start(bf16[256,1280]{1,0:T(8,128)(2,1)S(1)} %partial_sums.7), channel_id=1, source_target_pairs={{0,8},{1,33},{2,10},{3,35},{4,12},{5,37},{6,14},{7,39},{8,0},{9,41... | collective-permute-start | bytes 1966088 | tf_op jit(solution)/shard_map/ppermute | solution.py:269
  137.5 11.0 %collective-permute-start.23 = (bf16[256,1280]{1,0:T(8,128)(2,1)S(1)}, bf16[256,1280]{1,0:T(8,128)(2,1)S(1)}, u32[]{:S(2)}, u32[]{:S(2)}) collective-permute-start(bf16[256,1280]{1,0:T(8,128)(2,1)S(1)} %partial_sums.6), channel_id=1, source_target_pairs={{0,12},{1,49},{2,14},{3,51},{4,0},{5,53},{6,2},{7,55},{8,4},{9,57}... | collective-permute-start | bytes 1966088 | tf_op jit(solution)/shard_map/ppermute | solution.py:269
  143.7 11.0 %collective-permute-start.22 = (bf16[256,1280]{1,0:T(8,128)(2,1)S(1)}, bf16[256,1280]{1,0:T(8,128)(2,1)S(1)}, u32[]{:S(2)}, u32[]{:S(2)}) collective-permute-start(bf16[256,1280]{1,0:T(8,128)(2,1)S(1)} %partial_sums.5), channel_id=1, source_target_pairs={{0,4},{1,17},{2,6},{3,19},{4,8},{5,21},{6,10},{7,23},{8,12},{9,25}... | collective-permute-start | bytes 1966088 | tf_op jit(solution)/shard_map/ppermute | solution.py:269
  146.5 33.8 %copy-start.31 = (s32[4]{0:T(128)S(1)}, s32[4]{0:T(128)}, u32[]{:S(2)}) copy-start(s32[4]{0:T(128)} %constant.95) | copy-start | bytes 52
  146.6 33.8 %copy-start.6 = (bf16[2304,448]{0,1:T(8,128)(2,1)S(1)}, bf16[2304,448]{0,1:T(8,128)(2,1)}, u32[]{:S(2)}) copy-start(bf16[2304,448]{0,1:T(8,128)(2,1)} %param.24) | copy-start | bytes 6193156
  155.2 10.4 %collective-permute-start.26 = (bf16[256,640]{1,0:T(8,128)(2,1)S(1)}, bf16[256,640]{1,0:T(8,128)(2,1)S(1)}, u32[]{:S(2)}, u32[]{:S(2)}) collective-permute-start(bf16[256,640]{1,0:T(8,128)(2,1)S(1)} %activate.1), channel_id=1, source_target_pairs={{0,48},{1,13},{2,50},{3,15},{4,52},{5,1},{6,54},{7,3},{8,56},{9,5}... | collective-permute-start | bytes 983048 | tf_op jit(solution)/shard_map/ppermute | solution.py:269
  158.1 7.8 %collective-permute-start.27 = (bf16[256,640]{1,0:T(8,128)(2,1)S(1)}, bf16[256,640]{1,0:T(8,128)(2,1)S(1)}, u32[]{:S(2)}, u32[]{:S(2)}) collective-permute-start(bf16[256,640]{1,0:T(8,128)(2,1)S(1)} %activate.1), channel_id=1, source_target_pairs={{0,32},{1,9},{2,34},{3,11},{4,36},{5,13},{6,38},{7,15},{8,40},{9,1... | collective-permute-start | bytes 983048 | tf_op jit(solution)/shard_map/ppermute | solution.py:269
  158.1 10.9 %collective-permute-start.25 = (bf16[256,640]{1,0:T(8,128)(2,1)S(1)}, bf16[256,640]{1,0:T(8,128)(2,1)S(1)}, u32[]{:S(2)}, u32[]{:S(2)}) collective-permute-start(bf16[256,640]{1,0:T(8,128)(2,1)S(1)} %activate.1), channel_id=1, source_target_pairs={{0,16},{1,5},{2,18},{3,7},{4,20},{5,9},{6,22},{7,11},{8,24},{9,13}... | collective-permute-start | bytes 983048 | tf_op jit(solution)/shard_map/ppermute | solution.py:269
  165.9 9.8 %collective-permute-start.31 = (bf16[2,256,640]{2,1,0:T(8,128)(2,1)S(1)}, bf16[2,256,640]{2,1,0:T(8,128)(2,1)S(1)}, u32[]{:S(2)}, u32[]{:S(2)}) collective-permute-start(bf16[2,256,640]{2,1,0:T(8,128)(2,1)S(1)} %pad_maximum_fusion.1.high), channel_id=1, source_target_pairs={{0,12},{1,49},{2,14},{3,51},{4,0},{5,53},{6,2},{7,55},{8,4},{9,57}... | collective-permute-start | bytes 1966088 | tf_op jit(solution)/shard_map/ppermute | solution.py:269
  169.1 11.2 %collective-permute-start.28 = (bf16[2,256,640]{2,1,0:T(8,128)(2,1)S(1)}, bf16[2,256,640]{2,1,0:T(8,128)(2,1)S(1)}, u32[]{:S(2)}, u32[]{:S(2)}) collective-permute-start(bf16[2,256,640]{2,1,0:T(8,128)(2,1)S(1)} %pad_maximum_fusion.low), channel_id=1, source_target_pairs={{0,4},{1,17},{2,6},{3,19},{4,8},{5,21},{6,10},{7,23},{8,12},{9,25}... | collective-permute-start | bytes 1966088 | tf_op jit(solution)/shard_map/ppermute | solution.py:269
  169.4 17.9 %collective-permute-start.29 = (bf16[2,256,640]{2,1,0:T(8,128)(2,1)S(1)}, bf16[2,256,640]{2,1,0:T(8,128)(2,1)S(1)}, u32[]{:S(2)}, u32[]{:S(2)}) collective-permute-start(bf16[2,256,640]{2,1,0:T(8,128)(2,1)S(1)} %pad_maximum_fusion.1.high), channel_id=1, source_target_pairs={{0,4},{1,17},{2,6},{3,19},{4,8},{5,21},{6,10},{7,23},{8,12},{9,25}... | collective-permute-start | bytes 1966088 | tf_op jit(solution)/shard_map/ppermute | solution.py:269
  169.5 18.9 %collective-permute-start.30 = (bf16[2,256,640]{2,1,0:T(8,128)(2,1)S(1)}, bf16[2,256,640]{2,1,0:T(8,128)(2,1)S(1)}, u32[]{:S(2)}, u32[]{:S(2)}) collective-permute-start(bf16[2,256,640]{2,1,0:T(8,128)(2,1)S(1)} %pad_maximum_fusion.low), channel_id=1, source_target_pairs={{0,12},{1,49},{2,14},{3,51},{4,0},{5,53},{6,2},{7,55},{8,4},{9,57}... | collective-permute-start | bytes 1966088 | tf_op jit(solution)/shard_map/ppermute | solution.py:269
  175.7 14.0 %collective-permute-start.33 = (bf16[2,256,640]{2,1,0:T(8,128)(2,1)S(1)}, bf16[2,256,640]{2,1,0:T(8,128)(2,1)S(1)}, u32[]{:S(2)}, u32[]{:S(2)}) collective-permute-start(bf16[2,256,640]{2,1,0:T(8,128)(2,1)S(1)} %collective-permute-done.31.high), channel_id=1, source_target_pairs={{0,12},{1,49},{2,14},{3,51},{4,0},{5,53},{6,2},{7,55},{8,4},{9,57}... | collective-permute-start | bytes 1966088 | tf_op jit(solution)/shard_map/ppermute | solution.py:269
  180.4 14.0 %collective-permute-start.32 = (bf16[2,256,640]{2,1,0:T(8,128)(2,1)S(1)}, bf16[2,256,640]{2,1,0:T(8,128)(2,1)S(1)}, u32[]{:S(2)}, u32[]{:S(2)}) collective-permute-start(bf16[2,256,640]{2,1,0:T(8,128)(2,1)S(1)} %collective-permute-done.28.low), channel_id=1, source_target_pairs={{0,4},{1,17},{2,6},{3,19},{4,8},{5,21},{6,10},{7,23},{8,12},{9,25}... | collective-permute-start | bytes 1966088 | tf_op jit(solution)/shard_map/ppermute | solution.py:269
  195.4 5.4 %copy-start.12 = (f32[64,448]{1,0:T(8,128)S(1)}, f32[64,448]{1,0:T(8,128)}, u32[]{:S(2)}) copy-start(f32[64,448]{1,0:T(8,128)} %copy-done.10) | copy-start | bytes 344068
  195.4 5.4 %copy-start.15 = (f32[64,448]{1,0:T(8,128)S(1)}, f32[64,448]{1,0:T(8,128)}, u32[]{:S(2)}) copy-start(f32[64,448]{1,0:T(8,128)} %copy-done.13) | copy-start | bytes 344068
  195.4 5.4 %copy-start.18 = (f32[64,448]{1,0:T(8,128)S(1)}, f32[64,448]{1,0:T(8,128)}, u32[]{:S(2)}) copy-start(f32[64,448]{1,0:T(8,128)} %copy-done.16) | copy-start | bytes 344068
  195.4 5.4 %copy-start.21 = (bf16[4,4,2,8,448]{4,3,2,0,1:T(8,128)(2,1)S(1)}, bf16[4,4,2,8,448]{4,3,2,0,1:T(8,128)(2,1)}, u32[]{:S(2)}) copy-start(bf16[4,4,2,8,448]{4,3,2,0,1:T(8,128)(2,1)} %copy-done.19) | copy-start | bytes 688132
  195.4 5.4 %copy-start.25 = (f32[64,448]{1,0:T(8,128)S(1)}, f32[64,448]{1,0:T(8,128)}, u32[]{:S(2)}) copy-start(f32[64,448]{1,0:T(8,128)} %copy-done.23) | copy-start | bytes 344068
  195.4 5.4 %copy-start.28 = (bf16[4,1,2,8,448]{4,3,2,1,0:T(8,128)(2,1)S(1)}, bf16[4,1,2,8,448]{4,3,2,1,0:T(8,128)(2,1)}, u32[]{:S(2)}) copy-start(bf16[4,1,2,8,448]{4,3,2,1,0:T(8,128)(2,1)} %copy-done.26) | copy-start | bytes 172036
  195.5 5.1 %collective-permute-start.34 = (bf16[4,4,32,448]{3,2,1,0:T(8,128)(2,1)S(1)}, bf16[4,4,32,448]{3,2,1,0:T(8,128)(2,1)S(1)}, u32[]{:S(2)}, u32[]{:S(2)}) collective-permute-start(bf16[4,4,32,448]{3,2,1,0:T(8,128)(2,1)S(1)} %pad_maximum_fusion.4), channel_id=1, source_target_pairs={{0,1},{1,0},{2,3},{3,2},{4,5},{5,4},{6,7},{7,6},{8,9},{9,8},{10,11... | collective-permute-start | bytes 1376264 | tf_op jit(solution)/shard_map/ppermute | solution.py:287
  (3 other events, 2.4 us)

commit v4 on v3

--- a/solution.py
+++ b/solution.py
@@ -350,12 +350,6 @@
     in_weights = [cut_in(place_1, w_gate, w_up, gain)] + in_weights
     down_weights = cut_down((place_1 - steps) % 4, w_down)
 
-    residual = lax.dynamic_index_in_dim(
-        hidden_in.reshape(4, 4, 2, 2, tokens, width), core, 3, keepdims=False
-    )
-    residual = jnp.where(core == 0, jnp.swapaxes(residual, 0, 1), residual)
-    residual = wide(relative(relative(residual, place_2, 0), place_1, 1))
-
     near, far = attend(
         q_latent,
         kv_new,
@@ -366,7 +360,17 @@
         score_scale,
         latent,
     )
+    far, in_weights[1], in_weights[2] = lax.optimization_barrier(
+        (far, in_weights[1], in_weights[2])
+    )
     far = swap(far, "yh")
+    far, hidden_in = lax.optimization_barrier((far, hidden_in))
+    residual = lax.dynamic_index_in_dim(
+        hidden_in.reshape(4, 4, 2, 2, tokens, width), core, 3, keepdims=False
+    )
+    residual = jnp.where(core == 0, jnp.swapaxes(residual, 0, 1), residual)
+    residual = wide(relative(relative(residual, place_2, 0), place_1, 1))
+
     context = jnp.stack([jnp.where(yh == 0, near, far), jnp.where(yh == 0, far, near)], axis=1)
     context = context.reshape(2, 2 * tokens, heads // 4, latent)
     values = jnp.concatenate(
@@ -379,6 +383,7 @@
         axis=1,
     )
     values = jnp.concatenate(gather(values, shift_1))
+    values, in_weights[3] = lax.optimization_barrier((values, in_weights[3]))
     attn_part = jnp.stack(
         [
             jnp.dot(v, o_chip, preferred_element_type=jnp.float32)

time: 231 us -> 233 us (level)
  waiting for transfers between devices: 91.7 us -> 80.9 us
  starting transfers between devices: 51.8 us -> 57.9 us
  local copies, waits for them, and re-layouts: 17.8 us -> 21.1 us
    ppermute x27, waiting for transfers between devices: 82.8 us -> 65.8 us  [shift(): return lax.ppermute(value, ('grp', 'yh', 'core'), pairs)]
    ppermute x5, starting transfers between devices: 13 us -> 19.1 us  [swap(): return lax.ppermute(value, axis, [(0, 1), (1, 0)])]
    ppermute x3, waiting for transfers between devices: 5.73 us -> 8.81 us  [shift_y(): lax.ppermute(value, ('role', 'yh', 'core'), [(p, moved(p)) for p in range...]
    ppermute x5, waiting for transfers between devices: 3.2 us -> 6.26 us  [swap(): return lax.ppermute(value, axis, [(0, 1), (1, 0)])]
    unnamed x72 -> x63, local copies, waits for them, and re-layouts: 14.7 us -> 15.7 us
  transfers between devices with their start and end apart: 35 -> 35, of which waited for: 25 -> 28; matrix products, arithmetic and copies ran while one was open for 6% -> 7% of each run, Pallas kernels for 8% -> 12%
where the time goes in v4:
time: 233 us; the launch traced here: 232 us
  waiting for transfers between devices  80.9 us (35%)
  starting transfers between devices  57.9 us (25%)
  Pallas kernels  30 us (13%)
  blocking collectives  28.9 us (12%)
  local copies, waits for them, and re-layouts  21.1 us (9%)
  matrix products  8.97 us (4%)
  other arithmetic  3.76 us (2%)
    ppermute x27, waiting for transfers between devices, shift(): return lax.ppermute(value, ('grp', 'yh', 'core'), pairs)  65.8 us
    ppermute x27, starting transfers between devices, shift(): return lax.ppermute(value, ('grp', 'yh', 'core'), pairs)  34.2 us
    all_to_all x1, blocking collectives, body(): lax.all_to_all(down, ('role', 'grp', 'yh'), split_axis=0, concat_axis=0)  19.2 us
    ppermute x5, starting transfers between devices, swap(): return lax.ppermute(value, axis, [(0, 1), (1, 0)])  19.1 us
    pallas_call x9, Pallas kernels, whole_call(): pl.pallas_call(kernel, out_shape=out_shapes, in_specs=[pl.BlockSpec(memor...  16.6 us
    unnamed x63, local copies, waits for them, and re-layouts  15.7 us
    all_gather x1, blocking collectives, body(): return lax.all_gather(result, ('yh', 'core'), axis=0, tiled=True)  9.69 us
    ppermute x3, waiting for transfers between devices, shift_y(): lax.ppermute(value, ('role', 'yh', 'core'), [(p, moved(p)) for p in range...  8.81 us
  transfers between devices with their start and end apart: 35, of which 28 were waited for; matrix products, arithmetic and copies ran while one was open for 7% of the time, Pallas kernels for 12%

profile of v4, /device:TPU:1, one launch (start us, length us, event | category | flops | bytes accessed | tf_op | source)
XLA Modules:
  0.0 232.3 jit_solution(4121569128744875688)
XLA Ops:
  0.8 1.6 copy-done
  2.4 1.6 copy-done.2
  4.0 1.4 cut_in.4
  5.4 2.5 %collective-permute-start = (bf16[448,1152]{1,0:T(8,128)(2,1)}, bf16[448,1152]{1,0:T(8,128)(2,1)S(1)}, u32[]{:S(2)}, u32[]{:S(2)}) collective-permute-start(bf16[448,1152]{1,0:T(8,128)(2,1)} %cut_in.4), channel_id=1, source_target_pairs={{0,16},{1,5},{2,18},{3,7},{4,20},{5,9},{6,22},{7,11},{8,24},{9,13}... | collective-permute-start | bytes 3096584 | tf_op jit(solution)/shard_map/ppermute | solution.py:269
  7.9 1.6 copy-done.3
  9.5 1.4 cut_in.5
  10.9 2.6 %collective-permute-start.1 = (bf16[448,1152]{1,0:T(8,128)(2,1)}, bf16[448,1152]{1,0:T(8,128)(2,1)}, u32[]{:S(2)}, u32[]{:S(2)}) collective-permute-start(bf16[448,1152]{1,0:T(8,128)(2,1)} %cut_in.5), channel_id=1, source_target_pairs={{0,48},{1,13},{2,50},{3,15},{4,52},{5,1},{6,54},{7,3},{8,56},{9,5}... | collective-permute-start | bytes 3096584 | tf_op jit(solution)/shard_map/ppermute | solution.py:269
  13.5 1.6 copy-done.4
  15.1 1.4 cut_in.6
  16.5 3.3 %collective-permute-start.7 = (bf16[448,1152]{1,0:T(8,128)(2,1)}, bf16[448,1152]{1,0:T(8,128)(2,1)}, u32[]{:S(2)}, u32[]{:S(2)}) collective-permute-start(bf16[448,1152]{1,0:T(8,128)(2,1)} %cut_in.6), channel_id=1, source_target_pairs={{0,32},{1,9},{2,34},{3,11},{4,36},{5,13},{6,38},{7,15},{8,40},{9,1... | collective-permute-start | bytes 3096584 | tf_op jit(solution)/shard_map/ppermute | solution.py:269
  20.1 3.7 %copy-done.6 = bf16[8,1024,576]{1,2,0:T(8,128)(2,1)S(1)} copy-done((bf16[8,1024,576]{1,2,0:T(8,128)(2,1)S(1)}, bf16[8,1024,576]{1,2,0:T(8,128)(2,1)}, u32[]{:S(2)}) %copy-start.6) | copy-done | bytes 9437208
  24.8 7.2 %attend.1 = (bf16[2,8,16,512]{3,2,1,0:T(8,128)(2,1)S(1)}, bf16[2,8,16,512]{3,2,1,0:T(8,128)(2,1)S(1)}) custom-call(s32[8]{0:T(128)S(1)} %copy-done.11, s32[8]{0:T(128)S(1)} %copy-done.12, s32[1]{0:T(128)} %bitcast.place_ref, bf16[8,4,16,576]{3,2,1,0:T(8,128)(2,1)S(1)} %bitcast.105, f32[8,1,576]{2,1,0:T(1,128)S(1)} %reshape.87.new_ref, ...), custom_call_target="tpu_custom_call" | custom-call | flops 1140850688 | bytes 9437184 | tf_op jit(solution)/shard_map/attend/pallas_call | solution.py:60
  32.8 3.7 %collective-permute-done.1.refs_6_ = bf16[448,1152]{1,0:T(8,128)(2,1)} collective-permute-done((bf16[448,1152]{1,0:T(8,128)(2,1)}, bf16[448,1152]{1,0:T(8,128)(2,1)}, u32[]{:S(2)}, u32[]{:S(2)}) %collective-permute-start.1) | collective-permute-done | bytes 1032224 | tf_op jit(solution)/shard_map/ppermute | solution.py:269
  36.5 2.9 %collective-permute-start.2 = (bf16[2,8,16,512]{3,2,1,0:T(8,128)(2,1)S(1)}, bf16[2,8,16,512]{3,2,1,0:T(8,128)(2,1)}, u32[]{:S(2)}, u32[]{:S(2)}) collective-permute-start(bf16[2,8,16,512]{3,2,1,0:T(8,128)(2,1)S(1)} %get-tuple-element.23), channel_id=1, source_target_pairs={{0,2},{2,0},{1,3},{3,1},{4,6},{6,4},{5,7},{7,5},{8,10},{10,8},{9,1... | collective-permute-start | bytes 786440 | tf_op jit(solution)/shard_map/ppermute | solution.py:287
  39.4 3.0 %constant_dynamic-update-slice_fusion.1 = bf16[4096,448]{0,1:T(8,128)(2,1)} fusion(bf16[2048,448]{0,1:T(8,128)(2,1)} %param.20), kind=kLoop, calls=%fused_computation.66 | loop fusion | bytes 3670016
  42.4 3.3 %collective-permute-done.2 = bf16[2,8,16,512]{3,2,1,0:T(8,128)(2,1)} collective-permute-done((bf16[2,8,16,512]{3,2,1,0:T(8,128)(2,1)S(1)}, bf16[2,8,16,512]{3,2,1,0:T(8,128)(2,1)}, u32[]{:S(2)}, u32[]{:S(2)}) %collective-permute-start.2) | collective-permute-done | bytes 262176 | tf_op jit(solution)/shard_map/ppermute | solution.py:287
  45.8 2.0 copy.87
  50.1 2.1 fusion
  52.4 2.2 fusion.1
  54.7 2.4 %collective-permute-start.5 = (bf16[16,4096]{1,0:T(8,128)(2,1)S(1)}, bf16[16,4096]{1,0:T(8,128)(2,1)S(1)}, u32[]{:S(2)}, u32[]{:S(2)}) collective-permute-start(bf16[16,4096]{1,0:T(8,128)(2,1)S(1)} %bitcast_dynamic-update-slice_fusion), channel_id=1, source_target_pairs={{0,48},{1,13},{2,50},{3,15},{4,52},{5,1},{6,54},{7,3},{8,56},{9,5}... | collective-permute-start | bytes 393224 | tf_op jit(solution)/shard_map/ppermute | solution.py:269
  57.7 2.4 %collective-permute-done.6 = bf16[16,4096]{1,0:T(8,128)(2,1)S(1)} collective-permute-done((bf16[16,4096]{1,0:T(8,128)(2,1)S(1)}, bf16[16,4096]{1,0:T(8,128)(2,1)S(1)}, u32[]{:S(2)}, u32[]{:S(2)}) %collective-permute-start.6) | collective-permute-done | bytes 131104 | tf_op jit(solution)/shard_map/ppermute | solution.py:269
  60.1 1.7 collective-permute-done.5
  62.2 1.5 collective-permute-start.11
  63.7 1.6 constant_dynamic-update-slice_fusion
  65.3 1.2 collective-permute-start.10
  68.3 3.9 %collective-permute-done.11 = bf16[64,4096]{1,0:T(8,128)(2,1)S(1)} collective-permute-done((bf16[64,4096]{1,0:T(8,128)(2,1)S(1)}, bf16[64,4096]{1,0:T(8,128)(2,1)S(1)}, u32[]{:S(2)}, u32[]{:S(2)}) %collective-permute-start.11) | collective-permute-done | bytes 524320 | tf_op jit(solution)/shard_map/ppermute | solution.py:269
  73.3 4.5 %collective-permute-done.10 = bf16[64,4096]{1,0:T(8,128)(2,1)S(1)} collective-permute-done((bf16[64,4096]{1,0:T(8,128)(2,1)S(1)}, bf16[64,4096]{1,0:T(8,128)(2,1)S(1)}, u32[]{:S(2)}, u32[]{:S(2)}) %collective-permute-start.10) | collective-permute-done | bytes 524320 | tf_op jit(solution)/shard_map/ppermute | solution.py:269
  80.3 3.2 %collective-permute-start.12 = (bf16[4,4,2,8,448]{4,3,2,0,1:T(8,128)(2,1)S(1)}, bf16[4,4,2,8,448]{4,3,2,0,1:T(8,128)(2,1)S(1)}, u32[]{:S(2)}, u32[]{:S(2)}) collective-permute-start(bf16[4,4,2,8,448]{4,3,2,0,1:T(8,128)(2,1)S(1)} %copy.133), channel_id=1, source_target_pairs={{0,2},{1,3},{2,0},{3,1},{64,66},{65,67},{66,64},{67,65},{4,6},{5,7... | collective-permute-start | bytes 688136 | tf_op jit(solution)/shard_map/ppermute | solution.py:283
  85.0 2.3 %collective-permute-done.12 = bf16[4,4,2,8,448]{4,3,2,0,1:T(8,128)(2,1)S(1)} collective-permute-done((bf16[4,4,2,8,448]{4,3,2,0,1:T(8,128)(2,1)S(1)}, bf16[4,4,2,8,448]{4,3,2,0,1:T(8,128)(2,1)S(1)}, u32[]{:S(2)}, u32[]{:S(2)}) %collective-permute-start.12) | collective-permute-done | bytes 229408 | tf_op jit(solution)/shard_map/ppermute | solution.py:283
  87.5 4.0 %collective-permute-done.14 = bf16[4,4,2,8,448]{4,3,2,0,1:T(8,128)(2,1)S(1)} collective-permute-done((bf16[4,4,2,8,448]{4,3,2,0,1:T(8,128)(2,1)S(1)}, bf16[4,4,2,8,448]{4,3,2,0,1:T(8,128)(2,1)S(1)}, u32[]{:S(2)}, u32[]{:S(2)}) %collective-permute-start.14) | collective-permute-done | bytes 229408 | tf_op jit(solution)/shard_map/ppermute | solution.py:283
  91.5 2.4 %collective-permute-done.13 = bf16[4,4,2,8,448]{4,3,2,0,1:T(8,128)(2,1)S(1)} collective-permute-done((bf16[4,4,2,8,448]{4,3,2,0,1:T(8,128)(2,1)S(1)}, bf16[4,4,2,8,448]{4,3,2,0,1:T(8,128)(2,1)S(1)}, u32[]{:S(2)}, u32[]{:S(2)}) %collective-permute-start.13) | collective-permute-done | bytes 229408 | tf_op jit(solution)/shard_map/ppermute | solution.py:283
  94.1 3.2 %collective-permute-start.15 = (bf16[2,4,4,2,8,448]{5,4,3,2,1,0:T(8,128)(2,1)S(1)}, bf16[2,4,4,2,8,448]{5,4,3,2,1,0:T(8,128)(2,1)S(1)}, u32[]{:S(2)}, u32[]{:S(2)}) collective-permute-start(bf16[2,4,4,2,8,448]{5,4,3,2,1,0:T(8,128)(2,1)S(1)} %pad_maximum_fusion.3), channel_id=1, source_target_pairs={{0,1},{1,0},{2,3},{3,2},{4,5},{5,4},{6,7},{7,6},{8,9},{9,8},{10,11... | collective-permute-start | bytes 1376264 | tf_op jit(solution)/shard_map/ppermute | solution.py:287
  97.5 1.4 collective-permute-done.15
  99.2 2.7 %collective-permute-start.20 = (bf16[2,4,64,448]{3,2,1,0:T(8,128)(2,1)S(1)}, bf16[2,4,64,448]{3,2,1,0:T(8,128)(2,1)S(1)}, u32[]{:S(2)}, u32[]{:S(2)}) collective-permute-start(bf16[2,4,64,448]{3,2,1,0:T(8,128)(2,1)S(1)} %bitcast.95), channel_id=1, source_target_pairs={{0,48},{1,13},{2,50},{3,15},{4,52},{5,1},{6,54},{7,3},{8,56},{9,5}... | collective-permute-start | bytes 1376264 | tf_op jit(solution)/shard_map/ppermute | solution.py:269
  103.6 1.8 collective-permute-start.17
  105.4 3.4 %collective-permute-done.19.refs_1_ = bf16[2,4,64,448]{3,2,1,0:T(8,128)(2,1)S(1)} collective-permute-done((bf16[2,4,64,448]{3,2,1,0:T(8,128)(2,1)S(1)}, bf16[2,4,64,448]{3,2,1,0:T(8,128)(2,1)S(1)}, u32[]{:S(2)}, u32[]{:S(2)}) %collective-permute-start.19) | collective-permute-done | bytes 458784 | tf_op jit(solution)/shard_map/ppermute | solution.py:269
  109.2 4.5 %collective-permute-done.20.refs_2_ = bf16[2,4,64,448]{3,2,1,0:T(8,128)(2,1)S(1)} collective-permute-done((bf16[2,4,64,448]{3,2,1,0:T(8,128)(2,1)S(1)}, bf16[2,4,64,448]{3,2,1,0:T(8,128)(2,1)S(1)}, u32[]{:S(2)}, u32[]{:S(2)}) %collective-permute-start.20) | collective-permute-done | bytes 458784 | tf_op jit(solution)/shard_map/ppermute | solution.py:269
  113.7 1.5 collective-permute-done.21.refs_3_
  115.1 3.0 %partial_sums.5 = bf16[256,1280]{1,0:T(8,128)(2,1)S(1)} custom-call(bf16[2,4,64,448]{3,2,1,0:T(8,128)(2,1)S(1)} %bitcast.97, bf16[2,4,64,448]{3,2,1,0:T(8,128)(2,1)S(1)} %collective-permute-done.19.refs_1_, bf16[2,4,64,448]{3,2,1,0:T(8,128)(2,1)S(1)} %collective-permute-done.20.refs_2_, bf16[2,4,64,448]{3,2,1,0:T(8,128)(2,1)S(1)} %collective-permute-done.21.refs_3_, ...), custom_call_target="tpu_custom_call" | custom-call | flops 1056964608 | bytes 4718592 | tf_op jit(solution)/shard_map/partial_sums/pallas_call | solution.py:82
  118.3 1.7 collective-permute-done.16.refs_1_
  120.0 4.9 %collective-permute-done.17.refs_2_ = bf16[2,4,64,448]{3,2,1,0:T(8,128)(2,1)S(1)} collective-permute-done((bf16[2,4,64,448]{3,2,1,0:T(8,128)(2,1)S(1)}, bf16[2,4,64,448]{3,2,1,0:T(8,128)(2,1)S(1)}, u32[]{:S(2)}, u32[]{:S(2)}) %collective-permute-start.17) | collective-permute-done | bytes 458784 | tf_op jit(solution)/shard_map/ppermute | solution.py:269
  124.9 3.1 %collective-permute-done.18.refs_3_ = bf16[2,4,64,448]{3,2,1,0:T(8,128)(2,1)S(1)} collective-permute-done((bf16[2,4,64,448]{3,2,1,0:T(8,128)(2,1)S(1)}, bf16[2,4,64,448]{3,2,1,0:T(8,128)(2,1)S(1)}, u32[]{:S(2)}, u32[]{:S(2)}) %collective-permute-start.18) | collective-permute-done | bytes 458784 | tf_op jit(solution)/shard_map/ppermute | solution.py:269
  128.0 3.1 %partial_sums.6 = bf16[256,1280]{1,0:T(8,128)(2,1)S(1)} custom-call(bf16[2,4,64,448]{3,2,1,0:T(8,128)(2,1)S(1)} %bitcast.102, bf16[2,4,64,448]{3,2,1,0:T(8,128)(2,1)S(1)} %collective-permute-done.16.refs_1_, bf16[2,4,64,448]{3,2,1,0:T(8,128)(2,1)S(1)} %collective-permute-done.17.refs_2_, bf16[2,4,64,448]{3,2,1,0:T(8,128)(2,1)S(1)} %collective-permute-done.18.refs_3_, ...), custom_call_target="tpu_custom_call" | custom-call | flops 1056964608 | bytes 4718592 | tf_op jit(solution)/shard_map/partial_sums/pallas_call | solution.py:82
  131.3 3.0 %partial_sums.7 = bf16[256,1280]{1,0:T(8,128)(2,1)S(1)} custom-call(bf16[2,4,64,448]{3,2,1,0:T(8,128)(2,1)S(1)} %bitcast.98, bf16[2,4,64,448]{3,2,1,0:T(8,128)(2,1)S(1)} %collective-permute-done.19.refs_1_, bf16[2,4,64,448]{3,2,1,0:T(8,128)(2,1)S(1)} %collective-permute-done.20.refs_2_, bf16[2,4,64,448]{3,2,1,0:T(8,128)(2,1)S(1)} %collective-permute-done.21.refs_3_, ...), custom_call_target="tpu_custom_call" | custom-call | flops 1056964608 | bytes 4718592 | tf_op jit(solution)/shard_map/partial_sums/pallas_call | solution.py:82
  134.5 3.0 %partial_sums.4.refs_0_ = bf16[256,1280]{1,0:T(8,128)(2,1)S(1)} custom-call(bf16[2,4,64,448]{3,2,1,0:T(8,128)(2,1)S(1)} %bitcast.103, bf16[2,4,64,448]{3,2,1,0:T(8,128)(2,1)S(1)} %collective-permute-done.16.refs_1_, bf16[2,4,64,448]{3,2,1,0:T(8,128)(2,1)S(1)} %collective-permute-done.17.refs_2_, bf16[2,4,64,448]{3,2,1,0:T(8,128)(2,1)S(1)} %collective-permute-done.18.refs_3_, ...), custom_call_target="tpu_custom_call" | custom-call | flops 1056964608 | bytes 4718592 | tf_op jit(solution)/shard_map/partial_sums/pallas_call | solution.py:82
  137.6 3.2 %collective-permute-done.23.refs_2_ = bf16[256,1280]{1,0:T(8,128)(2,1)S(1)} collective-permute-done((bf16[256,1280]{1,0:T(8,128)(2,1)S(1)}, bf16[256,1280]{1,0:T(8,128)(2,1)S(1)}, u32[]{:S(2)}, u32[]{:S(2)}) %collective-permute-start.23) | collective-permute-done | bytes 655392 | tf_op jit(solution)/shard_map/ppermute | solution.py:269
  140.8 4.9 %collective-permute-done.24.refs_3_ = bf16[256,1280]{1,0:T(8,128)(2,1)S(1)} collective-permute-done((bf16[256,1280]{1,0:T(8,128)(2,1)S(1)}, bf16[256,1280]{1,0:T(8,128)(2,1)S(1)}, u32[]{:S(2)}, u32[]{:S(2)}) %collective-permute-start.24) | collective-permute-done | bytes 655392 | tf_op jit(solution)/shard_map/ppermute | solution.py:269
  146.3 3.7 %collective-permute-start.27 = (bf16[256,640]{1,0:T(8,128)(2,1)S(1)}, bf16[256,640]{1,0:T(8,128)(2,1)S(1)}, u32[]{:S(2)}, u32[]{:S(2)}) collective-permute-start(bf16[256,640]{1,0:T(8,128)(2,1)S(1)} %activate.1), channel_id=1, source_target_pairs={{0,32},{1,9},{2,34},{3,11},{4,36},{5,13},{6,38},{7,15},{8,40},{9,1... | collective-permute-start | bytes 983048 | tf_op jit(solution)/shard_map/ppermute | solution.py:269
  150.8 3.1 %collective-permute-done.25 = bf16[256,640]{1,0:T(8,128)(2,1)S(1)} collective-permute-done((bf16[256,640]{1,0:T(8,128)(2,1)S(1)}, bf16[256,640]{1,0:T(8,128)(2,1)S(1)}, u32[]{:S(2)}, u32[]{:S(2)}) %collective-permute-start.25) | collective-permute-done | bytes 327712 | tf_op jit(solution)/shard_map/ppermute | solution.py:269
  155.0 3.0 %collective-permute-done.27 = bf16[256,640]{1,0:T(8,128)(2,1)S(1)} collective-permute-done((bf16[256,640]{1,0:T(8,128)(2,1)S(1)}, bf16[256,640]{1,0:T(8,128)(2,1)S(1)}, u32[]{:S(2)}, u32[]{:S(2)}) %collective-permute-start.27) | collective-permute-done | bytes 327712 | tf_op jit(solution)/shard_map/ppermute | solution.py:269
  158.0 1.6 collective-permute-done.26
  159.7 3.0 %collective-permute-start.31 = (bf16[2,256,640]{2,1,0:T(8,128)(2,1)S(1)}, bf16[2,256,640]{2,1,0:T(8,128)(2,1)S(1)}, u32[]{:S(2)}, u32[]{:S(2)}) collective-permute-start(bf16[2,256,640]{2,1,0:T(8,128)(2,1)S(1)} %pad_maximum_fusion.1.high), channel_id=1, source_target_pairs={{0,12},{1,49},{2,14},{3,51},{4,0},{5,53},{6,2},{7,55},{8,4},{9,57}... | collective-permute-start | bytes 1966088 | tf_op jit(solution)/shard_map/ppermute | solution.py:269
  162.8 1.4 collective-permute-start.29
  164.2 5.6 %collective-permute-done.28.low = bf16[2,256,640]{2,1,0:T(8,128)(2,1)S(1)} collective-permute-done((bf16[2,256,640]{2,1,0:T(8,128)(2,1)S(1)}, bf16[2,256,640]{2,1,0:T(8,128)(2,1)S(1)}, u32[]{:S(2)}, u32[]{:S(2)}) %collective-permute-start.28) | collective-permute-done | bytes 655392 | tf_op jit(solution)/shard_map/ppermute | solution.py:269
  169.7 1.8 collective-permute-done.31.high
  171.5 2.7 %collective-permute-start.33 = (bf16[2,256,640]{2,1,0:T(8,128)(2,1)S(1)}, bf16[2,256,640]{2,1,0:T(8,128)(2,1)S(1)}, u32[]{:S(2)}, u32[]{:S(2)}) collective-permute-start(bf16[2,256,640]{2,1,0:T(8,128)(2,1)S(1)} %collective-permute-done.31.high), channel_id=1, source_target_pairs={{0,12},{1,49},{2,14},{3,51},{4,0},{5,53},{6,2},{7,55},{8,4},{9,57}... | collective-permute-start | bytes 1966088 | tf_op jit(solution)/shard_map/ppermute | solution.py:269
  174.2 1.5 cut_down.1.weights
  176.7 2.1 collective-permute-done.30.low
  180.8 3.2 %collective-permute-done.32.low = bf16[2,256,640]{2,1,0:T(8,128)(2,1)S(1)} collective-permute-done((bf16[2,256,640]{2,1,0:T(8,128)(2,1)S(1)}, bf16[2,256,640]{2,1,0:T(8,128)(2,1)S(1)}, u32[]{:S(2)}, u32[]{:S(2)}) %collective-permute-start.32) | collective-permute-done | bytes 655392 | tf_op jit(solution)/shard_map/ppermute | solution.py:269
  184.1 1.8 collective-permute-done.33.high
  187.0 12.8 %collective-permute-start.34 = (bf16[4,4,32,448]{3,2,1,0:T(8,128)(2,1)S(1)}, bf16[4,4,32,448]{3,2,1,0:T(8,128)(2,1)S(1)}, u32[]{:S(2)}, u32[]{:S(2)}) collective-permute-start(bf16[4,4,32,448]{3,2,1,0:T(8,128)(2,1)S(1)} %pad_maximum_fusion.4), channel_id=1, source_target_pairs={{0,1},{1,0},{2,3},{3,2},{4,5},{5,4},{6,7},{7,6},{8,9},{9,8},{10,11... | collective-permute-start | bytes 1376264 | tf_op jit(solution)/shard_map/ppermute | solution.py:287
  199.7 1.5 collective-permute-done.34
  202.3 19.2 %all_to_all.5 = bf16[64,8,448]{2,1,0:T(8,128)(2,1)S(1)} all-to-all(bf16[64,8,448]{2,1,0:T(8,128)(2,1)S(1)} %bitcast.132), channel_id=1, replica_groups=mesh['role'=2,'grp'=16,'yh'=2,'core'=2] {'role','grp','yh'}, dimensions={0} | all-to-all | bytes 917504 | tf_op jit(solution)/shard_map/all_to_all | solution.py:433
  221.8 9.7 %all_gather.3 = bf16[32,7168]{1,0:T(8,128)(2,1)S(1)} all-gather(bf16[8,7168]{1,0:T(8,128)(2,1)S(1)} %reshape.86), channel_id=1, replica_groups=mesh['role'=2,'grp'=16,'yh'=2,'core'=2] {'yh','core'}, dimensions={0}, use_global_device_ids=true | all-gather | bytes 573440 | tf_op jit(solution)/shard_map/all_gather | solution.py:437
  (140 shorter events, 25.5 us)
Async XLA Ops:
  0.8 1.6 copy-start
  2.4 1.6 copy-start.2
  4.0 3.9 %copy-start.1 = (bf16[448,2304]{1,0:T(8,128)(2,1)S(1)}, bf16[448,2304]{1,0:T(8,128)(2,1)}, u32[]{:S(2)}) copy-start(bf16[448,2304]{1,0:T(8,128)(2,1)} %gate_tail.7) | copy-start | bytes 6193156
  5.4 27.3 %collective-permute-start = (bf16[448,1152]{1,0:T(8,128)(2,1)}, bf16[448,1152]{1,0:T(8,128)(2,1)S(1)}, u32[]{:S(2)}, u32[]{:S(2)}) collective-permute-start(bf16[448,1152]{1,0:T(8,128)(2,1)} %cut_in.4), channel_id=1, source_target_pairs={{0,16},{1,5},{2,18},{3,7},{4,20},{5,9},{6,22},{7,11},{8,24},{9,13}... | collective-permute-start | bytes 3096584 | tf_op jit(solution)/shard_map/ppermute | solution.py:269
  7.9 1.6 copy-start.3
  10.9 25.6 %collective-permute-start.1 = (bf16[448,1152]{1,0:T(8,128)(2,1)}, bf16[448,1152]{1,0:T(8,128)(2,1)}, u32[]{:S(2)}, u32[]{:S(2)}) collective-permute-start(bf16[448,1152]{1,0:T(8,128)(2,1)} %cut_in.5), channel_id=1, source_target_pairs={{0,48},{1,13},{2,50},{3,15},{4,52},{5,1},{6,54},{7,3},{8,56},{9,5}... | collective-permute-start | bytes 3096584 | tf_op jit(solution)/shard_map/ppermute | solution.py:269
  13.5 38.9 %collective-permute-start.3 = (bf16[16,512,128]{2,1,0:T(8,128)(2,1)}, bf16[16,512,128]{2,1,0:T(8,128)(2,1)}, u32[]{:S(2)}, u32[]{:S(2)}) collective-permute-start(bf16[16,512,128]{2,1,0:T(8,128)(2,1)} %param.19), channel_id=1, source_target_pairs={{0,1},{1,0},{2,3},{3,2},{4,5},{5,4},{6,7},{7,6},{8,9},{9,8},{10,11... | collective-permute-start | bytes 6291464 | tf_op jit(solution)/shard_map/ppermute | solution.py:287
  13.5 1.6 copy-start.4
  15.1 4.9 %copy-start.26 = (bf16[8,576]{1,0:T(8,128)(2,1)S(1)}, bf16[8,576]{1,0:T(8,128)(2,1)}, u32[]{:S(2)}) copy-start(bf16[8,576]{1,0:T(8,128)(2,1)} %param.14) | copy-start | bytes 27652
  15.1 5.0 %copy-start.11 = (s32[8]{0:T(128)S(1)}, s32[8]{0:T(128)}, u32[]{:S(2)}) copy-start(s32[8]{0:T(128)} %members_ref.1) | copy-start | bytes 100
  15.1 5.0 %copy-start.12 = (s32[8]{0:T(128)S(1)}, s32[8]{0:T(128)}, u32[]{:S(2)}) copy-start(s32[8]{0:T(128)} %lengths_ref.1) | copy-start | bytes 100
  16.5 45.7 %collective-permute-start.7 = (bf16[448,1152]{1,0:T(8,128)(2,1)}, bf16[448,1152]{1,0:T(8,128)(2,1)}, u32[]{:S(2)}, u32[]{:S(2)}) collective-permute-start(bf16[448,1152]{1,0:T(8,128)(2,1)} %cut_in.6), channel_id=1, source_target_pairs={{0,32},{1,9},{2,34},{3,11},{4,36},{5,13},{6,38},{7,15},{8,40},{9,1... | collective-permute-start | bytes 3096584 | tf_op jit(solution)/shard_map/ppermute | solution.py:269
  19.8 43.9 %collective-permute-start.8 = (bf16[2048,448]{0,1:T(8,128)(2,1)}, bf16[2048,448]{0,1:T(8,128)(2,1)}, u32[]{:S(2)}, u32[]{:S(2)}) collective-permute-start(bf16[2048,448]{0,1:T(8,128)(2,1)} %param.20), channel_id=1, source_target_pairs={{0,1},{1,0},{2,3},{3,2},{4,5},{5,4},{6,7},{7,6},{8,9},{9,8},{10,11... | collective-permute-start | bytes 5505032 | tf_op jit(solution)/shard_map/ppermute | solution.py:287
  20.1 3.7 %copy-start.6 = (bf16[8,1024,576]{1,2,0:T(8,128)(2,1)S(1)}, bf16[8,1024,576]{1,2,0:T(8,128)(2,1)}, u32[]{:S(2)}) copy-start(bf16[8,1024,576]{1,2,0:T(8,128)(2,1)} %param.15) | copy-start | bytes 28311556
  23.8 1.1 copy-start.8
  32.0 0.7 copy-start.9
  36.5 9.3 %collective-permute-start.2 = (bf16[2,8,16,512]{3,2,1,0:T(8,128)(2,1)S(1)}, bf16[2,8,16,512]{3,2,1,0:T(8,128)(2,1)}, u32[]{:S(2)}, u32[]{:S(2)}) collective-permute-start(bf16[2,8,16,512]{3,2,1,0:T(8,128)(2,1)S(1)} %get-tuple-element.23), channel_id=1, source_target_pairs={{0,2},{2,0},{1,3},{3,1},{4,6},{6,4},{5,7},{7,5},{8,10},{10,8},{9,1... | collective-permute-start | bytes 786440 | tf_op jit(solution)/shard_map/ppermute | solution.py:287
  47.8 1.2 copy-start.10
  52.2 11.5 %copy-start.13 = (bf16[4096,448]{0,1:T(8,128)(2,1)S(1)}, bf16[4096,448]{0,1:T(8,128)(2,1)}, u32[]{:S(2)}) copy-start(bf16[4096,448]{0,1:T(8,128)(2,1)} %constant_dynamic-update-slice_fusion.1) | copy-start | bytes 11010052
  54.7 5.4 %collective-permute-start.6 = (bf16[16,4096]{1,0:T(8,128)(2,1)S(1)}, bf16[16,4096]{1,0:T(8,128)(2,1)S(1)}, u32[]{:S(2)}, u32[]{:S(2)}) collective-permute-start(bf16[16,4096]{1,0:T(8,128)(2,1)S(1)} %bitcast_dynamic-update-slice_fusion), channel_id=1, source_target_pairs={{0,32},{1,9},{2,34},{3,11},{4,36},{5,13},{6,38},{7,15},{8,40},{9,1... | collective-permute-start | bytes 393224 | tf_op jit(solution)/shard_map/ppermute | solution.py:269
  54.7 7.0 %collective-permute-start.5 = (bf16[16,4096]{1,0:T(8,128)(2,1)S(1)}, bf16[16,4096]{1,0:T(8,128)(2,1)S(1)}, u32[]{:S(2)}, u32[]{:S(2)}) collective-permute-start(bf16[16,4096]{1,0:T(8,128)(2,1)S(1)} %bitcast_dynamic-update-slice_fusion), channel_id=1, source_target_pairs={{0,48},{1,13},{2,50},{3,15},{4,52},{5,1},{6,54},{7,3},{8,56},{9,5}... | collective-permute-start | bytes 393224 | tf_op jit(solution)/shard_map/ppermute | solution.py:269
  57.1 5.0 %collective-permute-start.4 = (bf16[16,4096]{1,0:T(8,128)(2,1)S(1)}, bf16[16,4096]{1,0:T(8,128)(2,1)S(1)}, u32[]{:S(2)}, u32[]{:S(2)}) collective-permute-start(bf16[16,4096]{1,0:T(8,128)(2,1)S(1)} %bitcast_dynamic-update-slice_fusion), channel_id=1, source_target_pairs={{0,16},{1,5},{2,18},{3,7},{4,20},{5,9},{6,22},{7,11},{8,24},{9,13}... | collective-permute-start | bytes 393224 | tf_op jit(solution)/shard_map/ppermute | solution.py:269
  57.6 39.7 %copy-start.24 = (bf16[4,1,2,8,448]{4,3,2,1,0:T(8,128)(2,1)}, bf16[4,1,2,8,448]{4,3,2,1,0:T(8,128)(2,1)S(1)}, u32[]{:S(2)}) copy-start(bf16[4,1,2,8,448]{4,3,2,1,0:T(8,128)(2,1)S(1)} %get-tuple-element.48) | copy-start | bytes 172036
  62.2 9.9 %collective-permute-start.11 = (bf16[64,4096]{1,0:T(8,128)(2,1)S(1)}, bf16[64,4096]{1,0:T(8,128)(2,1)S(1)}, u32[]{:S(2)}, u32[]{:S(2)}) collective-permute-start(bf16[64,4096]{1,0:T(8,128)(2,1)S(1)} %pad_maximum_fusion.2), channel_id=1, source_target_pairs={{0,8},{1,33},{2,10},{3,35},{4,12},{5,37},{6,14},{7,39},{8,0},{9,41... | collective-permute-start | bytes 1572872 | tf_op jit(solution)/shard_map/ppermute | solution.py:269
  65.3 12.5 %collective-permute-start.10 = (bf16[64,4096]{1,0:T(8,128)(2,1)S(1)}, bf16[64,4096]{1,0:T(8,128)(2,1)S(1)}, u32[]{:S(2)}, u32[]{:S(2)}) collective-permute-start(bf16[64,4096]{1,0:T(8,128)(2,1)S(1)} %pad_maximum_fusion.2), channel_id=1, source_target_pairs={{0,12},{1,49},{2,14},{3,51},{4,0},{5,53},{6,2},{7,55},{8,4},{9,57}... | collective-permute-start | bytes 1572872 | tf_op jit(solution)/shard_map/ppermute | solution.py:269
  66.5 12.5 %collective-permute-start.9 = (bf16[64,4096]{1,0:T(8,128)(2,1)S(1)}, bf16[64,4096]{1,0:T(8,128)(2,1)S(1)}, u32[]{:S(2)}, u32[]{:S(2)}) collective-permute-start(bf16[64,4096]{1,0:T(8,128)(2,1)S(1)} %pad_maximum_fusion.2), channel_id=1, source_target_pairs={{0,4},{1,17},{2,6},{3,19},{4,8},{5,21},{6,10},{7,23},{8,12},{9,25}... | collective-permute-start | bytes 1572872 | tf_op jit(solution)/shard_map/ppermute | solution.py:269
  68.3 29.0 %copy-start.14 = (f32[64,448]{1,0:T(8,128)}, f32[64,448]{1,0:T(8,128)S(1)}, u32[]{:S(2)}) copy-start(f32[64,448]{1,0:T(8,128)S(1)} %fusion.25) | copy-start | bytes 344068
  73.3 24.0 %copy-start.16 = (f32[64,448]{1,0:T(8,128)}, f32[64,448]{1,0:T(8,128)S(1)}, u32[]{:S(2)}) copy-start(f32[64,448]{1,0:T(8,128)S(1)} %fusion.28) | copy-start | bytes 344068
  79.0 18.3 %copy-start.18 = (f32[64,448]{1,0:T(8,128)}, f32[64,448]{1,0:T(8,128)S(1)}, u32[]{:S(2)}) copy-start(f32[64,448]{1,0:T(8,128)S(1)} %fusion.27) | copy-start | bytes 344068
  80.2 17.1 %copy-start.20 = (f32[64,448]{1,0:T(8,128)}, f32[64,448]{1,0:T(8,128)S(1)}, u32[]{:S(2)}) copy-start(f32[64,448]{1,0:T(8,128)S(1)} %fusion.26) | copy-start | bytes 344068
  80.3 7.0 %collective-permute-start.12 = (bf16[4,4,2,8,448]{4,3,2,0,1:T(8,128)(2,1)S(1)}, bf16[4,4,2,8,448]{4,3,2,0,1:T(8,128)(2,1)S(1)}, u32[]{:S(2)}, u32[]{:S(2)}) collective-permute-start(bf16[4,4,2,8,448]{4,3,2,0,1:T(8,128)(2,1)S(1)} %copy.133), channel_id=1, source_target_pairs={{0,2},{1,3},{2,0},{3,1},{64,66},{65,67},{66,64},{67,65},{4,6},{5,7... | collective-permute-start | bytes 688136 | tf_op jit(solution)/shard_map/ppermute | solution.py:283
  83.5 8.0 %collective-permute-start.14 = (bf16[4,4,2,8,448]{4,3,2,0,1:T(8,128)(2,1)S(1)}, bf16[4,4,2,8,448]{4,3,2,0,1:T(8,128)(2,1)S(1)}, u32[]{:S(2)}, u32[]{:S(2)}) collective-permute-start(bf16[4,4,2,8,448]{4,3,2,0,1:T(8,128)(2,1)S(1)} %copy.133), channel_id=1, source_target_pairs={{0,66},{1,67},{2,64},{3,65},{64,0},{65,1},{66,2},{67,3},{4,70},{5,... | collective-permute-start | bytes 688136 | tf_op jit(solution)/shard_map/ppermute | solution.py:283
  84.3 9.6 %collective-permute-start.13 = (bf16[4,4,2,8,448]{4,3,2,0,1:T(8,128)(2,1)S(1)}, bf16[4,4,2,8,448]{4,3,2,0,1:T(8,128)(2,1)S(1)}, u32[]{:S(2)}, u32[]{:S(2)}) collective-permute-start(bf16[4,4,2,8,448]{4,3,2,0,1:T(8,128)(2,1)S(1)} %copy.133), channel_id=1, source_target_pairs={{0,64},{1,65},{2,66},{3,67},{64,2},{65,3},{66,0},{67,1},{4,68},{5,... | collective-permute-start | bytes 688136 | tf_op jit(solution)/shard_map/ppermute | solution.py:283
  87.3 10.1 %copy-start.22 = (bf16[4,4,2,8,448]{4,3,2,0,1:T(8,128)(2,1)}, bf16[4,4,2,8,448]{4,3,2,0,1:T(8,128)(2,1)S(1)}, u32[]{:S(2)}) copy-start(bf16[4,4,2,8,448]{4,3,2,0,1:T(8,128)(2,1)S(1)} %collective-permute-done.12) | copy-start | bytes 688132
  94.1 4.7 %collective-permute-start.15 = (bf16[2,4,4,2,8,448]{5,4,3,2,1,0:T(8,128)(2,1)S(1)}, bf16[2,4,4,2,8,448]{5,4,3,2,1,0:T(8,128)(2,1)S(1)}, u32[]{:S(2)}, u32[]{:S(2)}) collective-permute-start(bf16[2,4,4,2,8,448]{5,4,3,2,1,0:T(8,128)(2,1)S(1)} %pad_maximum_fusion.3), channel_id=1, source_target_pairs={{0,1},{1,0},{2,3},{3,2},{4,5},{5,4},{6,7},{7,6},{8,9},{9,8},{10,11... | collective-permute-start | bytes 1376264 | tf_op jit(solution)/shard_map/ppermute | solution.py:287
  99.0 9.8 %copy-start.5 = (bf16[448,2304]{1,0:T(8,128)(2,1)S(1)}, bf16[448,2304]{1,0:T(8,128)(2,1)}, u32[]{:S(2)}) copy-start(bf16[448,2304]{1,0:T(8,128)(2,1)} %up_tail.7) | copy-start | bytes 6193156
  99.2 9.6 %collective-permute-start.19 = (bf16[2,4,64,448]{3,2,1,0:T(8,128)(2,1)S(1)}, bf16[2,4,64,448]{3,2,1,0:T(8,128)(2,1)S(1)}, u32[]{:S(2)}, u32[]{:S(2)}) collective-permute-start(bf16[2,4,64,448]{3,2,1,0:T(8,128)(2,1)S(1)} %bitcast.94), channel_id=1, source_target_pairs={{0,16},{1,5},{2,18},{3,7},{4,20},{5,9},{6,22},{7,11},{8,24},{9,13}... | collective-permute-start | bytes 1376264 | tf_op jit(solution)/shard_map/ppermute | solution.py:269
  99.2 14.4 %collective-permute-start.20 = (bf16[2,4,64,448]{3,2,1,0:T(8,128)(2,1)S(1)}, bf16[2,4,64,448]{3,2,1,0:T(8,128)(2,1)S(1)}, u32[]{:S(2)}, u32[]{:S(2)}) collective-permute-start(bf16[2,4,64,448]{3,2,1,0:T(8,128)(2,1)S(1)} %bitcast.95), channel_id=1, source_target_pairs={{0,48},{1,13},{2,50},{3,15},{4,52},{5,1},{6,54},{7,3},{8,56},{9,5}... | collective-permute-start | bytes 1376264 | tf_op jit(solution)/shard_map/ppermute | solution.py:269
  101.9 13.2 %collective-permute-start.21 = (bf16[2,4,64,448]{3,2,1,0:T(8,128)(2,1)S(1)}, bf16[2,4,64,448]{3,2,1,0:T(8,128)(2,1)S(1)}, u32[]{:S(2)}, u32[]{:S(2)}) collective-permute-start(bf16[2,4,64,448]{3,2,1,0:T(8,128)(2,1)S(1)} %bitcast.96), channel_id=1, source_target_pairs={{0,32},{1,9},{2,34},{3,11},{4,36},{5,13},{6,38},{7,15},{8,40},{9,1... | collective-permute-start | bytes 1376264 | tf_op jit(solution)/shard_map/ppermute | solution.py:269
  102.7 17.4 %collective-permute-start.16 = (bf16[2,4,64,448]{3,2,1,0:T(8,128)(2,1)S(1)}, bf16[2,4,64,448]{3,2,1,0:T(8,128)(2,1)S(1)}, u32[]{:S(2)}, u32[]{:S(2)}) collective-permute-start(bf16[2,4,64,448]{3,2,1,0:T(8,128)(2,1)S(1)} %bitcast.99), channel_id=1, source_target_pairs={{0,16},{1,5},{2,18},{3,7},{4,20},{5,9},{6,22},{7,11},{8,24},{9,13}... | collective-permute-start | bytes 1376264 | tf_op jit(solution)/shard_map/ppermute | solution.py:269
  103.6 21.3 %collective-permute-start.17 = (bf16[2,4,64,448]{3,2,1,0:T(8,128)(2,1)S(1)}, bf16[2,4,64,448]{3,2,1,0:T(8,128)(2,1)S(1)}, u32[]{:S(2)}, u32[]{:S(2)}) collective-permute-start(bf16[2,4,64,448]{3,2,1,0:T(8,128)(2,1)S(1)} %bitcast.100), channel_id=1, source_target_pairs={{0,48},{1,13},{2,50},{3,15},{4,52},{5,1},{6,54},{7,3},{8,56},{9,5}... | collective-permute-start | bytes 1376264 | tf_op jit(solution)/shard_map/ppermute | solution.py:269
  108.8 19.2 %collective-permute-start.18 = (bf16[2,4,64,448]{3,2,1,0:T(8,128)(2,1)S(1)}, bf16[2,4,64,448]{3,2,1,0:T(8,128)(2,1)S(1)}, u32[]{:S(2)}, u32[]{:S(2)}) collective-permute-start(bf16[2,4,64,448]{3,2,1,0:T(8,128)(2,1)S(1)} %bitcast.101), channel_id=1, source_target_pairs={{0,32},{1,9},{2,34},{3,11},{4,36},{5,13},{6,38},{7,15},{8,40},{9,1... | collective-permute-start | bytes 1376264 | tf_op jit(solution)/shard_map/ppermute | solution.py:269
  118.2 19.4 %collective-permute-start.22 = (bf16[256,1280]{1,0:T(8,128)(2,1)S(1)}, bf16[256,1280]{1,0:T(8,128)(2,1)S(1)}, u32[]{:S(2)}, u32[]{:S(2)}) collective-permute-start(bf16[256,1280]{1,0:T(8,128)(2,1)S(1)} %partial_sums.5), channel_id=1, source_target_pairs={{0,4},{1,17},{2,6},{3,19},{4,8},{5,21},{6,10},{7,23},{8,12},{9,25}... | collective-permute-start | bytes 1966088 | tf_op jit(solution)/shard_map/ppermute | solution.py:269
  131.0 9.8 %collective-permute-start.23 = (bf16[256,1280]{1,0:T(8,128)(2,1)S(1)}, bf16[256,1280]{1,0:T(8,128)(2,1)S(1)}, u32[]{:S(2)}, u32[]{:S(2)}) collective-permute-start(bf16[256,1280]{1,0:T(8,128)(2,1)S(1)} %partial_sums.6), channel_id=1, source_target_pairs={{0,12},{1,49},{2,14},{3,51},{4,0},{5,53},{6,2},{7,55},{8,4},{9,57}... | collective-permute-start | bytes 1966088 | tf_op jit(solution)/shard_map/ppermute | solution.py:269
  134.4 11.3 %collective-permute-start.24 = (bf16[256,1280]{1,0:T(8,128)(2,1)S(1)}, bf16[256,1280]{1,0:T(8,128)(2,1)S(1)}, u32[]{:S(2)}, u32[]{:S(2)}) collective-permute-start(bf16[256,1280]{1,0:T(8,128)(2,1)S(1)} %partial_sums.7), channel_id=1, source_target_pairs={{0,8},{1,33},{2,10},{3,35},{4,12},{5,37},{6,14},{7,39},{8,0},{9,41... | collective-permute-start | bytes 1966088 | tf_op jit(solution)/shard_map/ppermute | solution.py:269
  137.5 36.6 %copy-start.27 = (s32[4]{0:T(128)S(1)}, s32[4]{0:T(128)}, u32[]{:S(2)}) copy-start(s32[4]{0:T(128)} %constant.95) | copy-start | bytes 52
  137.6 36.6 %copy-start.7 = (bf16[2304,448]{0,1:T(8,128)(2,1)S(1)}, bf16[2304,448]{0,1:T(8,128)(2,1)}, u32[]{:S(2)}) copy-start(bf16[2304,448]{0,1:T(8,128)(2,1)} %param.24) | copy-start | bytes 6193156
  146.2 7.6 %collective-permute-start.25 = (bf16[256,640]{1,0:T(8,128)(2,1)S(1)}, bf16[256,640]{1,0:T(8,128)(2,1)S(1)}, u32[]{:S(2)}, u32[]{:S(2)}) collective-permute-start(bf16[256,640]{1,0:T(8,128)(2,1)S(1)} %activate.1), channel_id=1, source_target_pairs={{0,16},{1,5},{2,18},{3,7},{4,20},{5,9},{6,22},{7,11},{8,24},{9,13}... | collective-permute-start | bytes 983048 | tf_op jit(solution)/shard_map/ppermute | solution.py:269
  146.3 11.7 %collective-permute-start.27 = (bf16[256,640]{1,0:T(8,128)(2,1)S(1)}, bf16[256,640]{1,0:T(8,128)(2,1)S(1)}, u32[]{:S(2)}, u32[]{:S(2)}) collective-permute-start(bf16[256,640]{1,0:T(8,128)(2,1)S(1)} %activate.1), channel_id=1, source_target_pairs={{0,32},{1,9},{2,34},{3,11},{4,36},{5,13},{6,38},{7,15},{8,40},{9,1... | collective-permute-start | bytes 983048 | tf_op jit(solution)/shard_map/ppermute | solution.py:269
  150.1 9.5 %collective-permute-start.26 = (bf16[256,640]{1,0:T(8,128)(2,1)S(1)}, bf16[256,640]{1,0:T(8,128)(2,1)S(1)}, u32[]{:S(2)}, u32[]{:S(2)}) collective-permute-start(bf16[256,640]{1,0:T(8,128)(2,1)S(1)} %activate.1), channel_id=1, source_target_pairs={{0,48},{1,13},{2,50},{3,15},{4,52},{5,1},{6,54},{7,3},{8,56},{9,5}... | collective-permute-start | bytes 983048 | tf_op jit(solution)/shard_map/ppermute | solution.py:269
  153.9 15.8 %collective-permute-start.28 = (bf16[2,256,640]{2,1,0:T(8,128)(2,1)S(1)}, bf16[2,256,640]{2,1,0:T(8,128)(2,1)S(1)}, u32[]{:S(2)}, u32[]{:S(2)}) collective-permute-start(bf16[2,256,640]{2,1,0:T(8,128)(2,1)S(1)} %pad_maximum_fusion.low), channel_id=1, source_target_pairs={{0,4},{1,17},{2,6},{3,19},{4,8},{5,21},{6,10},{7,23},{8,12},{9,25}... | collective-permute-start | bytes 1966088 | tf_op jit(solution)/shard_map/ppermute | solution.py:269
  159.7 11.8 %collective-permute-start.31 = (bf16[2,256,640]{2,1,0:T(8,128)(2,1)S(1)}, bf16[2,256,640]{2,1,0:T(8,128)(2,1)S(1)}, u32[]{:S(2)}, u32[]{:S(2)}) collective-permute-start(bf16[2,256,640]{2,1,0:T(8,128)(2,1)S(1)} %pad_maximum_fusion.1.high), channel_id=1, source_target_pairs={{0,12},{1,49},{2,14},{3,51},{4,0},{5,53},{6,2},{7,55},{8,4},{9,57}... | collective-permute-start | bytes 1966088 | tf_op jit(solution)/shard_map/ppermute | solution.py:269
  162.7 16.1 %collective-permute-start.30 = (bf16[2,256,640]{2,1,0:T(8,128)(2,1)S(1)}, bf16[2,256,640]{2,1,0:T(8,128)(2,1)S(1)}, u32[]{:S(2)}, u32[]{:S(2)}) collective-permute-start(bf16[2,256,640]{2,1,0:T(8,128)(2,1)S(1)} %pad_maximum_fusion.low), channel_id=1, source_target_pairs={{0,12},{1,49},{2,14},{3,51},{4,0},{5,53},{6,2},{7,55},{8,4},{9,57}... | collective-permute-start | bytes 1966088 | tf_op jit(solution)/shard_map/ppermute | solution.py:269
  162.8 17.0 %collective-permute-start.29 = (bf16[2,256,640]{2,1,0:T(8,128)(2,1)S(1)}, bf16[2,256,640]{2,1,0:T(8,128)(2,1)S(1)}, u32[]{:S(2)}, u32[]{:S(2)}) collective-permute-start(bf16[2,256,640]{2,1,0:T(8,128)(2,1)S(1)} %pad_maximum_fusion.1.high), channel_id=1, source_target_pairs={{0,4},{1,17},{2,6},{3,19},{4,8},{5,21},{6,10},{7,23},{8,12},{9,25}... | collective-permute-start | bytes 1966088 | tf_op jit(solution)/shard_map/ppermute | solution.py:269
  169.7 14.3 %collective-permute-start.32 = (bf16[2,256,640]{2,1,0:T(8,128)(2,1)S(1)}, bf16[2,256,640]{2,1,0:T(8,128)(2,1)S(1)}, u32[]{:S(2)}, u32[]{:S(2)}) collective-permute-start(bf16[2,256,640]{2,1,0:T(8,128)(2,1)S(1)} %collective-permute-done.28.low), channel_id=1, source_target_pairs={{0,4},{1,17},{2,6},{3,19},{4,8},{5,21},{6,10},{7,23},{8,12},{9,25}... | collective-permute-start | bytes 1966088 | tf_op jit(solution)/shard_map/ppermute | solution.py:269
  171.5 14.3 %collective-permute-start.33 = (bf16[2,256,640]{2,1,0:T(8,128)(2,1)S(1)}, bf16[2,256,640]{2,1,0:T(8,128)(2,1)S(1)}, u32[]{:S(2)}, u32[]{:S(2)}) collective-permute-start(bf16[2,256,640]{2,1,0:T(8,128)(2,1)S(1)} %collective-permute-done.31.high), channel_id=1, source_target_pairs={{0,12},{1,49},{2,14},{3,51},{4,0},{5,53},{6,2},{7,55},{8,4},{9,57}... | collective-permute-start | bytes 1966088 | tf_op jit(solution)/shard_map/ppermute | solution.py:269
  186.8 14.7 %copy-start.15 = (f32[64,448]{1,0:T(8,128)S(1)}, f32[64,448]{1,0:T(8,128)}, u32[]{:S(2)}) copy-start(f32[64,448]{1,0:T(8,128)} %copy-done.14) | copy-start | bytes 344068
  186.8 14.7 %copy-start.17 = (f32[64,448]{1,0:T(8,128)S(1)}, f32[64,448]{1,0:T(8,128)}, u32[]{:S(2)}) copy-start(f32[64,448]{1,0:T(8,128)} %copy-done.16) | copy-start | bytes 344068
  186.8 14.7 %copy-start.19 = (f32[64,448]{1,0:T(8,128)S(1)}, f32[64,448]{1,0:T(8,128)}, u32[]{:S(2)}) copy-start(f32[64,448]{1,0:T(8,128)} %copy-done.18) | copy-start | bytes 344068
  186.9 14.7 %copy-start.21 = (f32[64,448]{1,0:T(8,128)S(1)}, f32[64,448]{1,0:T(8,128)}, u32[]{:S(2)}) copy-start(f32[64,448]{1,0:T(8,128)} %copy-done.20) | copy-start | bytes 344068
  186.9 14.7 %copy-start.23 = (bf16[4,4,2,8,448]{4,3,2,0,1:T(8,128)(2,1)S(1)}, bf16[4,4,2,8,448]{4,3,2,0,1:T(8,128)(2,1)}, u32[]{:S(2)}) copy-start(bf16[4,4,2,8,448]{4,3,2,0,1:T(8,128)(2,1)} %copy-done.22) | copy-start | bytes 688132
  186.9 14.7 %copy-start.25 = (bf16[4,1,2,8,448]{4,3,2,1,0:T(8,128)(2,1)S(1)}, bf16[4,1,2,8,448]{4,3,2,1,0:T(8,128)(2,1)}, u32[]{:S(2)}) copy-start(bf16[4,1,2,8,448]{4,3,2,1,0:T(8,128)(2,1)} %copy-done.24) | copy-start | bytes 172036
  187.0 14.3 %collective-permute-start.34 = (bf16[4,4,32,448]{3,2,1,0:T(8,128)(2,1)S(1)}, bf16[4,4,32,448]{3,2,1,0:T(8,128)(2,1)S(1)}, u32[]{:S(2)}, u32[]{:S(2)}) collective-permute-start(bf16[4,4,32,448]{3,2,1,0:T(8,128)(2,1)S(1)} %pad_maximum_fusion.4), channel_id=1, source_target_pairs={{0,1},{1,0},{2,3},{3,2},{4,5},{5,4},{6,7},{7,6},{8,9},{9,8},{10,11... | collective-permute-start | bytes 1376264 | tf_op jit(solution)/shard_map/ppermute | solution.py:287

commit v5 on v2

--- a/solution.py
+++ b/solution.py
@@ -10,6 +10,7 @@
 
 epsilon = 1e-06
 VMEM_LIMIT = 20 * 1024 * 1024
+STREAM_LIMIT = 50 * 1024 * 1024
 
 
 SHIFTS = (0, 1, -1, 2)
@@ -61,7 +62,7 @@
         functools.partial(attend_kernel, scale, latent),
         grid_spec=grid_spec,
         out_shape=[jax.ShapeDtypeStruct((2, tokens, block, latent), jnp.bfloat16)] * 2,
-        compiler_params=pltpu.CompilerParams(vmem_limit_bytes=VMEM_LIMIT),
+        compiler_params=pltpu.CompilerParams(vmem_limit_bytes=STREAM_LIMIT),
         cost_estimate=pl.CostEstimate(
             flops=2 * tokens * heads * ctx * (kv + latent),
             bytes_accessed=2 * tokens * ctx * kv,
@@ -165,6 +166,75 @@
     )(*operands)
 
 
+def whole_call(kernel, name, out_shapes, operands, cost):
+    return pl.pallas_call(
+        kernel,
+        out_shape=out_shapes,
+        in_specs=[pl.BlockSpec(memory_space=pltpu.VMEM)] * len(operands),
+        out_specs=[pl.BlockSpec(memory_space=pltpu.VMEM)] * len(out_shapes),
+        compiler_params=pltpu.CompilerParams(vmem_limit_bytes=VMEM_LIMIT),
+        cost_estimate=pl.CostEstimate(flops=cost, bytes_accessed=cost, transcendentals=0),
+        name=name,
+    )(*operands)
+
+
+def join_kernel(*refs):
+    *blocks, out = refs
+    count = blocks[0].shape[0]
+    for i, block in enumerate(blocks):
+        out[i * count : (i + 1) * count] = block[...]
+
+
+def join(*blocks):
+    count, cols = blocks[0].shape
+    shape = jax.ShapeDtypeStruct((len(blocks) * count, cols), blocks[0].dtype)
+    return whole_call(join_kernel, "join", [shape], blocks, 4 * shape.size)[0]
+
+
+def settle_kernel(model_width, hidden, *refs):
+    parts, (mine, theirs) = refs[:4], refs[4:]
+    total = sum(wide(r[...]) for r in parts)
+    square = total[:, hidden : hidden + 1] + total[:, hidden + 64 : hidden + 65]
+    scale = lax.rsqrt(square / model_width + epsilon)
+    count = mine.shape[0]
+    for start, cols in ((0, slice(0, hidden)), (hidden, slice(hidden + 128, None))):
+        scaled = total[:, cols] * scale
+        mine[:, start : start + hidden] = scaled[:count]
+        theirs[:, start : start + hidden] = scaled[count:].astype(jnp.bfloat16)
+
+
+def settle(parts, model_width, hidden):
+    count = parts[0].shape[0] // 2
+    shapes = [jax.ShapeDtypeStruct((count, 2 * hidden), t) for t in (jnp.float32, jnp.bfloat16)]
+    kernel = functools.partial(settle_kernel, model_width, hidden)
+    return whole_call(kernel, "settle", shapes, parts, 32 * count * hidden)
+
+
+def activate_kernel(hidden, core_ref, mine, theirs, out):
+    core = core_ref[0]
+    for start, other in ((0, hidden), (hidden, 0)):
+        a = mine[:, start : start + hidden]
+        b = wide(theirs[:, other : other + hidden])
+        gate, up = jnp.where(core == 0, a, b), jnp.where(core == 0, b, a)
+        out[:, start : start + hidden] = (jax.nn.silu(gate) * up).astype(out.dtype)
+
+
+def activate(core, mine, theirs):
+    count, cols = mine.shape
+    return pl.pallas_call(
+        functools.partial(activate_kernel, cols // 2),
+        out_shape=jax.ShapeDtypeStruct((count, cols), jnp.bfloat16),
+        in_specs=[pl.BlockSpec(memory_space=pltpu.SMEM)]
+        + [pl.BlockSpec(memory_space=pltpu.VMEM)] * 2,
+        out_specs=pl.BlockSpec(memory_space=pltpu.VMEM),
+        compiler_params=pltpu.CompilerParams(vmem_limit_bytes=VMEM_LIMIT),
+        cost_estimate=pl.CostEstimate(
+            flops=8 * count * cols, bytes_accessed=8 * count * cols, transcendentals=count * cols
+        ),
+        name="activate",
+    )(core.astype(jnp.int32)[None], mine, theirs)
+
+
 def ring(first):
     def shift(value, by):
         pairs = []
@@ -199,6 +269,10 @@
 
 def gather(block, shift):
     return [block] + [shift(block, s) for s in SHIFTS[1:]]
+
+
+def gather_from(blocks, shift):
+    return [blocks[0]] + [shift(b, s) for b, s in zip(blocks[1:], SHIFTS[1:])]
 
 
 def wide(value):
@@ -275,29 +349,34 @@
         latent,
     )
     far = swap(far, "yh")
-    context = jnp.stack([jnp.where(yh == 0, near, far), jnp.where(yh == 0, far, near)], axis=1)
-    context = context.reshape(2, 2 * tokens, heads // 4, latent)
-    values = jnp.concatenate(
-        [
+
+    def head_values(context):
+        parts = [
             jnp.einsum("thl,hlv->thv", c, w, preferred_element_type=jnp.float32)
-            .astype(jnp.bfloat16)
-            .reshape(2 * tokens, -1)
             for c, w in zip(context, uv_pair)
-        ],
-        axis=1,
-    )
-    values = jnp.concatenate(gather(values, shift_1))
-    attn_part = jnp.stack(
-        [
-            jnp.dot(v, o_chip, preferred_element_type=jnp.float32)
-            for v in gather(values, shift_2)
         ]
-    ).reshape(4, 4, 2, tokens, width)
-    shared = 0.5 * residual + attn_part
-    sent = shared.astype(jnp.bfloat16)
-    behind, ahead, across = (shift_y(sent, s) for s in SHIFTS[1:])
-    stream = shared + wide(across)
-    rows = jnp.stack([stream, add(behind, ahead)]).astype(jnp.bfloat16)
+        return jnp.stack(parts, axis=1).astype(jnp.bfloat16).reshape(tokens, -1)
+
+    near, far = head_values(near), head_values(far)
+    values = jnp.where(
+        yh == 0, jnp.concatenate([near, far]), jnp.concatenate([far, near])
+    )
+    pieces = gather(join(*gather(values, shift_1)), shift_2)
+    rows, stream = [], []
+    for half in range(2):
+        attn_part = jnp.stack(
+            [
+                jnp.dot(v, o_chip, preferred_element_type=jnp.float32)
+                for v in pieces[2 * half : 2 * half + 2]
+            ]
+        ).reshape(2, 4, 2, tokens, width)
+        shared = 0.5 * residual[2 * half : 2 * half + 2] + attn_part
+        sent = shared.astype(jnp.bfloat16)
+        behind, ahead, across = (shift_y(sent, s) for s in SHIFTS[1:])
+        stream.append(shared + wide(across))
+        rows.append(jnp.stack([stream[-1], add(behind, ahead)]).astype(jnp.bfloat16))
+    stream = jnp.concatenate(stream)
+    rows = jnp.concatenate(rows, axis=1)
     rows = jnp.stack([rows, jnp.swapaxes(swap(rows, "core"), 1, 2)])
     rows = jnp.transpose(rows, (2, 3, 0, 1, 4, 5, 6)).reshape(4, 4, 8 * tokens, width)
 
@@ -313,27 +392,12 @@
     relay_a = shift_1(add(ahead_a, far_a).astype(jnp.bfloat16), 1)
     relay_c = shift_1(add(behind_c, far_c).astype(jnp.bfloat16), -1)
     blocks = merge(own_a, own_c, direct_a, direct_c, relay_a, relay_c)
-    sums = add(blocks[0], *(shift_2(blocks[i], SHIFTS[i]) for i in range(1, 4)))
-    square = sums[:, hidden : hidden + 1] + sums[:, hidden + 64 : hidden + 65]
-    scale = lax.rsqrt(square / model_width + epsilon)
-    sums = [sums[:, :hidden] * scale, sums[:, hidden + 128 :] * scale]
-    own = [s[: 4 * tokens] for s in sums]
-    other = swap(
-        jnp.concatenate([s[4 * tokens :].astype(jnp.bfloat16) for s in sums], axis=1), "core"
-    )
-    other = [wide(other[:, hidden:]), wide(other[:, :hidden])]
-    activated = jnp.concatenate(
-        [
-            (jax.nn.silu(jnp.where(core == 0, a, b)) * jnp.where(core == 0, b, a)).astype(
-                jnp.bfloat16
-            )
-            for a, b in zip(own, other)
-        ],
-        axis=1,
-    )
+    parts = gather_from(blocks, shift_2)
+    mine, theirs = settle(parts, model_width, hidden)
+    activated = activate(core, mine, swap(theirs, "core"))
 
     own, behind, ahead, far = gather(activated, shift_1)
-    low, high = jnp.concatenate([own, behind]), jnp.concatenate([ahead, far])
+    low, high = join(own, behind), join(ahead, far)
     behind_low, ahead_high = shift_2(low, 1), shift_2(high, -1)
     behind_high, ahead_low = shift_2(high, 1), shift_2(low, -1)
     far_low, far_high = shift_2(behind_low, 1), shift_2(ahead_high, -1)

time: 219 us -> 227 us (1.037)
  starting transfers between devices: 45.6 us -> 54.7 us
  Pallas kernels: 18.3 us -> 22.4 us
  other arithmetic: 9.3 us -> 5.91 us
  local copies, waits for them, and re-layouts: 16.1 us -> 13.5 us
  matrix products: 19.2 us -> 21.5 us
    ppermute x3 -> x6, starting transfers between devices: 3.12 us -> 9.5 us  [shift_y(): lax.ppermute(value, ('role', 'yh', 'core'), [(p, moved(p)) for p in range...]
    ppermute x3 -> x6, waiting for transfers between devices: 11.3 us -> 5.53 us  [shift_y(): lax.ppermute(value, ('role', 'yh', 'core'), [(p, moved(p)) for p in range...]
    ppermute x7, starting transfers between devices: 8.02 us -> 13.2 us  [swap(): return lax.ppermute(value, axis, [(0, 1), (1, 0)])]
    ppermute x24, waiting for transfers between devices: 65.4 us -> 69.4 us  [shift(): return lax.ppermute(value, ('grp', 'yh', 'core'), pairs)]
    unnamed x20 -> x18, local copies, waits for them, and re-layouts: 11.5 us -> 7.98 us
    pallas_call x1, Pallas kernels: 7.2 us -> 10 us  [attend(): pl.pallas_call(functools.partial(attend_kernel, scale, latent), grid_spec...]
    ppermute x24, starting transfers between devices: 34.5 us -> 32 us  [shift(): return lax.ppermute(value, ('grp', 'yh', 'core'), pairs)]
    dot_general x2 -> x4, matrix products: 4.13 us -> 6.45 us  [head_values(): jnp.einsum('thl,hlv->thv', c, w, preferred_element_type=jnp.float32)]
  transfers between devices with their start and end apart: 34 -> 37, of which waited for: 20 -> 18; matrix products, arithmetic and copies ran while one was open for 16% -> 16% of each run, Pallas kernels for 3% -> 9%
where the time goes in v5:
time: 227 us; the launch traced here: 226 us
  waiting for transfers between devices  76.5 us (34%)
  starting transfers between devices  54.7 us (24%)
  blocking collectives  30.8 us (14%)
  Pallas kernels  22.4 us (10%)
  matrix products  21.5 us (9%)
  local copies, waits for them, and re-layouts  13.5 us (6%)
  other arithmetic  5.91 us (3%)
    ppermute x24, waiting for transfers between devices, shift(): return lax.ppermute(value, ('grp', 'yh', 'core'), pairs)  69.4 us
    ppermute x24, starting transfers between devices, shift(): return lax.ppermute(value, ('grp', 'yh', 'core'), pairs)  32 us
    all_to_all x1, blocking collectives, body(): lax.all_to_all(down, ('role', 'grp', 'yh'), split_axis=0, concat_axis=0)  19.3 us
    ppermute x7, starting transfers between devices, swap(): return lax.ppermute(value, axis, [(0, 1), (1, 0)])  13.2 us
    all_gather x1, blocking collectives, body(): return lax.all_gather(result, ('yh', 'core'), axis=0, tiled=True)  11.5 us
    dot_general x8, matrix products, body(): jnp.dot(p, down_chip, preferred_element_type=jnp.float32)  10.4 us
    pallas_call x3, Pallas kernels, partial_sums(): pl.pallas_call(functools.partial(partial_kernel, jobs), grid=(1,), in_spe...  10.2 us
    pallas_call x1, Pallas kernels, attend(): pl.pallas_call(functools.partial(attend_kernel, scale, latent), grid_spec...  10 us
  transfers between devices with their start and end apart: 37, of which 18 were waited for; matrix products, arithmetic and copies ran while one was open for 16% of the time, Pallas kernels for 9%

profile of v5, /device:TPU:1, one launch (start us, length us, event | category | flops | bytes accessed | tf_op | source)
XLA Modules:
  0.0 226.0 jit_solution(14550064461360905225)
XLA Ops:
  0.0 1.4 collective-permute-start
  4.5 10.0 %attend.1 = (bf16[2,8,16,512]{3,2,1,0:T(8,128)(2,1)S(1)}, bf16[2,8,16,512]{3,2,1,0:T(8,128)(2,1)S(1)}) custom-call(s32[8]{0:T(128)S(1)} %copy-done.1, s32[8]{0:T(128)S(1)} %copy-done.2, s32[1]{0:T(128)} %bitcast.4.place_ref, bf16[8,4,16,576]{3,2,1,0:T(8,128)(2,1)S(1)} %bitcast.138, f32[8,1,576]{2,1,0:T(1,128)S(1)} %reshape.88.new_ref, ...), custom_call_target="tpu_custom_call" | custom-call | flops 1140850688 | bytes 9437184 | tf_op jit(solution)/shard_map/attend/pallas_call | solution.py:61
  14.6 3.1 %collective-permute-start.1 = (bf16[2,8,16,512]{3,2,1,0:T(8,128)(2,1)S(1)}, bf16[2,8,16,512]{3,2,1,0:T(8,128)(2,1)}, u32[]{:S(2)}, u32[]{:S(2)}) collective-permute-start(bf16[2,8,16,512]{3,2,1,0:T(8,128)(2,1)S(1)} %get-tuple-element.22), channel_id=1, source_target_pairs={{0,2},{2,0},{1,3},{3,1},{4,6},{6,4},{5,7},{7,5},{8,10},{10,8},{9,1... | collective-permute-start | bytes 786440 | tf_op jit(solution)/shard_map/ppermute | solution.py:267
  17.9 3.8 %broadcast_select_fusion = (bf16[448,2304]{1,0:T(8,128)(2,1)}, bf16[448,2304]{1,0:T(8,128)(2,1)S(1)}) fusion(bf16[448,2304]{1,0:T(8,128)(2,1)} %param.22, bf16[448,2304]{1,0:T(8,128)(2,1)} %param.21, pred[]{:T(512)S(6)} %eq.30), kind=kLoop, calls=%fused_computation.2 | loop fusion | flops 2064384 | bytes 8257537 | tf_op jit(solution)/shard_map/jit(_where)/select_n | solution.py:332
  22.0 1.2 copy.77
  23.7 2.0 fusion.8
  25.7 1.8 constant_dynamic-update-slice_fusion.1
  28.9 2.0 fusion.9
  30.9 2.0 fusion.11
  33.0 1.7 collective-permute-start.2
  34.7 2.2 collective-permute-start.3
  36.9 1.2 collective-permute-start.4
  39.2 3.3 %collective-permute-done.4.refs_3_ = bf16[16,4096]{1,0:T(8,128)(2,1)S(1)} collective-permute-done((bf16[16,4096]{1,0:T(8,128)(2,1)S(1)}, bf16[16,4096]{1,0:T(8,128)(2,1)S(1)}, u32[]{:S(2)}, u32[]{:S(2)}) %collective-permute-start.4) | collective-permute-done | bytes 131104 | tf_op jit(solution)/shard_map/ppermute | solution.py:249
  43.6 1.6 constant_dynamic-update-slice_fusion
  45.2 1.8 collective-permute-start.10
  47.0 1.2 collective-permute-start.11
  49.4 2.8 %collective-permute-done.6 = bf16[64,4096]{1,0:T(8,128)(2,1)S(1)} collective-permute-done((bf16[64,4096]{1,0:T(8,128)(2,1)S(1)}, bf16[64,4096]{1,0:T(8,128)(2,1)S(1)}, u32[]{:S(2)}, u32[]{:S(2)}) %collective-permute-start.6) | collective-permute-done | bytes 524320 | tf_op jit(solution)/shard_map/ppermute | solution.py:249
  52.2 1.2 fusion.40
  53.4 5.4 %collective-permute-done.10 = bf16[64,4096]{1,0:T(8,128)(2,1)S(1)} collective-permute-done((bf16[64,4096]{1,0:T(8,128)(2,1)S(1)}, bf16[64,4096]{1,0:T(8,128)(2,1)S(1)}, u32[]{:S(2)}, u32[]{:S(2)}) %collective-permute-start.10) | collective-permute-done | bytes 524320 | tf_op jit(solution)/shard_map/ppermute | solution.py:249
  58.8 1.2 fusion.41
  60.0 1.2 fusion.42
  61.7 2.3 %collective-permute-start.9 = (bf16[2,4,2,8,448]{4,3,2,1,0:T(8,128)(2,1)S(1)}, bf16[2,4,2,8,448]{4,3,2,1,0:T(8,128)(2,1)S(1)}, u32[]{:S(2)}, u32[]{:S(2)}) collective-permute-start(bf16[2,4,2,8,448]{4,3,2,1,0:T(8,128)(2,1)S(1)} %get-tuple-element.47), channel_id=1, source_target_pairs={{0,66},{1,67},{2,64},{3,65},{64,0},{65,1},{66,2},{67,3},{4,70},{5,... | collective-permute-start | bytes 344072 | tf_op jit(solution)/shard_map/ppermute | solution.py:263
  64.0 3.0 %collective-permute-start.12 = (bf16[2,4,2,8,448]{4,3,2,1,0:T(8,128)(2,1)S(1)}, bf16[2,4,2,8,448]{4,3,2,1,0:T(8,128)(2,1)S(1)}, u32[]{:S(2)}, u32[]{:S(2)}) collective-permute-start(bf16[2,4,2,8,448]{4,3,2,1,0:T(8,128)(2,1)S(1)} %get-tuple-element.48), channel_id=1, source_target_pairs={{0,2},{1,3},{2,0},{3,1},{64,66},{65,67},{66,64},{67,65},{4,6},{5,7... | collective-permute-start | bytes 344072 | tf_op jit(solution)/shard_map/ppermute | solution.py:263
  67.0 1.7 collective-permute-done.9
  68.7 3.8 %collective-permute-start.14 = (bf16[2,4,2,8,448]{4,3,2,1,0:T(8,128)(2,1)S(1)}, bf16[2,4,2,8,448]{4,3,2,1,0:T(8,128)(2,1)S(1)}, u32[]{:S(2)}, u32[]{:S(2)}) collective-permute-start(bf16[2,4,2,8,448]{4,3,2,1,0:T(8,128)(2,1)S(1)} %get-tuple-element.48), channel_id=1, source_target_pairs={{0,66},{1,67},{2,64},{3,65},{64,0},{65,1},{66,2},{67,3},{4,70},{5,... | collective-permute-start | bytes 344072 | tf_op jit(solution)/shard_map/ppermute | solution.py:263
  72.5 3.8 %collective-permute-done.13 = bf16[2,4,2,8,448]{4,3,2,1,0:T(8,128)(2,1)S(1)} collective-permute-done((bf16[2,4,2,8,448]{4,3,2,1,0:T(8,128)(2,1)S(1)}, bf16[2,4,2,8,448]{4,3,2,1,0:T(8,128)(2,1)S(1)}, u32[]{:S(2)}, u32[]{:S(2)}) %collective-permute-start.13) | collective-permute-done | bytes 114720 | tf_op jit(solution)/shard_map/ppermute | solution.py:263
  76.6 4.7 %collective-permute-start.15 = (bf16[2,4,4,2,8,448]{5,4,3,2,1,0:T(8,128)(2,1)S(1)}, bf16[2,4,4,2,8,448]{5,4,3,2,1,0:T(8,128)(2,1)S(1)}, u32[]{:S(2)}, u32[]{:S(2)}) collective-permute-start(bf16[2,4,4,2,8,448]{5,4,3,2,1,0:T(8,128)(2,1)S(1)} %get-tuple-element.44), channel_id=1, source_target_pairs={{0,1},{1,0},{2,3},{3,2},{4,5},{5,4},{6,7},{7,6},{8,9},{9,8},{10,11... | collective-permute-start | bytes 1376264 | tf_op jit(solution)/shard_map/ppermute | solution.py:267
  81.4 1.5 collective-permute-done.15
  83.2 3.0 %partial_sums.5 = (bf16[256,2432]{1,0:T(8,128)(2,1)S(1)}, bf16[256,2304]{1,0:T(8,128)(2,1)S(1)}) custom-call(bf16[4,4,64,448]{3,2,1,0:T(8,128)(2,1)S(1)} %bitcast.132, f32[1,448]{1,0:T(1,128)S(1)} %bitcast.139, bf16[448,2304]{1,0:T(8,128)(2,1)S(1)} %get-tuple-element.42.refs_4_.refs_3_.refs_2_, bf16[448,2304]{1,0:T(8,128)(2,1)} %collective-permute-done.16.refs_5_.refs_4_.refs_3_), custom_call_target="tpu_custom_call" | custom-call | flops 1086324736 | bytes 6553600 | tf_op jit(solution)/shard_map/partial_sums/pallas_call | solution.py:123
  86.2 2.7 %collective-permute-start.21 = (bf16[256,2304]{1,0:T(8,128)(2,1)S(1)}, bf16[256,2304]{1,0:T(8,128)(2,1)S(1)}, u32[]{:S(2)}, u32[]{:S(2)}) collective-permute-start(bf16[256,2304]{1,0:T(8,128)(2,1)S(1)} %get-tuple-element.30), channel_id=1, source_target_pairs={{0,48},{1,13},{2,50},{3,15},{4,52},{5,1},{6,54},{7,3},{8,56},{9,5}... | collective-permute-start | bytes 3538952 | tf_op jit(solution)/shard_map/ppermute | solution.py:249
  88.9 3.0 %partial_sums.4 = (bf16[256,2304]{1,0:T(8,128)(2,1)S(1)}, bf16[256,2432]{1,0:T(8,128)(2,1)S(1)}) custom-call(bf16[4,4,64,448]{3,2,1,0:T(8,128)(2,1)S(1)} %bitcast.133, bf16[4,4,64,448]{3,2,1,0:T(8,128)(2,1)S(1)} %bitcast.134, f32[1,448]{1,0:T(1,128)S(1)} %bitcast.140, bf16[448,2304]{1,0:T(8,128)(2,1)S(1)} %get-tuple-element.42.refs_4_.refs_3_.refs_2_, ...), custom_call_target="tpu_custom_call" | custom-call | flops 1086324736 | bytes 6553600 | tf_op jit(solution)/shard_map/partial_sums/pallas_call | solution.py:123
  92.0 1.5 collective-permute-start.18
  93.4 4.2 %partial_sums.3 = (bf16[256,2432]{1,0:T(8,128)(2,1)S(1)}, bf16[256,2304]{1,0:T(8,128)(2,1)S(1)}, bf16[256,2432]{1,0:T(8,128)(2,1)S(1)}, bf16[256,2304]{1,0:T(8,128)(2,1)S(1)}) custom-call(bf16[4,4,64,448]{3,2,1,0:T(8,128)(2,1)S(1)} %bitcast.135, bf16[4,4,64,448]{3,2,1,0:T(8,128)(2,1)S(1)} %bitcast.136, bf16[4,4,64,448]{3,2,1,0:T(8,128)(2,1)S(1)} %bitcast.137, ...), custom_call_target="tpu_custom_call" | custom-call | flops 2172649472 | bytes 8978432 | tf_op jit(solution)/shard_map/partial_sums/pallas_call | solution.py:123
  97.7 5.8 %collective-permute-done.19 = bf16[256,2432]{1,0:T(8,128)(2,1)S(1)} collective-permute-done((bf16[256,2432]{1,0:T(8,128)(2,1)S(1)}, bf16[256,2432]{1,0:T(8,128)(2,1)S(1)}, u32[]{:S(2)}, u32[]{:S(2)}) %collective-permute-start.19) | collective-permute-done | bytes 1245216 | tf_op jit(solution)/shard_map/ppermute | solution.py:249
  104.2 2.7 %collective-permute-start.22 = (bf16[256,2304]{1,0:T(8,128)(2,1)S(1)}, bf16[256,2304]{1,0:T(8,128)(2,1)S(1)}, u32[]{:S(2)}, u32[]{:S(2)}) collective-permute-start(bf16[256,2304]{1,0:T(8,128)(2,1)S(1)} %add_convert_fusion.1), channel_id=1, source_target_pairs={{0,48},{1,13},{2,50},{3,15},{4,52},{5,1},{6,54},{7,3},{8,56},{9,5}... | collective-permute-start | bytes 3538952 | tf_op jit(solution)/shard_map/ppermute | solution.py:249
  106.9 1.8 collective-permute-start.28
  108.7 7.5 %collective-permute-done.18.direct_c = bf16[256,2304]{1,0:T(8,128)(2,1)S(1)} collective-permute-done((bf16[256,2304]{1,0:T(8,128)(2,1)S(1)}, bf16[256,2304]{1,0:T(8,128)(2,1)S(1)}, u32[]{:S(2)}, u32[]{:S(2)}) %collective-permute-start.18) | collective-permute-done | bytes 1179680 | tf_op jit(solution)/shard_map/ppermute | solution.py:249
  116.1 11.9 %collective-permute-done.22.relay_c = bf16[256,2304]{1,0:T(8,128)(2,1)S(1)} collective-permute-done((bf16[256,2304]{1,0:T(8,128)(2,1)S(1)}, bf16[256,2304]{1,0:T(8,128)(2,1)S(1)}, u32[]{:S(2)}, u32[]{:S(2)}) %collective-permute-start.22) | collective-permute-done | bytes 1179680 | tf_op jit(solution)/shard_map/ppermute | solution.py:249
  128.0 1.4 collective-permute-done.20.relay_a
  129.5 1.3 merge.1
  130.7 2.7 %collective-permute-start.24 = (bf16[64,4736]{1,0:T(8,128)(2,1)}, bf16[64,4736]{1,0:T(8,128)(2,1)S(1)}, u32[]{:S(2)}, u32[]{:S(2)}) collective-permute-start(bf16[64,4736]{1,0:T(8,128)(2,1)} %get-tuple-element.33), channel_id=1, source_target_pairs={{0,12},{1,49},{2,14},{3,51},{4,0},{5,53},{6,2},{7,55},{8,4},{9,57}... | collective-permute-start | bytes 1818632 | tf_op jit(solution)/shard_map/ppermute | solution.py:249
  134.0 7.4 %collective-permute-done.23.refs_1_ = bf16[64,4736]{1,0:T(8,128)(2,1)S(1)} collective-permute-done((bf16[64,4736]{1,0:T(8,128)(2,1)}, bf16[64,4736]{1,0:T(8,128)(2,1)S(1)}, u32[]{:S(2)}, u32[]{:S(2)}) %collective-permute-start.23) | collective-permute-done | bytes 606240 | tf_op jit(solution)/shard_map/ppermute | solution.py:249
  141.4 5.9 %collective-permute-done.24.refs_2_ = bf16[64,4736]{1,0:T(8,128)(2,1)S(1)} collective-permute-done((bf16[64,4736]{1,0:T(8,128)(2,1)}, bf16[64,4736]{1,0:T(8,128)(2,1)S(1)}, u32[]{:S(2)}, u32[]{:S(2)}) %collective-permute-start.24) | collective-permute-done | bytes 606240 | tf_op jit(solution)/shard_map/ppermute | solution.py:249
  147.2 1.2 collective-permute-done.25.refs_3_
  149.1 1.7 collective-permute-start.26
  150.8 1.7 constant_dynamic-update-slice_fusion.3
  152.7 2.9 %collective-permute-start.29 = (bf16[32,4608]{1,0:T(8,128)(2,1)S(1)}, bf16[32,4608]{1,0:T(8,128)(2,1)S(1)}, u32[]{:S(2)}, u32[]{:S(2)}) collective-permute-start(bf16[32,4608]{1,0:T(8,128)(2,1)S(1)} %activate.1.refs_0_), channel_id=1, source_target_pairs={{0,48},{1,13},{2,50},{3,15},{4,52},{5,1},{6,54},{7,3},{8,56},{9,5}... | collective-permute-start | bytes 884744 | tf_op jit(solution)/shard_map/ppermute | solution.py:249
  156.3 1.7 constant_dynamic-update-slice_fusion.2
  158.0 7.9 %collective-permute-done.27.refs_1_ = bf16[32,4608]{1,0:T(8,128)(2,1)S(1)} collective-permute-done((bf16[32,4608]{1,0:T(8,128)(2,1)S(1)}, bf16[32,4608]{1,0:T(8,128)(2,1)S(1)}, u32[]{:S(2)}, u32[]{:S(2)}) %collective-permute-start.27) | collective-permute-done | bytes 294944 | tf_op jit(solution)/shard_map/ppermute | solution.py:249
  166.0 2.7 %collective-permute-start.33 = (bf16[64,4608]{1,0:T(8,128)(2,1)S(1)}, bf16[64,4608]{1,0:T(8,128)(2,1)S(1)}, u32[]{:S(2)}, u32[]{:S(2)}) collective-permute-start(bf16[64,4608]{1,0:T(8,128)(2,1)S(1)} %join.4), channel_id=1, source_target_pairs={{0,12},{1,49},{2,14},{3,51},{4,0},{5,53},{6,2},{7,55},{8,4},{9,57}... | collective-permute-start | bytes 1769480 | tf_op jit(solution)/shard_map/ppermute | solution.py:249
  168.8 2.7 %collective-permute-start.34 = (bf16[64,4608]{1,0:T(8,128)(2,1)S(1)}, bf16[64,4608]{1,0:T(8,128)(2,1)S(1)}, u32[]{:S(2)}, u32[]{:S(2)}) collective-permute-start(bf16[64,4608]{1,0:T(8,128)(2,1)S(1)} %join.5), channel_id=1, source_target_pairs={{0,12},{1,49},{2,14},{3,51},{4,0},{5,53},{6,2},{7,55},{8,4},{9,57}... | collective-permute-start | bytes 1769480 | tf_op jit(solution)/shard_map/ppermute | solution.py:249
  171.5 1.3 fusion.7
  172.8 1.3 fusion.6
  174.1 2.2 collective-permute-done.31
  176.3 5.6 %collective-permute-done.34 = bf16[64,4608]{1,0:T(8,128)(2,1)S(1)} collective-permute-done((bf16[64,4608]{1,0:T(8,128)(2,1)S(1)}, bf16[64,4608]{1,0:T(8,128)(2,1)S(1)}, u32[]{:S(2)}, u32[]{:S(2)}) %collective-permute-start.34) | collective-permute-done | bytes 589856 | tf_op jit(solution)/shard_map/ppermute | solution.py:249
  181.9 3.4 %collective-permute-start.36 = (bf16[64,4608]{1,0:T(8,128)(2,1)S(1)}, bf16[64,4608]{1,0:T(8,128)(2,1)S(1)}, u32[]{:S(2)}, u32[]{:S(2)}) collective-permute-start(bf16[64,4608]{1,0:T(8,128)(2,1)S(1)} %collective-permute-done.34), channel_id=1, source_target_pairs={{0,12},{1,49},{2,14},{3,51},{4,0},{5,53},{6,2},{7,55},{8,4},{9,57}... | collective-permute-start | bytes 1769480 | tf_op jit(solution)/shard_map/ppermute | solution.py:249
  185.3 1.3 fusion.5
  186.6 1.3 fusion.4
  187.9 1.3 fusion.3
  189.2 1.3 fusion.2
  190.5 1.3 fusion.1
  192.1 1.3 fusion
  194.1 19.3 %all_to_all.5 = bf16[64,8,448]{2,1,0:T(8,128)(2,1)S(1)} all-to-all(bf16[64,8,448]{2,1,0:T(8,128)(2,1)S(1)} %bitcast.143), channel_id=1, replica_groups=mesh['role'=2,'grp'=16,'yh'=2,'core'=2] {'role','grp','yh'}, dimensions={0} | all-to-all | bytes 917504 | tf_op jit(solution)/shard_map/all_to_all | solution.py:416
  213.7 11.5 %all_gather.3 = bf16[32,7168]{1,0:T(8,128)(2,1)S(1)} all-gather(bf16[8,7168]{1,0:T(8,128)(2,1)S(1)} %reshape.87), channel_id=1, replica_groups=mesh['role'=2,'grp'=16,'yh'=2,'core'=2] {'yh','core'}, dimensions={0}, use_global_device_ids=true | all-gather | bytes 573440 | tf_op jit(solution)/shard_map/all_gather | solution.py:420
  (100 shorter events, 14.9 us)
Async XLA Ops:
  0.0 28.9 %collective-permute-start = (bf16[16,512,128]{2,1,0:T(8,128)(2,1)}, bf16[16,512,128]{2,1,0:T(8,128)(2,1)}, u32[]{:S(2)}, u32[]{:S(2)}) collective-permute-start(bf16[16,512,128]{2,1,0:T(8,128)(2,1)} %param.18), channel_id=1, source_target_pairs={{0,1},{1,0},{2,3},{3,2},{4,5},{5,4},{6,7},{7,6},{8,9},{9,8},{10,11... | collective-permute-start | bytes 6291464 | tf_op jit(solution)/shard_map/ppermute | solution.py:267
  2.1 1.1 copy-start
  3.2 0.7 copy-start.1
  3.9 0.7 copy-start.2
  14.6 12.9 %collective-permute-start.1 = (bf16[2,8,16,512]{3,2,1,0:T(8,128)(2,1)S(1)}, bf16[2,8,16,512]{3,2,1,0:T(8,128)(2,1)}, u32[]{:S(2)}, u32[]{:S(2)}) collective-permute-start(bf16[2,8,16,512]{3,2,1,0:T(8,128)(2,1)S(1)} %get-tuple-element.22), channel_id=1, source_target_pairs={{0,2},{2,0},{1,3},{3,1},{4,6},{6,4},{5,7},{7,5},{8,10},{10,8},{9,1... | collective-permute-start | bytes 786440 | tf_op jit(solution)/shard_map/ppermute | solution.py:267
  17.7 25.9 %collective-permute-start.5 = (bf16[2048,448]{0,1:T(8,128)(2,1)}, bf16[2048,448]{0,1:T(8,128)(2,1)}, u32[]{:S(2)}, u32[]{:S(2)}) collective-permute-start(bf16[2048,448]{0,1:T(8,128)(2,1)} %param.19), channel_id=1, source_target_pairs={{0,1},{1,0},{2,3},{3,2},{4,5},{5,4},{6,7},{7,6},{8,9},{9,8},{10,11... | collective-permute-start | bytes 5505032 | tf_op jit(solution)/shard_map/ppermute | solution.py:267
  21.7 61.4 %collective-permute-start.16 = (bf16[448,2304]{1,0:T(8,128)(2,1)}, bf16[448,2304]{1,0:T(8,128)(2,1)}, u32[]{:S(2)}, u32[]{:S(2)}) collective-permute-start(bf16[448,2304]{1,0:T(8,128)(2,1)} %get-tuple-element.41), channel_id=1, source_target_pairs={{0,1},{1,0},{2,3},{3,2},{4,5},{5,4},{6,7},{7,6},{8,9},{9,8},{10,11... | collective-permute-start | bytes 6193160 | tf_op jit(solution)/shard_map/ppermute | solution.py:267
  25.7 2.8 %copy-start.3 = (bf16[16,512,128]{2,1,0:T(8,128)(2,1)S(1)}, bf16[16,512,128]{2,1,0:T(8,128)(2,1)}, u32[]{:S(2)}) copy-start(bf16[16,512,128]{2,1,0:T(8,128)(2,1)} %param.18) | copy-start | bytes 6291460
  33.0 6.2 %collective-permute-start.2 = (bf16[16,4096]{1,0:T(8,128)(2,1)S(1)}, bf16[16,4096]{1,0:T(8,128)(2,1)S(1)}, u32[]{:S(2)}, u32[]{:S(2)}) collective-permute-start(bf16[16,4096]{1,0:T(8,128)(2,1)S(1)} %maximum_select_fusion.1.refs_0_), channel_id=1, source_target_pairs={{0,16},{1,5},{2,18},{3,7},{4,20},{5,9},{6,22},{7,11},{8,24},{9,13}... | collective-permute-start | bytes 393224 | tf_op jit(solution)/shard_map/ppermute | solution.py:249
  34.7 4.5 %collective-permute-start.3 = (bf16[16,4096]{1,0:T(8,128)(2,1)S(1)}, bf16[16,4096]{1,0:T(8,128)(2,1)S(1)}, u32[]{:S(2)}, u32[]{:S(2)}) collective-permute-start(bf16[16,4096]{1,0:T(8,128)(2,1)S(1)} %maximum_select_fusion.1.refs_0_), channel_id=1, source_target_pairs={{0,48},{1,13},{2,50},{3,15},{4,52},{5,1},{6,54},{7,3},{8,56},{9,5}... | collective-permute-start | bytes 393224 | tf_op jit(solution)/shard_map/ppermute | solution.py:249
  36.9 5.6 %collective-permute-start.4 = (bf16[16,4096]{1,0:T(8,128)(2,1)S(1)}, bf16[16,4096]{1,0:T(8,128)(2,1)S(1)}, u32[]{:S(2)}, u32[]{:S(2)}) collective-permute-start(bf16[16,4096]{1,0:T(8,128)(2,1)S(1)} %maximum_select_fusion.1.refs_0_), channel_id=1, source_target_pairs={{0,32},{1,9},{2,34},{3,11},{4,36},{5,13},{6,38},{7,15},{8,40},{9,1... | collective-permute-start | bytes 393224 | tf_op jit(solution)/shard_map/ppermute | solution.py:249
  42.6 9.6 %collective-permute-start.6 = (bf16[64,4096]{1,0:T(8,128)(2,1)S(1)}, bf16[64,4096]{1,0:T(8,128)(2,1)S(1)}, u32[]{:S(2)}, u32[]{:S(2)}) collective-permute-start(bf16[64,4096]{1,0:T(8,128)(2,1)S(1)} %join.3), channel_id=1, source_target_pairs={{0,4},{1,17},{2,6},{3,19},{4,8},{5,21},{6,10},{7,23},{8,12},{9,25}... | collective-permute-start | bytes 1572872 | tf_op jit(solution)/shard_map/ppermute | solution.py:249
  45.2 13.6 %collective-permute-start.10 = (bf16[64,4096]{1,0:T(8,128)(2,1)S(1)}, bf16[64,4096]{1,0:T(8,128)(2,1)S(1)}, u32[]{:S(2)}, u32[]{:S(2)}) collective-permute-start(bf16[64,4096]{1,0:T(8,128)(2,1)S(1)} %join.3), channel_id=1, source_target_pairs={{0,12},{1,49},{2,14},{3,51},{4,0},{5,53},{6,2},{7,55},{8,4},{9,57}... | collective-permute-start | bytes 1572872 | tf_op jit(solution)/shard_map/ppermute | solution.py:249
  47.0 12.9 %collective-permute-start.11 = (bf16[64,4096]{1,0:T(8,128)(2,1)S(1)}, bf16[64,4096]{1,0:T(8,128)(2,1)S(1)}, u32[]{:S(2)}, u32[]{:S(2)}) collective-permute-start(bf16[64,4096]{1,0:T(8,128)(2,1)S(1)} %join.3), channel_id=1, source_target_pairs={{0,8},{1,33},{2,10},{3,35},{4,12},{5,37},{6,14},{7,39},{8,0},{9,41... | collective-permute-start | bytes 1572872 | tf_op jit(solution)/shard_map/ppermute | solution.py:249
  61.2 5.7 %collective-permute-start.8 = (bf16[2,4,2,8,448]{4,3,2,1,0:T(8,128)(2,1)S(1)}, bf16[2,4,2,8,448]{4,3,2,1,0:T(8,128)(2,1)S(1)}, u32[]{:S(2)}, u32[]{:S(2)}) collective-permute-start(bf16[2,4,2,8,448]{4,3,2,1,0:T(8,128)(2,1)S(1)} %get-tuple-element.47), channel_id=1, source_target_pairs={{0,64},{1,65},{2,66},{3,67},{64,2},{65,3},{66,0},{67,1},{4,68},{5,... | collective-permute-start | bytes 344072 | tf_op jit(solution)/shard_map/ppermute | solution.py:263
  61.7 6.9 %collective-permute-start.9 = (bf16[2,4,2,8,448]{4,3,2,1,0:T(8,128)(2,1)S(1)}, bf16[2,4,2,8,448]{4,3,2,1,0:T(8,128)(2,1)S(1)}, u32[]{:S(2)}, u32[]{:S(2)}) collective-permute-start(bf16[2,4,2,8,448]{4,3,2,1,0:T(8,128)(2,1)S(1)} %get-tuple-element.47), channel_id=1, source_target_pairs={{0,66},{1,67},{2,64},{3,65},{64,0},{65,1},{66,2},{67,3},{4,70},{5,... | collective-permute-start | bytes 344072 | tf_op jit(solution)/shard_map/ppermute | solution.py:263
  64.0 12.4 %collective-permute-start.7 = (bf16[2,4,2,8,448]{4,3,2,1,0:T(8,128)(2,1)S(1)}, bf16[2,4,2,8,448]{4,3,2,1,0:T(8,128)(2,1)S(1)}, u32[]{:S(2)}, u32[]{:S(2)}) collective-permute-start(bf16[2,4,2,8,448]{4,3,2,1,0:T(8,128)(2,1)S(1)} %get-tuple-element.47), channel_id=1, source_target_pairs={{0,2},{1,3},{2,0},{3,1},{64,66},{65,67},{66,64},{67,65},{4,6},{5,7... | collective-permute-start | bytes 344072 | tf_op jit(solution)/shard_map/ppermute | solution.py:263
  64.0 12.4 %collective-permute-start.12 = (bf16[2,4,2,8,448]{4,3,2,1,0:T(8,128)(2,1)S(1)}, bf16[2,4,2,8,448]{4,3,2,1,0:T(8,128)(2,1)S(1)}, u32[]{:S(2)}, u32[]{:S(2)}) collective-permute-start(bf16[2,4,2,8,448]{4,3,2,1,0:T(8,128)(2,1)S(1)} %get-tuple-element.48), channel_id=1, source_target_pairs={{0,2},{1,3},{2,0},{3,1},{64,66},{65,67},{66,64},{67,65},{4,6},{5,7... | collective-permute-start | bytes 344072 | tf_op jit(solution)/shard_map/ppermute | solution.py:263
  67.0 9.4 %collective-permute-start.13 = (bf16[2,4,2,8,448]{4,3,2,1,0:T(8,128)(2,1)S(1)}, bf16[2,4,2,8,448]{4,3,2,1,0:T(8,128)(2,1)S(1)}, u32[]{:S(2)}, u32[]{:S(2)}) collective-permute-start(bf16[2,4,2,8,448]{4,3,2,1,0:T(8,128)(2,1)S(1)} %get-tuple-element.48), channel_id=1, source_target_pairs={{0,64},{1,65},{2,66},{3,67},{64,2},{65,3},{66,0},{67,1},{4,68},{5,... | collective-permute-start | bytes 344072 | tf_op jit(solution)/shard_map/ppermute | solution.py:263
  68.7 7.7 %collective-permute-start.14 = (bf16[2,4,2,8,448]{4,3,2,1,0:T(8,128)(2,1)S(1)}, bf16[2,4,2,8,448]{4,3,2,1,0:T(8,128)(2,1)S(1)}, u32[]{:S(2)}, u32[]{:S(2)}) collective-permute-start(bf16[2,4,2,8,448]{4,3,2,1,0:T(8,128)(2,1)S(1)} %get-tuple-element.48), channel_id=1, source_target_pairs={{0,66},{1,67},{2,64},{3,65},{64,0},{65,1},{66,2},{67,3},{4,70},{5,... | collective-permute-start | bytes 344072 | tf_op jit(solution)/shard_map/ppermute | solution.py:263
  72.5 8.9 %copy-start.4 = (bf16[448]{0:T(512)(128)(2,1)S(1)}, bf16[448]{0:T(512)(128)(2,1)}, u32[]{:S(2)}) copy-start(bf16[448]{0:T(512)(128)(2,1)} %param.20) | copy-start | bytes 2692
  76.6 6.3 %collective-permute-start.15 = (bf16[2,4,4,2,8,448]{5,4,3,2,1,0:T(8,128)(2,1)S(1)}, bf16[2,4,4,2,8,448]{5,4,3,2,1,0:T(8,128)(2,1)S(1)}, u32[]{:S(2)}, u32[]{:S(2)}) collective-permute-start(bf16[2,4,4,2,8,448]{5,4,3,2,1,0:T(8,128)(2,1)S(1)} %get-tuple-element.44), channel_id=1, source_target_pairs={{0,1},{1,0},{2,3},{3,2},{4,5},{5,4},{6,7},{7,6},{8,9},{9,8},{10,11... | collective-permute-start | bytes 1376264 | tf_op jit(solution)/shard_map/ppermute | solution.py:267
  86.2 17.3 %collective-permute-start.19 = (bf16[256,2432]{1,0:T(8,128)(2,1)S(1)}, bf16[256,2432]{1,0:T(8,128)(2,1)S(1)}, u32[]{:S(2)}, u32[]{:S(2)}) collective-permute-start(bf16[256,2432]{1,0:T(8,128)(2,1)S(1)} %get-tuple-element.28), channel_id=1, source_target_pairs={{0,16},{1,5},{2,18},{3,7},{4,20},{5,9},{6,22},{7,11},{8,24},{9,13}... | collective-permute-start | bytes 3735560 | tf_op jit(solution)/shard_map/ppermute | solution.py:249
  86.2 17.6 %collective-permute-start.21 = (bf16[256,2304]{1,0:T(8,128)(2,1)S(1)}, bf16[256,2304]{1,0:T(8,128)(2,1)S(1)}, u32[]{:S(2)}, u32[]{:S(2)}) collective-permute-start(bf16[256,2304]{1,0:T(8,128)(2,1)S(1)} %get-tuple-element.30), channel_id=1, source_target_pairs={{0,48},{1,13},{2,50},{3,15},{4,52},{5,1},{6,54},{7,3},{8,56},{9,5}... | collective-permute-start | bytes 3538952 | tf_op jit(solution)/shard_map/ppermute | solution.py:249
  91.9 24.2 %collective-permute-start.17 = (bf16[256,2432]{1,0:T(8,128)(2,1)S(1)}, bf16[256,2432]{1,0:T(8,128)(2,1)S(1)}, u32[]{:S(2)}, u32[]{:S(2)}) collective-permute-start(bf16[256,2432]{1,0:T(8,128)(2,1)S(1)} %get-tuple-element.25), channel_id=1, source_target_pairs={{0,48},{1,13},{2,50},{3,15},{4,52},{5,1},{6,54},{7,3},{8,56},{9,5}... | collective-permute-start | bytes 3735560 | tf_op jit(solution)/shard_map/ppermute | solution.py:249
  92.0 24.1 %collective-permute-start.18 = (bf16[256,2304]{1,0:T(8,128)(2,1)S(1)}, bf16[256,2304]{1,0:T(8,128)(2,1)S(1)}, u32[]{:S(2)}, u32[]{:S(2)}) collective-permute-start(bf16[256,2304]{1,0:T(8,128)(2,1)S(1)} %get-tuple-element.26), channel_id=1, source_target_pairs={{0,16},{1,5},{2,18},{3,7},{4,20},{5,9},{6,22},{7,11},{8,24},{9,13}... | collective-permute-start | bytes 3538952 | tf_op jit(solution)/shard_map/ppermute | solution.py:249
  103.8 25.7 %collective-permute-start.20 = (bf16[256,2432]{1,0:T(8,128)(2,1)S(1)}, bf16[256,2432]{1,0:T(8,128)(2,1)S(1)}, u32[]{:S(2)}, u32[]{:S(2)}) collective-permute-start(bf16[256,2432]{1,0:T(8,128)(2,1)S(1)} %add_convert_fusion), channel_id=1, source_target_pairs={{0,16},{1,5},{2,18},{3,7},{4,20},{5,9},{6,22},{7,11},{8,24},{9,13}... | collective-permute-start | bytes 3735560 | tf_op jit(solution)/shard_map/ppermute | solution.py:249
  104.2 23.9 %collective-permute-start.22 = (bf16[256,2304]{1,0:T(8,128)(2,1)S(1)}, bf16[256,2304]{1,0:T(8,128)(2,1)S(1)}, u32[]{:S(2)}, u32[]{:S(2)}) collective-permute-start(bf16[256,2304]{1,0:T(8,128)(2,1)S(1)} %add_convert_fusion.1), channel_id=1, source_target_pairs={{0,48},{1,13},{2,50},{3,15},{4,52},{5,1},{6,54},{7,3},{8,56},{9,5}... | collective-permute-start | bytes 3538952 | tf_op jit(solution)/shard_map/ppermute | solution.py:249
  106.9 49.4 %collective-permute-start.28 = (bf16[2304,448]{0,1:T(8,128)(2,1)}, bf16[2304,448]{0,1:T(8,128)(2,1)}, u32[]{:S(2)}, u32[]{:S(2)}) collective-permute-start(bf16[2304,448]{0,1:T(8,128)(2,1)} %param.23), channel_id=1, source_target_pairs={{0,1},{1,0},{2,3},{3,2},{4,5},{5,4},{6,7},{7,6},{8,9},{9,8},{10,11... | collective-permute-start | bytes 6193160 | tf_op jit(solution)/shard_map/ppermute | solution.py:267
  130.7 10.6 %collective-permute-start.23 = (bf16[64,4736]{1,0:T(8,128)(2,1)}, bf16[64,4736]{1,0:T(8,128)(2,1)S(1)}, u32[]{:S(2)}, u32[]{:S(2)}) collective-permute-start(bf16[64,4736]{1,0:T(8,128)(2,1)} %get-tuple-element.32), channel_id=1, source_target_pairs={{0,4},{1,17},{2,6},{3,19},{4,8},{5,21},{6,10},{7,23},{8,12},{9,25}... | collective-permute-start | bytes 1818632 | tf_op jit(solution)/shard_map/ppermute | solution.py:249
  130.7 16.5 %collective-permute-start.24 = (bf16[64,4736]{1,0:T(8,128)(2,1)}, bf16[64,4736]{1,0:T(8,128)(2,1)S(1)}, u32[]{:S(2)}, u32[]{:S(2)}) collective-permute-start(bf16[64,4736]{1,0:T(8,128)(2,1)} %get-tuple-element.33), channel_id=1, source_target_pairs={{0,12},{1,49},{2,14},{3,51},{4,0},{5,53},{6,2},{7,55},{8,4},{9,57}... | collective-permute-start | bytes 1818632 | tf_op jit(solution)/shard_map/ppermute | solution.py:249
  133.4 15.0 %collective-permute-start.25 = (bf16[64,4736]{1,0:T(8,128)(2,1)S(1)}, bf16[64,4736]{1,0:T(8,128)(2,1)S(1)}, u32[]{:S(2)}, u32[]{:S(2)}) collective-permute-start(bf16[64,4736]{1,0:T(8,128)(2,1)S(1)} %get-tuple-element.34), channel_id=1, source_target_pairs={{0,8},{1,33},{2,10},{3,35},{4,12},{5,37},{6,14},{7,39},{8,0},{9,41... | collective-permute-start | bytes 1818632 | tf_op jit(solution)/shard_map/ppermute | solution.py:249
  149.1 3.4 %collective-permute-start.26 = (bf16[32,4608]{1,0:T(8,128)(2,1)S(1)}, bf16[32,4608]{1,0:T(8,128)(2,1)S(1)}, u32[]{:S(2)}, u32[]{:S(2)}) collective-permute-start(bf16[32,4608]{1,0:T(8,128)(2,1)S(1)} %get-tuple-element.36), channel_id=1, source_target_pairs={{0,1},{1,0},{2,3},{3,2},{4,5},{5,4},{6,7},{7,6},{8,9},{9,8},{10,11... | collective-permute-start | bytes 884744 | tf_op jit(solution)/shard_map/ppermute | solution.py:267
  152.7 16.0 %collective-permute-start.29 = (bf16[32,4608]{1,0:T(8,128)(2,1)S(1)}, bf16[32,4608]{1,0:T(8,128)(2,1)S(1)}, u32[]{:S(2)}, u32[]{:S(2)}) collective-permute-start(bf16[32,4608]{1,0:T(8,128)(2,1)S(1)} %activate.1.refs_0_), channel_id=1, source_target_pairs={{0,48},{1,13},{2,50},{3,15},{4,52},{5,1},{6,54},{7,3},{8,56},{9,5}... | collective-permute-start | bytes 884744 | tf_op jit(solution)/shard_map/ppermute | solution.py:249
  155.6 13.1 %collective-permute-start.30 = (bf16[32,4608]{1,0:T(8,128)(2,1)S(1)}, bf16[32,4608]{1,0:T(8,128)(2,1)S(1)}, u32[]{:S(2)}, u32[]{:S(2)}) collective-permute-start(bf16[32,4608]{1,0:T(8,128)(2,1)S(1)} %activate.1.refs_0_), channel_id=1, source_target_pairs={{0,32},{1,9},{2,34},{3,11},{4,36},{5,13},{6,38},{7,15},{8,40},{9,1... | collective-permute-start | bytes 884744 | tf_op jit(solution)/shard_map/ppermute | solution.py:249
  155.7 10.2 %collective-permute-start.27 = (bf16[32,4608]{1,0:T(8,128)(2,1)S(1)}, bf16[32,4608]{1,0:T(8,128)(2,1)S(1)}, u32[]{:S(2)}, u32[]{:S(2)}) collective-permute-start(bf16[32,4608]{1,0:T(8,128)(2,1)S(1)} %activate.1.refs_0_), channel_id=1, source_target_pairs={{0,16},{1,5},{2,18},{3,7},{4,20},{5,9},{6,22},{7,11},{8,24},{9,13}... | collective-permute-start | bytes 884744 | tf_op jit(solution)/shard_map/ppermute | solution.py:249
  166.0 10.3 %collective-permute-start.31 = (bf16[64,4608]{1,0:T(8,128)(2,1)S(1)}, bf16[64,4608]{1,0:T(8,128)(2,1)S(1)}, u32[]{:S(2)}, u32[]{:S(2)}) collective-permute-start(bf16[64,4608]{1,0:T(8,128)(2,1)S(1)} %join.4), channel_id=1, source_target_pairs={{0,4},{1,17},{2,6},{3,19},{4,8},{5,21},{6,10},{7,23},{8,12},{9,25}... | collective-permute-start | bytes 1769480 | tf_op jit(solution)/shard_map/ppermute | solution.py:249
  166.0 21.8 %collective-permute-start.33 = (bf16[64,4608]{1,0:T(8,128)(2,1)S(1)}, bf16[64,4608]{1,0:T(8,128)(2,1)S(1)}, u32[]{:S(2)}, u32[]{:S(2)}) collective-permute-start(bf16[64,4608]{1,0:T(8,128)(2,1)S(1)} %join.4), channel_id=1, source_target_pairs={{0,12},{1,49},{2,14},{3,51},{4,0},{5,53},{6,2},{7,55},{8,4},{9,57}... | collective-permute-start | bytes 1769480 | tf_op jit(solution)/shard_map/ppermute | solution.py:249
  168.8 17.8 %collective-permute-start.32 = (bf16[64,4608]{1,0:T(8,128)(2,1)S(1)}, bf16[64,4608]{1,0:T(8,128)(2,1)S(1)}, u32[]{:S(2)}, u32[]{:S(2)}) collective-permute-start(bf16[64,4608]{1,0:T(8,128)(2,1)S(1)} %join.5), channel_id=1, source_target_pairs={{0,4},{1,17},{2,6},{3,19},{4,8},{5,21},{6,10},{7,23},{8,12},{9,25}... | collective-permute-start | bytes 1769480 | tf_op jit(solution)/shard_map/ppermute | solution.py:249
  168.8 13.0 %collective-permute-start.34 = (bf16[64,4608]{1,0:T(8,128)(2,1)S(1)}, bf16[64,4608]{1,0:T(8,128)(2,1)S(1)}, u32[]{:S(2)}, u32[]{:S(2)}) collective-permute-start(bf16[64,4608]{1,0:T(8,128)(2,1)S(1)} %join.5), channel_id=1, source_target_pairs={{0,12},{1,49},{2,14},{3,51},{4,0},{5,53},{6,2},{7,55},{8,4},{9,57}... | collective-permute-start | bytes 1769480 | tf_op jit(solution)/shard_map/ppermute | solution.py:249
  176.3 14.2 %collective-permute-start.35 = (bf16[64,4608]{1,0:T(8,128)(2,1)S(1)}, bf16[64,4608]{1,0:T(8,128)(2,1)S(1)}, u32[]{:S(2)}, u32[]{:S(2)}) collective-permute-start(bf16[64,4608]{1,0:T(8,128)(2,1)S(1)} %collective-permute-done.31), channel_id=1, source_target_pairs={{0,4},{1,17},{2,6},{3,19},{4,8},{5,21},{6,10},{7,23},{8,12},{9,25}... | collective-permute-start | bytes 1769480 | tf_op jit(solution)/shard_map/ppermute | solution.py:249
  181.9 10.2 %collective-permute-start.36 = (bf16[64,4608]{1,0:T(8,128)(2,1)S(1)}, bf16[64,4608]{1,0:T(8,128)(2,1)S(1)}, u32[]{:S(2)}, u32[]{:S(2)}) collective-permute-start(bf16[64,4608]{1,0:T(8,128)(2,1)S(1)} %collective-permute-done.34), channel_id=1, source_target_pairs={{0,12},{1,49},{2,14},{3,51},{4,0},{5,53},{6,2},{7,55},{8,4},{9,57}... | collective-permute-start | bytes 1769480 | tf_op jit(solution)/shard_map/ppermute | solution.py:249

commit v6 on v5

--- a/solution.py
+++ b/solution.py
@@ -18,14 +18,17 @@
 
 
 def attend_kernel(
-    scale, latent, members_ref, lengths_ref, place_ref, q_ref, new_ref, kv_ref, near_ref, far_ref
+    scale, latent, plan_ref, q_ref, new_ref, kv_ref, near_ref, far_ref
 ):
     token = pl.program_id(0)
-    length = lengths_ref[members_ref[token]]
-    place = place_ref[0]
+    tokens = pl.num_programs(0)
+    length = plan_ref[tokens + plan_ref[token]]
+    place = plan_ref[2 * tokens]
     queries = jnp.concatenate([q_ref[0, place ^ i] for i in range(4)], axis=0)
     cache = kv_ref[0]
-    newest = new_ref[0]
+    newest = wide(new_ref[...])
+    picked = lax.broadcasted_iota(jnp.int32, newest.shape, 0) == token
+    newest = jnp.sum(jnp.where(picked, newest, 0.0), axis=0, keepdims=True)
     scores = scale * jnp.dot(queries, cache, preferred_element_type=jnp.float32)
     own = scale * jnp.sum(queries.astype(jnp.float32) * newest, axis=1, keepdims=True)
     usable = lax.broadcasted_iota(jnp.int32, scores.shape, 1) < length
@@ -49,14 +52,14 @@
     ctx = kv_cache.shape[1]
     block = heads // 4
     grid_spec = pltpu.PrefetchScalarGridSpec(
-        num_scalar_prefetch=3,
+        num_scalar_prefetch=1,
         grid=(tokens,),
         in_specs=[
-            pl.BlockSpec((1, 4, block, kv), lambda t, m, n, p: (t, 0, 0, 0)),
-            pl.BlockSpec((1, 1, kv), lambda t, m, n, p: (t, 0, 0)),
-            pl.BlockSpec((1, kv, ctx), lambda t, m, n, p: (m[t], 0, 0)),
+            pl.BlockSpec((1, 4, block, kv), lambda t, m: (t, 0, 0, 0)),
+            pl.BlockSpec((tokens, kv), lambda t, m: (0, 0)),
+            pl.BlockSpec((1, kv, ctx), lambda t, m: (m[t], 0, 0)),
         ],
-        out_specs=[pl.BlockSpec((2, 1, block, latent), lambda t, m, n, p: (0, t, 0, 0))] * 2,
+        out_specs=[pl.BlockSpec((2, 1, block, latent), lambda t, m: (0, t, 0, 0))] * 2,
     )
     return pl.pallas_call(
         functools.partial(attend_kernel, scale, latent),
@@ -70,11 +73,9 @@
         ),
         name="attend",
     )(
-        members,
-        lengths,
-        place,
+        jnp.concatenate([members, lengths, place]),
         q_latent.reshape(tokens, 4, block, kv),
-        kv_new.astype(jnp.float32)[:, None, :],
+        kv_new,
         jnp.swapaxes(kv_cache, 1, 2),
     )
 
@@ -189,6 +190,66 @@
     count, cols = blocks[0].shape
     shape = jax.ShapeDtypeStruct((len(blocks) * count, cols), blocks[0].dtype)
     return whole_call(join_kernel, "join", [shape], blocks, 4 * shape.size)[0]
+
+
+def pair_dot_kernel(*refs):
+    *blocks, weights, out = refs
+    half, width = weights.shape[1], out.shape[1]
+    step = half // 4 if half % 512 == 0 else half // 3
+    total = 0.0
+    for side in range(2):
+        for k in range(0, half, step):
+            cols = slice(side * half + k, side * half + k + step)
+            rows = jnp.concatenate([b[:, cols] for b in blocks])
+            total += lax.dot_general(
+                rows,
+                weights[side * width : (side + 1) * width, k : k + step],
+                (((1,), (1,)), ((), ())),
+                preferred_element_type=jnp.float32,
+            )
+    out[...] = total
+
+
+def pair_dot(blocks, weights):
+    count = sum(b.shape[0] for b in blocks)
+    width, half = weights.shape[0] // 2, weights.shape[1]
+    shape = jax.ShapeDtypeStruct((count, width), jnp.float32)
+    return whole_call(pair_dot_kernel, "pair_dot", [shape], (*blocks, weights), 4 * width * half)[0]
+
+
+def head_values_kernel(yh_ref, near, far, *refs):
+    *weights, out = refs
+    yh = yh_ref[0]
+    count, heads = near.shape[1:3]
+    width = weights[0].shape[2]
+    for c, weight in enumerate(weights):
+        own, other = wide(near[c]), wide(far[c])
+        rows = jnp.concatenate([jnp.where(yh == 0, own, other), jnp.where(yh == 0, other, own)])
+        rows = jnp.swapaxes(rows, 0, 1).astype(jnp.bfloat16)
+        for h in range(heads):
+            start = (c * heads + h) * width
+            out[:, start : start + width] = jnp.dot(
+                rows[h], weight[h], preferred_element_type=jnp.float32
+            ).astype(out.dtype)
+
+
+def head_values(yh, near, far, weights):
+    tokens, heads = near.shape[1:3]
+    shape = jax.ShapeDtypeStruct((2 * tokens, 2 * heads * weights[0].shape[2]), jnp.bfloat16)
+    return pl.pallas_call(
+        head_values_kernel,
+        out_shape=shape,
+        in_specs=[pl.BlockSpec(memory_space=pltpu.SMEM)]
+        + [pl.BlockSpec(memory_space=pltpu.VMEM)] * 4,
+        out_specs=pl.BlockSpec(memory_space=pltpu.VMEM),
+        compiler_params=pltpu.CompilerParams(vmem_limit_bytes=VMEM_LIMIT),
+        cost_estimate=pl.CostEstimate(
+            flops=2 * shape.size * near.shape[3],
+            bytes_accessed=4 * weights[0].size,
+            transcendentals=0,
+        ),
+        name="head_values",
+    )(yh.astype(jnp.int32)[None], near, far, *weights)
 
 
 def settle_kernel(model_width, hidden, *refs):
@@ -325,19 +386,8 @@
     score_scale = (value_width + kv - latent) ** (-0.5)
 
     uv_pair = (w_uv, swap(w_uv, "core"))
-    o_chip = jnp.concatenate([w_o, swap(w_o, "core")], axis=0)
-    down_chip = jnp.concatenate([w_down, swap(w_down, "core")], axis=0)
-    in_pair = (
-        jnp.where(core == 0, w_gate, w_up),
-        swap(jnp.where(core == 0, w_up, w_gate), "core"),
-    )
-
-    residual = lax.dynamic_index_in_dim(
-        hidden_in.reshape(4, 4, 2, 2, tokens, width), core, 3, keepdims=False
-    )
-    residual = jnp.where(core == 0, jnp.swapaxes(residual, 0, 1), residual)
-    residual = wide(relative(relative(residual, place_2, 0), place_1, 1))
-
+    o_pair = join(*(jnp.swapaxes(w, 0, 1) for w in (w_o, swap(w_o, "core"))))
+    down_pair = join(*(jnp.swapaxes(w, 0, 1) for w in (w_down, swap(w_down, "core"))))
     near, far = attend(
         q_latent,
         kv_new,
@@ -349,34 +399,29 @@
         latent,
     )
     far = swap(far, "yh")
-
-    def head_values(context):
-        parts = [
-            jnp.einsum("thl,hlv->thv", c, w, preferred_element_type=jnp.float32)
-            for c, w in zip(context, uv_pair)
-        ]
-        return jnp.stack(parts, axis=1).astype(jnp.bfloat16).reshape(tokens, -1)
-
-    near, far = head_values(near), head_values(far)
-    values = jnp.where(
-        yh == 0, jnp.concatenate([near, far]), jnp.concatenate([far, near])
-    )
+    values = head_values(yh, near, far, uv_pair)
+    values, hidden_in, w_gate, w_up = lax.optimization_barrier(
+        (values, hidden_in, w_gate, w_up)
+    )
+    in_pair = (
+        jnp.where(core == 0, w_gate, w_up),
+        swap(jnp.where(core == 0, w_up, w_gate), "core"),
+    )
+
+    residual = lax.dynamic_index_in_dim(
+        hidden_in.reshape(4, 4, 2, 2, tokens, width), core, 3, keepdims=False
+    )
+    residual = jnp.where(core == 0, jnp.swapaxes(residual, 0, 1), residual)
+    residual = wide(relative(relative(residual, place_2, 0), place_1, 1))
+
+
     pieces = gather(join(*gather(values, shift_1)), shift_2)
-    rows, stream = [], []
-    for half in range(2):
-        attn_part = jnp.stack(
-            [
-                jnp.dot(v, o_chip, preferred_element_type=jnp.float32)
-                for v in pieces[2 * half : 2 * half + 2]
-            ]
-        ).reshape(2, 4, 2, tokens, width)
-        shared = 0.5 * residual[2 * half : 2 * half + 2] + attn_part
-        sent = shared.astype(jnp.bfloat16)
-        behind, ahead, across = (shift_y(sent, s) for s in SHIFTS[1:])
-        stream.append(shared + wide(across))
-        rows.append(jnp.stack([stream[-1], add(behind, ahead)]).astype(jnp.bfloat16))
-    stream = jnp.concatenate(stream)
-    rows = jnp.concatenate(rows, axis=1)
+    attn_part = jnp.concatenate([pair_dot(p, o_pair) for p in (pieces[:1], pieces[1:])]).reshape(4, 4, 2, tokens, width)
+    shared = 0.5 * residual + attn_part
+    sent = shared.astype(jnp.bfloat16)
+    behind, ahead, across = (shift_y(sent, s) for s in SHIFTS[1:])
+    stream = shared + wide(across)
+    rows = jnp.stack([stream, add(behind, ahead)]).astype(jnp.bfloat16)
     rows = jnp.stack([rows, jnp.swapaxes(swap(rows, "core"), 1, 2)])
     rows = jnp.transpose(rows, (2, 3, 0, 1, 4, 5, 6)).reshape(4, 4, 8 * tokens, width)
 
@@ -401,9 +446,13 @@
     behind_low, ahead_high = shift_2(low, 1), shift_2(high, -1)
     behind_high, ahead_low = shift_2(high, 1), shift_2(low, -1)
     far_low, far_high = shift_2(behind_low, 1), shift_2(ahead_high, -1)
-    pieces = (low, high, behind_low, behind_high, ahead_low, ahead_high, far_low, far_high)
-    down = jnp.stack(
-        [jnp.dot(p, down_chip, preferred_element_type=jnp.float32) for p in pieces]
+    pieces = (
+        (low, high),
+        (behind_low, behind_high, ahead_low, ahead_high),
+        (far_low, far_high),
+    )
+    down = jnp.concatenate(
+        [pair_dot(p, down_pair) for p in pieces]
     ).reshape(4, 4, 2, 2, tokens, width)
     at_home = jnp.arange(2)[None, None, :, None, None] == yh
     down = jnp.stack([down[:, :, 0] + jnp.where(at_home, stream, 0.0), down[:, :, 1]])
@@ -411,13 +460,18 @@
     down = absolute(absolute(down, place_2, 1), place_1, 2)
     down = jnp.where(core == 0, jnp.swapaxes(down, 1, 2), down)
     role = lax.axis_index("role")
-    down = jnp.where(role == 0, down, down[::-1])
-    down = down.reshape(2 * groups * 2, tokens, width)
+    down = jnp.where(role == 0, down, down[::-1]).reshape(2, groups, 1, 2 * tokens, width)
+    down = jnp.broadcast_to(down, (2, groups, 2, 2 * tokens, width))
+    down = down.reshape(2 * groups * 2, 2 * tokens, width)
     landed = lax.all_to_all(down, ("role", "grp", "yh"), split_axis=0, concat_axis=0)
-    landed = landed.reshape(2, groups, 2, tokens, width)
+    landed = landed.reshape(2, groups, 2, 2 * tokens, width)
     result = jnp.sum(wide(landed), axis=(0, 2)).astype(jnp.bfloat16)
-    result = jnp.swapaxes(result, 0, 1).reshape(tokens, model_width)
-    return lax.all_gather(result, ("yh", "core"), axis=0, tiled=True)
+    result = jnp.swapaxes(result, 0, 1).reshape(2, tokens, model_width)
+    other = swap(result, "core")
+    result = jnp.stack(
+        [jnp.where(core == 0, result, other), jnp.where(core == 0, other, result)], axis=1
+    )
+    return result.reshape(4 * tokens, model_width)
 
 
 def solution(mesh):

time: 227 us -> 206 us (0.907)
  matrix products: 21.5 us -> 0 us
  blocking collectives: 30.8 us -> 21 us
  Pallas kernels: 22.4 us -> 31 us
  waiting for transfers between devices: 76.5 us -> 83.6 us
  local copies, waits for them, and re-layouts: 13.5 us -> 7.92 us
    dot_general x16 -> x0, matrix products: 21.5 us -> none  [the longest x8 10.4 us: body(): jnp.dot(p, down_chip, preferred_element_type=jnp.float32)]
    pallas_call x4 -> x11, Pallas kernels: 0.75 us -> 13.8 us  [whole_call(): pl.pallas_call(kernel, out_shape=out_shapes, in_specs=[pl.BlockSpec(memor...]
    all_gather x1 -> x0, blocking collectives: 11.5 us -> none  [body(): return lax.all_gather(result, ('yh', 'core'), axis=0, tiled=True)]
    ppermute x7 -> x8, starting transfers between devices: 13.2 us -> 19.3 us  [swap(): return lax.ppermute(value, axis, [(0, 1), (1, 0)])]
    ppermute x6 -> x3, starting transfers between devices: 9.5 us -> 4.43 us  [shift_y(): lax.ppermute(value, ('role', 'yh', 'core'), [(p, moved(p)) for p in range...]
    pallas_call x3, Pallas kernels: 10.2 us -> 5.46 us  [partial_sums(): pl.pallas_call(functools.partial(partial_kernel, jobs), grid=(1,), in_spe...]
    concatenate x2 -> x0, local copies, waits for them, and re-layouts: 3.34 us -> none  [the longest x1 1.73 us: body(): down_chip = jnp.concatenate([w_down, swap(w_down, 'core')], axis=0)]
    ppermute x7 -> x8, waiting for transfers between devices: 1.55 us -> 4.53 us  [swap(): return lax.ppermute(value, axis, [(0, 1), (1, 0)])]
  transfers between devices with their start and end apart: 37 -> 35, of which waited for: 18 -> 25; matrix products, arithmetic and copies ran while one was open for 16% -> 2% of each run, Pallas kernels for 9% -> 12%
where the time goes in v6:
time: 206 us; the launch traced here: 205 us
  waiting for transfers between devices  83.6 us (41%)
  starting transfers between devices  55.8 us (27%)
  Pallas kernels  31 us (15%)
  blocking collectives  21 us (10%)
  local copies, waits for them, and re-layouts  7.92 us (4%)
  other arithmetic  5.53 us (3%)
    ppermute x24, waiting for transfers between devices, shift(): return lax.ppermute(value, ('grp', 'yh', 'core'), pairs)  71.7 us
    ppermute x24, starting transfers between devices, shift(): return lax.ppermute(value, ('grp', 'yh', 'core'), pairs)  32.1 us
    all_to_all x1, blocking collectives, body(): lax.all_to_all(down, ('role', 'grp', 'yh'), split_axis=0, concat_axis=0)  21 us
    ppermute x8, starting transfers between devices, swap(): return lax.ppermute(value, axis, [(0, 1), (1, 0)])  19.3 us
    pallas_call x11, Pallas kernels, whole_call(): pl.pallas_call(kernel, out_shape=out_shapes, in_specs=[pl.BlockSpec(memor...  13.8 us
    pallas_call x1, Pallas kernels, attend(): pl.pallas_call(functools.partial(attend_kernel, scale, latent), grid_spec...  10 us
    ppermute x3, waiting for transfers between devices, shift_y(): lax.ppermute(value, ('role', 'yh', 'core'), [(p, moved(p)) for p in range...  7.34 us
    unnamed x28, local copies, waits for them, and re-layouts  6.11 us
  transfers between devices with their start and end apart: 35, of which 25 were waited for; matrix products, arithmetic and copies ran while one was open for 2% of the time, Pallas kernels for 12%

profile of v6, /device:TPU:1, one launch (start us, length us, event | category | flops | bytes accessed | tf_op | source)
XLA Modules:
  0.0 205.5 jit_solution(6868858400390670644)
XLA Ops:
  0.0 1.4 collective-permute-start.1
  2.2 1.1 copy-done.5
  4.0 10.0 %attend.1 = (bf16[2,8,16,512]{3,2,1,0:T(8,128)(2,1)S(1)}, bf16[2,8,16,512]{3,2,1,0:T(8,128)(2,1)S(1)}) custom-call(s32[17]{0:T(128)S(1)} %pad_add_fusion.plan_ref, bf16[8,4,16,576]{3,2,1,0:T(8,128)(2,1)S(1)} %bitcast.62, bf16[8,576]{1,0:T(8,128)(2,1)S(1)} %copy-done.6, bf16[8,576,1024]{2,1,0:T(8,128)(2,1)} %bitcast.66), custom_call_target="tpu_custom_call" | custom-call | flops 1140850688 | bytes 9437184 | tf_op jit(solution)/shard_map/attend/pallas_call | solution.py:64
  14.0 3.1 %collective-permute-start = (bf16[2,8,16,512]{3,2,1,0:T(8,128)(2,1)S(1)}, bf16[2,8,16,512]{3,2,1,0:T(8,128)(2,1)S(1)}, u32[]{:S(2)}, u32[]{:S(2)}) collective-permute-start(bf16[2,8,16,512]{3,2,1,0:T(8,128)(2,1)S(1)} %get-tuple-element.26), channel_id=1, source_target_pairs={{0,2},{2,0},{1,3},{3,1},{4,6},{6,4},{5,7},{7,5},{8,10},{10,8},{9,1... | collective-permute-start | bytes 786440 | tf_op jit(solution)/shard_map/ppermute | solution.py:328
  17.1 1.5 copy-done.4
  18.6 1.9 join.6.refs_1_.refs_3_
  20.5 1.8 copy-done
  23.8 1.7 collective-permute-start.2
  25.5 2.2 %collective-permute-start.3 = (bf16[16,4096]{1,0:T(8,128)(2,1)S(1)}, bf16[16,4096]{1,0:T(8,128)(2,1)S(1)}, u32[]{:S(2)}, u32[]{:S(2)}) collective-permute-start(bf16[16,4096]{1,0:T(8,128)(2,1)S(1)} %head_values.1.refs_0_), channel_id=1, source_target_pairs={{0,48},{1,13},{2,50},{3,15},{4,52},{5,1},{6,54},{7,3},{8,56},{9,5}... | collective-permute-start | bytes 393224 | tf_op jit(solution)/shard_map/ppermute | solution.py:310
  27.7 1.2 collective-permute-start.4
  29.2 2.5 %broadcast_select_fusion = (bf16[448,2304]{1,0:T(8,128)(2,1)S(1)}, bf16[448,2304]{1,0:T(8,128)(2,1)S(1)}) fusion(bf16[448,2304]{1,0:T(8,128)(2,1)} %param.22, bf16[448,2304]{1,0:T(8,128)(2,1)} %param.21, pred[]{:T(512)S(6)} %eq.28), kind=kLoop, calls=%fused_computation.2 | loop fusion | flops 2064384 | bytes 8257537 | tf_op jit(solution)/shard_map/jit(_where)/select_n | solution.py:408
  31.9 1.4 collective-permute-start.13
  33.4 1.0 collective-permute-start.6
  34.4 1.8 collective-permute-start.7
  36.1 1.2 collective-permute-start.8
  37.6 1.2 pair_dot.5
  38.8 4.2 %collective-permute-done.6.refs_0_ = bf16[64,4096]{1,0:T(8,128)(2,1)S(1)} collective-permute-done((bf16[64,4096]{1,0:T(8,128)(2,1)S(1)}, bf16[64,4096]{1,0:T(8,128)(2,1)S(1)}, u32[]{:S(2)}, u32[]{:S(2)}) %collective-permute-start.6) | collective-permute-done | bytes 524320 | tf_op jit(solution)/shard_map/ppermute | solution.py:310
  43.0 4.9 %collective-permute-done.7.refs_1_ = bf16[64,4096]{1,0:T(8,128)(2,1)S(1)} collective-permute-done((bf16[64,4096]{1,0:T(8,128)(2,1)S(1)}, bf16[64,4096]{1,0:T(8,128)(2,1)S(1)}, u32[]{:S(2)}, u32[]{:S(2)}) %collective-permute-start.7) | collective-permute-done | bytes 524320 | tf_op jit(solution)/shard_map/ppermute | solution.py:310
  47.9 1.7 collective-permute-done.8.refs_2_
  49.6 1.2 pair_dot.6
  51.0 1.4 collective-permute-start.10
  52.3 1.5 collective-permute-start.11
  53.8 1.6 collective-permute-start.9
  55.4 2.1 %collective-permute-done.10 = bf16[4,4,2,8,448]{4,3,2,0,1:T(8,128)(2,1)S(1)} collective-permute-done((bf16[4,4,2,8,448]{4,3,2,0,1:T(8,128)(2,1)S(1)}, bf16[4,4,2,8,448]{4,3,2,0,1:T(8,128)(2,1)S(1)}, u32[]{:S(2)}, u32[]{:S(2)}) %collective-permute-start.10) | collective-permute-done | bytes 229408 | tf_op jit(solution)/shard_map/ppermute | solution.py:324
  57.5 1.5 collective-permute-done.11
  59.1 3.8 %collective-permute-done.9 = bf16[4,4,2,8,448]{4,3,2,0,1:T(8,128)(2,1)S(1)} collective-permute-done((bf16[4,4,2,8,448]{4,3,2,0,1:T(8,128)(2,1)S(1)}, bf16[4,4,2,8,448]{4,3,2,0,1:T(8,128)(2,1)S(1)}, u32[]{:S(2)}, u32[]{:S(2)}) %collective-permute-start.9) | collective-permute-done | bytes 229408 | tf_op jit(solution)/shard_map/ppermute | solution.py:324
  63.0 5.1 %collective-permute-start.12 = (bf16[2,4,4,2,8,448]{5,4,3,2,1,0:T(8,128)(2,1)S(1)}, bf16[2,4,4,2,8,448]{5,4,3,2,1,0:T(8,128)(2,1)S(1)}, u32[]{:S(2)}, u32[]{:S(2)}) collective-permute-start(bf16[2,4,4,2,8,448]{5,4,3,2,1,0:T(8,128)(2,1)S(1)} %pad_maximum_fusion.2), channel_id=1, source_target_pairs={{0,1},{1,0},{2,3},{3,2},{4,5},{5,4},{6,7},{7,6},{8,9},{9,8},{10,11... | collective-permute-start | bytes 1376264 | tf_op jit(solution)/shard_map/ppermute | solution.py:328
  68.2 1.4 collective-permute-done.12
  69.9 1.4 partial_sums.5
  71.8 2.5 %collective-permute-start.18 = (bf16[256,2304]{1,0:T(8,128)(2,1)S(1)}, bf16[256,2304]{1,0:T(8,128)(2,1)S(1)}, u32[]{:S(2)}, u32[]{:S(2)}) collective-permute-start(bf16[256,2304]{1,0:T(8,128)(2,1)S(1)} %get-tuple-element.38), channel_id=1, source_target_pairs={{0,48},{1,13},{2,50},{3,15},{4,52},{5,1},{6,54},{7,3},{8,56},{9,5}... | collective-permute-start | bytes 3538952 | tf_op jit(solution)/shard_map/ppermute | solution.py:310
  74.4 1.4 partial_sums.4
  75.8 1.3 collective-permute-start.14
  77.3 2.6 %partial_sums.3 = (bf16[256,2432]{1,0:T(8,128)(2,1)S(1)}, bf16[256,2304]{1,0:T(8,128)(2,1)S(1)}, bf16[256,2432]{1,0:T(8,128)(2,1)S(1)}, bf16[256,2304]{1,0:T(8,128)(2,1)S(1)}) custom-call(bf16[4,4,64,448]{3,2,1,0:T(8,128)(2,1)S(1)} %bitcast.57, bf16[4,4,64,448]{3,2,1,0:T(8,128)(2,1)S(1)} %bitcast.58, bf16[4,4,64,448]{3,2,1,0:T(8,128)(2,1)S(1)} %bitcast.59, ...), custom_call_target="tpu_custom_call" | custom-call | flops 2172649472 | bytes 8978432 | tf_op jit(solution)/shard_map/partial_sums/pallas_call | solution.py:124
  80.0 8.7 %collective-permute-done.16 = bf16[256,2432]{1,0:T(8,128)(2,1)S(1)} collective-permute-done((bf16[256,2432]{1,0:T(8,128)(2,1)S(1)}, bf16[256,2432]{1,0:T(8,128)(2,1)S(1)}, u32[]{:S(2)}, u32[]{:S(2)}) %collective-permute-start.16) | collective-permute-done | bytes 1245216 | tf_op jit(solution)/shard_map/ppermute | solution.py:310
  89.4 2.7 %collective-permute-start.19 = (bf16[256,2304]{1,0:T(8,128)(2,1)S(1)}, bf16[256,2304]{1,0:T(8,128)(2,1)S(1)}, u32[]{:S(2)}, u32[]{:S(2)}) collective-permute-start(bf16[256,2304]{1,0:T(8,128)(2,1)S(1)} %add_convert_fusion.1), channel_id=1, source_target_pairs={{0,48},{1,13},{2,50},{3,15},{4,52},{5,1},{6,54},{7,3},{8,56},{9,5}... | collective-permute-start | bytes 3538952 | tf_op jit(solution)/shard_map/ppermute | solution.py:310
  92.1 9.2 %collective-permute-done.15.direct_c = bf16[256,2304]{1,0:T(8,128)(2,1)S(1)} collective-permute-done((bf16[256,2304]{1,0:T(8,128)(2,1)S(1)}, bf16[256,2304]{1,0:T(8,128)(2,1)S(1)}, u32[]{:S(2)}, u32[]{:S(2)}) %collective-permute-start.15) | collective-permute-done | bytes 1179680 | tf_op jit(solution)/shard_map/ppermute | solution.py:310
  101.3 12.2 %collective-permute-done.19.relay_c = bf16[256,2304]{1,0:T(8,128)(2,1)S(1)} collective-permute-done((bf16[256,2304]{1,0:T(8,128)(2,1)S(1)}, bf16[256,2304]{1,0:T(8,128)(2,1)S(1)}, u32[]{:S(2)}, u32[]{:S(2)}) %collective-permute-start.19) | collective-permute-done | bytes 1179680 | tf_op jit(solution)/shard_map/ppermute | solution.py:310
  113.5 1.2 collective-permute-done.17.relay_a
  116.1 2.3 %collective-permute-start.21 = (bf16[64,4736]{1,0:T(8,128)(2,1)S(1)}, bf16[64,4736]{1,0:T(8,128)(2,1)S(1)}, u32[]{:S(2)}, u32[]{:S(2)}) collective-permute-start(bf16[64,4736]{1,0:T(8,128)(2,1)S(1)} %get-tuple-element.41), channel_id=1, source_target_pairs={{0,12},{1,49},{2,14},{3,51},{4,0},{5,53},{6,2},{7,55},{8,4},{9,57}... | collective-permute-start | bytes 1818632 | tf_op jit(solution)/shard_map/ppermute | solution.py:310
  118.4 1.1 collective-permute-start.22
  119.5 2.0 collective-permute-start.27
  121.5 4.5 %collective-permute-done.20.refs_1_ = bf16[64,4736]{1,0:T(8,128)(2,1)S(1)} collective-permute-done((bf16[64,4736]{1,0:T(8,128)(2,1)S(1)}, bf16[64,4736]{1,0:T(8,128)(2,1)S(1)}, u32[]{:S(2)}, u32[]{:S(2)}) %collective-permute-start.20) | collective-permute-done | bytes 606240 | tf_op jit(solution)/shard_map/ppermute | solution.py:310
  126.0 5.8 %collective-permute-done.21.refs_2_ = bf16[64,4736]{1,0:T(8,128)(2,1)S(1)} collective-permute-done((bf16[64,4736]{1,0:T(8,128)(2,1)S(1)}, bf16[64,4736]{1,0:T(8,128)(2,1)S(1)}, u32[]{:S(2)}, u32[]{:S(2)}) %collective-permute-start.21) | collective-permute-done | bytes 606240 | tf_op jit(solution)/shard_map/ppermute | solution.py:310
  131.9 1.8 collective-permute-done.22.refs_3_
  134.3 2.2 %collective-permute-start.23 = (bf16[32,4608]{1,0:T(8,128)(2,1)S(1)}, bf16[32,4608]{1,0:T(8,128)(2,1)S(1)}, u32[]{:S(2)}, u32[]{:S(2)}) collective-permute-start(bf16[32,4608]{1,0:T(8,128)(2,1)S(1)} %get-tuple-element.44), channel_id=1, source_target_pairs={{0,1},{1,0},{2,3},{3,2},{4,5},{5,4},{6,7},{7,6},{8,9},{9,8},{10,11... | collective-permute-start | bytes 884744 | tf_op jit(solution)/shard_map/ppermute | solution.py:328
  136.5 1.2 collective-permute-done.23.theirs
  137.9 1.8 collective-permute-start.25
  139.6 1.2 collective-permute-start.26
  140.9 5.6 %collective-permute-done.25.refs_0_ = bf16[32,4608]{1,0:T(8,128)(2,1)S(1)} collective-permute-done((bf16[32,4608]{1,0:T(8,128)(2,1)S(1)}, bf16[32,4608]{1,0:T(8,128)(2,1)S(1)}, u32[]{:S(2)}, u32[]{:S(2)}) %collective-permute-start.25) | collective-permute-done | bytes 294944 | tf_op jit(solution)/shard_map/ppermute | solution.py:310
  147.1 2.3 %collective-permute-start.31 = (bf16[64,4608]{1,0:T(8,128)(2,1)S(1)}, bf16[64,4608]{1,0:T(8,128)(2,1)}, u32[]{:S(2)}, u32[]{:S(2)}) collective-permute-start(bf16[64,4608]{1,0:T(8,128)(2,1)S(1)} %join.8.refs_1_), channel_id=1, source_target_pairs={{0,12},{1,49},{2,14},{3,51},{4,0},{5,53},{6,2},{7,55},{8,4},{9,57}... | collective-permute-start | bytes 1769480 | tf_op jit(solution)/shard_map/ppermute | solution.py:310
  150.3 1.5 collective-permute-start.29
  151.8 1.3 collective-permute-start.30
  153.0 3.3 %collective-permute-done.31.refs_3_ = bf16[64,4608]{1,0:T(8,128)(2,1)} collective-permute-done((bf16[64,4608]{1,0:T(8,128)(2,1)S(1)}, bf16[64,4608]{1,0:T(8,128)(2,1)}, u32[]{:S(2)}, u32[]{:S(2)}) %collective-permute-start.31) | collective-permute-done | bytes 589856 | tf_op jit(solution)/shard_map/ppermute | solution.py:310
  156.3 3.5 %collective-permute-start.33 = (bf16[64,4608]{1,0:T(8,128)(2,1)}, bf16[64,4608]{1,0:T(8,128)(2,1)}, u32[]{:S(2)}, u32[]{:S(2)}) collective-permute-start(bf16[64,4608]{1,0:T(8,128)(2,1)} %collective-permute-done.31.refs_3_), channel_id=1, source_target_pairs={{0,12},{1,49},{2,14},{3,51},{4,0},{5,53},{6,2},{7,55},{8,4},{9,57}... | collective-permute-start | bytes 1769480 | tf_op jit(solution)/shard_map/ppermute | solution.py:310
  160.7 1.8 join.9.refs_2_.refs_4_
  162.5 1.4 pair_dot.7
  163.9 3.1 %collective-permute-done.29.refs_1_ = bf16[64,4608]{1,0:T(8,128)(2,1)} collective-permute-done((bf16[64,4608]{1,0:T(8,128)(2,1)S(1)}, bf16[64,4608]{1,0:T(8,128)(2,1)}, u32[]{:S(2)}, u32[]{:S(2)}) %collective-permute-start.29) | collective-permute-done | bytes 589856 | tf_op jit(solution)/shard_map/ppermute | solution.py:310
  167.0 3.0 %pair_dot.8 = f32[256,448]{1,0:T(8,128)S(1)} custom-call(bf16[64,4608]{1,0:T(8,128)(2,1)} %collective-permute-done.28.refs_0_, bf16[64,4608]{1,0:T(8,128)(2,1)} %collective-permute-done.29.refs_1_, bf16[64,4608]{1,0:T(8,128)(2,1)} %collective-permute-done.30.refs_2_, bf16[64,4608]{1,0:T(8,128)(2,1)} %collective-permute-done.31.refs_3_, ...), custom_call_target="tpu_custom_call" | custom-call | flops 4128768 | bytes 4128768 | tf_op jit(solution)/shard_map/pair_dot/pallas_call | solution.py:171
  170.0 3.3 %collective-permute-done.32.refs_0_ = bf16[64,4608]{1,0:T(8,128)(2,1)} collective-permute-done((bf16[64,4608]{1,0:T(8,128)(2,1)}, bf16[64,4608]{1,0:T(8,128)(2,1)}, u32[]{:S(2)}, u32[]{:S(2)}) %collective-permute-start.32) | collective-permute-done | bytes 589856 | tf_op jit(solution)/shard_map/ppermute | solution.py:310
  173.3 2.6 %pair_dot.9 = f32[128,448]{1,0:T(8,128)S(1)} custom-call(bf16[64,4608]{1,0:T(8,128)(2,1)} %collective-permute-done.32.refs_0_, bf16[64,4608]{1,0:T(8,128)(2,1)} %collective-permute-done.33.refs_1_, bf16[896,2304]{1,0:T(8,128)(2,1)S(1)} %join.9.refs_2_.refs_4_), custom_call_target="tpu_custom_call" | custom-call | flops 4128768 | bytes 4128768 | tf_op jit(solution)/shard_map/pair_dot/pallas_call | solution.py:171
  176.0 0.9 copy-done.8
  177.7 21.0 %all_to_all.5 = bf16[64,16,448]{2,1,0:T(8,128)(2,1)S(1)} all-to-all(bf16[64,16,448]{2,1,0:T(8,128)(2,1)S(1)} %bitcast.68), channel_id=1, replica_groups=mesh['role'=2,'grp'=16,'yh'=2,'core'=2] {'role','grp','yh'}, dimensions={0} | all-to-all | bytes 1835008 | tf_op jit(solution)/shard_map/all_to_all | solution.py:466
  199.4 4.1 %collective-permute-start.34 = (bf16[2,8,7168]{2,1,0:T(8,128)(2,1)S(1)}, bf16[2,8,7168]{2,1,0:T(8,128)(2,1)S(1)}, u32[]{:S(2)}, u32[]{:S(2)}) collective-permute-start(bf16[2,8,7168]{2,1,0:T(8,128)(2,1)S(1)} %reshape.74), channel_id=1, source_target_pairs={{0,1},{1,0},{2,3},{3,2},{4,5},{5,4},{6,7},{7,6},{8,9},{9,8},{10,11... | collective-permute-start | bytes 688136 | tf_op jit(solution)/shard_map/ppermute | solution.py:328
  203.5 1.1 collective-permute-done.34
  (98 shorter events, 12.8 us)
Async XLA Ops:
  0.0 23.0 %collective-permute-start.1 = (bf16[16,512,128]{2,1,0:T(8,128)(2,1)}, bf16[16,512,128]{2,1,0:T(8,128)(2,1)S(1)}, u32[]{:S(2)}, u32[]{:S(2)}) collective-permute-start(bf16[16,512,128]{2,1,0:T(8,128)(2,1)} %refs_0_.1), channel_id=1, source_target_pairs={{0,1},{1,0},{2,3},{3,2},{4,5},{5,4},{6,7},{7,6},{8,9},{9,8},{10,11... | collective-permute-start | bytes 6291464 | tf_op jit(solution)/shard_map/ppermute | solution.py:328
  1.4 15.7 %collective-permute-start.5 = (bf16[2048,448]{0,1:T(8,128)(2,1)}, bf16[2048,448]{0,1:T(8,128)(2,1)}, u32[]{:S(2)}, u32[]{:S(2)}) collective-permute-start(bf16[2048,448]{0,1:T(8,128)(2,1)} %param.19), channel_id=1, source_target_pairs={{0,1},{1,0},{2,3},{3,2},{4,5},{5,4},{6,7},{7,6},{8,9},{9,8},{10,11... | collective-permute-start | bytes 5505032 | tf_op jit(solution)/shard_map/ppermute | solution.py:328
  2.2 1.1 copy-start.5
  3.3 0.7 copy-start.6
  14.0 9.0 %collective-permute-start = (bf16[2,8,16,512]{3,2,1,0:T(8,128)(2,1)S(1)}, bf16[2,8,16,512]{3,2,1,0:T(8,128)(2,1)S(1)}, u32[]{:S(2)}, u32[]{:S(2)}) collective-permute-start(bf16[2,8,16,512]{3,2,1,0:T(8,128)(2,1)S(1)} %get-tuple-element.26), channel_id=1, source_target_pairs={{0,2},{2,0},{1,3},{3,1},{4,6},{6,4},{5,7},{7,5},{8,10},{10,8},{9,1... | collective-permute-start | bytes 786440 | tf_op jit(solution)/shard_map/ppermute | solution.py:328
  17.1 1.5 copy-start.4
  18.6 4.4 %copy-start.2 = (bf16[16,512,128]{2,1,0:T(8,128)(2,1)S(1)}, bf16[16,512,128]{2,1,0:T(8,128)(2,1)}, u32[]{:S(2)}) copy-start(bf16[16,512,128]{2,1,0:T(8,128)(2,1)} %refs_0_.1) | copy-start | bytes 6291460
  20.5 1.8 copy-start
  23.0 5.9 %copy-start.10 = (bf16[512,448]{0,1:T(8,128)(2,1)S(1)}, bf16[512,448]{0,1:T(8,128)(2,1)}, u32[]{:S(2)}) copy-start(bf16[512,448]{0,1:T(8,128)(2,1)} %param.17) | copy-start | bytes 1376260
  23.8 9.5 %collective-permute-start.2 = (bf16[16,4096]{1,0:T(8,128)(2,1)S(1)}, bf16[16,4096]{1,0:T(8,128)(2,1)S(1)}, u32[]{:S(2)}, u32[]{:S(2)}) collective-permute-start(bf16[16,4096]{1,0:T(8,128)(2,1)S(1)} %head_values.1.refs_0_), channel_id=1, source_target_pairs={{0,16},{1,5},{2,18},{3,7},{4,20},{5,9},{6,22},{7,11},{8,24},{9,13}... | collective-permute-start | bytes 393224 | tf_op jit(solution)/shard_map/ppermute | solution.py:310
  25.5 7.8 %collective-permute-start.3 = (bf16[16,4096]{1,0:T(8,128)(2,1)S(1)}, bf16[16,4096]{1,0:T(8,128)(2,1)S(1)}, u32[]{:S(2)}, u32[]{:S(2)}) collective-permute-start(bf16[16,4096]{1,0:T(8,128)(2,1)S(1)} %head_values.1.refs_0_), channel_id=1, source_target_pairs={{0,48},{1,13},{2,50},{3,15},{4,52},{5,1},{6,54},{7,3},{8,56},{9,5}... | collective-permute-start | bytes 393224 | tf_op jit(solution)/shard_map/ppermute | solution.py:310
  27.7 5.6 %collective-permute-start.4 = (bf16[16,4096]{1,0:T(8,128)(2,1)S(1)}, bf16[16,4096]{1,0:T(8,128)(2,1)S(1)}, u32[]{:S(2)}, u32[]{:S(2)}) collective-permute-start(bf16[16,4096]{1,0:T(8,128)(2,1)S(1)} %head_values.1.refs_0_), channel_id=1, source_target_pairs={{0,32},{1,9},{2,34},{3,11},{4,36},{5,13},{6,38},{7,15},{8,40},{9,1... | collective-permute-start | bytes 393224 | tf_op jit(solution)/shard_map/ppermute | solution.py:310
  31.7 5.9 %copy-start.1 = (bf16[896,2048]{1,0:T(8,128)(2,1)S(1)}, bf16[896,2048]{1,0:T(8,128)(2,1)}, u32[]{:S(2)}) copy-start(bf16[896,2048]{1,0:T(8,128)(2,1)} %copy-done) | copy-start | bytes 11010052
  31.9 38.0 %collective-permute-start.13 = (bf16[448,2304]{1,0:T(8,128)(2,1)S(1)}, bf16[448,2304]{1,0:T(8,128)(2,1)S(1)}, u32[]{:S(2)}, u32[]{:S(2)}) collective-permute-start(bf16[448,2304]{1,0:T(8,128)(2,1)S(1)} %get-tuple-element.45), channel_id=1, source_target_pairs={{0,1},{1,0},{2,3},{3,2},{4,5},{5,4},{6,7},{7,6},{8,9},{9,8},{10,11... | collective-permute-start | bytes 6193160 | tf_op jit(solution)/shard_map/ppermute | solution.py:328
  33.4 9.6 %collective-permute-start.6 = (bf16[64,4096]{1,0:T(8,128)(2,1)S(1)}, bf16[64,4096]{1,0:T(8,128)(2,1)S(1)}, u32[]{:S(2)}, u32[]{:S(2)}) collective-permute-start(bf16[64,4096]{1,0:T(8,128)(2,1)S(1)} %join.5.refs_0_), channel_id=1, source_target_pairs={{0,4},{1,17},{2,6},{3,19},{4,8},{5,21},{6,10},{7,23},{8,12},{9,25}... | collective-permute-start | bytes 1572872 | tf_op jit(solution)/shard_map/ppermute | solution.py:310
  34.4 13.5 %collective-permute-start.7 = (bf16[64,4096]{1,0:T(8,128)(2,1)S(1)}, bf16[64,4096]{1,0:T(8,128)(2,1)S(1)}, u32[]{:S(2)}, u32[]{:S(2)}) collective-permute-start(bf16[64,4096]{1,0:T(8,128)(2,1)S(1)} %join.5.refs_0_), channel_id=1, source_target_pairs={{0,12},{1,49},{2,14},{3,51},{4,0},{5,53},{6,2},{7,55},{8,4},{9,57}... | collective-permute-start | bytes 1572872 | tf_op jit(solution)/shard_map/ppermute | solution.py:310
  36.1 13.4 %collective-permute-start.8 = (bf16[64,4096]{1,0:T(8,128)(2,1)S(1)}, bf16[64,4096]{1,0:T(8,128)(2,1)S(1)}, u32[]{:S(2)}, u32[]{:S(2)}) collective-permute-start(bf16[64,4096]{1,0:T(8,128)(2,1)S(1)} %join.5.refs_0_), channel_id=1, source_target_pairs={{0,8},{1,33},{2,10},{3,35},{4,12},{5,37},{6,14},{7,39},{8,0},{9,41... | collective-permute-start | bytes 1572872 | tf_op jit(solution)/shard_map/ppermute | solution.py:310
  37.6 1.2 copy-start.9
  43.0 7.8 %slice-start = ((bf16[4,4,2,8,448]{4,3,2,1,0:T(8,128)(2,1)}), bf16[4,2,2,8,448]{4,3,2,1,0:T(8,128)(2,1)S(1)}, s32[]{:S(2)}) async-start(bf16[4,4,2,8,448]{4,3,2,1,0:T(8,128)(2,1)} %copy-done.9), calls=%async_computation.1 | async-start | bytes 262144 | tf_op jit(solution)/shard_map/slice | solution.py:357
  50.9 17.2 %copy-start.7 = (f32[4,4,2,8,448]{4,3,2,1,0:T(8,128)}, f32[4,4,2,8,448]{4,3,2,1,0:T(8,128)S(1)}, u32[]{:S(2)}) copy-start(f32[4,4,2,8,448]{4,3,2,1,0:T(8,128)S(1)} %multiply_add_fusion) | copy-start | bytes 1376260
  50.9 17.1 %copy-start.11 = (bf16[448]{0:T(512)(128)(2,1)S(1)}, bf16[448]{0:T(512)(128)(2,1)}, u32[]{:S(2)}) copy-start(bf16[448]{0:T(512)(128)(2,1)} %param.20) | copy-start | bytes 2692
  51.0 6.5 %collective-permute-start.10 = (bf16[4,4,2,8,448]{4,3,2,0,1:T(8,128)(2,1)S(1)}, bf16[4,4,2,8,448]{4,3,2,0,1:T(8,128)(2,1)S(1)}, u32[]{:S(2)}, u32[]{:S(2)}) collective-permute-start(bf16[4,4,2,8,448]{4,3,2,0,1:T(8,128)(2,1)S(1)} %copy.98), channel_id=1, source_target_pairs={{0,64},{1,65},{2,66},{3,67},{64,2},{65,3},{66,0},{67,1},{4,68},{5,... | collective-permute-start | bytes 688136 | tf_op jit(solution)/shard_map/ppermute | solution.py:324
  52.3 6.6 %collective-permute-start.11 = (bf16[4,4,2,8,448]{4,3,2,0,1:T(8,128)(2,1)S(1)}, bf16[4,4,2,8,448]{4,3,2,0,1:T(8,128)(2,1)S(1)}, u32[]{:S(2)}, u32[]{:S(2)}) collective-permute-start(bf16[4,4,2,8,448]{4,3,2,0,1:T(8,128)(2,1)S(1)} %copy.98), channel_id=1, source_target_pairs={{0,66},{1,67},{2,64},{3,65},{64,0},{65,1},{66,2},{67,3},{4,70},{5,... | collective-permute-start | bytes 688136 | tf_op jit(solution)/shard_map/ppermute | solution.py:324
  53.8 9.0 %collective-permute-start.9 = (bf16[4,4,2,8,448]{4,3,2,0,1:T(8,128)(2,1)S(1)}, bf16[4,4,2,8,448]{4,3,2,0,1:T(8,128)(2,1)S(1)}, u32[]{:S(2)}, u32[]{:S(2)}) collective-permute-start(bf16[4,4,2,8,448]{4,3,2,0,1:T(8,128)(2,1)S(1)} %copy.98), channel_id=1, source_target_pairs={{0,2},{1,3},{2,0},{3,1},{64,66},{65,67},{66,64},{67,65},{4,6},{5,7... | collective-permute-start | bytes 688136 | tf_op jit(solution)/shard_map/ppermute | solution.py:324
  63.0 6.6 %collective-permute-start.12 = (bf16[2,4,4,2,8,448]{5,4,3,2,1,0:T(8,128)(2,1)S(1)}, bf16[2,4,4,2,8,448]{5,4,3,2,1,0:T(8,128)(2,1)S(1)}, u32[]{:S(2)}, u32[]{:S(2)}) collective-permute-start(bf16[2,4,4,2,8,448]{5,4,3,2,1,0:T(8,128)(2,1)S(1)} %pad_maximum_fusion.2), channel_id=1, source_target_pairs={{0,1},{1,0},{2,3},{3,2},{4,5},{5,4},{6,7},{7,6},{8,9},{9,8},{10,11... | collective-permute-start | bytes 1376264 | tf_op jit(solution)/shard_map/ppermute | solution.py:328
  71.3 17.4 %collective-permute-start.16 = (bf16[256,2432]{1,0:T(8,128)(2,1)S(1)}, bf16[256,2432]{1,0:T(8,128)(2,1)S(1)}, u32[]{:S(2)}, u32[]{:S(2)}) collective-permute-start(bf16[256,2432]{1,0:T(8,128)(2,1)S(1)} %get-tuple-element.36), channel_id=1, source_target_pairs={{0,16},{1,5},{2,18},{3,7},{4,20},{5,9},{6,22},{7,11},{8,24},{9,13}... | collective-permute-start | bytes 3735560 | tf_op jit(solution)/shard_map/ppermute | solution.py:310
  71.8 17.3 %collective-permute-start.18 = (bf16[256,2304]{1,0:T(8,128)(2,1)S(1)}, bf16[256,2304]{1,0:T(8,128)(2,1)S(1)}, u32[]{:S(2)}, u32[]{:S(2)}) collective-permute-start(bf16[256,2304]{1,0:T(8,128)(2,1)S(1)} %get-tuple-element.38), channel_id=1, source_target_pairs={{0,48},{1,13},{2,50},{3,15},{4,52},{5,1},{6,54},{7,3},{8,56},{9,5}... | collective-permute-start | bytes 3538952 | tf_op jit(solution)/shard_map/ppermute | solution.py:310
  75.8 25.6 %collective-permute-start.14 = (bf16[256,2432]{1,0:T(8,128)(2,1)S(1)}, bf16[256,2432]{1,0:T(8,128)(2,1)S(1)}, u32[]{:S(2)}, u32[]{:S(2)}) collective-permute-start(bf16[256,2432]{1,0:T(8,128)(2,1)S(1)} %get-tuple-element.33), channel_id=1, source_target_pairs={{0,48},{1,13},{2,50},{3,15},{4,52},{5,1},{6,54},{7,3},{8,56},{9,5}... | collective-permute-start | bytes 3735560 | tf_op jit(solution)/shard_map/ppermute | solution.py:310
  77.1 24.3 %collective-permute-start.15 = (bf16[256,2304]{1,0:T(8,128)(2,1)S(1)}, bf16[256,2304]{1,0:T(8,128)(2,1)S(1)}, u32[]{:S(2)}, u32[]{:S(2)}) collective-permute-start(bf16[256,2304]{1,0:T(8,128)(2,1)S(1)} %get-tuple-element.34), channel_id=1, source_target_pairs={{0,16},{1,5},{2,18},{3,7},{4,20},{5,9},{6,22},{7,11},{8,24},{9,13}... | collective-permute-start | bytes 3538952 | tf_op jit(solution)/shard_map/ppermute | solution.py:310
  89.0 25.7 %collective-permute-start.17 = (bf16[256,2432]{1,0:T(8,128)(2,1)S(1)}, bf16[256,2432]{1,0:T(8,128)(2,1)S(1)}, u32[]{:S(2)}, u32[]{:S(2)}) collective-permute-start(bf16[256,2432]{1,0:T(8,128)(2,1)S(1)} %add_convert_fusion), channel_id=1, source_target_pairs={{0,16},{1,5},{2,18},{3,7},{4,20},{5,9},{6,22},{7,11},{8,24},{9,13}... | collective-permute-start | bytes 3735560 | tf_op jit(solution)/shard_map/ppermute | solution.py:310
  89.4 24.1 %collective-permute-start.19 = (bf16[256,2304]{1,0:T(8,128)(2,1)S(1)}, bf16[256,2304]{1,0:T(8,128)(2,1)S(1)}, u32[]{:S(2)}, u32[]{:S(2)}) collective-permute-start(bf16[256,2304]{1,0:T(8,128)(2,1)S(1)} %add_convert_fusion.1), channel_id=1, source_target_pairs={{0,48},{1,13},{2,50},{3,15},{4,52},{5,1},{6,54},{7,3},{8,56},{9,5}... | collective-permute-start | bytes 3538952 | tf_op jit(solution)/shard_map/ppermute | solution.py:310
  114.7 4.8 %copy-start.3 = (bf16[2304,448]{0,1:T(8,128)(2,1)S(1)}, bf16[2304,448]{0,1:T(8,128)(2,1)}, u32[]{:S(2)}) copy-start(bf16[2304,448]{0,1:T(8,128)(2,1)} %param.23) | copy-start | bytes 6193156
  115.5 10.5 %collective-permute-start.20 = (bf16[64,4736]{1,0:T(8,128)(2,1)S(1)}, bf16[64,4736]{1,0:T(8,128)(2,1)S(1)}, u32[]{:S(2)}, u32[]{:S(2)}) collective-permute-start(bf16[64,4736]{1,0:T(8,128)(2,1)S(1)} %get-tuple-element.40), channel_id=1, source_target_pairs={{0,4},{1,17},{2,6},{3,19},{4,8},{5,21},{6,10},{7,23},{8,12},{9,25}... | collective-permute-start | bytes 1818632 | tf_op jit(solution)/shard_map/ppermute | solution.py:310
  116.1 15.8 %collective-permute-start.21 = (bf16[64,4736]{1,0:T(8,128)(2,1)S(1)}, bf16[64,4736]{1,0:T(8,128)(2,1)S(1)}, u32[]{:S(2)}, u32[]{:S(2)}) collective-permute-start(bf16[64,4736]{1,0:T(8,128)(2,1)S(1)} %get-tuple-element.41), channel_id=1, source_target_pairs={{0,12},{1,49},{2,14},{3,51},{4,0},{5,53},{6,2},{7,55},{8,4},{9,57}... | collective-permute-start | bytes 1818632 | tf_op jit(solution)/shard_map/ppermute | solution.py:310
  118.4 15.3 %collective-permute-start.22 = (bf16[64,4736]{1,0:T(8,128)(2,1)S(1)}, bf16[64,4736]{1,0:T(8,128)(2,1)S(1)}, u32[]{:S(2)}, u32[]{:S(2)}) collective-permute-start(bf16[64,4736]{1,0:T(8,128)(2,1)S(1)} %get-tuple-element.42), channel_id=1, source_target_pairs={{0,8},{1,33},{2,10},{3,35},{4,12},{5,37},{6,14},{7,39},{8,0},{9,41... | collective-permute-start | bytes 1818632 | tf_op jit(solution)/shard_map/ppermute | solution.py:310
  119.5 41.2 %collective-permute-start.27 = (bf16[2304,448]{0,1:T(8,128)(2,1)S(1)}, bf16[2304,448]{0,1:T(8,128)(2,1)}, u32[]{:S(2)}, u32[]{:S(2)}) collective-permute-start(bf16[2304,448]{0,1:T(8,128)(2,1)S(1)} %copy-done.3), channel_id=1, source_target_pairs={{0,1},{1,0},{2,3},{3,2},{4,5},{5,4},{6,7},{7,6},{8,9},{9,8},{10,11... | collective-permute-start | bytes 6193160 | tf_op jit(solution)/shard_map/ppermute | solution.py:328
  134.3 3.4 %collective-permute-start.23 = (bf16[32,4608]{1,0:T(8,128)(2,1)S(1)}, bf16[32,4608]{1,0:T(8,128)(2,1)S(1)}, u32[]{:S(2)}, u32[]{:S(2)}) collective-permute-start(bf16[32,4608]{1,0:T(8,128)(2,1)S(1)} %get-tuple-element.44), channel_id=1, source_target_pairs={{0,1},{1,0},{2,3},{3,2},{4,5},{5,4},{6,7},{7,6},{8,9},{9,8},{10,11... | collective-permute-start | bytes 884744 | tf_op jit(solution)/shard_map/ppermute | solution.py:328
  137.9 8.6 %collective-permute-start.25 = (bf16[32,4608]{1,0:T(8,128)(2,1)S(1)}, bf16[32,4608]{1,0:T(8,128)(2,1)S(1)}, u32[]{:S(2)}, u32[]{:S(2)}) collective-permute-start(bf16[32,4608]{1,0:T(8,128)(2,1)S(1)} %activate.1.refs_0_), channel_id=1, source_target_pairs={{0,48},{1,13},{2,50},{3,15},{4,52},{5,1},{6,54},{7,3},{8,56},{9,5}... | collective-permute-start | bytes 884744 | tf_op jit(solution)/shard_map/ppermute | solution.py:310
  139.6 7.4 %collective-permute-start.26 = (bf16[32,4608]{1,0:T(8,128)(2,1)S(1)}, bf16[32,4608]{1,0:T(8,128)(2,1)S(1)}, u32[]{:S(2)}, u32[]{:S(2)}) collective-permute-start(bf16[32,4608]{1,0:T(8,128)(2,1)S(1)} %activate.1.refs_0_), channel_id=1, source_target_pairs={{0,32},{1,9},{2,34},{3,11},{4,36},{5,13},{6,38},{7,15},{8,40},{9,1... | collective-permute-start | bytes 884744 | tf_op jit(solution)/shard_map/ppermute | solution.py:310
  140.9 9.3 %collective-permute-start.24 = (bf16[32,4608]{1,0:T(8,128)(2,1)S(1)}, bf16[32,4608]{1,0:T(8,128)(2,1)S(1)}, u32[]{:S(2)}, u32[]{:S(2)}) collective-permute-start(bf16[32,4608]{1,0:T(8,128)(2,1)S(1)} %activate.1.refs_0_), channel_id=1, source_target_pairs={{0,16},{1,5},{2,18},{3,7},{4,20},{5,9},{6,22},{7,11},{8,24},{9,13}... | collective-permute-start | bytes 884744 | tf_op jit(solution)/shard_map/ppermute | solution.py:310
  147.1 9.2 %collective-permute-start.31 = (bf16[64,4608]{1,0:T(8,128)(2,1)S(1)}, bf16[64,4608]{1,0:T(8,128)(2,1)}, u32[]{:S(2)}, u32[]{:S(2)}) collective-permute-start(bf16[64,4608]{1,0:T(8,128)(2,1)S(1)} %join.8.refs_1_), channel_id=1, source_target_pairs={{0,12},{1,49},{2,14},{3,51},{4,0},{5,53},{6,2},{7,55},{8,4},{9,57}... | collective-permute-start | bytes 1769480 | tf_op jit(solution)/shard_map/ppermute | solution.py:310
  150.2 10.4 %collective-permute-start.28 = (bf16[64,4608]{1,0:T(8,128)(2,1)S(1)}, bf16[64,4608]{1,0:T(8,128)(2,1)}, u32[]{:S(2)}, u32[]{:S(2)}) collective-permute-start(bf16[64,4608]{1,0:T(8,128)(2,1)S(1)} %join.7.refs_0_), channel_id=1, source_target_pairs={{0,4},{1,17},{2,6},{3,19},{4,8},{5,21},{6,10},{7,23},{8,12},{9,25}... | collective-permute-start | bytes 1769480 | tf_op jit(solution)/shard_map/ppermute | solution.py:310
  150.3 16.6 %collective-permute-start.29 = (bf16[64,4608]{1,0:T(8,128)(2,1)S(1)}, bf16[64,4608]{1,0:T(8,128)(2,1)}, u32[]{:S(2)}, u32[]{:S(2)}) collective-permute-start(bf16[64,4608]{1,0:T(8,128)(2,1)S(1)} %join.8.refs_1_), channel_id=1, source_target_pairs={{0,4},{1,17},{2,6},{3,19},{4,8},{5,21},{6,10},{7,23},{8,12},{9,25}... | collective-permute-start | bytes 1769480 | tf_op jit(solution)/shard_map/ppermute | solution.py:310
  151.8 15.2 %collective-permute-start.30 = (bf16[64,4608]{1,0:T(8,128)(2,1)S(1)}, bf16[64,4608]{1,0:T(8,128)(2,1)}, u32[]{:S(2)}, u32[]{:S(2)}) collective-permute-start(bf16[64,4608]{1,0:T(8,128)(2,1)S(1)} %join.7.refs_0_), channel_id=1, source_target_pairs={{0,12},{1,49},{2,14},{3,51},{4,0},{5,53},{6,2},{7,55},{8,4},{9,57}... | collective-permute-start | bytes 1769480 | tf_op jit(solution)/shard_map/ppermute | solution.py:310
  156.3 13.7 %collective-permute-start.33 = (bf16[64,4608]{1,0:T(8,128)(2,1)}, bf16[64,4608]{1,0:T(8,128)(2,1)}, u32[]{:S(2)}, u32[]{:S(2)}) collective-permute-start(bf16[64,4608]{1,0:T(8,128)(2,1)} %collective-permute-done.31.refs_3_), channel_id=1, source_target_pairs={{0,12},{1,49},{2,14},{3,51},{4,0},{5,53},{6,2},{7,55},{8,4},{9,57}... | collective-permute-start | bytes 1769480 | tf_op jit(solution)/shard_map/ppermute | solution.py:310
  160.6 12.6 %collective-permute-start.32 = (bf16[64,4608]{1,0:T(8,128)(2,1)}, bf16[64,4608]{1,0:T(8,128)(2,1)}, u32[]{:S(2)}, u32[]{:S(2)}) collective-permute-start(bf16[64,4608]{1,0:T(8,128)(2,1)} %collective-permute-done.28.refs_0_), channel_id=1, source_target_pairs={{0,4},{1,17},{2,6},{3,19},{4,8},{5,21},{6,10},{7,23},{8,12},{9,25}... | collective-permute-start | bytes 1769480 | tf_op jit(solution)/shard_map/ppermute | solution.py:310
  175.9 1.0 copy-start.8
  199.4 5.2 %collective-permute-start.34 = (bf16[2,8,7168]{2,1,0:T(8,128)(2,1)S(1)}, bf16[2,8,7168]{2,1,0:T(8,128)(2,1)S(1)}, u32[]{:S(2)}, u32[]{:S(2)}) collective-permute-start(bf16[2,8,7168]{2,1,0:T(8,128)(2,1)S(1)} %reshape.74), channel_id=1, source_target_pairs={{0,1},{1,0},{2,3},{3,2},{4,5},{5,4},{6,7},{7,6},{8,9},{9,8},{10,11... | collective-permute-start | bytes 688136 | tf_op jit(solution)/shard_map/ppermute | solution.py:328

commit v7 on v6

--- a/solution.py
+++ b/solution.py
@@ -10,59 +10,65 @@
 
 epsilon = 1e-06
 VMEM_LIMIT = 20 * 1024 * 1024
-STREAM_LIMIT = 50 * 1024 * 1024
+STREAM_LIMIT = 61 * 1024 * 1024
 
 
 SHIFTS = (0, 1, -1, 2)
 FACING = (0, 2, 1, 3)
 
 
-def attend_kernel(
-    scale, latent, plan_ref, q_ref, new_ref, kv_ref, near_ref, far_ref
-):
-    token = pl.program_id(0)
-    tokens = pl.num_programs(0)
-    length = plan_ref[tokens + plan_ref[token]]
+def attend_kernel(scale, latent, per_step, plan_ref, q_ref, new_ref, *refs):
+    kv_refs, near_ref, far_ref = refs[:per_step], refs[per_step], refs[per_step + 1]
+    step = pl.program_id(0)
+    tokens = per_step * pl.num_programs(0)
     place = plan_ref[2 * tokens]
-    queries = jnp.concatenate([q_ref[0, place ^ i] for i in range(4)], axis=0)
-    cache = kv_ref[0]
-    newest = wide(new_ref[...])
-    picked = lax.broadcasted_iota(jnp.int32, newest.shape, 0) == token
-    newest = jnp.sum(jnp.where(picked, newest, 0.0), axis=0, keepdims=True)
-    scores = scale * jnp.dot(queries, cache, preferred_element_type=jnp.float32)
-    own = scale * jnp.sum(queries.astype(jnp.float32) * newest, axis=1, keepdims=True)
-    usable = lax.broadcasted_iota(jnp.int32, scores.shape, 1) < length
-    scores = jnp.where(usable, scores, -1e30)
-    peak = jnp.maximum(jnp.max(scores, axis=1, keepdims=True), own)
-    probs = jnp.exp(scores - peak).astype(jnp.bfloat16)
-    self_weight = jnp.exp(own - peak)
-    denom = jnp.sum(probs.astype(jnp.float32), axis=1, keepdims=True) + self_weight
-    accum = lax.dot_general(
-        probs, cache[:latent], (((1,), (1,)), ((), ())), preferred_element_type=jnp.float32
-    )
-    accum = accum + self_weight * newest[:, :latent]
-    context = (accum / denom).astype(near_ref.dtype)
-    half = context.shape[0] // 2
-    near_ref[...] = context[:half].reshape(near_ref.shape)
-    far_ref[...] = context[half:].reshape(far_ref.shape)
+    for i, kv_ref in enumerate(kv_refs):
+        token = step * per_step + i
+        length = plan_ref[tokens + plan_ref[token]]
+        queries = jnp.concatenate([q_ref[i, place ^ k] for k in range(4)], axis=0)
+        cache = kv_ref[0]
+        newest = wide(new_ref[...])
+        picked = lax.broadcasted_iota(jnp.int32, newest.shape, 0) == token
+        newest = jnp.sum(jnp.where(picked, newest, 0.0), axis=0, keepdims=True)
+        scores = scale * jnp.dot(queries, cache, preferred_element_type=jnp.float32)
+        own = scale * jnp.sum(queries.astype(jnp.float32) * newest, axis=1, keepdims=True)
+        usable = lax.broadcasted_iota(jnp.int32, scores.shape, 1) < length
+        scores = jnp.where(usable, scores, -1e30)
+        peak = jnp.maximum(jnp.max(scores, axis=1, keepdims=True), own)
+        probs = jnp.exp(scores - peak).astype(jnp.bfloat16)
+        self_weight = jnp.exp(own - peak)
+        denom = jnp.sum(probs.astype(jnp.float32), axis=1, keepdims=True) + self_weight
+        accum = lax.dot_general(
+            cache[:latent], probs, (((1,), (1,)), ((), ())), preferred_element_type=jnp.float32
+        ).T
+        accum = accum + self_weight * newest[:, :latent]
+        context = (accum / denom).astype(near_ref.dtype)
+        half = context.shape[0] // 2
+        near_ref[:, i] = context[:half].reshape(near_ref.shape[0], -1, latent)
+        far_ref[:, i] = context[half:].reshape(far_ref.shape[0], -1, latent)
 
 
 def attend(q_latent, kv_new, kv_cache, lengths, members, place, scale, latent):
     tokens, heads, kv = q_latent.shape
     ctx = kv_cache.shape[1]
     block = heads // 4
+    per_step = 2
+
+    def request(i):
+        return lambda t, m: (m[t * per_step + i], 0, 0)
+
     grid_spec = pltpu.PrefetchScalarGridSpec(
         num_scalar_prefetch=1,
-        grid=(tokens,),
+        grid=(tokens // per_step,),
         in_specs=[
-            pl.BlockSpec((1, 4, block, kv), lambda t, m: (t, 0, 0, 0)),
+            pl.BlockSpec((per_step, 4, block, kv), lambda t, m: (t, 0, 0, 0)),
             pl.BlockSpec((tokens, kv), lambda t, m: (0, 0)),
-            pl.BlockSpec((1, kv, ctx), lambda t, m: (m[t], 0, 0)),
-        ],
-        out_specs=[pl.BlockSpec((2, 1, block, latent), lambda t, m: (0, t, 0, 0))] * 2,
+        ]
+        + [pl.BlockSpec((1, kv, ctx), request(i)) for i in range(per_step)],
+        out_specs=[pl.BlockSpec((2, per_step, block, latent), lambda t, m: (0, t, 0, 0))] * 2,
     )
     return pl.pallas_call(
-        functools.partial(attend_kernel, scale, latent),
+        functools.partial(attend_kernel, scale, latent, per_step),
         grid_spec=grid_spec,
         out_shape=[jax.ShapeDtypeStruct((2, tokens, block, latent), jnp.bfloat16)] * 2,
         compiler_params=pltpu.CompilerParams(vmem_limit_bytes=STREAM_LIMIT),
@@ -76,7 +82,7 @@
         jnp.concatenate([members, lengths, place]),
         q_latent.reshape(tokens, 4, block, kv),
         kv_new,
-        jnp.swapaxes(kv_cache, 1, 2),
+        *([jnp.swapaxes(kv_cache, 1, 2)] * per_step),
     )
 
 

time: 206 us -> 204 us (level)
    unnamed x28 -> x26, local copies, waits for them, and re-layouts: 6.11 us -> 4.33 us
  transfers between devices with their start and end apart: 35 -> 35, of which waited for: 25 -> 25; matrix products, arithmetic and copies ran while one was open for 2% -> 3% of each run, Pallas kernels for 12% -> 12%
where the time goes in v7:
time: 204 us; the launch traced here: 203 us
  waiting for transfers between devices  83.9 us (41%)
  starting transfers between devices  55.7 us (27%)
  Pallas kernels  30.1 us (15%)
  blocking collectives  21 us (10%)
  local copies, waits for them, and re-layouts  6.14 us (3%)
  other arithmetic  6.04 us (3%)
    ppermute x24, waiting for transfers between devices, shift(): return lax.ppermute(value, ('grp', 'yh', 'core'), pairs)  71.9 us
    ppermute x24, starting transfers between devices, shift(): return lax.ppermute(value, ('grp', 'yh', 'core'), pairs)  31.9 us
    all_to_all x1, blocking collectives, body(): lax.all_to_all(down, ('role', 'grp', 'yh'), split_axis=0, concat_axis=0)  21 us
    ppermute x8, starting transfers between devices, swap(): return lax.ppermute(value, axis, [(0, 1), (1, 0)])  19.3 us
    pallas_call x11, Pallas kernels, whole_call(): pl.pallas_call(kernel, out_shape=out_shapes, in_specs=[pl.BlockSpec(memor...  13.8 us
    pallas_call x1, Pallas kernels, attend(): pl.pallas_call(functools.partial(attend_kernel, scale, latent, per_step),...  9.11 us
    ppermute x3, waiting for transfers between devices, shift_y(): lax.ppermute(value, ('role', 'yh', 'core'), [(p, moved(p)) for p in range...  7.23 us
    pallas_call x3, Pallas kernels, partial_sums(): pl.pallas_call(functools.partial(partial_kernel, jobs), grid=(1,), in_spe...  5.46 us
  transfers between devices with their start and end apart: 35, of which 25 were waited for; matrix products, arithmetic and copies ran while one was open for 3% of the time, Pallas kernels for 12%

profile of v7, /device:TPU:1, one launch (start us, length us, event | category | flops | bytes accessed | tf_op | source)
XLA Modules:
  0.0 203.4 jit_solution(18048833153911504052)
XLA Ops:
  0.0 1.4 collective-permute-start.1
  1.4 1.3 pad_add_fusion.plan_ref
  2.7 9.1 %attend.1 = (bf16[2,8,16,512]{3,2,1,0:T(8,128)(2,1)}, bf16[2,8,16,512]{3,2,1,0:T(8,128)(2,1)}) custom-call(s32[17]{0:T(128)} %pad_add_fusion.plan_ref, bf16[8,4,16,576]{3,2,1,0:T(8,128)(2,1)} %bitcast.75, bf16[8,576]{1,0:T(8,128)(2,1)} %new_ref.1, bf16[8,576,1024]{2,1,0:T(8,128)(2,1)} %bitcast.65, bf16[8,576,1024]{2,1,0:T(8,128)(2,1)} %bitcast.66), custom_call_target="tpu_custom_call" | custom-call | flops 1140850688 | bytes 9437184 | tf_op jit(solution)/shard_map/attend/pallas_call | solution.py:70
  11.8 3.1 %collective-permute-start = (bf16[2,8,16,512]{3,2,1,0:T(8,128)(2,1)}, bf16[2,8,16,512]{3,2,1,0:T(8,128)(2,1)S(1)}, u32[]{:S(2)}, u32[]{:S(2)}) collective-permute-start(bf16[2,8,16,512]{3,2,1,0:T(8,128)(2,1)} %get-tuple-element.26), channel_id=1, source_target_pairs={{0,2},{2,0},{1,3},{3,1},{4,6},{6,4},{5,7},{7,5},{8,10},{10,8},{9,1... | collective-permute-start | bytes 786440 | tf_op jit(solution)/shard_map/ppermute | solution.py:334
  14.9 1.5 copy-done.4
  16.4 1.9 join.6.refs_1_.refs_3_
  18.3 1.8 copy-done
  20.1 1.0 collective-permute-done.far
  21.9 1.5 collective-permute-start.2
  23.4 2.4 %collective-permute-start.3 = (bf16[16,4096]{1,0:T(8,128)(2,1)S(1)}, bf16[16,4096]{1,0:T(8,128)(2,1)S(1)}, u32[]{:S(2)}, u32[]{:S(2)}) collective-permute-start(bf16[16,4096]{1,0:T(8,128)(2,1)S(1)} %head_values.1.refs_0_), channel_id=1, source_target_pairs={{0,48},{1,13},{2,50},{3,15},{4,52},{5,1},{6,54},{7,3},{8,56},{9,5}... | collective-permute-start | bytes 393224 | tf_op jit(solution)/shard_map/ppermute | solution.py:316
  25.8 1.2 collective-permute-start.4
  27.2 2.5 %broadcast_select_fusion = (bf16[448,2304]{1,0:T(8,128)(2,1)S(1)}, bf16[448,2304]{1,0:T(8,128)(2,1)S(1)}) fusion(bf16[448,2304]{1,0:T(8,128)(2,1)} %param.22, bf16[448,2304]{1,0:T(8,128)(2,1)} %param.21, pred[]{:T(512)S(6)} %eq.28), kind=kLoop, calls=%fused_computation.2 | loop fusion | flops 2064384 | bytes 8257537 | tf_op jit(solution)/shard_map/jit(_where)/select_n | solution.py:414
  29.9 1.4 collective-permute-start.13
  31.4 1.0 collective-permute-start.6
  32.4 1.8 collective-permute-start.7
  34.2 1.1 collective-permute-start.8
  35.5 1.2 pair_dot.5
  36.7 4.3 %collective-permute-done.6.refs_0_ = bf16[64,4096]{1,0:T(8,128)(2,1)S(1)} collective-permute-done((bf16[64,4096]{1,0:T(8,128)(2,1)S(1)}, bf16[64,4096]{1,0:T(8,128)(2,1)S(1)}, u32[]{:S(2)}, u32[]{:S(2)}) %collective-permute-start.6) | collective-permute-done | bytes 524320 | tf_op jit(solution)/shard_map/ppermute | solution.py:316
  41.1 4.9 %collective-permute-done.7.refs_1_ = bf16[64,4096]{1,0:T(8,128)(2,1)S(1)} collective-permute-done((bf16[64,4096]{1,0:T(8,128)(2,1)S(1)}, bf16[64,4096]{1,0:T(8,128)(2,1)S(1)}, u32[]{:S(2)}, u32[]{:S(2)}) %collective-permute-start.7) | collective-permute-done | bytes 524320 | tf_op jit(solution)/shard_map/ppermute | solution.py:316
  45.9 1.6 collective-permute-done.8.refs_2_
  47.5 1.2 pair_dot.6
  48.9 1.3 collective-permute-start.10
  50.3 1.5 collective-permute-start.11
  51.8 1.6 collective-permute-start.9
  53.4 2.1 %collective-permute-done.10 = bf16[4,4,2,8,448]{4,3,2,0,1:T(8,128)(2,1)S(1)} collective-permute-done((bf16[4,4,2,8,448]{4,3,2,0,1:T(8,128)(2,1)S(1)}, bf16[4,4,2,8,448]{4,3,2,0,1:T(8,128)(2,1)S(1)}, u32[]{:S(2)}, u32[]{:S(2)}) %collective-permute-start.10) | collective-permute-done | bytes 229408 | tf_op jit(solution)/shard_map/ppermute | solution.py:330
  55.5 1.5 collective-permute-done.11
  57.1 3.6 %collective-permute-done.9 = bf16[4,4,2,8,448]{4,3,2,0,1:T(8,128)(2,1)S(1)} collective-permute-done((bf16[4,4,2,8,448]{4,3,2,0,1:T(8,128)(2,1)S(1)}, bf16[4,4,2,8,448]{4,3,2,0,1:T(8,128)(2,1)S(1)}, u32[]{:S(2)}, u32[]{:S(2)}) %collective-permute-start.9) | collective-permute-done | bytes 229408 | tf_op jit(solution)/shard_map/ppermute | solution.py:330
  60.9 5.1 %collective-permute-start.12 = (bf16[2,4,4,2,8,448]{5,4,3,2,1,0:T(8,128)(2,1)S(1)}, bf16[2,4,4,2,8,448]{5,4,3,2,1,0:T(8,128)(2,1)S(1)}, u32[]{:S(2)}, u32[]{:S(2)}) collective-permute-start(bf16[2,4,4,2,8,448]{5,4,3,2,1,0:T(8,128)(2,1)S(1)} %pad_maximum_fusion.2), channel_id=1, source_target_pairs={{0,1},{1,0},{2,3},{3,2},{4,5},{5,4},{6,7},{7,6},{8,9},{9,8},{10,11... | collective-permute-start | bytes 1376264 | tf_op jit(solution)/shard_map/ppermute | solution.py:334
  66.1 1.4 collective-permute-done.12
  67.8 1.4 partial_sums.5
  69.8 2.5 %collective-permute-start.18 = (bf16[256,2304]{1,0:T(8,128)(2,1)S(1)}, bf16[256,2304]{1,0:T(8,128)(2,1)S(1)}, u32[]{:S(2)}, u32[]{:S(2)}) collective-permute-start(bf16[256,2304]{1,0:T(8,128)(2,1)S(1)} %get-tuple-element.38), channel_id=1, source_target_pairs={{0,48},{1,13},{2,50},{3,15},{4,52},{5,1},{6,54},{7,3},{8,56},{9,5}... | collective-permute-start | bytes 3538952 | tf_op jit(solution)/shard_map/ppermute | solution.py:316
  72.3 1.4 partial_sums.4
  73.7 1.3 collective-permute-start.14
  75.2 2.6 %partial_sums.3 = (bf16[256,2432]{1,0:T(8,128)(2,1)S(1)}, bf16[256,2304]{1,0:T(8,128)(2,1)S(1)}, bf16[256,2432]{1,0:T(8,128)(2,1)S(1)}, bf16[256,2304]{1,0:T(8,128)(2,1)S(1)}) custom-call(bf16[4,4,64,448]{3,2,1,0:T(8,128)(2,1)S(1)} %bitcast.57, bf16[4,4,64,448]{3,2,1,0:T(8,128)(2,1)S(1)} %bitcast.58, bf16[4,4,64,448]{3,2,1,0:T(8,128)(2,1)S(1)} %bitcast.59, ...), custom_call_target="tpu_custom_call" | custom-call | flops 2172649472 | bytes 8978432 | tf_op jit(solution)/shard_map/partial_sums/pallas_call | solution.py:130
  77.9 8.7 %collective-permute-done.16 = bf16[256,2432]{1,0:T(8,128)(2,1)S(1)} collective-permute-done((bf16[256,2432]{1,0:T(8,128)(2,1)S(1)}, bf16[256,2432]{1,0:T(8,128)(2,1)S(1)}, u32[]{:S(2)}, u32[]{:S(2)}) %collective-permute-start.16) | collective-permute-done | bytes 1245216 | tf_op jit(solution)/shard_map/ppermute | solution.py:316
  87.3 2.7 %collective-permute-start.19 = (bf16[256,2304]{1,0:T(8,128)(2,1)S(1)}, bf16[256,2304]{1,0:T(8,128)(2,1)S(1)}, u32[]{:S(2)}, u32[]{:S(2)}) collective-permute-start(bf16[256,2304]{1,0:T(8,128)(2,1)S(1)} %add_convert_fusion.1), channel_id=1, source_target_pairs={{0,48},{1,13},{2,50},{3,15},{4,52},{5,1},{6,54},{7,3},{8,56},{9,5}... | collective-permute-start | bytes 3538952 | tf_op jit(solution)/shard_map/ppermute | solution.py:316
  90.0 9.2 %collective-permute-done.15.direct_c = bf16[256,2304]{1,0:T(8,128)(2,1)S(1)} collective-permute-done((bf16[256,2304]{1,0:T(8,128)(2,1)S(1)}, bf16[256,2304]{1,0:T(8,128)(2,1)S(1)}, u32[]{:S(2)}, u32[]{:S(2)}) %collective-permute-start.15) | collective-permute-done | bytes 1179680 | tf_op jit(solution)/shard_map/ppermute | solution.py:316
  99.3 12.2 %collective-permute-done.19.relay_c = bf16[256,2304]{1,0:T(8,128)(2,1)S(1)} collective-permute-done((bf16[256,2304]{1,0:T(8,128)(2,1)S(1)}, bf16[256,2304]{1,0:T(8,128)(2,1)S(1)}, u32[]{:S(2)}, u32[]{:S(2)}) %collective-permute-start.19) | collective-permute-done | bytes 1179680 | tf_op jit(solution)/shard_map/ppermute | solution.py:316
  111.4 1.2 collective-permute-done.17.relay_a
  114.0 2.3 %collective-permute-start.21 = (bf16[64,4736]{1,0:T(8,128)(2,1)S(1)}, bf16[64,4736]{1,0:T(8,128)(2,1)S(1)}, u32[]{:S(2)}, u32[]{:S(2)}) collective-permute-start(bf16[64,4736]{1,0:T(8,128)(2,1)S(1)} %get-tuple-element.41), channel_id=1, source_target_pairs={{0,12},{1,49},{2,14},{3,51},{4,0},{5,53},{6,2},{7,55},{8,4},{9,57}... | collective-permute-start | bytes 1818632 | tf_op jit(solution)/shard_map/ppermute | solution.py:316
  116.3 1.1 collective-permute-start.22
  117.4 2.0 %collective-permute-start.27 = (bf16[2304,448]{0,1:T(8,128)(2,1)S(1)}, bf16[2304,448]{0,1:T(8,128)(2,1)}, u32[]{:S(2)}, u32[]{:S(2)}) collective-permute-start(bf16[2304,448]{0,1:T(8,128)(2,1)S(1)} %copy-done.3), channel_id=1, source_target_pairs={{0,1},{1,0},{2,3},{3,2},{4,5},{5,4},{6,7},{7,6},{8,9},{9,8},{10,11... | collective-permute-start | bytes 6193160 | tf_op jit(solution)/shard_map/ppermute | solution.py:334
  119.4 4.5 %collective-permute-done.20.refs_1_ = bf16[64,4736]{1,0:T(8,128)(2,1)S(1)} collective-permute-done((bf16[64,4736]{1,0:T(8,128)(2,1)S(1)}, bf16[64,4736]{1,0:T(8,128)(2,1)S(1)}, u32[]{:S(2)}, u32[]{:S(2)}) %collective-permute-start.20) | collective-permute-done | bytes 606240 | tf_op jit(solution)/shard_map/ppermute | solution.py:316
  124.0 5.8 %collective-permute-done.21.refs_2_ = bf16[64,4736]{1,0:T(8,128)(2,1)S(1)} collective-permute-done((bf16[64,4736]{1,0:T(8,128)(2,1)S(1)}, bf16[64,4736]{1,0:T(8,128)(2,1)S(1)}, u32[]{:S(2)}, u32[]{:S(2)}) %collective-permute-start.21) | collective-permute-done | bytes 606240 | tf_op jit(solution)/shard_map/ppermute | solution.py:316
  129.8 1.8 collective-permute-done.22.refs_3_
  132.3 2.2 %collective-permute-start.23 = (bf16[32,4608]{1,0:T(8,128)(2,1)S(1)}, bf16[32,4608]{1,0:T(8,128)(2,1)S(1)}, u32[]{:S(2)}, u32[]{:S(2)}) collective-permute-start(bf16[32,4608]{1,0:T(8,128)(2,1)S(1)} %get-tuple-element.44), channel_id=1, source_target_pairs={{0,1},{1,0},{2,3},{3,2},{4,5},{5,4},{6,7},{7,6},{8,9},{9,8},{10,11... | collective-permute-start | bytes 884744 | tf_op jit(solution)/shard_map/ppermute | solution.py:334
  134.4 1.2 collective-permute-done.23.theirs
  135.8 1.8 collective-permute-start.25
  137.6 1.2 collective-permute-start.26
  138.8 5.6 %collective-permute-done.25.refs_0_ = bf16[32,4608]{1,0:T(8,128)(2,1)S(1)} collective-permute-done((bf16[32,4608]{1,0:T(8,128)(2,1)S(1)}, bf16[32,4608]{1,0:T(8,128)(2,1)S(1)}, u32[]{:S(2)}, u32[]{:S(2)}) %collective-permute-start.25) | collective-permute-done | bytes 294944 | tf_op jit(solution)/shard_map/ppermute | solution.py:316
  145.0 2.3 %collective-permute-start.31 = (bf16[64,4608]{1,0:T(8,128)(2,1)S(1)}, bf16[64,4608]{1,0:T(8,128)(2,1)}, u32[]{:S(2)}, u32[]{:S(2)}) collective-permute-start(bf16[64,4608]{1,0:T(8,128)(2,1)S(1)} %join.8.refs_1_), channel_id=1, source_target_pairs={{0,12},{1,49},{2,14},{3,51},{4,0},{5,53},{6,2},{7,55},{8,4},{9,57}... | collective-permute-start | bytes 1769480 | tf_op jit(solution)/shard_map/ppermute | solution.py:316
  148.2 1.5 collective-permute-start.29
  149.7 1.3 collective-permute-start.30
  151.0 3.3 %collective-permute-done.31.refs_3_ = bf16[64,4608]{1,0:T(8,128)(2,1)} collective-permute-done((bf16[64,4608]{1,0:T(8,128)(2,1)S(1)}, bf16[64,4608]{1,0:T(8,128)(2,1)}, u32[]{:S(2)}, u32[]{:S(2)}) %collective-permute-start.31) | collective-permute-done | bytes 589856 | tf_op jit(solution)/shard_map/ppermute | solution.py:316
  154.2 3.5 %collective-permute-start.33 = (bf16[64,4608]{1,0:T(8,128)(2,1)}, bf16[64,4608]{1,0:T(8,128)(2,1)}, u32[]{:S(2)}, u32[]{:S(2)}) collective-permute-start(bf16[64,4608]{1,0:T(8,128)(2,1)} %collective-permute-done.31.refs_3_), channel_id=1, source_target_pairs={{0,12},{1,49},{2,14},{3,51},{4,0},{5,53},{6,2},{7,55},{8,4},{9,57}... | collective-permute-start | bytes 1769480 | tf_op jit(solution)/shard_map/ppermute | solution.py:316
  158.6 1.8 join.9.refs_2_.refs_4_
  160.4 1.4 pair_dot.7
  161.8 3.1 %collective-permute-done.29.refs_1_ = bf16[64,4608]{1,0:T(8,128)(2,1)} collective-permute-done((bf16[64,4608]{1,0:T(8,128)(2,1)S(1)}, bf16[64,4608]{1,0:T(8,128)(2,1)}, u32[]{:S(2)}, u32[]{:S(2)}) %collective-permute-start.29) | collective-permute-done | bytes 589856 | tf_op jit(solution)/shard_map/ppermute | solution.py:316
  164.9 3.0 %pair_dot.8 = f32[256,448]{1,0:T(8,128)S(1)} custom-call(bf16[64,4608]{1,0:T(8,128)(2,1)} %collective-permute-done.28.refs_0_, bf16[64,4608]{1,0:T(8,128)(2,1)} %collective-permute-done.29.refs_1_, bf16[64,4608]{1,0:T(8,128)(2,1)} %collective-permute-done.30.refs_2_, bf16[64,4608]{1,0:T(8,128)(2,1)} %collective-permute-done.31.refs_3_, ...), custom_call_target="tpu_custom_call" | custom-call | flops 4128768 | bytes 4128768 | tf_op jit(solution)/shard_map/pair_dot/pallas_call | solution.py:177
  167.9 3.3 %collective-permute-done.32.refs_0_ = bf16[64,4608]{1,0:T(8,128)(2,1)} collective-permute-done((bf16[64,4608]{1,0:T(8,128)(2,1)}, bf16[64,4608]{1,0:T(8,128)(2,1)}, u32[]{:S(2)}, u32[]{:S(2)}) %collective-permute-start.32) | collective-permute-done | bytes 589856 | tf_op jit(solution)/shard_map/ppermute | solution.py:316
  171.2 2.6 %pair_dot.9 = f32[128,448]{1,0:T(8,128)S(1)} custom-call(bf16[64,4608]{1,0:T(8,128)(2,1)} %collective-permute-done.32.refs_0_, bf16[64,4608]{1,0:T(8,128)(2,1)} %collective-permute-done.33.refs_1_, bf16[896,2304]{1,0:T(8,128)(2,1)S(1)} %join.9.refs_2_.refs_4_), custom_call_target="tpu_custom_call" | custom-call | flops 4128768 | bytes 4128768 | tf_op jit(solution)/shard_map/pair_dot/pallas_call | solution.py:177
  175.7 21.0 %all_to_all.5 = bf16[64,16,448]{2,1,0:T(8,128)(2,1)S(1)} all-to-all(bf16[64,16,448]{2,1,0:T(8,128)(2,1)S(1)} %bitcast.68), channel_id=1, replica_groups=mesh['role'=2,'grp'=16,'yh'=2,'core'=2] {'role','grp','yh'}, dimensions={0} | all-to-all | bytes 1835008 | tf_op jit(solution)/shard_map/all_to_all | solution.py:472
  197.3 4.1 %collective-permute-start.34 = (bf16[2,8,7168]{2,1,0:T(8,128)(2,1)S(1)}, bf16[2,8,7168]{2,1,0:T(8,128)(2,1)S(1)}, u32[]{:S(2)}, u32[]{:S(2)}) collective-permute-start(bf16[2,8,7168]{2,1,0:T(8,128)(2,1)S(1)} %reshape.74), channel_id=1, source_target_pairs={{0,1},{1,0},{2,3},{3,2},{4,5},{5,4},{6,7},{7,6},{8,9},{9,8},{10,11... | collective-permute-start | bytes 688136 | tf_op jit(solution)/shard_map/ppermute | solution.py:334
  201.4 1.1 collective-permute-done.34
  (96 shorter events, 11.6 us)
Async XLA Ops:
  0.0 21.1 %collective-permute-start.1 = (bf16[16,512,128]{2,1,0:T(8,128)(2,1)}, bf16[16,512,128]{2,1,0:T(8,128)(2,1)S(1)}, u32[]{:S(2)}, u32[]{:S(2)}) collective-permute-start(bf16[16,512,128]{2,1,0:T(8,128)(2,1)} %refs_0_.1), channel_id=1, source_target_pairs={{0,1},{1,0},{2,3},{3,2},{4,5},{5,4},{6,7},{7,6},{8,9},{9,8},{10,11... | collective-permute-start | bytes 6291464 | tf_op jit(solution)/shard_map/ppermute | solution.py:334
  1.4 13.5 %collective-permute-start.5 = (bf16[2048,448]{0,1:T(8,128)(2,1)}, bf16[2048,448]{0,1:T(8,128)(2,1)}, u32[]{:S(2)}, u32[]{:S(2)}) collective-permute-start(bf16[2048,448]{0,1:T(8,128)(2,1)} %param.19), channel_id=1, source_target_pairs={{0,1},{1,0},{2,3},{3,2},{4,5},{5,4},{6,7},{7,6},{8,9},{9,8},{10,11... | collective-permute-start | bytes 5505032 | tf_op jit(solution)/shard_map/ppermute | solution.py:334
  11.8 9.3 %collective-permute-start = (bf16[2,8,16,512]{3,2,1,0:T(8,128)(2,1)}, bf16[2,8,16,512]{3,2,1,0:T(8,128)(2,1)S(1)}, u32[]{:S(2)}, u32[]{:S(2)}) collective-permute-start(bf16[2,8,16,512]{3,2,1,0:T(8,128)(2,1)} %get-tuple-element.26), channel_id=1, source_target_pairs={{0,2},{2,0},{1,3},{3,1},{4,6},{6,4},{5,7},{7,5},{8,10},{10,8},{9,1... | collective-permute-start | bytes 786440 | tf_op jit(solution)/shard_map/ppermute | solution.py:334
  14.9 1.5 copy-start.4
  16.4 4.7 %copy-start.2 = (bf16[16,512,128]{2,1,0:T(8,128)(2,1)S(1)}, bf16[16,512,128]{2,1,0:T(8,128)(2,1)}, u32[]{:S(2)}) copy-start(bf16[16,512,128]{2,1,0:T(8,128)(2,1)} %refs_0_.1) | copy-start | bytes 6291460
  16.4 4.7 %copy-start.5 = (bf16[2,8,16,512]{3,2,1,0:T(8,128)(2,1)S(1)}, bf16[2,8,16,512]{3,2,1,0:T(8,128)(2,1)}, u32[]{:S(2)}) copy-start(bf16[2,8,16,512]{3,2,1,0:T(8,128)(2,1)} %get-tuple-element.25.near) | copy-start | bytes 786436
  18.3 1.8 copy-start
  21.1 5.8 %copy-start.9 = (bf16[512,448]{0,1:T(8,128)(2,1)S(1)}, bf16[512,448]{0,1:T(8,128)(2,1)}, u32[]{:S(2)}) copy-start(bf16[512,448]{0,1:T(8,128)(2,1)} %param.17) | copy-start | bytes 1376260
  21.9 9.4 %collective-permute-start.2 = (bf16[16,4096]{1,0:T(8,128)(2,1)S(1)}, bf16[16,4096]{1,0:T(8,128)(2,1)S(1)}, u32[]{:S(2)}, u32[]{:S(2)}) collective-permute-start(bf16[16,4096]{1,0:T(8,128)(2,1)S(1)} %head_values.1.refs_0_), channel_id=1, source_target_pairs={{0,16},{1,5},{2,18},{3,7},{4,20},{5,9},{6,22},{7,11},{8,24},{9,13}... | collective-permute-start | bytes 393224 | tf_op jit(solution)/shard_map/ppermute | solution.py:316
  23.4 7.9 %collective-permute-start.3 = (bf16[16,4096]{1,0:T(8,128)(2,1)S(1)}, bf16[16,4096]{1,0:T(8,128)(2,1)S(1)}, u32[]{:S(2)}, u32[]{:S(2)}) collective-permute-start(bf16[16,4096]{1,0:T(8,128)(2,1)S(1)} %head_values.1.refs_0_), channel_id=1, source_target_pairs={{0,48},{1,13},{2,50},{3,15},{4,52},{5,1},{6,54},{7,3},{8,56},{9,5}... | collective-permute-start | bytes 393224 | tf_op jit(solution)/shard_map/ppermute | solution.py:316
  25.8 5.6 %collective-permute-start.4 = (bf16[16,4096]{1,0:T(8,128)(2,1)S(1)}, bf16[16,4096]{1,0:T(8,128)(2,1)S(1)}, u32[]{:S(2)}, u32[]{:S(2)}) collective-permute-start(bf16[16,4096]{1,0:T(8,128)(2,1)S(1)} %head_values.1.refs_0_), channel_id=1, source_target_pairs={{0,32},{1,9},{2,34},{3,11},{4,36},{5,13},{6,38},{7,15},{8,40},{9,1... | collective-permute-start | bytes 393224 | tf_op jit(solution)/shard_map/ppermute | solution.py:316
  29.7 5.9 %copy-start.1 = (bf16[896,2048]{1,0:T(8,128)(2,1)S(1)}, bf16[896,2048]{1,0:T(8,128)(2,1)}, u32[]{:S(2)}) copy-start(bf16[896,2048]{1,0:T(8,128)(2,1)} %copy-done) | copy-start | bytes 11010052
  29.9 37.9 %collective-permute-start.13 = (bf16[448,2304]{1,0:T(8,128)(2,1)S(1)}, bf16[448,2304]{1,0:T(8,128)(2,1)S(1)}, u32[]{:S(2)}, u32[]{:S(2)}) collective-permute-start(bf16[448,2304]{1,0:T(8,128)(2,1)S(1)} %get-tuple-element.45), channel_id=1, source_target_pairs={{0,1},{1,0},{2,3},{3,2},{4,5},{5,4},{6,7},{7,6},{8,9},{9,8},{10,11... | collective-permute-start | bytes 6193160 | tf_op jit(solution)/shard_map/ppermute | solution.py:334
  31.4 9.6 %collective-permute-start.6 = (bf16[64,4096]{1,0:T(8,128)(2,1)S(1)}, bf16[64,4096]{1,0:T(8,128)(2,1)S(1)}, u32[]{:S(2)}, u32[]{:S(2)}) collective-permute-start(bf16[64,4096]{1,0:T(8,128)(2,1)S(1)} %join.5.refs_0_), channel_id=1, source_target_pairs={{0,4},{1,17},{2,6},{3,19},{4,8},{5,21},{6,10},{7,23},{8,12},{9,25}... | collective-permute-start | bytes 1572872 | tf_op jit(solution)/shard_map/ppermute | solution.py:316
  32.4 13.5 %collective-permute-start.7 = (bf16[64,4096]{1,0:T(8,128)(2,1)S(1)}, bf16[64,4096]{1,0:T(8,128)(2,1)S(1)}, u32[]{:S(2)}, u32[]{:S(2)}) collective-permute-start(bf16[64,4096]{1,0:T(8,128)(2,1)S(1)} %join.5.refs_0_), channel_id=1, source_target_pairs={{0,12},{1,49},{2,14},{3,51},{4,0},{5,53},{6,2},{7,55},{8,4},{9,57}... | collective-permute-start | bytes 1572872 | tf_op jit(solution)/shard_map/ppermute | solution.py:316
  34.2 13.3 %collective-permute-start.8 = (bf16[64,4096]{1,0:T(8,128)(2,1)S(1)}, bf16[64,4096]{1,0:T(8,128)(2,1)S(1)}, u32[]{:S(2)}, u32[]{:S(2)}) collective-permute-start(bf16[64,4096]{1,0:T(8,128)(2,1)S(1)} %join.5.refs_0_), channel_id=1, source_target_pairs={{0,8},{1,33},{2,10},{3,35},{4,12},{5,37},{6,14},{7,39},{8,0},{9,41... | collective-permute-start | bytes 1572872 | tf_op jit(solution)/shard_map/ppermute | solution.py:316
  35.5 1.2 copy-start.8
  41.0 7.7 %slice-start = ((bf16[4,4,2,8,448]{4,3,2,1,0:T(8,128)(2,1)}), bf16[4,2,2,8,448]{4,3,2,1,0:T(8,128)(2,1)S(1)}, s32[]{:S(2)}) async-start(bf16[4,4,2,8,448]{4,3,2,1,0:T(8,128)(2,1)} %copy-done.8), calls=%async_computation.1 | async-start | bytes 262144 | tf_op jit(solution)/shard_map/slice | solution.py:363
  48.9 17.2 %copy-start.6 = (f32[4,4,2,8,448]{4,3,2,1,0:T(8,128)}, f32[4,4,2,8,448]{4,3,2,1,0:T(8,128)S(1)}, u32[]{:S(2)}) copy-start(f32[4,4,2,8,448]{4,3,2,1,0:T(8,128)S(1)} %multiply_add_fusion) | copy-start | bytes 1376260
  48.9 17.1 %copy-start.10 = (bf16[448]{0:T(512)(128)(2,1)S(1)}, bf16[448]{0:T(512)(128)(2,1)}, u32[]{:S(2)}) copy-start(bf16[448]{0:T(512)(128)(2,1)} %param.20) | copy-start | bytes 2692
  48.9 6.5 %collective-permute-start.10 = (bf16[4,4,2,8,448]{4,3,2,0,1:T(8,128)(2,1)S(1)}, bf16[4,4,2,8,448]{4,3,2,0,1:T(8,128)(2,1)S(1)}, u32[]{:S(2)}, u32[]{:S(2)}) collective-permute-start(bf16[4,4,2,8,448]{4,3,2,0,1:T(8,128)(2,1)S(1)} %copy.98), channel_id=1, source_target_pairs={{0,64},{1,65},{2,66},{3,67},{64,2},{65,3},{66,0},{67,1},{4,68},{5,... | collective-permute-start | bytes 688136 | tf_op jit(solution)/shard_map/ppermute | solution.py:330
  50.3 6.7 %collective-permute-start.11 = (bf16[4,4,2,8,448]{4,3,2,0,1:T(8,128)(2,1)S(1)}, bf16[4,4,2,8,448]{4,3,2,0,1:T(8,128)(2,1)S(1)}, u32[]{:S(2)}, u32[]{:S(2)}) collective-permute-start(bf16[4,4,2,8,448]{4,3,2,0,1:T(8,128)(2,1)S(1)} %copy.98), channel_id=1, source_target_pairs={{0,66},{1,67},{2,64},{3,65},{64,0},{65,1},{66,2},{67,3},{4,70},{5,... | collective-permute-start | bytes 688136 | tf_op jit(solution)/shard_map/ppermute | solution.py:330
  51.8 8.9 %collective-permute-start.9 = (bf16[4,4,2,8,448]{4,3,2,0,1:T(8,128)(2,1)S(1)}, bf16[4,4,2,8,448]{4,3,2,0,1:T(8,128)(2,1)S(1)}, u32[]{:S(2)}, u32[]{:S(2)}) collective-permute-start(bf16[4,4,2,8,448]{4,3,2,0,1:T(8,128)(2,1)S(1)} %copy.98), channel_id=1, source_target_pairs={{0,2},{1,3},{2,0},{3,1},{64,66},{65,67},{66,64},{67,65},{4,6},{5,7... | collective-permute-start | bytes 688136 | tf_op jit(solution)/shard_map/ppermute | solution.py:330
  60.9 6.6 %collective-permute-start.12 = (bf16[2,4,4,2,8,448]{5,4,3,2,1,0:T(8,128)(2,1)S(1)}, bf16[2,4,4,2,8,448]{5,4,3,2,1,0:T(8,128)(2,1)S(1)}, u32[]{:S(2)}, u32[]{:S(2)}) collective-permute-start(bf16[2,4,4,2,8,448]{5,4,3,2,1,0:T(8,128)(2,1)S(1)} %pad_maximum_fusion.2), channel_id=1, source_target_pairs={{0,1},{1,0},{2,3},{3,2},{4,5},{5,4},{6,7},{7,6},{8,9},{9,8},{10,11... | collective-permute-start | bytes 1376264 | tf_op jit(solution)/shard_map/ppermute | solution.py:334
  69.2 17.4 %collective-permute-start.16 = (bf16[256,2432]{1,0:T(8,128)(2,1)S(1)}, bf16[256,2432]{1,0:T(8,128)(2,1)S(1)}, u32[]{:S(2)}, u32[]{:S(2)}) collective-permute-start(bf16[256,2432]{1,0:T(8,128)(2,1)S(1)} %get-tuple-element.36), channel_id=1, source_target_pairs={{0,16},{1,5},{2,18},{3,7},{4,20},{5,9},{6,22},{7,11},{8,24},{9,13}... | collective-permute-start | bytes 3735560 | tf_op jit(solution)/shard_map/ppermute | solution.py:316
  69.8 17.2 %collective-permute-start.18 = (bf16[256,2304]{1,0:T(8,128)(2,1)S(1)}, bf16[256,2304]{1,0:T(8,128)(2,1)S(1)}, u32[]{:S(2)}, u32[]{:S(2)}) collective-permute-start(bf16[256,2304]{1,0:T(8,128)(2,1)S(1)} %get-tuple-element.38), channel_id=1, source_target_pairs={{0,48},{1,13},{2,50},{3,15},{4,52},{5,1},{6,54},{7,3},{8,56},{9,5}... | collective-permute-start | bytes 3538952 | tf_op jit(solution)/shard_map/ppermute | solution.py:316
  73.7 25.6 %collective-permute-start.14 = (bf16[256,2432]{1,0:T(8,128)(2,1)S(1)}, bf16[256,2432]{1,0:T(8,128)(2,1)S(1)}, u32[]{:S(2)}, u32[]{:S(2)}) collective-permute-start(bf16[256,2432]{1,0:T(8,128)(2,1)S(1)} %get-tuple-element.33), channel_id=1, source_target_pairs={{0,48},{1,13},{2,50},{3,15},{4,52},{5,1},{6,54},{7,3},{8,56},{9,5}... | collective-permute-start | bytes 3735560 | tf_op jit(solution)/shard_map/ppermute | solution.py:316
  75.0 24.3 %collective-permute-start.15 = (bf16[256,2304]{1,0:T(8,128)(2,1)S(1)}, bf16[256,2304]{1,0:T(8,128)(2,1)S(1)}, u32[]{:S(2)}, u32[]{:S(2)}) collective-permute-start(bf16[256,2304]{1,0:T(8,128)(2,1)S(1)} %get-tuple-element.34), channel_id=1, source_target_pairs={{0,16},{1,5},{2,18},{3,7},{4,20},{5,9},{6,22},{7,11},{8,24},{9,13}... | collective-permute-start | bytes 3538952 | tf_op jit(solution)/shard_map/ppermute | solution.py:316
  86.9 25.7 %collective-permute-start.17 = (bf16[256,2432]{1,0:T(8,128)(2,1)S(1)}, bf16[256,2432]{1,0:T(8,128)(2,1)S(1)}, u32[]{:S(2)}, u32[]{:S(2)}) collective-permute-start(bf16[256,2432]{1,0:T(8,128)(2,1)S(1)} %add_convert_fusion), channel_id=1, source_target_pairs={{0,16},{1,5},{2,18},{3,7},{4,20},{5,9},{6,22},{7,11},{8,24},{9,13}... | collective-permute-start | bytes 3735560 | tf_op jit(solution)/shard_map/ppermute | solution.py:316
  87.3 24.1 %collective-permute-start.19 = (bf16[256,2304]{1,0:T(8,128)(2,1)S(1)}, bf16[256,2304]{1,0:T(8,128)(2,1)S(1)}, u32[]{:S(2)}, u32[]{:S(2)}) collective-permute-start(bf16[256,2304]{1,0:T(8,128)(2,1)S(1)} %add_convert_fusion.1), channel_id=1, source_target_pairs={{0,48},{1,13},{2,50},{3,15},{4,52},{5,1},{6,54},{7,3},{8,56},{9,5}... | collective-permute-start | bytes 3538952 | tf_op jit(solution)/shard_map/ppermute | solution.py:316
  112.6 4.8 %copy-start.3 = (bf16[2304,448]{0,1:T(8,128)(2,1)S(1)}, bf16[2304,448]{0,1:T(8,128)(2,1)}, u32[]{:S(2)}) copy-start(bf16[2304,448]{0,1:T(8,128)(2,1)} %param.23) | copy-start | bytes 6193156
  113.5 10.5 %collective-permute-start.20 = (bf16[64,4736]{1,0:T(8,128)(2,1)S(1)}, bf16[64,4736]{1,0:T(8,128)(2,1)S(1)}, u32[]{:S(2)}, u32[]{:S(2)}) collective-permute-start(bf16[64,4736]{1,0:T(8,128)(2,1)S(1)} %get-tuple-element.40), channel_id=1, source_target_pairs={{0,4},{1,17},{2,6},{3,19},{4,8},{5,21},{6,10},{7,23},{8,12},{9,25}... | collective-permute-start | bytes 1818632 | tf_op jit(solution)/shard_map/ppermute | solution.py:316
  114.0 15.8 %collective-permute-start.21 = (bf16[64,4736]{1,0:T(8,128)(2,1)S(1)}, bf16[64,4736]{1,0:T(8,128)(2,1)S(1)}, u32[]{:S(2)}, u32[]{:S(2)}) collective-permute-start(bf16[64,4736]{1,0:T(8,128)(2,1)S(1)} %get-tuple-element.41), channel_id=1, source_target_pairs={{0,12},{1,49},{2,14},{3,51},{4,0},{5,53},{6,2},{7,55},{8,4},{9,57}... | collective-permute-start | bytes 1818632 | tf_op jit(solution)/shard_map/ppermute | solution.py:316
  116.3 15.3 %collective-permute-start.22 = (bf16[64,4736]{1,0:T(8,128)(2,1)S(1)}, bf16[64,4736]{1,0:T(8,128)(2,1)S(1)}, u32[]{:S(2)}, u32[]{:S(2)}) collective-permute-start(bf16[64,4736]{1,0:T(8,128)(2,1)S(1)} %get-tuple-element.42), channel_id=1, source_target_pairs={{0,8},{1,33},{2,10},{3,35},{4,12},{5,37},{6,14},{7,39},{8,0},{9,41... | collective-permute-start | bytes 1818632 | tf_op jit(solution)/shard_map/ppermute | solution.py:316
  117.4 41.2 %collective-permute-start.27 = (bf16[2304,448]{0,1:T(8,128)(2,1)S(1)}, bf16[2304,448]{0,1:T(8,128)(2,1)}, u32[]{:S(2)}, u32[]{:S(2)}) collective-permute-start(bf16[2304,448]{0,1:T(8,128)(2,1)S(1)} %copy-done.3), channel_id=1, source_target_pairs={{0,1},{1,0},{2,3},{3,2},{4,5},{5,4},{6,7},{7,6},{8,9},{9,8},{10,11... | collective-permute-start | bytes 6193160 | tf_op jit(solution)/shard_map/ppermute | solution.py:334
  132.3 3.4 %collective-permute-start.23 = (bf16[32,4608]{1,0:T(8,128)(2,1)S(1)}, bf16[32,4608]{1,0:T(8,128)(2,1)S(1)}, u32[]{:S(2)}, u32[]{:S(2)}) collective-permute-start(bf16[32,4608]{1,0:T(8,128)(2,1)S(1)} %get-tuple-element.44), channel_id=1, source_target_pairs={{0,1},{1,0},{2,3},{3,2},{4,5},{5,4},{6,7},{7,6},{8,9},{9,8},{10,11... | collective-permute-start | bytes 884744 | tf_op jit(solution)/shard_map/ppermute | solution.py:334
  135.8 8.6 %collective-permute-start.25 = (bf16[32,4608]{1,0:T(8,128)(2,1)S(1)}, bf16[32,4608]{1,0:T(8,128)(2,1)S(1)}, u32[]{:S(2)}, u32[]{:S(2)}) collective-permute-start(bf16[32,4608]{1,0:T(8,128)(2,1)S(1)} %activate.1.refs_0_), channel_id=1, source_target_pairs={{0,48},{1,13},{2,50},{3,15},{4,52},{5,1},{6,54},{7,3},{8,56},{9,5}... | collective-permute-start | bytes 884744 | tf_op jit(solution)/shard_map/ppermute | solution.py:316
  137.6 7.4 %collective-permute-start.26 = (bf16[32,4608]{1,0:T(8,128)(2,1)S(1)}, bf16[32,4608]{1,0:T(8,128)(2,1)S(1)}, u32[]{:S(2)}, u32[]{:S(2)}) collective-permute-start(bf16[32,4608]{1,0:T(8,128)(2,1)S(1)} %activate.1.refs_0_), channel_id=1, source_target_pairs={{0,32},{1,9},{2,34},{3,11},{4,36},{5,13},{6,38},{7,15},{8,40},{9,1... | collective-permute-start | bytes 884744 | tf_op jit(solution)/shard_map/ppermute | solution.py:316
  138.8 9.3 %collective-permute-start.24 = (bf16[32,4608]{1,0:T(8,128)(2,1)S(1)}, bf16[32,4608]{1,0:T(8,128)(2,1)S(1)}, u32[]{:S(2)}, u32[]{:S(2)}) collective-permute-start(bf16[32,4608]{1,0:T(8,128)(2,1)S(1)} %activate.1.refs_0_), channel_id=1, source_target_pairs={{0,16},{1,5},{2,18},{3,7},{4,20},{5,9},{6,22},{7,11},{8,24},{9,13}... | collective-permute-start | bytes 884744 | tf_op jit(solution)/shard_map/ppermute | solution.py:316
  145.0 9.2 %collective-permute-start.31 = (bf16[64,4608]{1,0:T(8,128)(2,1)S(1)}, bf16[64,4608]{1,0:T(8,128)(2,1)}, u32[]{:S(2)}, u32[]{:S(2)}) collective-permute-start(bf16[64,4608]{1,0:T(8,128)(2,1)S(1)} %join.8.refs_1_), channel_id=1, source_target_pairs={{0,12},{1,49},{2,14},{3,51},{4,0},{5,53},{6,2},{7,55},{8,4},{9,57}... | collective-permute-start | bytes 1769480 | tf_op jit(solution)/shard_map/ppermute | solution.py:316
  148.2 10.4 %collective-permute-start.28 = (bf16[64,4608]{1,0:T(8,128)(2,1)S(1)}, bf16[64,4608]{1,0:T(8,128)(2,1)}, u32[]{:S(2)}, u32[]{:S(2)}) collective-permute-start(bf16[64,4608]{1,0:T(8,128)(2,1)S(1)} %join.7.refs_0_), channel_id=1, source_target_pairs={{0,4},{1,17},{2,6},{3,19},{4,8},{5,21},{6,10},{7,23},{8,12},{9,25}... | collective-permute-start | bytes 1769480 | tf_op jit(solution)/shard_map/ppermute | solution.py:316
  148.2 16.6 %collective-permute-start.29 = (bf16[64,4608]{1,0:T(8,128)(2,1)S(1)}, bf16[64,4608]{1,0:T(8,128)(2,1)}, u32[]{:S(2)}, u32[]{:S(2)}) collective-permute-start(bf16[64,4608]{1,0:T(8,128)(2,1)S(1)} %join.8.refs_1_), channel_id=1, source_target_pairs={{0,4},{1,17},{2,6},{3,19},{4,8},{5,21},{6,10},{7,23},{8,12},{9,25}... | collective-permute-start | bytes 1769480 | tf_op jit(solution)/shard_map/ppermute | solution.py:316
  149.7 15.2 %collective-permute-start.30 = (bf16[64,4608]{1,0:T(8,128)(2,1)S(1)}, bf16[64,4608]{1,0:T(8,128)(2,1)}, u32[]{:S(2)}, u32[]{:S(2)}) collective-permute-start(bf16[64,4608]{1,0:T(8,128)(2,1)S(1)} %join.7.refs_0_), channel_id=1, source_target_pairs={{0,12},{1,49},{2,14},{3,51},{4,0},{5,53},{6,2},{7,55},{8,4},{9,57}... | collective-permute-start | bytes 1769480 | tf_op jit(solution)/shard_map/ppermute | solution.py:316
  154.2 13.7 %collective-permute-start.33 = (bf16[64,4608]{1,0:T(8,128)(2,1)}, bf16[64,4608]{1,0:T(8,128)(2,1)}, u32[]{:S(2)}, u32[]{:S(2)}) collective-permute-start(bf16[64,4608]{1,0:T(8,128)(2,1)} %collective-permute-done.31.refs_3_), channel_id=1, source_target_pairs={{0,12},{1,49},{2,14},{3,51},{4,0},{5,53},{6,2},{7,55},{8,4},{9,57}... | collective-permute-start | bytes 1769480 | tf_op jit(solution)/shard_map/ppermute | solution.py:316
  158.6 12.6 %collective-permute-start.32 = (bf16[64,4608]{1,0:T(8,128)(2,1)}, bf16[64,4608]{1,0:T(8,128)(2,1)}, u32[]{:S(2)}, u32[]{:S(2)}) collective-permute-start(bf16[64,4608]{1,0:T(8,128)(2,1)} %collective-permute-done.28.refs_0_), channel_id=1, source_target_pairs={{0,4},{1,17},{2,6},{3,19},{4,8},{5,21},{6,10},{7,23},{8,12},{9,25}... | collective-permute-start | bytes 1769480 | tf_op jit(solution)/shard_map/ppermute | solution.py:316
  173.8 1.0 copy-start.7
  197.3 5.3 %collective-permute-start.34 = (bf16[2,8,7168]{2,1,0:T(8,128)(2,1)S(1)}, bf16[2,8,7168]{2,1,0:T(8,128)(2,1)S(1)}, u32[]{:S(2)}, u32[]{:S(2)}) collective-permute-start(bf16[2,8,7168]{2,1,0:T(8,128)(2,1)S(1)} %reshape.74), channel_id=1, source_target_pairs={{0,1},{1,0},{2,3},{3,2},{4,5},{5,4},{6,7},{7,6},{8,9},{9,8},{10,11... | collective-permute-start | bytes 688136 | tf_op jit(solution)/shard_map/ppermute | solution.py:334

commit v8 on v7

--- a/solution.py
+++ b/solution.py
@@ -145,32 +145,25 @@
     )(*([rows] * len(places)), gain, *weights)
 
 
-def merge_kernel(own_a, own_c, direct_a, direct_c, relay_a, relay_c, *outs):
+def merge_kernel(first_row, own_a, own_c, direct_a, direct_c, relay_a, relay_c, *outs):
     wide_a = own_a.shape[1]
     rows = outs[0].shape[0]
-    for out, place in zip(outs, FACING):
-        part = pl.ds(place * rows, rows)
-        total = wide(own_a[part, :]) + wide(relay_a[part, :]) + wide(direct_a[part, :])
+    for place, out in enumerate(outs):
+        here = pl.ds(place * rows, rows)
+        part = pl.ds(first_row + place * rows, rows)
+        total = wide(own_a[part, :]) + wide(relay_a[here, :]) + wide(direct_a[part, :])
         out[:, :wide_a] = total.astype(jnp.bfloat16)
-        total = wide(own_c[part, :]) + wide(relay_c[part, :]) + wide(direct_c[part, :])
+        total = wide(own_c[part, :]) + wide(relay_c[here, :]) + wide(direct_c[part, :])
         out[:, wide_a:] = total.astype(jnp.bfloat16)
 
 
-def merge(*operands):
+def merge(first_row, *operands):
     own_a, own_c = operands[:2]
     rows = own_a.shape[0] // 4
     cols = own_a.shape[1] + own_c.shape[1]
-    return pl.pallas_call(
-        merge_kernel,
-        out_shape=[jax.ShapeDtypeStruct((rows, cols), jnp.bfloat16)] * 4,
-        in_specs=[pl.BlockSpec(memory_space=pltpu.VMEM)] * 6,
-        out_specs=[pl.BlockSpec(memory_space=pltpu.VMEM)] * 4,
-        compiler_params=pltpu.CompilerParams(vmem_limit_bytes=VMEM_LIMIT),
-        cost_estimate=pl.CostEstimate(
-            flops=12 * rows * cols, bytes_accessed=32 * rows * cols, transcendentals=0
-        ),
-        name="merge",
-    )(*operands)
+    shapes = [jax.ShapeDtypeStruct((rows, cols), jnp.bfloat16)] * 2
+    kernel = functools.partial(merge_kernel, first_row)
+    return whole_call(kernel, "merge", shapes, operands, 16 * rows * cols)
 
 
 def whole_call(kernel, name, out_shapes, operands, cost):
@@ -428,6 +421,7 @@
     behind, ahead, across = (shift_y(sent, s) for s in SHIFTS[1:])
     stream = shared + wide(across)
     rows = jnp.stack([stream, add(behind, ahead)]).astype(jnp.bfloat16)
+    home = jnp.where(yh == 0, stream[:, :, 0], stream[:, :, 1])
     rows = jnp.stack([rows, jnp.swapaxes(swap(rows, "core"), 1, 2)])
     rows = jnp.transpose(rows, (2, 3, 0, 1, 4, 5, 6)).reshape(4, 4, 8 * tokens, width)
 
@@ -440,10 +434,14 @@
     )
     far_a, far_c = shift_1(far_a, 1), shift_1(far_c, -1)
     direct_c, direct_a = shift_1(ahead_c, 1), shift_1(behind_a, -1)
-    relay_a = shift_1(add(ahead_a, far_a).astype(jnp.bfloat16), 1)
-    relay_c = shift_1(add(behind_c, far_c).astype(jnp.bfloat16), -1)
-    blocks = merge(own_a, own_c, direct_a, direct_c, relay_a, relay_c)
-    parts = gather_from(blocks, shift_2)
+    middle = far_a.shape[0] // 2
+    blocks = {}
+    for places, cut in (((2, 3), slice(middle, None)), ((0, 1), slice(0, middle))):
+        relay_a = shift_1(add(ahead_a[cut], far_a[cut]).astype(jnp.bfloat16), 1)
+        relay_c = shift_1(add(behind_c[cut], far_c[cut]).astype(jnp.bfloat16), -1)
+        merged = merge(cut.start, own_a, own_c, direct_a, direct_c, relay_a, relay_c)
+        blocks.update(zip(places, merged))
+    parts = gather_from([blocks[FACING[i]] for i in range(4)], shift_2)
     mine, theirs = settle(parts, model_width, hidden)
     activated = activate(core, mine, swap(theirs, "core"))
 
@@ -461,7 +459,7 @@
         [pair_dot(p, down_pair) for p in pieces]
     ).reshape(4, 4, 2, 2, tokens, width)
     at_home = jnp.arange(2)[None, None, :, None, None] == yh
-    down = jnp.stack([down[:, :, 0] + jnp.where(at_home, stream, 0.0), down[:, :, 1]])
+    down = jnp.stack([down[:, :, 0] + jnp.where(at_home, home[:, :, None], 0.0), down[:, :, 1]])
     down = down.astype(jnp.bfloat16)
     down = absolute(absolute(down, place_2, 1), place_1, 2)
     down = jnp.where(core == 0, jnp.swapaxes(down, 1, 2), down)

time: 204 us -> 201 us (0.985)
  waiting for transfers between devices: 83.9 us -> 69.8 us
  starting transfers between devices: 55.7 us -> 66.5 us
    ppermute x24 -> x26, waiting for transfers between devices: 71.9 us -> 59.3 us  [shift(): return lax.ppermute(value, ('grp', 'yh', 'core'), pairs)]
    ppermute x8, starting transfers between devices: 19.3 us -> 27.1 us  [swap(): return lax.ppermute(value, axis, [(0, 1), (1, 0)])]
    ppermute x24 -> x26, starting transfers between devices: 31.9 us -> 33.8 us  [shift(): return lax.ppermute(value, ('grp', 'yh', 'core'), pairs)]
    pallas_call x11 -> x13, Pallas kernels: 13.8 us -> 14.7 us  [whole_call(): pl.pallas_call(kernel, out_shape=out_shapes, in_specs=[pl.BlockSpec(memor...]
  transfers between devices with their start and end apart: 35 -> 37, of which waited for: 25 -> 25; matrix products, arithmetic and copies ran while one was open for 3% -> 3% of each run, Pallas kernels for 12% -> 13%
where the time goes in v8:
time: 201 us
  waiting for transfers between devices  69.8 us (35%)
  starting transfers between devices  66.5 us (33%)
  Pallas kernels  30.1 us (15%)
  blocking collectives  22.2 us (11%)
  other arithmetic  6.06 us (3%)
  local copies, waits for them, and re-layouts  5.25 us (3%)
    ppermute x26, waiting for transfers between devices, shift(): return lax.ppermute(value, ('grp', 'yh', 'core'), pairs)  59.3 us
    ppermute x26, starting transfers between devices, shift(): return lax.ppermute(value, ('grp', 'yh', 'core'), pairs)  33.8 us
    ppermute x8, starting transfers between devices, swap(): return lax.ppermute(value, axis, [(0, 1), (1, 0)])  27.1 us
    all_to_all x1, blocking collectives, body(): lax.all_to_all(down, ('role', 'grp', 'yh'), split_axis=0, concat_axis=0)  22.2 us
    pallas_call x13, Pallas kernels, whole_call(): pl.pallas_call(kernel, out_shape=out_shapes, in_specs=[pl.BlockSpec(memor...  14.7 us
    pallas_call x1, Pallas kernels, attend(): pl.pallas_call(functools.partial(attend_kernel, scale, latent, per_step),...  9.1 us
    ppermute x3, waiting for transfers between devices, shift_y(): lax.ppermute(value, ('role', 'yh', 'core'), [(p, moved(p)) for p in range...  5.64 us
    ppermute x3, starting transfers between devices, shift_y(): lax.ppermute(value, ('role', 'yh', 'core'), [(p, moved(p)) for p in range...  5.61 us
  transfers between devices with their start and end apart: 37, of which 25 were waited for; matrix products, arithmetic and copies ran while one was open for 3% of the time, Pallas kernels for 13%

profile of v8, /device:TPU:1, one launch (start us, length us, event | category | flops | bytes accessed | tf_op | source)
XLA Modules:
  0.0 200.5 jit_solution(6694392982877814028)
XLA Ops:
  0.0 1.4 collective-permute-start.1
  1.4 1.3 pad_add_fusion.plan_ref
  2.7 9.1 %attend.1 = (bf16[2,8,16,512]{3,2,1,0:T(8,128)(2,1)}, bf16[2,8,16,512]{3,2,1,0:T(8,128)(2,1)}) custom-call(s32[17]{0:T(128)} %pad_add_fusion.plan_ref, bf16[8,4,16,576]{3,2,1,0:T(8,128)(2,1)} %bitcast.75, bf16[8,576]{1,0:T(8,128)(2,1)} %new_ref.1, bf16[8,576,1024]{2,1,0:T(8,128)(2,1)} %bitcast.65, bf16[8,576,1024]{2,1,0:T(8,128)(2,1)} %bitcast.66), custom_call_target="tpu_custom_call" | custom-call | flops 1140850688 | bytes 9437184 | tf_op jit(solution)/shard_map/attend/pallas_call | solution.py:70
  11.8 3.0 %collective-permute-start = (bf16[2,8,16,512]{3,2,1,0:T(8,128)(2,1)}, bf16[2,8,16,512]{3,2,1,0:T(8,128)(2,1)S(1)}, u32[]{:S(2)}, u32[]{:S(2)}) collective-permute-start(bf16[2,8,16,512]{3,2,1,0:T(8,128)(2,1)} %get-tuple-element.26), channel_id=1, source_target_pairs={{0,2},{2,0},{1,3},{3,1},{4,6},{6,4},{5,7},{7,5},{8,10},{10,8},{9,1... | collective-permute-start | bytes 786440 | tf_op jit(solution)/shard_map/ppermute | solution.py:327
  14.8 1.5 copy-done.4
  16.3 1.9 join.6.refs_1_.refs_3_
  18.2 1.8 copy-done
  20.0 1.0 collective-permute-done.far
  21.0 0.7 head_values.1.refs_0_
  21.7 1.7 collective-permute-start.2
  23.4 2.3 %collective-permute-start.3 = (bf16[16,4096]{1,0:T(8,128)(2,1)S(1)}, bf16[16,4096]{1,0:T(8,128)(2,1)S(1)}, u32[]{:S(2)}, u32[]{:S(2)}) collective-permute-start(bf16[16,4096]{1,0:T(8,128)(2,1)S(1)} %head_values.1.refs_0_), channel_id=1, source_target_pairs={{0,48},{1,13},{2,50},{3,15},{4,52},{5,1},{6,54},{7,3},{8,56},{9,5}... | collective-permute-start | bytes 393224 | tf_op jit(solution)/shard_map/ppermute | solution.py:309
  25.7 1.2 collective-permute-start.4
  27.2 2.5 %broadcast_select_fusion = (bf16[448,2304]{1,0:T(8,128)(2,1)S(1)}, bf16[448,2304]{1,0:T(8,128)(2,1)S(1)}) fusion(bf16[448,2304]{1,0:T(8,128)(2,1)} %param.22, bf16[448,2304]{1,0:T(8,128)(2,1)} %param.21, pred[]{:T(512)S(6)} %eq.31), kind=kLoop, calls=%fused_computation | loop fusion | flops 2064384 | bytes 8257537 | tf_op jit(solution)/shard_map/jit(_where)/select_n | solution.py:407
  29.9 1.4 collective-permute-done.4.refs_3_
  31.4 0.9 collective-permute-start.6
  32.2 1.9 collective-permute-start.7
  34.1 1.1 collective-permute-start.8
  35.5 3.8 %collective-permute-start.13 = (bf16[448,2304]{1,0:T(8,128)(2,1)S(1)}, bf16[448,2304]{1,0:T(8,128)(2,1)S(1)}, u32[]{:S(2)}, u32[]{:S(2)}) collective-permute-start(bf16[448,2304]{1,0:T(8,128)(2,1)S(1)} %get-tuple-element.47), channel_id=1, source_target_pairs={{0,1},{1,0},{2,3},{3,2},{4,5},{5,4},{6,7},{7,6},{8,9},{9,8},{10,11... | collective-permute-start | bytes 6193160 | tf_op jit(solution)/shard_map/ppermute | solution.py:327
  39.2 1.2 pair_dot.5
  41.0 4.9 %collective-permute-done.7.refs_1_ = bf16[64,4096]{1,0:T(8,128)(2,1)S(1)} collective-permute-done((bf16[64,4096]{1,0:T(8,128)(2,1)S(1)}, bf16[64,4096]{1,0:T(8,128)(2,1)S(1)}, u32[]{:S(2)}, u32[]{:S(2)}) %collective-permute-start.7) | collective-permute-done | bytes 524320 | tf_op jit(solution)/shard_map/ppermute | solution.py:309
  45.9 1.6 collective-permute-done.8.refs_2_
  47.5 1.2 pair_dot.6
  48.9 2.9 %collective-permute-start.9 = (bf16[4,4,2,8,448]{4,3,2,0,1:T(8,128)(2,1)S(1)}, bf16[4,4,2,8,448]{4,3,2,0,1:T(8,128)(2,1)S(1)}, u32[]{:S(2)}, u32[]{:S(2)}) collective-permute-start(bf16[4,4,2,8,448]{4,3,2,0,1:T(8,128)(2,1)S(1)} %copy.86), channel_id=1, source_target_pairs={{0,2},{1,3},{2,0},{3,1},{64,66},{65,67},{66,64},{67,65},{4,6},{5,7... | collective-permute-start | bytes 688136 | tf_op jit(solution)/shard_map/ppermute | solution.py:323
  52.2 2.3 %collective-permute-start.11 = (bf16[4,4,2,8,448]{4,3,2,0,1:T(8,128)(2,1)S(1)}, bf16[4,4,2,8,448]{4,3,2,0,1:T(8,128)(2,1)S(1)}, u32[]{:S(2)}, u32[]{:S(2)}) collective-permute-start(bf16[4,4,2,8,448]{4,3,2,0,1:T(8,128)(2,1)S(1)} %copy.86), channel_id=1, source_target_pairs={{0,66},{1,67},{2,64},{3,65},{64,0},{65,1},{66,2},{67,3},{4,70},{5,... | collective-permute-start | bytes 688136 | tf_op jit(solution)/shard_map/ppermute | solution.py:323
  54.5 1.2 collective-permute-done.9
  55.9 4.2 %collective-permute-done.10 = bf16[4,4,2,8,448]{4,3,2,0,1:T(8,128)(2,1)S(1)} collective-permute-done((bf16[4,4,2,8,448]{4,3,2,0,1:T(8,128)(2,1)S(1)}, bf16[4,4,2,8,448]{4,3,2,0,1:T(8,128)(2,1)S(1)}, u32[]{:S(2)}, u32[]{:S(2)}) %collective-permute-start.10) | collective-permute-done | bytes 229408 | tf_op jit(solution)/shard_map/ppermute | solution.py:323
  60.5 4.9 %collective-permute-start.12 = (bf16[2,4,4,2,8,448]{5,4,3,2,1,0:T(8,128)(2,1)S(1)}, bf16[2,4,4,2,8,448]{5,4,3,2,1,0:T(8,128)(2,1)S(1)}, u32[]{:S(2)}, u32[]{:S(2)}) collective-permute-start(bf16[2,4,4,2,8,448]{5,4,3,2,1,0:T(8,128)(2,1)S(1)} %pad_maximum_fusion.2), channel_id=1, source_target_pairs={{0,1},{1,0},{2,3},{3,2},{4,5},{5,4},{6,7},{7,6},{8,9},{9,8},{10,11... | collective-permute-start | bytes 1376264 | tf_op jit(solution)/shard_map/ppermute | solution.py:327
  65.4 1.5 collective-permute-done.12
  67.2 1.4 partial_sums.5
  68.8 2.6 %collective-permute-start.18 = (bf16[256,2304]{1,0:T(8,128)(2,1)S(1)}, bf16[256,2304]{1,0:T(8,128)(2,1)S(1)}, u32[]{:S(2)}, u32[]{:S(2)}) collective-permute-start(bf16[256,2304]{1,0:T(8,128)(2,1)S(1)} %get-tuple-element.38), channel_id=1, source_target_pairs={{0,48},{1,13},{2,50},{3,15},{4,52},{5,1},{6,54},{7,3},{8,56},{9,5}... | collective-permute-start | bytes 3538952 | tf_op jit(solution)/shard_map/ppermute | solution.py:309
  71.3 1.4 partial_sums.4
  72.8 1.5 collective-permute-start.15
  74.3 2.6 %partial_sums.3 = (bf16[256,2432]{1,0:T(8,128)(2,1)S(1)}, bf16[256,2304]{1,0:T(8,128)(2,1)S(1)}, bf16[256,2432]{1,0:T(8,128)(2,1)S(1)}, bf16[256,2304]{1,0:T(8,128)(2,1)S(1)}) custom-call(bf16[4,4,64,448]{3,2,1,0:T(8,128)(2,1)S(1)} %bitcast.57, bf16[4,4,64,448]{3,2,1,0:T(8,128)(2,1)S(1)} %bitcast.58, bf16[4,4,64,448]{3,2,1,0:T(8,128)(2,1)S(1)} %bitcast.59, ...), custom_call_target="tpu_custom_call" | custom-call | flops 2172649472 | bytes 8978432 | tf_op jit(solution)/shard_map/partial_sums/pallas_call | solution.py:130
  76.9 9.0 %collective-permute-done.16 = bf16[256,2432]{1,0:T(8,128)(2,1)S(1)} collective-permute-done((bf16[256,2432]{1,0:T(8,128)(2,1)S(1)}, bf16[256,2432]{1,0:T(8,128)(2,1)S(1)}, u32[]{:S(2)}, u32[]{:S(2)}) %collective-permute-start.16) | collective-permute-done | bytes 1245216 | tf_op jit(solution)/shard_map/ppermute | solution.py:309
  86.7 2.7 %collective-permute-start.21 = (bf16[128,2304]{1,0:T(8,128)(2,1)S(1)}, bf16[128,2304]{1,0:T(8,128)(2,1)S(1)}, u32[]{:S(2)}, u32[]{:S(2)}) collective-permute-start(bf16[128,2304]{1,0:T(8,128)(2,1)S(1)} %get-tuple-element.51), channel_id=1, source_target_pairs={{0,48},{1,13},{2,50},{3,15},{4,52},{5,1},{6,54},{7,3},{8,56},{9,5}... | collective-permute-start | bytes 1769480 | tf_op jit(solution)/shard_map/ppermute | solution.py:309
  89.4 9.2 %collective-permute-done.15.direct_c = bf16[256,2304]{1,0:T(8,128)(2,1)S(1)} collective-permute-done((bf16[256,2304]{1,0:T(8,128)(2,1)S(1)}, bf16[256,2304]{1,0:T(8,128)(2,1)S(1)}, u32[]{:S(2)}, u32[]{:S(2)}) %collective-permute-start.15) | collective-permute-done | bytes 1179680 | tf_op jit(solution)/shard_map/ppermute | solution.py:309
  98.6 5.6 %collective-permute-done.21.relay_c = bf16[128,2304]{1,0:T(8,128)(2,1)S(1)} collective-permute-done((bf16[128,2304]{1,0:T(8,128)(2,1)S(1)}, bf16[128,2304]{1,0:T(8,128)(2,1)S(1)}, u32[]{:S(2)}, u32[]{:S(2)}) %collective-permute-start.21) | collective-permute-done | bytes 589856 | tf_op jit(solution)/shard_map/ppermute | solution.py:309
  104.1 1.1 collective-permute-done.20.relay_a
  105.7 0.6 collective-permute-start.22
  106.3 2.5 %collective-permute-start.24 = (bf16[64,4736]{1,0:T(8,128)(2,1)S(1)}, bf16[64,4736]{1,0:T(8,128)(2,1)S(1)}, u32[]{:S(2)}, u32[]{:S(2)}) collective-permute-start(bf16[64,4736]{1,0:T(8,128)(2,1)S(1)} %get-tuple-element.42), channel_id=1, source_target_pairs={{0,8},{1,33},{2,10},{3,35},{4,12},{5,37},{6,14},{7,39},{8,0},{9,41... | collective-permute-start | bytes 1818632 | tf_op jit(solution)/shard_map/ppermute | solution.py:309
  108.8 1.7 collective-permute-done.19.relay_c
  110.5 1.9 collective-permute-done.17.relay_a
  112.8 1.4 collective-permute-start.23
  114.3 6.4 %collective-permute-start.29 = (bf16[2304,448]{0,1:T(8,128)(2,1)S(1)}, bf16[2304,448]{0,1:T(8,128)(2,1)}, u32[]{:S(2)}, u32[]{:S(2)}) collective-permute-start(bf16[2304,448]{0,1:T(8,128)(2,1)S(1)} %copy-done.3), channel_id=1, source_target_pairs={{0,1},{1,0},{2,3},{3,2},{4,5},{5,4},{6,7},{7,6},{8,9},{9,8},{10,11... | collective-permute-start | bytes 6193160 | tf_op jit(solution)/shard_map/ppermute | solution.py:327
  120.6 5.2 %collective-permute-done.24.refs_3_ = bf16[64,4736]{1,0:T(8,128)(2,1)S(1)} collective-permute-done((bf16[64,4736]{1,0:T(8,128)(2,1)S(1)}, bf16[64,4736]{1,0:T(8,128)(2,1)S(1)}, u32[]{:S(2)}, u32[]{:S(2)}) %collective-permute-start.24) | collective-permute-done | bytes 606240 | tf_op jit(solution)/shard_map/ppermute | solution.py:309
  126.8 3.2 %collective-permute-start.25 = (bf16[32,4608]{1,0:T(8,128)(2,1)S(1)}, bf16[32,4608]{1,0:T(8,128)(2,1)S(1)}, u32[]{:S(2)}, u32[]{:S(2)}) collective-permute-start(bf16[32,4608]{1,0:T(8,128)(2,1)S(1)} %get-tuple-element.44), channel_id=1, source_target_pairs={{0,1},{1,0},{2,3},{3,2},{4,5},{5,4},{6,7},{7,6},{8,9},{9,8},{10,11... | collective-permute-start | bytes 884744 | tf_op jit(solution)/shard_map/ppermute | solution.py:327
  130.1 1.2 collective-permute-done.25.theirs
  131.4 2.3 %collective-permute-start.27 = (bf16[32,4608]{1,0:T(8,128)(2,1)S(1)}, bf16[32,4608]{1,0:T(8,128)(2,1)S(1)}, u32[]{:S(2)}, u32[]{:S(2)}) collective-permute-start(bf16[32,4608]{1,0:T(8,128)(2,1)S(1)} %activate.1.refs_0_), channel_id=1, source_target_pairs={{0,48},{1,13},{2,50},{3,15},{4,52},{5,1},{6,54},{7,3},{8,56},{9,5}... | collective-permute-start | bytes 884744 | tf_op jit(solution)/shard_map/ppermute | solution.py:309
  133.8 0.7 collective-permute-start.26
  134.5 6.2 %collective-permute-done.27.refs_0_ = bf16[32,4608]{1,0:T(8,128)(2,1)S(1)} collective-permute-done((bf16[32,4608]{1,0:T(8,128)(2,1)S(1)}, bf16[32,4608]{1,0:T(8,128)(2,1)S(1)}, u32[]{:S(2)}, u32[]{:S(2)}) %collective-permute-start.27) | collective-permute-done | bytes 294944 | tf_op jit(solution)/shard_map/ppermute | solution.py:309
  141.2 3.4 %collective-permute-start.33 = (bf16[64,4608]{1,0:T(8,128)(2,1)S(1)}, bf16[64,4608]{1,0:T(8,128)(2,1)}, u32[]{:S(2)}, u32[]{:S(2)}) collective-permute-start(bf16[64,4608]{1,0:T(8,128)(2,1)S(1)} %join.8.refs_1_), channel_id=1, source_target_pairs={{0,12},{1,49},{2,14},{3,51},{4,0},{5,53},{6,2},{7,55},{8,4},{9,57}... | collective-permute-start | bytes 1769480 | tf_op jit(solution)/shard_map/ppermute | solution.py:309
  144.8 2.9 %collective-permute-start.32 = (bf16[64,4608]{1,0:T(8,128)(2,1)S(1)}, bf16[64,4608]{1,0:T(8,128)(2,1)}, u32[]{:S(2)}, u32[]{:S(2)}) collective-permute-start(bf16[64,4608]{1,0:T(8,128)(2,1)S(1)} %join.7.refs_0_), channel_id=1, source_target_pairs={{0,12},{1,49},{2,14},{3,51},{4,0},{5,53},{6,2},{7,55},{8,4},{9,57}... | collective-permute-start | bytes 1769480 | tf_op jit(solution)/shard_map/ppermute | solution.py:309
  147.8 3.7 %collective-permute-done.33.refs_3_ = bf16[64,4608]{1,0:T(8,128)(2,1)} collective-permute-done((bf16[64,4608]{1,0:T(8,128)(2,1)S(1)}, bf16[64,4608]{1,0:T(8,128)(2,1)}, u32[]{:S(2)}, u32[]{:S(2)}) %collective-permute-start.33) | collective-permute-done | bytes 589856 | tf_op jit(solution)/shard_map/ppermute | solution.py:309
  151.5 3.5 %collective-permute-start.35 = (bf16[64,4608]{1,0:T(8,128)(2,1)}, bf16[64,4608]{1,0:T(8,128)(2,1)}, u32[]{:S(2)}, u32[]{:S(2)}) collective-permute-start(bf16[64,4608]{1,0:T(8,128)(2,1)} %collective-permute-done.33.refs_3_), channel_id=1, source_target_pairs={{0,12},{1,49},{2,14},{3,51},{4,0},{5,53},{6,2},{7,55},{8,4},{9,57}... | collective-permute-start | bytes 1769480 | tf_op jit(solution)/shard_map/ppermute | solution.py:309
  155.1 1.9 join.9.refs_2_.refs_4_
  157.1 1.3 pair_dot.7
  158.4 3.0 %collective-permute-done.31.refs_1_ = bf16[64,4608]{1,0:T(8,128)(2,1)} collective-permute-done((bf16[64,4608]{1,0:T(8,128)(2,1)S(1)}, bf16[64,4608]{1,0:T(8,128)(2,1)}, u32[]{:S(2)}, u32[]{:S(2)}) %collective-permute-start.31) | collective-permute-done | bytes 589856 | tf_op jit(solution)/shard_map/ppermute | solution.py:309
  161.4 3.0 %pair_dot.8 = f32[256,448]{1,0:T(8,128)S(1)} custom-call(bf16[64,4608]{1,0:T(8,128)(2,1)} %collective-permute-done.30.refs_0_, bf16[64,4608]{1,0:T(8,128)(2,1)} %collective-permute-done.31.refs_1_, bf16[64,4608]{1,0:T(8,128)(2,1)} %collective-permute-done.32.refs_2_, bf16[64,4608]{1,0:T(8,128)(2,1)} %collective-permute-done.33.refs_3_, ...), custom_call_target="tpu_custom_call" | custom-call | flops 4128768 | bytes 4128768 | tf_op jit(solution)/shard_map/pair_dot/pallas_call | solution.py:170
  164.4 3.3 %collective-permute-done.34.refs_0_ = bf16[64,4608]{1,0:T(8,128)(2,1)} collective-permute-done((bf16[64,4608]{1,0:T(8,128)(2,1)}, bf16[64,4608]{1,0:T(8,128)(2,1)}, u32[]{:S(2)}, u32[]{:S(2)}) %collective-permute-start.34) | collective-permute-done | bytes 589856 | tf_op jit(solution)/shard_map/ppermute | solution.py:309
  167.7 2.6 %pair_dot.9 = f32[128,448]{1,0:T(8,128)S(1)} custom-call(bf16[64,4608]{1,0:T(8,128)(2,1)} %collective-permute-done.34.refs_0_, bf16[64,4608]{1,0:T(8,128)(2,1)} %collective-permute-done.35.refs_1_, bf16[896,2304]{1,0:T(8,128)(2,1)S(1)} %join.9.refs_2_.refs_4_), custom_call_target="tpu_custom_call" | custom-call | flops 4128768 | bytes 4128768 | tf_op jit(solution)/shard_map/pair_dot/pallas_call | solution.py:170
  171.2 22.2 %all_to_all.5 = bf16[64,16,448]{2,1,0:T(8,128)(2,1)S(1)} all-to-all(bf16[64,16,448]{2,1,0:T(8,128)(2,1)S(1)} %bitcast.68), channel_id=1, replica_groups=mesh['role'=2,'grp'=16,'yh'=2,'core'=2] {'role','grp','yh'}, dimensions={0} | all-to-all | bytes 1835008 | tf_op jit(solution)/shard_map/all_to_all | solution.py:470
  194.1 4.4 %collective-permute-start.36 = (bf16[2,8,7168]{2,1,0:T(8,128)(2,1)S(1)}, bf16[2,8,7168]{2,1,0:T(8,128)(2,1)S(1)}, u32[]{:S(2)}, u32[]{:S(2)}) collective-permute-start(bf16[2,8,7168]{2,1,0:T(8,128)(2,1)S(1)} %reshape.87), channel_id=1, source_target_pairs={{0,1},{1,0},{2,3},{3,2},{4,5},{5,4},{6,7},{7,6},{8,9},{9,8},{10,11... | collective-permute-start | bytes 688136 | tf_op jit(solution)/shard_map/ppermute | solution.py:327
  198.5 1.1 collective-permute-done.36
  199.7 0.8 copy.80
  (102 shorter events, 8.2 us)
Async XLA Ops:
  0.0 20.9 %collective-permute-start.1 = (bf16[16,512,128]{2,1,0:T(8,128)(2,1)}, bf16[16,512,128]{2,1,0:T(8,128)(2,1)S(1)}, u32[]{:S(2)}, u32[]{:S(2)}) collective-permute-start(bf16[16,512,128]{2,1,0:T(8,128)(2,1)} %refs_0_.1), channel_id=1, source_target_pairs={{0,1},{1,0},{2,3},{3,2},{4,5},{5,4},{6,7},{7,6},{8,9},{9,8},{10,11... | collective-permute-start | bytes 6291464 | tf_op jit(solution)/shard_map/ppermute | solution.py:327
  1.4 13.4 %collective-permute-start.5 = (bf16[2048,448]{0,1:T(8,128)(2,1)}, bf16[2048,448]{0,1:T(8,128)(2,1)}, u32[]{:S(2)}, u32[]{:S(2)}) collective-permute-start(bf16[2048,448]{0,1:T(8,128)(2,1)} %param.19), channel_id=1, source_target_pairs={{0,1},{1,0},{2,3},{3,2},{4,5},{5,4},{6,7},{7,6},{8,9},{9,8},{10,11... | collective-permute-start | bytes 5505032 | tf_op jit(solution)/shard_map/ppermute | solution.py:327
  11.8 9.1 %collective-permute-start = (bf16[2,8,16,512]{3,2,1,0:T(8,128)(2,1)}, bf16[2,8,16,512]{3,2,1,0:T(8,128)(2,1)S(1)}, u32[]{:S(2)}, u32[]{:S(2)}) collective-permute-start(bf16[2,8,16,512]{3,2,1,0:T(8,128)(2,1)} %get-tuple-element.26), channel_id=1, source_target_pairs={{0,2},{2,0},{1,3},{3,1},{4,6},{6,4},{5,7},{7,5},{8,10},{10,8},{9,1... | collective-permute-start | bytes 786440 | tf_op jit(solution)/shard_map/ppermute | solution.py:327
  14.8 1.5 copy-start.4
  16.3 4.7 %copy-start.2 = (bf16[16,512,128]{2,1,0:T(8,128)(2,1)S(1)}, bf16[16,512,128]{2,1,0:T(8,128)(2,1)}, u32[]{:S(2)}) copy-start(bf16[16,512,128]{2,1,0:T(8,128)(2,1)} %refs_0_.1) | copy-start | bytes 6291460
  16.3 4.7 %copy-start.5 = (bf16[2,8,16,512]{3,2,1,0:T(8,128)(2,1)S(1)}, bf16[2,8,16,512]{3,2,1,0:T(8,128)(2,1)}, u32[]{:S(2)}) copy-start(bf16[2,8,16,512]{3,2,1,0:T(8,128)(2,1)} %get-tuple-element.25.near) | copy-start | bytes 786436
  18.2 1.8 copy-start
  21.0 6.0 %copy-start.9 = (bf16[512,448]{0,1:T(8,128)(2,1)S(1)}, bf16[512,448]{0,1:T(8,128)(2,1)}, u32[]{:S(2)}) copy-start(bf16[512,448]{0,1:T(8,128)(2,1)} %param.17) | copy-start | bytes 1376260
  21.7 8.2 %collective-permute-start.2 = (bf16[16,4096]{1,0:T(8,128)(2,1)S(1)}, bf16[16,4096]{1,0:T(8,128)(2,1)S(1)}, u32[]{:S(2)}, u32[]{:S(2)}) collective-permute-start(bf16[16,4096]{1,0:T(8,128)(2,1)S(1)} %head_values.1.refs_0_), channel_id=1, source_target_pairs={{0,16},{1,5},{2,18},{3,7},{4,20},{5,9},{6,22},{7,11},{8,24},{9,13}... | collective-permute-start | bytes 393224 | tf_op jit(solution)/shard_map/ppermute | solution.py:309
  23.4 6.5 %collective-permute-start.3 = (bf16[16,4096]{1,0:T(8,128)(2,1)S(1)}, bf16[16,4096]{1,0:T(8,128)(2,1)S(1)}, u32[]{:S(2)}, u32[]{:S(2)}) collective-permute-start(bf16[16,4096]{1,0:T(8,128)(2,1)S(1)} %head_values.1.refs_0_), channel_id=1, source_target_pairs={{0,48},{1,13},{2,50},{3,15},{4,52},{5,1},{6,54},{7,3},{8,56},{9,5}... | collective-permute-start | bytes 393224 | tf_op jit(solution)/shard_map/ppermute | solution.py:309
  25.7 5.6 %collective-permute-start.4 = (bf16[16,4096]{1,0:T(8,128)(2,1)S(1)}, bf16[16,4096]{1,0:T(8,128)(2,1)S(1)}, u32[]{:S(2)}, u32[]{:S(2)}) collective-permute-start(bf16[16,4096]{1,0:T(8,128)(2,1)S(1)} %head_values.1.refs_0_), channel_id=1, source_target_pairs={{0,32},{1,9},{2,34},{3,11},{4,36},{5,13},{6,38},{7,15},{8,40},{9,1... | collective-permute-start | bytes 393224 | tf_op jit(solution)/shard_map/ppermute | solution.py:309
  29.7 9.5 %copy-start.1 = (bf16[896,2048]{1,0:T(8,128)(2,1)S(1)}, bf16[896,2048]{1,0:T(8,128)(2,1)}, u32[]{:S(2)}) copy-start(bf16[896,2048]{1,0:T(8,128)(2,1)} %copy-done) | copy-start | bytes 11010052
  31.4 9.6 %collective-permute-start.6 = (bf16[64,4096]{1,0:T(8,128)(2,1)S(1)}, bf16[64,4096]{1,0:T(8,128)(2,1)S(1)}, u32[]{:S(2)}, u32[]{:S(2)}) collective-permute-start(bf16[64,4096]{1,0:T(8,128)(2,1)S(1)} %join.5.refs_0_), channel_id=1, source_target_pairs={{0,4},{1,17},{2,6},{3,19},{4,8},{5,21},{6,10},{7,23},{8,12},{9,25}... | collective-permute-start | bytes 1572872 | tf_op jit(solution)/shard_map/ppermute | solution.py:309
  32.2 13.6 %collective-permute-start.7 = (bf16[64,4096]{1,0:T(8,128)(2,1)S(1)}, bf16[64,4096]{1,0:T(8,128)(2,1)S(1)}, u32[]{:S(2)}, u32[]{:S(2)}) collective-permute-start(bf16[64,4096]{1,0:T(8,128)(2,1)S(1)} %join.5.refs_0_), channel_id=1, source_target_pairs={{0,12},{1,49},{2,14},{3,51},{4,0},{5,53},{6,2},{7,55},{8,4},{9,57}... | collective-permute-start | bytes 1572872 | tf_op jit(solution)/shard_map/ppermute | solution.py:309
  34.1 13.4 %collective-permute-start.8 = (bf16[64,4096]{1,0:T(8,128)(2,1)S(1)}, bf16[64,4096]{1,0:T(8,128)(2,1)S(1)}, u32[]{:S(2)}, u32[]{:S(2)}) collective-permute-start(bf16[64,4096]{1,0:T(8,128)(2,1)S(1)} %join.5.refs_0_), channel_id=1, source_target_pairs={{0,8},{1,33},{2,10},{3,35},{4,12},{5,37},{6,14},{7,39},{8,0},{9,41... | collective-permute-start | bytes 1572872 | tf_op jit(solution)/shard_map/ppermute | solution.py:309
  35.5 5.0 %copy-start.8 = (bf16[4,4,2,8,448]{4,3,2,1,0:T(8,128)(2,1)}, bf16[4,4,2,8,448]{4,3,2,1,0:T(8,128)(2,1)S(1)}, u32[]{:S(2)}) copy-start(bf16[4,4,2,8,448]{4,3,2,1,0:T(8,128)(2,1)S(1)} %fusion.4) | copy-start | bytes 688132
  35.5 31.7 %collective-permute-start.13 = (bf16[448,2304]{1,0:T(8,128)(2,1)S(1)}, bf16[448,2304]{1,0:T(8,128)(2,1)S(1)}, u32[]{:S(2)}, u32[]{:S(2)}) collective-permute-start(bf16[448,2304]{1,0:T(8,128)(2,1)S(1)} %get-tuple-element.47), channel_id=1, source_target_pairs={{0,1},{1,0},{2,3},{3,2},{4,5},{5,4},{6,7},{7,6},{8,9},{9,8},{10,11... | collective-permute-start | bytes 6193160 | tf_op jit(solution)/shard_map/ppermute | solution.py:327
  41.0 7.7 %slice-start = ((bf16[4,4,2,8,448]{4,3,2,1,0:T(8,128)(2,1)}), bf16[4,2,2,8,448]{4,3,2,1,0:T(8,128)(2,1)S(1)}, s32[]{:S(2)}) async-start(bf16[4,4,2,8,448]{4,3,2,1,0:T(8,128)(2,1)} %copy-done.8), calls=%async_computation.1 | async-start | bytes 262144 | tf_op jit(solution)/shard_map/slice | solution.py:356
  48.9 6.8 %collective-permute-start.9 = (bf16[4,4,2,8,448]{4,3,2,0,1:T(8,128)(2,1)S(1)}, bf16[4,4,2,8,448]{4,3,2,0,1:T(8,128)(2,1)S(1)}, u32[]{:S(2)}, u32[]{:S(2)}) collective-permute-start(bf16[4,4,2,8,448]{4,3,2,0,1:T(8,128)(2,1)S(1)} %copy.86), channel_id=1, source_target_pairs={{0,2},{1,3},{2,0},{3,1},{64,66},{65,67},{66,64},{67,65},{4,6},{5,7... | collective-permute-start | bytes 688136 | tf_op jit(solution)/shard_map/ppermute | solution.py:323
  51.8 8.3 %collective-permute-start.10 = (bf16[4,4,2,8,448]{4,3,2,0,1:T(8,128)(2,1)S(1)}, bf16[4,4,2,8,448]{4,3,2,0,1:T(8,128)(2,1)S(1)}, u32[]{:S(2)}, u32[]{:S(2)}) collective-permute-start(bf16[4,4,2,8,448]{4,3,2,0,1:T(8,128)(2,1)S(1)} %copy.86), channel_id=1, source_target_pairs={{0,64},{1,65},{2,66},{3,67},{64,2},{65,3},{66,0},{67,1},{4,68},{5,... | collective-permute-start | bytes 688136 | tf_op jit(solution)/shard_map/ppermute | solution.py:323
  52.2 8.1 %collective-permute-start.11 = (bf16[4,4,2,8,448]{4,3,2,0,1:T(8,128)(2,1)S(1)}, bf16[4,4,2,8,448]{4,3,2,0,1:T(8,128)(2,1)S(1)}, u32[]{:S(2)}, u32[]{:S(2)}) collective-permute-start(bf16[4,4,2,8,448]{4,3,2,0,1:T(8,128)(2,1)S(1)} %copy.86), channel_id=1, source_target_pairs={{0,66},{1,67},{2,64},{3,65},{64,0},{65,1},{66,2},{67,3},{4,70},{5,... | collective-permute-start | bytes 688136 | tf_op jit(solution)/shard_map/ppermute | solution.py:323
  55.8 4.7 %copy-start.6 = (f32[4,4,2,8,448]{4,3,2,1,0:T(8,128)}, f32[4,4,2,8,448]{4,3,2,1,0:T(8,128)S(1)}, u32[]{:S(2)}) copy-start(f32[4,4,2,8,448]{4,3,2,1,0:T(8,128)S(1)} %get-tuple-element.46) | copy-start | bytes 1376260
  55.8 9.5 %copy-start.10 = (bf16[448]{0:T(512)(128)(2,1)S(1)}, bf16[448]{0:T(512)(128)(2,1)}, u32[]{:S(2)}) copy-start(bf16[448]{0:T(512)(128)(2,1)} %param.20) | copy-start | bytes 2692
  60.5 6.4 %collective-permute-start.12 = (bf16[2,4,4,2,8,448]{5,4,3,2,1,0:T(8,128)(2,1)S(1)}, bf16[2,4,4,2,8,448]{5,4,3,2,1,0:T(8,128)(2,1)S(1)}, u32[]{:S(2)}, u32[]{:S(2)}) collective-permute-start(bf16[2,4,4,2,8,448]{5,4,3,2,1,0:T(8,128)(2,1)S(1)} %pad_maximum_fusion.2), channel_id=1, source_target_pairs={{0,1},{1,0},{2,3},{3,2},{4,5},{5,4},{6,7},{7,6},{8,9},{9,8},{10,11... | collective-permute-start | bytes 1376264 | tf_op jit(solution)/shard_map/ppermute | solution.py:327
  68.6 17.3 %collective-permute-start.16 = (bf16[256,2432]{1,0:T(8,128)(2,1)S(1)}, bf16[256,2432]{1,0:T(8,128)(2,1)S(1)}, u32[]{:S(2)}, u32[]{:S(2)}) collective-permute-start(bf16[256,2432]{1,0:T(8,128)(2,1)S(1)} %get-tuple-element.36), channel_id=1, source_target_pairs={{0,16},{1,5},{2,18},{3,7},{4,20},{5,9},{6,22},{7,11},{8,24},{9,13}... | collective-permute-start | bytes 3735560 | tf_op jit(solution)/shard_map/ppermute | solution.py:309
  68.8 17.6 %collective-permute-start.18 = (bf16[256,2304]{1,0:T(8,128)(2,1)S(1)}, bf16[256,2304]{1,0:T(8,128)(2,1)S(1)}, u32[]{:S(2)}, u32[]{:S(2)}) collective-permute-start(bf16[256,2304]{1,0:T(8,128)(2,1)S(1)} %get-tuple-element.38), channel_id=1, source_target_pairs={{0,48},{1,13},{2,50},{3,15},{4,52},{5,1},{6,54},{7,3},{8,56},{9,5}... | collective-permute-start | bytes 3538952 | tf_op jit(solution)/shard_map/ppermute | solution.py:309
  72.7 25.8 %collective-permute-start.14 = (bf16[256,2432]{1,0:T(8,128)(2,1)S(1)}, bf16[256,2432]{1,0:T(8,128)(2,1)S(1)}, u32[]{:S(2)}, u32[]{:S(2)}) collective-permute-start(bf16[256,2432]{1,0:T(8,128)(2,1)S(1)} %get-tuple-element.33), channel_id=1, source_target_pairs={{0,48},{1,13},{2,50},{3,15},{4,52},{5,1},{6,54},{7,3},{8,56},{9,5}... | collective-permute-start | bytes 3735560 | tf_op jit(solution)/shard_map/ppermute | solution.py:309
  72.8 25.7 %collective-permute-start.15 = (bf16[256,2304]{1,0:T(8,128)(2,1)S(1)}, bf16[256,2304]{1,0:T(8,128)(2,1)S(1)}, u32[]{:S(2)}, u32[]{:S(2)}) collective-permute-start(bf16[256,2304]{1,0:T(8,128)(2,1)S(1)} %get-tuple-element.34), channel_id=1, source_target_pairs={{0,16},{1,5},{2,18},{3,7},{4,20},{5,9},{6,22},{7,11},{8,24},{9,13}... | collective-permute-start | bytes 3538952 | tf_op jit(solution)/shard_map/ppermute | solution.py:309
  86.2 19.0 %collective-permute-start.20 = (bf16[128,2432]{1,0:T(8,128)(2,1)S(1)}, bf16[128,2432]{1,0:T(8,128)(2,1)S(1)}, u32[]{:S(2)}, u32[]{:S(2)}) collective-permute-start(bf16[128,2432]{1,0:T(8,128)(2,1)S(1)} %get-tuple-element.49), channel_id=1, source_target_pairs={{0,16},{1,5},{2,18},{3,7},{4,20},{5,9},{6,22},{7,11},{8,24},{9,13}... | collective-permute-start | bytes 1867784 | tf_op jit(solution)/shard_map/ppermute | solution.py:309
  86.3 26.1 %collective-permute-start.17 = (bf16[128,2432]{1,0:T(8,128)(2,1)S(1)}, bf16[128,2432]{1,0:T(8,128)(2,1)S(1)}, u32[]{:S(2)}, u32[]{:S(2)}) collective-permute-start(bf16[128,2432]{1,0:T(8,128)(2,1)S(1)} %get-tuple-element.50), channel_id=1, source_target_pairs={{0,16},{1,5},{2,18},{3,7},{4,20},{5,9},{6,22},{7,11},{8,24},{9,13}... | collective-permute-start | bytes 1867784 | tf_op jit(solution)/shard_map/ppermute | solution.py:309
  86.7 17.5 %collective-permute-start.21 = (bf16[128,2304]{1,0:T(8,128)(2,1)S(1)}, bf16[128,2304]{1,0:T(8,128)(2,1)S(1)}, u32[]{:S(2)}, u32[]{:S(2)}) collective-permute-start(bf16[128,2304]{1,0:T(8,128)(2,1)S(1)} %get-tuple-element.51), channel_id=1, source_target_pairs={{0,48},{1,13},{2,50},{3,15},{4,52},{5,1},{6,54},{7,3},{8,56},{9,5}... | collective-permute-start | bytes 1769480 | tf_op jit(solution)/shard_map/ppermute | solution.py:309
  98.6 11.9 %collective-permute-start.19 = (bf16[128,2304]{1,0:T(8,128)(2,1)S(1)}, bf16[128,2304]{1,0:T(8,128)(2,1)S(1)}, u32[]{:S(2)}, u32[]{:S(2)}) collective-permute-start(bf16[128,2304]{1,0:T(8,128)(2,1)S(1)} %get-tuple-element.52), channel_id=1, source_target_pairs={{0,48},{1,13},{2,50},{3,15},{4,52},{5,1},{6,54},{7,3},{8,56},{9,5}... | collective-permute-start | bytes 1769480 | tf_op jit(solution)/shard_map/ppermute | solution.py:309
  105.7 15.0 %collective-permute-start.22 = (bf16[64,4736]{1,0:T(8,128)(2,1)S(1)}, bf16[64,4736]{1,0:T(8,128)(2,1)S(1)}, u32[]{:S(2)}, u32[]{:S(2)}) collective-permute-start(bf16[64,4736]{1,0:T(8,128)(2,1)S(1)} %get-tuple-element.40), channel_id=1, source_target_pairs={{0,4},{1,17},{2,6},{3,19},{4,8},{5,21},{6,10},{7,23},{8,12},{9,25}... | collective-permute-start | bytes 1818632 | tf_op jit(solution)/shard_map/ppermute | solution.py:309
  106.3 8.0 %copy-start.3 = (bf16[2304,448]{0,1:T(8,128)(2,1)S(1)}, bf16[2304,448]{0,1:T(8,128)(2,1)}, u32[]{:S(2)}) copy-start(bf16[2304,448]{0,1:T(8,128)(2,1)} %param.23) | copy-start | bytes 6193156
  106.3 19.5 %collective-permute-start.24 = (bf16[64,4736]{1,0:T(8,128)(2,1)S(1)}, bf16[64,4736]{1,0:T(8,128)(2,1)S(1)}, u32[]{:S(2)}, u32[]{:S(2)}) collective-permute-start(bf16[64,4736]{1,0:T(8,128)(2,1)S(1)} %get-tuple-element.42), channel_id=1, source_target_pairs={{0,8},{1,33},{2,10},{3,35},{4,12},{5,37},{6,14},{7,39},{8,0},{9,41... | collective-permute-start | bytes 1818632 | tf_op jit(solution)/shard_map/ppermute | solution.py:309
  112.8 13.4 %collective-permute-start.23 = (bf16[64,4736]{1,0:T(8,128)(2,1)S(1)}, bf16[64,4736]{1,0:T(8,128)(2,1)S(1)}, u32[]{:S(2)}, u32[]{:S(2)}) collective-permute-start(bf16[64,4736]{1,0:T(8,128)(2,1)S(1)} %get-tuple-element.41), channel_id=1, source_target_pairs={{0,12},{1,49},{2,14},{3,51},{4,0},{5,53},{6,2},{7,55},{8,4},{9,57}... | collective-permute-start | bytes 1818632 | tf_op jit(solution)/shard_map/ppermute | solution.py:309
  114.3 40.8 %collective-permute-start.29 = (bf16[2304,448]{0,1:T(8,128)(2,1)S(1)}, bf16[2304,448]{0,1:T(8,128)(2,1)}, u32[]{:S(2)}, u32[]{:S(2)}) collective-permute-start(bf16[2304,448]{0,1:T(8,128)(2,1)S(1)} %copy-done.3), channel_id=1, source_target_pairs={{0,1},{1,0},{2,3},{3,2},{4,5},{5,4},{6,7},{7,6},{8,9},{9,8},{10,11... | collective-permute-start | bytes 6193160 | tf_op jit(solution)/shard_map/ppermute | solution.py:327
  126.8 4.4 %collective-permute-start.25 = (bf16[32,4608]{1,0:T(8,128)(2,1)S(1)}, bf16[32,4608]{1,0:T(8,128)(2,1)S(1)}, u32[]{:S(2)}, u32[]{:S(2)}) collective-permute-start(bf16[32,4608]{1,0:T(8,128)(2,1)S(1)} %get-tuple-element.44), channel_id=1, source_target_pairs={{0,1},{1,0},{2,3},{3,2},{4,5},{5,4},{6,7},{7,6},{8,9},{9,8},{10,11... | collective-permute-start | bytes 884744 | tf_op jit(solution)/shard_map/ppermute | solution.py:327
  131.4 9.2 %collective-permute-start.27 = (bf16[32,4608]{1,0:T(8,128)(2,1)S(1)}, bf16[32,4608]{1,0:T(8,128)(2,1)S(1)}, u32[]{:S(2)}, u32[]{:S(2)}) collective-permute-start(bf16[32,4608]{1,0:T(8,128)(2,1)S(1)} %activate.1.refs_0_), channel_id=1, source_target_pairs={{0,48},{1,13},{2,50},{3,15},{4,52},{5,1},{6,54},{7,3},{8,56},{9,5}... | collective-permute-start | bytes 884744 | tf_op jit(solution)/shard_map/ppermute | solution.py:309
  133.8 7.4 %collective-permute-start.28 = (bf16[32,4608]{1,0:T(8,128)(2,1)S(1)}, bf16[32,4608]{1,0:T(8,128)(2,1)S(1)}, u32[]{:S(2)}, u32[]{:S(2)}) collective-permute-start(bf16[32,4608]{1,0:T(8,128)(2,1)S(1)} %activate.1.refs_0_), channel_id=1, source_target_pairs={{0,32},{1,9},{2,34},{3,11},{4,36},{5,13},{6,38},{7,15},{8,40},{9,1... | collective-permute-start | bytes 884744 | tf_op jit(solution)/shard_map/ppermute | solution.py:309
  133.8 10.8 %collective-permute-start.26 = (bf16[32,4608]{1,0:T(8,128)(2,1)S(1)}, bf16[32,4608]{1,0:T(8,128)(2,1)S(1)}, u32[]{:S(2)}, u32[]{:S(2)}) collective-permute-start(bf16[32,4608]{1,0:T(8,128)(2,1)S(1)} %activate.1.refs_0_), channel_id=1, source_target_pairs={{0,16},{1,5},{2,18},{3,7},{4,20},{5,9},{6,22},{7,11},{8,24},{9,13}... | collective-permute-start | bytes 884744 | tf_op jit(solution)/shard_map/ppermute | solution.py:309
  141.2 10.2 %collective-permute-start.33 = (bf16[64,4608]{1,0:T(8,128)(2,1)S(1)}, bf16[64,4608]{1,0:T(8,128)(2,1)}, u32[]{:S(2)}, u32[]{:S(2)}) collective-permute-start(bf16[64,4608]{1,0:T(8,128)(2,1)S(1)} %join.8.refs_1_), channel_id=1, source_target_pairs={{0,12},{1,49},{2,14},{3,51},{4,0},{5,53},{6,2},{7,55},{8,4},{9,57}... | collective-permute-start | bytes 1769480 | tf_op jit(solution)/shard_map/ppermute | solution.py:309
  144.7 10.4 %collective-permute-start.30 = (bf16[64,4608]{1,0:T(8,128)(2,1)S(1)}, bf16[64,4608]{1,0:T(8,128)(2,1)}, u32[]{:S(2)}, u32[]{:S(2)}) collective-permute-start(bf16[64,4608]{1,0:T(8,128)(2,1)S(1)} %join.7.refs_0_), channel_id=1, source_target_pairs={{0,4},{1,17},{2,6},{3,19},{4,8},{5,21},{6,10},{7,23},{8,12},{9,25}... | collective-permute-start | bytes 1769480 | tf_op jit(solution)/shard_map/ppermute | solution.py:309
  144.8 16.6 %collective-permute-start.31 = (bf16[64,4608]{1,0:T(8,128)(2,1)S(1)}, bf16[64,4608]{1,0:T(8,128)(2,1)}, u32[]{:S(2)}, u32[]{:S(2)}) collective-permute-start(bf16[64,4608]{1,0:T(8,128)(2,1)S(1)} %join.8.refs_1_), channel_id=1, source_target_pairs={{0,4},{1,17},{2,6},{3,19},{4,8},{5,21},{6,10},{7,23},{8,12},{9,25}... | collective-permute-start | bytes 1769480 | tf_op jit(solution)/shard_map/ppermute | solution.py:309
  144.8 16.6 %collective-permute-start.32 = (bf16[64,4608]{1,0:T(8,128)(2,1)S(1)}, bf16[64,4608]{1,0:T(8,128)(2,1)}, u32[]{:S(2)}, u32[]{:S(2)}) collective-permute-start(bf16[64,4608]{1,0:T(8,128)(2,1)S(1)} %join.7.refs_0_), channel_id=1, source_target_pairs={{0,12},{1,49},{2,14},{3,51},{4,0},{5,53},{6,2},{7,55},{8,4},{9,57}... | collective-permute-start | bytes 1769480 | tf_op jit(solution)/shard_map/ppermute | solution.py:309
  151.5 13.0 %collective-permute-start.35 = (bf16[64,4608]{1,0:T(8,128)(2,1)}, bf16[64,4608]{1,0:T(8,128)(2,1)}, u32[]{:S(2)}, u32[]{:S(2)}) collective-permute-start(bf16[64,4608]{1,0:T(8,128)(2,1)} %collective-permute-done.33.refs_3_), channel_id=1, source_target_pairs={{0,12},{1,49},{2,14},{3,51},{4,0},{5,53},{6,2},{7,55},{8,4},{9,57}... | collective-permute-start | bytes 1769480 | tf_op jit(solution)/shard_map/ppermute | solution.py:309
  155.1 12.6 %collective-permute-start.34 = (bf16[64,4608]{1,0:T(8,128)(2,1)}, bf16[64,4608]{1,0:T(8,128)(2,1)}, u32[]{:S(2)}, u32[]{:S(2)}) collective-permute-start(bf16[64,4608]{1,0:T(8,128)(2,1)} %collective-permute-done.30.refs_0_), channel_id=1, source_target_pairs={{0,4},{1,17},{2,6},{3,19},{4,8},{5,21},{6,10},{7,23},{8,12},{9,25}... | collective-permute-start | bytes 1769480 | tf_op jit(solution)/shard_map/ppermute | solution.py:309
  155.1 1.9 copy-start.7
  194.1 5.5 %collective-permute-start.36 = (bf16[2,8,7168]{2,1,0:T(8,128)(2,1)S(1)}, bf16[2,8,7168]{2,1,0:T(8,128)(2,1)S(1)}, u32[]{:S(2)}, u32[]{:S(2)}) collective-permute-start(bf16[2,8,7168]{2,1,0:T(8,128)(2,1)S(1)} %reshape.87), channel_id=1, source_target_pairs={{0,1},{1,0},{2,3},{3,2},{4,5},{5,4},{6,7},{7,6},{8,9},{9,8},{10,11... | collective-permute-start | bytes 688136 | tf_op jit(solution)/shard_map/ppermute | solution.py:327

commit v9 on v8

--- a/solution.py
+++ b/solution.py
@@ -9,7 +9,7 @@
 from jax.sharding import PartitionSpec as P
 
 epsilon = 1e-06
-VMEM_LIMIT = 20 * 1024 * 1024
+VMEM_LIMIT = 17 * 1024 * 1024
 STREAM_LIMIT = 61 * 1024 * 1024
 
 
@@ -464,13 +464,15 @@
     down = absolute(absolute(down, place_2, 1), place_1, 2)
     down = jnp.where(core == 0, jnp.swapaxes(down, 1, 2), down)
     role = lax.axis_index("role")
-    down = jnp.where(role == 0, down, down[::-1]).reshape(2, groups, 1, 2 * tokens, width)
-    down = jnp.broadcast_to(down, (2, groups, 2, 2 * tokens, width))
-    down = down.reshape(2 * groups * 2, 2 * tokens, width)
+    down = jnp.where(role == 0, down, down[::-1]).reshape(2, groups, 2, tokens, width)
+    down = jnp.concatenate([down[:, :, 0], down[:, :, 1]], axis=-1)[:, :, None]
+    down = jnp.broadcast_to(down, (2, groups, 2, tokens, 2 * width))
+    down = down.reshape(2 * groups * 2, tokens, 2 * width)
     landed = lax.all_to_all(down, ("role", "grp", "yh"), split_axis=0, concat_axis=0)
-    landed = landed.reshape(2, groups, 2, 2 * tokens, width)
+    landed = landed.reshape(2, groups, 2, tokens, 2 * width)
     result = jnp.sum(wide(landed), axis=(0, 2)).astype(jnp.bfloat16)
-    result = jnp.swapaxes(result, 0, 1).reshape(2, tokens, model_width)
+    result = jnp.stack([result[:, :, :width], result[:, :, width:]])
+    result = jnp.swapaxes(result, 1, 2).reshape(2, tokens, model_width)
     other = swap(result, "core")
     result = jnp.stack(
         [jnp.where(core == 0, result, other), jnp.where(core == 0, other, result)], axis=1

time: 201 us -> 200 us (level)
  no operation moved by 1% of the time
where the time goes in v9:
time: 200 us; the launch traced here: 199 us
  waiting for transfers between devices  70.2 us (35%)
  starting transfers between devices  66.1 us (33%)
  Pallas kernels  30.1 us (15%)
  blocking collectives  20.9 us (10%)
  other arithmetic  6.11 us (3%)
  local copies, waits for them, and re-layouts  5.26 us (3%)
    ppermute x26, waiting for transfers between devices, shift(): return lax.ppermute(value, ('grp', 'yh', 'core'), pairs)  59.6 us
    ppermute x26, starting transfers between devices, shift(): return lax.ppermute(value, ('grp', 'yh', 'core'), pairs)  33.4 us
    ppermute x8, starting transfers between devices, swap(): return lax.ppermute(value, axis, [(0, 1), (1, 0)])  27 us
    all_to_all x1, blocking collectives, body(): lax.all_to_all(down, ('role', 'grp', 'yh'), split_axis=0, concat_axis=0)  20.9 us
    pallas_call x13, Pallas kernels, whole_call(): pl.pallas_call(kernel, out_shape=out_shapes, in_specs=[pl.BlockSpec(memor...  14.7 us
    pallas_call x1, Pallas kernels, attend(): pl.pallas_call(functools.partial(attend_kernel, scale, latent, per_step),...  9.11 us
    ppermute x3, waiting for transfers between devices, shift_y(): lax.ppermute(value, ('role', 'yh', 'core'), [(p, moved(p)) for p in range...  5.77 us
    ppermute x3, starting transfers between devices, shift_y(): lax.ppermute(value, ('role', 'yh', 'core'), [(p, moved(p)) for p in range...  5.7 us
  transfers between devices with their start and end apart: 37, of which 25 were waited for; matrix products, arithmetic and copies ran while one was open for 3% of the time, Pallas kernels for 13%

profile of v9, /device:TPU:1, one launch (start us, length us, event | category | flops | bytes accessed | tf_op | source)
XLA Modules:
  0.0 199.4 jit_solution(6362859617623538033)
XLA Ops:
  0.0 1.4 collective-permute-start.1
  1.4 1.3 pad_add_fusion.plan_ref
  2.7 9.1 %attend.1 = (bf16[2,8,16,512]{3,2,1,0:T(8,128)(2,1)}, bf16[2,8,16,512]{3,2,1,0:T(8,128)(2,1)}) custom-call(s32[17]{0:T(128)} %pad_add_fusion.plan_ref, bf16[8,4,16,576]{3,2,1,0:T(8,128)(2,1)} %bitcast.87, bf16[8,576]{1,0:T(8,128)(2,1)} %new_ref.1, bf16[8,576,1024]{2,1,0:T(8,128)(2,1)} %bitcast.78, bf16[8,576,1024]{2,1,0:T(8,128)(2,1)} %bitcast.79), custom_call_target="tpu_custom_call" | custom-call | flops 1140850688 | bytes 9437184 | tf_op jit(solution)/shard_map/attend/pallas_call | solution.py:70
  11.8 3.0 %collective-permute-start = (bf16[2,8,16,512]{3,2,1,0:T(8,128)(2,1)}, bf16[2,8,16,512]{3,2,1,0:T(8,128)(2,1)S(1)}, u32[]{:S(2)}, u32[]{:S(2)}) collective-permute-start(bf16[2,8,16,512]{3,2,1,0:T(8,128)(2,1)} %get-tuple-element.26), channel_id=1, source_target_pairs={{0,2},{2,0},{1,3},{3,1},{4,6},{6,4},{5,7},{7,5},{8,10},{10,8},{9,1... | collective-permute-start | bytes 786440 | tf_op jit(solution)/shard_map/ppermute | solution.py:327
  14.8 1.5 copy-done.4
  16.3 1.9 join.6.refs_1_.refs_3_
  18.2 1.8 copy-done
  20.0 1.0 collective-permute-done.far
  21.0 0.7 head_values.1.refs_0_
  21.7 1.7 collective-permute-start.2
  23.5 2.2 %collective-permute-start.3 = (bf16[16,4096]{1,0:T(8,128)(2,1)S(1)}, bf16[16,4096]{1,0:T(8,128)(2,1)S(1)}, u32[]{:S(2)}, u32[]{:S(2)}) collective-permute-start(bf16[16,4096]{1,0:T(8,128)(2,1)S(1)} %head_values.1.refs_0_), channel_id=1, source_target_pairs={{0,48},{1,13},{2,50},{3,15},{4,52},{5,1},{6,54},{7,3},{8,56},{9,5}... | collective-permute-start | bytes 393224 | tf_op jit(solution)/shard_map/ppermute | solution.py:309
  25.6 1.2 collective-permute-start.4
  27.1 2.5 %broadcast_select_fusion = (bf16[448,2304]{1,0:T(8,128)(2,1)S(1)}, bf16[448,2304]{1,0:T(8,128)(2,1)S(1)}) fusion(bf16[448,2304]{1,0:T(8,128)(2,1)} %param.22, bf16[448,2304]{1,0:T(8,128)(2,1)} %param.21, pred[]{:T(512)S(6)} %eq.31), kind=kLoop, calls=%fused_computation | loop fusion | flops 2064384 | bytes 8257537 | tf_op jit(solution)/shard_map/jit(_where)/select_n | solution.py:407
  29.8 1.5 collective-permute-done.4.refs_3_
  31.3 1.1 collective-permute-start.6
  32.4 1.6 collective-permute-start.7
  34.0 1.3 collective-permute-start.8
  35.5 3.6 %collective-permute-start.13 = (bf16[448,2304]{1,0:T(8,128)(2,1)S(1)}, bf16[448,2304]{1,0:T(8,128)(2,1)S(1)}, u32[]{:S(2)}, u32[]{:S(2)}) collective-permute-start(bf16[448,2304]{1,0:T(8,128)(2,1)S(1)} %get-tuple-element.47), channel_id=1, source_target_pairs={{0,1},{1,0},{2,3},{3,2},{4,5},{5,4},{6,7},{7,6},{8,9},{9,8},{10,11... | collective-permute-start | bytes 6193160 | tf_op jit(solution)/shard_map/ppermute | solution.py:327
  39.2 1.2 pair_dot.5
  40.9 4.9 %collective-permute-done.7.refs_1_ = bf16[64,4096]{1,0:T(8,128)(2,1)S(1)} collective-permute-done((bf16[64,4096]{1,0:T(8,128)(2,1)S(1)}, bf16[64,4096]{1,0:T(8,128)(2,1)S(1)}, u32[]{:S(2)}, u32[]{:S(2)}) %collective-permute-start.7) | collective-permute-done | bytes 524320 | tf_op jit(solution)/shard_map/ppermute | solution.py:309
  45.8 1.8 collective-permute-done.8.refs_2_
  47.5 1.2 pair_dot.6
  48.9 3.0 %collective-permute-start.9 = (bf16[4,4,2,8,448]{4,3,2,0,1:T(8,128)(2,1)S(1)}, bf16[4,4,2,8,448]{4,3,2,0,1:T(8,128)(2,1)S(1)}, u32[]{:S(2)}, u32[]{:S(2)}) collective-permute-start(bf16[4,4,2,8,448]{4,3,2,0,1:T(8,128)(2,1)S(1)} %copy.94), channel_id=1, source_target_pairs={{0,2},{1,3},{2,0},{3,1},{64,66},{65,67},{66,64},{67,65},{4,6},{5,7... | collective-permute-start | bytes 688136 | tf_op jit(solution)/shard_map/ppermute | solution.py:323
  52.3 2.3 %collective-permute-start.11 = (bf16[4,4,2,8,448]{4,3,2,0,1:T(8,128)(2,1)S(1)}, bf16[4,4,2,8,448]{4,3,2,0,1:T(8,128)(2,1)S(1)}, u32[]{:S(2)}, u32[]{:S(2)}) collective-permute-start(bf16[4,4,2,8,448]{4,3,2,0,1:T(8,128)(2,1)S(1)} %copy.94), channel_id=1, source_target_pairs={{0,66},{1,67},{2,64},{3,65},{64,0},{65,1},{66,2},{67,3},{4,70},{5,... | collective-permute-start | bytes 688136 | tf_op jit(solution)/shard_map/ppermute | solution.py:323
  54.6 1.1 collective-permute-done.9
  55.9 4.3 %collective-permute-done.10 = bf16[4,4,2,8,448]{4,3,2,0,1:T(8,128)(2,1)S(1)} collective-permute-done((bf16[4,4,2,8,448]{4,3,2,0,1:T(8,128)(2,1)S(1)}, bf16[4,4,2,8,448]{4,3,2,0,1:T(8,128)(2,1)S(1)}, u32[]{:S(2)}, u32[]{:S(2)}) %collective-permute-start.10) | collective-permute-done | bytes 229408 | tf_op jit(solution)/shard_map/ppermute | solution.py:323
  60.7 4.7 %collective-permute-start.12 = (bf16[2,4,4,2,8,448]{5,4,3,2,1,0:T(8,128)(2,1)S(1)}, bf16[2,4,4,2,8,448]{5,4,3,2,1,0:T(8,128)(2,1)S(1)}, u32[]{:S(2)}, u32[]{:S(2)}) collective-permute-start(bf16[2,4,4,2,8,448]{5,4,3,2,1,0:T(8,128)(2,1)S(1)} %pad_maximum_fusion.2), channel_id=1, source_target_pairs={{0,1},{1,0},{2,3},{3,2},{4,5},{5,4},{6,7},{7,6},{8,9},{9,8},{10,11... | collective-permute-start | bytes 1376264 | tf_op jit(solution)/shard_map/ppermute | solution.py:327
  65.4 1.5 collective-permute-done.12
  67.2 1.4 partial_sums.5
  68.8 2.6 %collective-permute-start.18 = (bf16[256,2304]{1,0:T(8,128)(2,1)S(1)}, bf16[256,2304]{1,0:T(8,128)(2,1)S(1)}, u32[]{:S(2)}, u32[]{:S(2)}) collective-permute-start(bf16[256,2304]{1,0:T(8,128)(2,1)S(1)} %get-tuple-element.38), channel_id=1, source_target_pairs={{0,48},{1,13},{2,50},{3,15},{4,52},{5,1},{6,54},{7,3},{8,56},{9,5}... | collective-permute-start | bytes 3538952 | tf_op jit(solution)/shard_map/ppermute | solution.py:309
  71.4 1.4 partial_sums.4
  72.9 1.5 collective-permute-start.15
  74.3 2.6 %partial_sums.3 = (bf16[256,2432]{1,0:T(8,128)(2,1)S(1)}, bf16[256,2304]{1,0:T(8,128)(2,1)S(1)}, bf16[256,2432]{1,0:T(8,128)(2,1)S(1)}, bf16[256,2304]{1,0:T(8,128)(2,1)S(1)}) custom-call(bf16[4,4,64,448]{3,2,1,0:T(8,128)(2,1)S(1)} %bitcast.70, bf16[4,4,64,448]{3,2,1,0:T(8,128)(2,1)S(1)} %bitcast.71, bf16[4,4,64,448]{3,2,1,0:T(8,128)(2,1)S(1)} %bitcast.72, ...), custom_call_target="tpu_custom_call" | custom-call | flops 2172649472 | bytes 8978432 | tf_op jit(solution)/shard_map/partial_sums/pallas_call | solution.py:130
  77.0 9.0 %collective-permute-done.16 = bf16[256,2432]{1,0:T(8,128)(2,1)S(1)} collective-permute-done((bf16[256,2432]{1,0:T(8,128)(2,1)S(1)}, bf16[256,2432]{1,0:T(8,128)(2,1)S(1)}, u32[]{:S(2)}, u32[]{:S(2)}) %collective-permute-start.16) | collective-permute-done | bytes 1245216 | tf_op jit(solution)/shard_map/ppermute | solution.py:309
  86.7 2.7 %collective-permute-start.21 = (bf16[128,2304]{1,0:T(8,128)(2,1)S(1)}, bf16[128,2304]{1,0:T(8,128)(2,1)S(1)}, u32[]{:S(2)}, u32[]{:S(2)}) collective-permute-start(bf16[128,2304]{1,0:T(8,128)(2,1)S(1)} %get-tuple-element.51), channel_id=1, source_target_pairs={{0,48},{1,13},{2,50},{3,15},{4,52},{5,1},{6,54},{7,3},{8,56},{9,5}... | collective-permute-start | bytes 1769480 | tf_op jit(solution)/shard_map/ppermute | solution.py:309
  89.4 9.2 %collective-permute-done.15.direct_c = bf16[256,2304]{1,0:T(8,128)(2,1)S(1)} collective-permute-done((bf16[256,2304]{1,0:T(8,128)(2,1)S(1)}, bf16[256,2304]{1,0:T(8,128)(2,1)S(1)}, u32[]{:S(2)}, u32[]{:S(2)}) %collective-permute-start.15) | collective-permute-done | bytes 1179680 | tf_op jit(solution)/shard_map/ppermute | solution.py:309
  98.6 5.6 %collective-permute-done.21.relay_c = bf16[128,2304]{1,0:T(8,128)(2,1)S(1)} collective-permute-done((bf16[128,2304]{1,0:T(8,128)(2,1)S(1)}, bf16[128,2304]{1,0:T(8,128)(2,1)S(1)}, u32[]{:S(2)}, u32[]{:S(2)}) %collective-permute-start.21) | collective-permute-done | bytes 589856 | tf_op jit(solution)/shard_map/ppermute | solution.py:309
  104.2 1.1 collective-permute-done.20.relay_a
  106.3 2.3 %collective-permute-start.24 = (bf16[64,4736]{1,0:T(8,128)(2,1)S(1)}, bf16[64,4736]{1,0:T(8,128)(2,1)S(1)}, u32[]{:S(2)}, u32[]{:S(2)}) collective-permute-start(bf16[64,4736]{1,0:T(8,128)(2,1)S(1)} %get-tuple-element.42), channel_id=1, source_target_pairs={{0,8},{1,33},{2,10},{3,35},{4,12},{5,37},{6,14},{7,39},{8,0},{9,41... | collective-permute-start | bytes 1818632 | tf_op jit(solution)/shard_map/ppermute | solution.py:309
  108.6 1.9 collective-permute-done.19.relay_c
  110.5 1.9 collective-permute-done.17.relay_a
  112.9 1.2 collective-permute-start.23
  114.1 6.6 %collective-permute-start.29 = (bf16[2304,448]{0,1:T(8,128)(2,1)S(1)}, bf16[2304,448]{0,1:T(8,128)(2,1)}, u32[]{:S(2)}, u32[]{:S(2)}) collective-permute-start(bf16[2304,448]{0,1:T(8,128)(2,1)S(1)} %copy-done.3), channel_id=1, source_target_pairs={{0,1},{1,0},{2,3},{3,2},{4,5},{5,4},{6,7},{7,6},{8,9},{9,8},{10,11... | collective-permute-start | bytes 6193160 | tf_op jit(solution)/shard_map/ppermute | solution.py:327
  120.7 4.9 %collective-permute-done.24.refs_3_ = bf16[64,4736]{1,0:T(8,128)(2,1)S(1)} collective-permute-done((bf16[64,4736]{1,0:T(8,128)(2,1)S(1)}, bf16[64,4736]{1,0:T(8,128)(2,1)S(1)}, u32[]{:S(2)}, u32[]{:S(2)}) %collective-permute-start.24) | collective-permute-done | bytes 606240 | tf_op jit(solution)/shard_map/ppermute | solution.py:309
  126.2 0.6 settle.1
  126.9 3.3 %collective-permute-start.25 = (bf16[32,4608]{1,0:T(8,128)(2,1)S(1)}, bf16[32,4608]{1,0:T(8,128)(2,1)S(1)}, u32[]{:S(2)}, u32[]{:S(2)}) collective-permute-start(bf16[32,4608]{1,0:T(8,128)(2,1)S(1)} %get-tuple-element.44), channel_id=1, source_target_pairs={{0,1},{1,0},{2,3},{3,2},{4,5},{5,4},{6,7},{7,6},{8,9},{9,8},{10,11... | collective-permute-start | bytes 884744 | tf_op jit(solution)/shard_map/ppermute | solution.py:327
  130.1 1.2 collective-permute-done.25.theirs
  131.5 2.3 %collective-permute-start.27 = (bf16[32,4608]{1,0:T(8,128)(2,1)S(1)}, bf16[32,4608]{1,0:T(8,128)(2,1)S(1)}, u32[]{:S(2)}, u32[]{:S(2)}) collective-permute-start(bf16[32,4608]{1,0:T(8,128)(2,1)S(1)} %activate.1.refs_0_), channel_id=1, source_target_pairs={{0,48},{1,13},{2,50},{3,15},{4,52},{5,1},{6,54},{7,3},{8,56},{9,5}... | collective-permute-start | bytes 884744 | tf_op jit(solution)/shard_map/ppermute | solution.py:309
  133.8 0.7 collective-permute-start.26
  134.5 6.2 %collective-permute-done.27.refs_0_ = bf16[32,4608]{1,0:T(8,128)(2,1)S(1)} collective-permute-done((bf16[32,4608]{1,0:T(8,128)(2,1)S(1)}, bf16[32,4608]{1,0:T(8,128)(2,1)S(1)}, u32[]{:S(2)}, u32[]{:S(2)}) %collective-permute-start.27) | collective-permute-done | bytes 294944 | tf_op jit(solution)/shard_map/ppermute | solution.py:309
  141.3 3.4 %collective-permute-start.33 = (bf16[64,4608]{1,0:T(8,128)(2,1)S(1)}, bf16[64,4608]{1,0:T(8,128)(2,1)}, u32[]{:S(2)}, u32[]{:S(2)}) collective-permute-start(bf16[64,4608]{1,0:T(8,128)(2,1)S(1)} %join.8.refs_1_), channel_id=1, source_target_pairs={{0,12},{1,49},{2,14},{3,51},{4,0},{5,53},{6,2},{7,55},{8,4},{9,57}... | collective-permute-start | bytes 1769480 | tf_op jit(solution)/shard_map/ppermute | solution.py:309
  144.9 2.9 %collective-permute-start.32 = (bf16[64,4608]{1,0:T(8,128)(2,1)S(1)}, bf16[64,4608]{1,0:T(8,128)(2,1)}, u32[]{:S(2)}, u32[]{:S(2)}) collective-permute-start(bf16[64,4608]{1,0:T(8,128)(2,1)S(1)} %join.7.refs_0_), channel_id=1, source_target_pairs={{0,12},{1,49},{2,14},{3,51},{4,0},{5,53},{6,2},{7,55},{8,4},{9,57}... | collective-permute-start | bytes 1769480 | tf_op jit(solution)/shard_map/ppermute | solution.py:309
  147.8 3.7 %collective-permute-done.33.refs_3_ = bf16[64,4608]{1,0:T(8,128)(2,1)} collective-permute-done((bf16[64,4608]{1,0:T(8,128)(2,1)S(1)}, bf16[64,4608]{1,0:T(8,128)(2,1)}, u32[]{:S(2)}, u32[]{:S(2)}) %collective-permute-start.33) | collective-permute-done | bytes 589856 | tf_op jit(solution)/shard_map/ppermute | solution.py:309
  151.5 3.5 %collective-permute-start.35 = (bf16[64,4608]{1,0:T(8,128)(2,1)}, bf16[64,4608]{1,0:T(8,128)(2,1)}, u32[]{:S(2)}, u32[]{:S(2)}) collective-permute-start(bf16[64,4608]{1,0:T(8,128)(2,1)} %collective-permute-done.33.refs_3_), channel_id=1, source_target_pairs={{0,12},{1,49},{2,14},{3,51},{4,0},{5,53},{6,2},{7,55},{8,4},{9,57}... | collective-permute-start | bytes 1769480 | tf_op jit(solution)/shard_map/ppermute | solution.py:309
  155.1 1.9 join.9.refs_2_.refs_4_
  157.1 1.3 pair_dot.7
  158.5 3.0 %collective-permute-done.31.refs_1_ = bf16[64,4608]{1,0:T(8,128)(2,1)} collective-permute-done((bf16[64,4608]{1,0:T(8,128)(2,1)S(1)}, bf16[64,4608]{1,0:T(8,128)(2,1)}, u32[]{:S(2)}, u32[]{:S(2)}) %collective-permute-start.31) | collective-permute-done | bytes 589856 | tf_op jit(solution)/shard_map/ppermute | solution.py:309
  161.4 3.0 %pair_dot.8 = f32[256,448]{1,0:T(8,128)S(1)} custom-call(bf16[64,4608]{1,0:T(8,128)(2,1)} %collective-permute-done.30.refs_0_, bf16[64,4608]{1,0:T(8,128)(2,1)} %collective-permute-done.31.refs_1_, bf16[64,4608]{1,0:T(8,128)(2,1)} %collective-permute-done.32.refs_2_, bf16[64,4608]{1,0:T(8,128)(2,1)} %collective-permute-done.33.refs_3_, ...), custom_call_target="tpu_custom_call" | custom-call | flops 4128768 | bytes 4128768 | tf_op jit(solution)/shard_map/pair_dot/pallas_call | solution.py:170
  164.4 3.3 %collective-permute-done.34.refs_0_ = bf16[64,4608]{1,0:T(8,128)(2,1)} collective-permute-done((bf16[64,4608]{1,0:T(8,128)(2,1)}, bf16[64,4608]{1,0:T(8,128)(2,1)}, u32[]{:S(2)}, u32[]{:S(2)}) %collective-permute-start.34) | collective-permute-done | bytes 589856 | tf_op jit(solution)/shard_map/ppermute | solution.py:309
  167.7 2.6 %pair_dot.9 = f32[128,448]{1,0:T(8,128)S(1)} custom-call(bf16[64,4608]{1,0:T(8,128)(2,1)} %collective-permute-done.34.refs_0_, bf16[64,4608]{1,0:T(8,128)(2,1)} %collective-permute-done.35.refs_1_, bf16[896,2304]{1,0:T(8,128)(2,1)S(1)} %join.9.refs_2_.refs_4_), custom_call_target="tpu_custom_call" | custom-call | flops 4128768 | bytes 4128768 | tf_op jit(solution)/shard_map/pair_dot/pallas_call | solution.py:170
  171.4 20.9 %all_to_all.5 = bf16[64,8,896]{2,1,0:T(8,128)(2,1)S(1)} all-to-all(bf16[64,8,896]{2,1,0:T(8,128)(2,1)S(1)} %bitcast.81), channel_id=1, replica_groups=mesh['role'=2,'grp'=16,'yh'=2,'core'=2] {'role','grp','yh'}, dimensions={0} | all-to-all | bytes 1835008 | tf_op jit(solution)/shard_map/all_to_all | solution.py:471
  192.9 4.4 %collective-permute-start.36 = (bf16[2,8,7168]{2,1,0:T(8,128)(2,1)S(1)}, bf16[2,8,7168]{2,1,0:T(8,128)(2,1)S(1)}, u32[]{:S(2)}, u32[]{:S(2)}) collective-permute-start(bf16[2,8,7168]{2,1,0:T(8,128)(2,1)S(1)} %reshape.90), channel_id=1, source_target_pairs={{0,1},{1,0},{2,3},{3,2},{4,5},{5,4},{6,7},{7,6},{8,9},{9,8},{10,11... | collective-permute-start | bytes 688136 | tf_op jit(solution)/shard_map/ppermute | solution.py:327
  197.3 1.1 collective-permute-done.36
  198.6 0.8 copy.87
  (106 shorter events, 8.5 us)
Async XLA Ops:
  0.0 21.0 %collective-permute-start.1 = (bf16[16,512,128]{2,1,0:T(8,128)(2,1)}, bf16[16,512,128]{2,1,0:T(8,128)(2,1)S(1)}, u32[]{:S(2)}, u32[]{:S(2)}) collective-permute-start(bf16[16,512,128]{2,1,0:T(8,128)(2,1)} %refs_0_.1), channel_id=1, source_target_pairs={{0,1},{1,0},{2,3},{3,2},{4,5},{5,4},{6,7},{7,6},{8,9},{9,8},{10,11... | collective-permute-start | bytes 6291464 | tf_op jit(solution)/shard_map/ppermute | solution.py:327
  1.4 13.4 %collective-permute-start.5 = (bf16[2048,448]{0,1:T(8,128)(2,1)}, bf16[2048,448]{0,1:T(8,128)(2,1)}, u32[]{:S(2)}, u32[]{:S(2)}) collective-permute-start(bf16[2048,448]{0,1:T(8,128)(2,1)} %param.19), channel_id=1, source_target_pairs={{0,1},{1,0},{2,3},{3,2},{4,5},{5,4},{6,7},{7,6},{8,9},{9,8},{10,11... | collective-permute-start | bytes 5505032 | tf_op jit(solution)/shard_map/ppermute | solution.py:327
  11.8 9.2 %collective-permute-start = (bf16[2,8,16,512]{3,2,1,0:T(8,128)(2,1)}, bf16[2,8,16,512]{3,2,1,0:T(8,128)(2,1)S(1)}, u32[]{:S(2)}, u32[]{:S(2)}) collective-permute-start(bf16[2,8,16,512]{3,2,1,0:T(8,128)(2,1)} %get-tuple-element.26), channel_id=1, source_target_pairs={{0,2},{2,0},{1,3},{3,1},{4,6},{6,4},{5,7},{7,5},{8,10},{10,8},{9,1... | collective-permute-start | bytes 786440 | tf_op jit(solution)/shard_map/ppermute | solution.py:327
  14.8 1.5 copy-start.4
  16.3 4.7 %copy-start.2 = (bf16[16,512,128]{2,1,0:T(8,128)(2,1)S(1)}, bf16[16,512,128]{2,1,0:T(8,128)(2,1)}, u32[]{:S(2)}) copy-start(bf16[16,512,128]{2,1,0:T(8,128)(2,1)} %refs_0_.1) | copy-start | bytes 6291460
  16.3 4.7 %copy-start.5 = (bf16[2,8,16,512]{3,2,1,0:T(8,128)(2,1)S(1)}, bf16[2,8,16,512]{3,2,1,0:T(8,128)(2,1)}, u32[]{:S(2)}) copy-start(bf16[2,8,16,512]{3,2,1,0:T(8,128)(2,1)} %get-tuple-element.25.near) | copy-start | bytes 786436
  18.2 1.8 copy-start
  21.0 5.9 %copy-start.9 = (bf16[512,448]{0,1:T(8,128)(2,1)S(1)}, bf16[512,448]{0,1:T(8,128)(2,1)}, u32[]{:S(2)}) copy-start(bf16[512,448]{0,1:T(8,128)(2,1)} %param.17) | copy-start | bytes 1376260
  21.7 8.0 %collective-permute-start.2 = (bf16[16,4096]{1,0:T(8,128)(2,1)S(1)}, bf16[16,4096]{1,0:T(8,128)(2,1)S(1)}, u32[]{:S(2)}, u32[]{:S(2)}) collective-permute-start(bf16[16,4096]{1,0:T(8,128)(2,1)S(1)} %head_values.1.refs_0_), channel_id=1, source_target_pairs={{0,16},{1,5},{2,18},{3,7},{4,20},{5,9},{6,22},{7,11},{8,24},{9,13}... | collective-permute-start | bytes 393224 | tf_op jit(solution)/shard_map/ppermute | solution.py:309
  23.5 6.3 %collective-permute-start.3 = (bf16[16,4096]{1,0:T(8,128)(2,1)S(1)}, bf16[16,4096]{1,0:T(8,128)(2,1)S(1)}, u32[]{:S(2)}, u32[]{:S(2)}) collective-permute-start(bf16[16,4096]{1,0:T(8,128)(2,1)S(1)} %head_values.1.refs_0_), channel_id=1, source_target_pairs={{0,48},{1,13},{2,50},{3,15},{4,52},{5,1},{6,54},{7,3},{8,56},{9,5}... | collective-permute-start | bytes 393224 | tf_op jit(solution)/shard_map/ppermute | solution.py:309
  25.6 5.6 %collective-permute-start.4 = (bf16[16,4096]{1,0:T(8,128)(2,1)S(1)}, bf16[16,4096]{1,0:T(8,128)(2,1)S(1)}, u32[]{:S(2)}, u32[]{:S(2)}) collective-permute-start(bf16[16,4096]{1,0:T(8,128)(2,1)S(1)} %head_values.1.refs_0_), channel_id=1, source_target_pairs={{0,32},{1,9},{2,34},{3,11},{4,36},{5,13},{6,38},{7,15},{8,40},{9,1... | collective-permute-start | bytes 393224 | tf_op jit(solution)/shard_map/ppermute | solution.py:309
  29.6 9.6 %copy-start.1 = (bf16[896,2048]{1,0:T(8,128)(2,1)S(1)}, bf16[896,2048]{1,0:T(8,128)(2,1)}, u32[]{:S(2)}) copy-start(bf16[896,2048]{1,0:T(8,128)(2,1)} %copy-done) | copy-start | bytes 11010052
  31.3 9.6 %collective-permute-start.6 = (bf16[64,4096]{1,0:T(8,128)(2,1)S(1)}, bf16[64,4096]{1,0:T(8,128)(2,1)S(1)}, u32[]{:S(2)}, u32[]{:S(2)}) collective-permute-start(bf16[64,4096]{1,0:T(8,128)(2,1)S(1)} %join.5.refs_0_), channel_id=1, source_target_pairs={{0,4},{1,17},{2,6},{3,19},{4,8},{5,21},{6,10},{7,23},{8,12},{9,25}... | collective-permute-start | bytes 1572872 | tf_op jit(solution)/shard_map/ppermute | solution.py:309
  32.4 13.4 %collective-permute-start.7 = (bf16[64,4096]{1,0:T(8,128)(2,1)S(1)}, bf16[64,4096]{1,0:T(8,128)(2,1)S(1)}, u32[]{:S(2)}, u32[]{:S(2)}) collective-permute-start(bf16[64,4096]{1,0:T(8,128)(2,1)S(1)} %join.5.refs_0_), channel_id=1, source_target_pairs={{0,12},{1,49},{2,14},{3,51},{4,0},{5,53},{6,2},{7,55},{8,4},{9,57}... | collective-permute-start | bytes 1572872 | tf_op jit(solution)/shard_map/ppermute | solution.py:309
  34.0 13.5 %collective-permute-start.8 = (bf16[64,4096]{1,0:T(8,128)(2,1)S(1)}, bf16[64,4096]{1,0:T(8,128)(2,1)S(1)}, u32[]{:S(2)}, u32[]{:S(2)}) collective-permute-start(bf16[64,4096]{1,0:T(8,128)(2,1)S(1)} %join.5.refs_0_), channel_id=1, source_target_pairs={{0,8},{1,33},{2,10},{3,35},{4,12},{5,37},{6,14},{7,39},{8,0},{9,41... | collective-permute-start | bytes 1572872 | tf_op jit(solution)/shard_map/ppermute | solution.py:309
  35.5 4.8 %copy-start.8 = (bf16[4,4,2,8,448]{4,3,2,1,0:T(8,128)(2,1)}, bf16[4,4,2,8,448]{4,3,2,1,0:T(8,128)(2,1)S(1)}, u32[]{:S(2)}) copy-start(bf16[4,4,2,8,448]{4,3,2,1,0:T(8,128)(2,1)S(1)} %fusion.4) | copy-start | bytes 688132
  35.5 31.7 %collective-permute-start.13 = (bf16[448,2304]{1,0:T(8,128)(2,1)S(1)}, bf16[448,2304]{1,0:T(8,128)(2,1)S(1)}, u32[]{:S(2)}, u32[]{:S(2)}) collective-permute-start(bf16[448,2304]{1,0:T(8,128)(2,1)S(1)} %get-tuple-element.47), channel_id=1, source_target_pairs={{0,1},{1,0},{2,3},{3,2},{4,5},{5,4},{6,7},{7,6},{8,9},{9,8},{10,11... | collective-permute-start | bytes 6193160 | tf_op jit(solution)/shard_map/ppermute | solution.py:327
  40.9 7.9 %slice-start = ((bf16[4,4,2,8,448]{4,3,2,1,0:T(8,128)(2,1)}), bf16[4,2,2,8,448]{4,3,2,1,0:T(8,128)(2,1)S(1)}, s32[]{:S(2)}) async-start(bf16[4,4,2,8,448]{4,3,2,1,0:T(8,128)(2,1)} %copy-done.8), calls=%async_computation.1 | async-start | bytes 262144 | tf_op jit(solution)/shard_map/slice | solution.py:356
  48.9 6.8 %collective-permute-start.9 = (bf16[4,4,2,8,448]{4,3,2,0,1:T(8,128)(2,1)S(1)}, bf16[4,4,2,8,448]{4,3,2,0,1:T(8,128)(2,1)S(1)}, u32[]{:S(2)}, u32[]{:S(2)}) collective-permute-start(bf16[4,4,2,8,448]{4,3,2,0,1:T(8,128)(2,1)S(1)} %copy.94), channel_id=1, source_target_pairs={{0,2},{1,3},{2,0},{3,1},{64,66},{65,67},{66,64},{67,65},{4,6},{5,7... | collective-permute-start | bytes 688136 | tf_op jit(solution)/shard_map/ppermute | solution.py:323
  51.9 8.3 %collective-permute-start.10 = (bf16[4,4,2,8,448]{4,3,2,0,1:T(8,128)(2,1)S(1)}, bf16[4,4,2,8,448]{4,3,2,0,1:T(8,128)(2,1)S(1)}, u32[]{:S(2)}, u32[]{:S(2)}) collective-permute-start(bf16[4,4,2,8,448]{4,3,2,0,1:T(8,128)(2,1)S(1)} %copy.94), channel_id=1, source_target_pairs={{0,64},{1,65},{2,66},{3,67},{64,2},{65,3},{66,0},{67,1},{4,68},{5,... | collective-permute-start | bytes 688136 | tf_op jit(solution)/shard_map/ppermute | solution.py:323
  52.3 8.3 %collective-permute-start.11 = (bf16[4,4,2,8,448]{4,3,2,0,1:T(8,128)(2,1)S(1)}, bf16[4,4,2,8,448]{4,3,2,0,1:T(8,128)(2,1)S(1)}, u32[]{:S(2)}, u32[]{:S(2)}) collective-permute-start(bf16[4,4,2,8,448]{4,3,2,0,1:T(8,128)(2,1)S(1)} %copy.94), channel_id=1, source_target_pairs={{0,66},{1,67},{2,64},{3,65},{64,0},{65,1},{66,2},{67,3},{4,70},{5,... | collective-permute-start | bytes 688136 | tf_op jit(solution)/shard_map/ppermute | solution.py:323
  55.8 4.9 %copy-start.6 = (f32[4,4,2,8,448]{4,3,2,1,0:T(8,128)}, f32[4,4,2,8,448]{4,3,2,1,0:T(8,128)S(1)}, u32[]{:S(2)}) copy-start(f32[4,4,2,8,448]{4,3,2,1,0:T(8,128)S(1)} %get-tuple-element.46) | copy-start | bytes 1376260
  55.9 9.5 %copy-start.10 = (bf16[448]{0:T(512)(128)(2,1)S(1)}, bf16[448]{0:T(512)(128)(2,1)}, u32[]{:S(2)}) copy-start(bf16[448]{0:T(512)(128)(2,1)} %param.20) | copy-start | bytes 2692
  60.7 6.2 %collective-permute-start.12 = (bf16[2,4,4,2,8,448]{5,4,3,2,1,0:T(8,128)(2,1)S(1)}, bf16[2,4,4,2,8,448]{5,4,3,2,1,0:T(8,128)(2,1)S(1)}, u32[]{:S(2)}, u32[]{:S(2)}) collective-permute-start(bf16[2,4,4,2,8,448]{5,4,3,2,1,0:T(8,128)(2,1)S(1)} %pad_maximum_fusion.2), channel_id=1, source_target_pairs={{0,1},{1,0},{2,3},{3,2},{4,5},{5,4},{6,7},{7,6},{8,9},{9,8},{10,11... | collective-permute-start | bytes 1376264 | tf_op jit(solution)/shard_map/ppermute | solution.py:327
  68.6 17.3 %collective-permute-start.16 = (bf16[256,2432]{1,0:T(8,128)(2,1)S(1)}, bf16[256,2432]{1,0:T(8,128)(2,1)S(1)}, u32[]{:S(2)}, u32[]{:S(2)}) collective-permute-start(bf16[256,2432]{1,0:T(8,128)(2,1)S(1)} %get-tuple-element.36), channel_id=1, source_target_pairs={{0,16},{1,5},{2,18},{3,7},{4,20},{5,9},{6,22},{7,11},{8,24},{9,13}... | collective-permute-start | bytes 3735560 | tf_op jit(solution)/shard_map/ppermute | solution.py:309
  68.8 17.6 %collective-permute-start.18 = (bf16[256,2304]{1,0:T(8,128)(2,1)S(1)}, bf16[256,2304]{1,0:T(8,128)(2,1)S(1)}, u32[]{:S(2)}, u32[]{:S(2)}) collective-permute-start(bf16[256,2304]{1,0:T(8,128)(2,1)S(1)} %get-tuple-element.38), channel_id=1, source_target_pairs={{0,48},{1,13},{2,50},{3,15},{4,52},{5,1},{6,54},{7,3},{8,56},{9,5}... | collective-permute-start | bytes 3538952 | tf_op jit(solution)/shard_map/ppermute | solution.py:309
  72.8 25.8 %collective-permute-start.14 = (bf16[256,2432]{1,0:T(8,128)(2,1)S(1)}, bf16[256,2432]{1,0:T(8,128)(2,1)S(1)}, u32[]{:S(2)}, u32[]{:S(2)}) collective-permute-start(bf16[256,2432]{1,0:T(8,128)(2,1)S(1)} %get-tuple-element.33), channel_id=1, source_target_pairs={{0,48},{1,13},{2,50},{3,15},{4,52},{5,1},{6,54},{7,3},{8,56},{9,5}... | collective-permute-start | bytes 3735560 | tf_op jit(solution)/shard_map/ppermute | solution.py:309
  72.9 25.7 %collective-permute-start.15 = (bf16[256,2304]{1,0:T(8,128)(2,1)S(1)}, bf16[256,2304]{1,0:T(8,128)(2,1)S(1)}, u32[]{:S(2)}, u32[]{:S(2)}) collective-permute-start(bf16[256,2304]{1,0:T(8,128)(2,1)S(1)} %get-tuple-element.34), channel_id=1, source_target_pairs={{0,16},{1,5},{2,18},{3,7},{4,20},{5,9},{6,22},{7,11},{8,24},{9,13}... | collective-permute-start | bytes 3538952 | tf_op jit(solution)/shard_map/ppermute | solution.py:309
  86.2 19.0 %collective-permute-start.20 = (bf16[128,2432]{1,0:T(8,128)(2,1)S(1)}, bf16[128,2432]{1,0:T(8,128)(2,1)S(1)}, u32[]{:S(2)}, u32[]{:S(2)}) collective-permute-start(bf16[128,2432]{1,0:T(8,128)(2,1)S(1)} %get-tuple-element.49), channel_id=1, source_target_pairs={{0,16},{1,5},{2,18},{3,7},{4,20},{5,9},{6,22},{7,11},{8,24},{9,13}... | collective-permute-start | bytes 1867784 | tf_op jit(solution)/shard_map/ppermute | solution.py:309
  86.3 26.1 %collective-permute-start.17 = (bf16[128,2432]{1,0:T(8,128)(2,1)S(1)}, bf16[128,2432]{1,0:T(8,128)(2,1)S(1)}, u32[]{:S(2)}, u32[]{:S(2)}) collective-permute-start(bf16[128,2432]{1,0:T(8,128)(2,1)S(1)} %get-tuple-element.50), channel_id=1, source_target_pairs={{0,16},{1,5},{2,18},{3,7},{4,20},{5,9},{6,22},{7,11},{8,24},{9,13}... | collective-permute-start | bytes 1867784 | tf_op jit(solution)/shard_map/ppermute | solution.py:309
  86.7 17.5 %collective-permute-start.21 = (bf16[128,2304]{1,0:T(8,128)(2,1)S(1)}, bf16[128,2304]{1,0:T(8,128)(2,1)S(1)}, u32[]{:S(2)}, u32[]{:S(2)}) collective-permute-start(bf16[128,2304]{1,0:T(8,128)(2,1)S(1)} %get-tuple-element.51), channel_id=1, source_target_pairs={{0,48},{1,13},{2,50},{3,15},{4,52},{5,1},{6,54},{7,3},{8,56},{9,5}... | collective-permute-start | bytes 1769480 | tf_op jit(solution)/shard_map/ppermute | solution.py:309
  98.6 11.9 %collective-permute-start.19 = (bf16[128,2304]{1,0:T(8,128)(2,1)S(1)}, bf16[128,2304]{1,0:T(8,128)(2,1)S(1)}, u32[]{:S(2)}, u32[]{:S(2)}) collective-permute-start(bf16[128,2304]{1,0:T(8,128)(2,1)S(1)} %get-tuple-element.52), channel_id=1, source_target_pairs={{0,48},{1,13},{2,50},{3,15},{4,52},{5,1},{6,54},{7,3},{8,56},{9,5}... | collective-permute-start | bytes 1769480 | tf_op jit(solution)/shard_map/ppermute | solution.py:309
  105.7 15.0 %collective-permute-start.22 = (bf16[64,4736]{1,0:T(8,128)(2,1)S(1)}, bf16[64,4736]{1,0:T(8,128)(2,1)S(1)}, u32[]{:S(2)}, u32[]{:S(2)}) collective-permute-start(bf16[64,4736]{1,0:T(8,128)(2,1)S(1)} %get-tuple-element.40), channel_id=1, source_target_pairs={{0,4},{1,17},{2,6},{3,19},{4,8},{5,21},{6,10},{7,23},{8,12},{9,25}... | collective-permute-start | bytes 1818632 | tf_op jit(solution)/shard_map/ppermute | solution.py:309
  106.3 7.7 %copy-start.3 = (bf16[2304,448]{0,1:T(8,128)(2,1)S(1)}, bf16[2304,448]{0,1:T(8,128)(2,1)}, u32[]{:S(2)}) copy-start(bf16[2304,448]{0,1:T(8,128)(2,1)} %param.23) | copy-start | bytes 6193156
  106.3 19.3 %collective-permute-start.24 = (bf16[64,4736]{1,0:T(8,128)(2,1)S(1)}, bf16[64,4736]{1,0:T(8,128)(2,1)S(1)}, u32[]{:S(2)}, u32[]{:S(2)}) collective-permute-start(bf16[64,4736]{1,0:T(8,128)(2,1)S(1)} %get-tuple-element.42), channel_id=1, source_target_pairs={{0,8},{1,33},{2,10},{3,35},{4,12},{5,37},{6,14},{7,39},{8,0},{9,41... | collective-permute-start | bytes 1818632 | tf_op jit(solution)/shard_map/ppermute | solution.py:309
  112.9 13.4 %collective-permute-start.23 = (bf16[64,4736]{1,0:T(8,128)(2,1)S(1)}, bf16[64,4736]{1,0:T(8,128)(2,1)S(1)}, u32[]{:S(2)}, u32[]{:S(2)}) collective-permute-start(bf16[64,4736]{1,0:T(8,128)(2,1)S(1)} %get-tuple-element.41), channel_id=1, source_target_pairs={{0,12},{1,49},{2,14},{3,51},{4,0},{5,53},{6,2},{7,55},{8,4},{9,57}... | collective-permute-start | bytes 1818632 | tf_op jit(solution)/shard_map/ppermute | solution.py:309
  114.1 41.0 %collective-permute-start.29 = (bf16[2304,448]{0,1:T(8,128)(2,1)S(1)}, bf16[2304,448]{0,1:T(8,128)(2,1)}, u32[]{:S(2)}, u32[]{:S(2)}) collective-permute-start(bf16[2304,448]{0,1:T(8,128)(2,1)S(1)} %copy-done.3), channel_id=1, source_target_pairs={{0,1},{1,0},{2,3},{3,2},{4,5},{5,4},{6,7},{7,6},{8,9},{9,8},{10,11... | collective-permute-start | bytes 6193160 | tf_op jit(solution)/shard_map/ppermute | solution.py:327
  126.9 4.5 %collective-permute-start.25 = (bf16[32,4608]{1,0:T(8,128)(2,1)S(1)}, bf16[32,4608]{1,0:T(8,128)(2,1)S(1)}, u32[]{:S(2)}, u32[]{:S(2)}) collective-permute-start(bf16[32,4608]{1,0:T(8,128)(2,1)S(1)} %get-tuple-element.44), channel_id=1, source_target_pairs={{0,1},{1,0},{2,3},{3,2},{4,5},{5,4},{6,7},{7,6},{8,9},{9,8},{10,11... | collective-permute-start | bytes 884744 | tf_op jit(solution)/shard_map/ppermute | solution.py:327
  131.5 9.2 %collective-permute-start.27 = (bf16[32,4608]{1,0:T(8,128)(2,1)S(1)}, bf16[32,4608]{1,0:T(8,128)(2,1)S(1)}, u32[]{:S(2)}, u32[]{:S(2)}) collective-permute-start(bf16[32,4608]{1,0:T(8,128)(2,1)S(1)} %activate.1.refs_0_), channel_id=1, source_target_pairs={{0,48},{1,13},{2,50},{3,15},{4,52},{5,1},{6,54},{7,3},{8,56},{9,5}... | collective-permute-start | bytes 884744 | tf_op jit(solution)/shard_map/ppermute | solution.py:309
  133.8 7.4 %collective-permute-start.28 = (bf16[32,4608]{1,0:T(8,128)(2,1)S(1)}, bf16[32,4608]{1,0:T(8,128)(2,1)S(1)}, u32[]{:S(2)}, u32[]{:S(2)}) collective-permute-start(bf16[32,4608]{1,0:T(8,128)(2,1)S(1)} %activate.1.refs_0_), channel_id=1, source_target_pairs={{0,32},{1,9},{2,34},{3,11},{4,36},{5,13},{6,38},{7,15},{8,40},{9,1... | collective-permute-start | bytes 884744 | tf_op jit(solution)/shard_map/ppermute | solution.py:309
  133.8 10.9 %collective-permute-start.26 = (bf16[32,4608]{1,0:T(8,128)(2,1)S(1)}, bf16[32,4608]{1,0:T(8,128)(2,1)S(1)}, u32[]{:S(2)}, u32[]{:S(2)}) collective-permute-start(bf16[32,4608]{1,0:T(8,128)(2,1)S(1)} %activate.1.refs_0_), channel_id=1, source_target_pairs={{0,16},{1,5},{2,18},{3,7},{4,20},{5,9},{6,22},{7,11},{8,24},{9,13}... | collective-permute-start | bytes 884744 | tf_op jit(solution)/shard_map/ppermute | solution.py:309
  141.3 10.2 %collective-permute-start.33 = (bf16[64,4608]{1,0:T(8,128)(2,1)S(1)}, bf16[64,4608]{1,0:T(8,128)(2,1)}, u32[]{:S(2)}, u32[]{:S(2)}) collective-permute-start(bf16[64,4608]{1,0:T(8,128)(2,1)S(1)} %join.8.refs_1_), channel_id=1, source_target_pairs={{0,12},{1,49},{2,14},{3,51},{4,0},{5,53},{6,2},{7,55},{8,4},{9,57}... | collective-permute-start | bytes 1769480 | tf_op jit(solution)/shard_map/ppermute | solution.py:309
  144.7 10.4 %collective-permute-start.30 = (bf16[64,4608]{1,0:T(8,128)(2,1)S(1)}, bf16[64,4608]{1,0:T(8,128)(2,1)}, u32[]{:S(2)}, u32[]{:S(2)}) collective-permute-start(bf16[64,4608]{1,0:T(8,128)(2,1)S(1)} %join.7.refs_0_), channel_id=1, source_target_pairs={{0,4},{1,17},{2,6},{3,19},{4,8},{5,21},{6,10},{7,23},{8,12},{9,25}... | collective-permute-start | bytes 1769480 | tf_op jit(solution)/shard_map/ppermute | solution.py:309
  144.8 16.6 %collective-permute-start.31 = (bf16[64,4608]{1,0:T(8,128)(2,1)S(1)}, bf16[64,4608]{1,0:T(8,128)(2,1)}, u32[]{:S(2)}, u32[]{:S(2)}) collective-permute-start(bf16[64,4608]{1,0:T(8,128)(2,1)S(1)} %join.8.refs_1_), channel_id=1, source_target_pairs={{0,4},{1,17},{2,6},{3,19},{4,8},{5,21},{6,10},{7,23},{8,12},{9,25}... | collective-permute-start | bytes 1769480 | tf_op jit(solution)/shard_map/ppermute | solution.py:309
  144.9 16.6 %collective-permute-start.32 = (bf16[64,4608]{1,0:T(8,128)(2,1)S(1)}, bf16[64,4608]{1,0:T(8,128)(2,1)}, u32[]{:S(2)}, u32[]{:S(2)}) collective-permute-start(bf16[64,4608]{1,0:T(8,128)(2,1)S(1)} %join.7.refs_0_), channel_id=1, source_target_pairs={{0,12},{1,49},{2,14},{3,51},{4,0},{5,53},{6,2},{7,55},{8,4},{9,57}... | collective-permute-start | bytes 1769480 | tf_op jit(solution)/shard_map/ppermute | solution.py:309
  151.5 13.0 %collective-permute-start.35 = (bf16[64,4608]{1,0:T(8,128)(2,1)}, bf16[64,4608]{1,0:T(8,128)(2,1)}, u32[]{:S(2)}, u32[]{:S(2)}) collective-permute-start(bf16[64,4608]{1,0:T(8,128)(2,1)} %collective-permute-done.33.refs_3_), channel_id=1, source_target_pairs={{0,12},{1,49},{2,14},{3,51},{4,0},{5,53},{6,2},{7,55},{8,4},{9,57}... | collective-permute-start | bytes 1769480 | tf_op jit(solution)/shard_map/ppermute | solution.py:309
  155.1 12.6 %collective-permute-start.34 = (bf16[64,4608]{1,0:T(8,128)(2,1)}, bf16[64,4608]{1,0:T(8,128)(2,1)}, u32[]{:S(2)}, u32[]{:S(2)}) collective-permute-start(bf16[64,4608]{1,0:T(8,128)(2,1)} %collective-permute-done.30.refs_0_), channel_id=1, source_target_pairs={{0,4},{1,17},{2,6},{3,19},{4,8},{5,21},{6,10},{7,23},{8,12},{9,25}... | collective-permute-start | bytes 1769480 | tf_op jit(solution)/shard_map/ppermute | solution.py:309
  155.1 1.9 copy-start.7
  192.9 5.5 %collective-permute-start.36 = (bf16[2,8,7168]{2,1,0:T(8,128)(2,1)S(1)}, bf16[2,8,7168]{2,1,0:T(8,128)(2,1)S(1)}, u32[]{:S(2)}, u32[]{:S(2)}) collective-permute-start(bf16[2,8,7168]{2,1,0:T(8,128)(2,1)S(1)} %reshape.90), channel_id=1, source_target_pairs={{0,1},{1,0},{2,3},{3,2},{4,5},{5,4},{6,7},{7,6},{8,9},{9,8},{10,11... | collective-permute-start | bytes 688136 | tf_op jit(solution)/shard_map/ppermute | solution.py:327
